TPU v7x, 32 devices: a whole 2x2x4 slice. The times are simulated.
32 devices in a mesh: seq: 4 (over y, core), item: 8 (over z, x).
Axes of the slice: x: 2, y: 2, z: 4, core: 2. Of those that a mesh axis runs over, the one named last changes fastest.
Arguments:
- events: float32 [8, 512, 512], P('item', 'seq'), may hold values from -6 to 6
- w_uvqk: float32 [512, 2048], replicated, may hold values from -0.25 to 0.25
- out_gain: float32 [512], replicated, may hold values from 0.5 to 1.5
- w_out: float32 [512, 512], replicated, may hold values from -0.25 to 0.25
- item_table: float32 [8192, 512], P('item'), may hold values from -0.25 to 0.25
- user_lengths: int32 [8, 4], P('item'), may hold values from 1 to 256, 512 in all within a row
- neg_ids: int32 [4, 512], replicated, may hold values from 0 to 1023
- panel_owner: int32 [4], replicated, may hold values from 0 to 7
- block_mask: int32 [8, 4], P('item', 'seq'), may hold values from 1 to 65535
- targets: int32 [8, 512], P('item', 'seq'), may hold values from 0 to 2047
Outputs:
- mean_loss: float32 [], replicated
- event_grad: float32 [8, 512, 512], P('item', 'seq')
- table_grad: float32 [8192, 512], P('item')
Inputs may be any that keep to these rules, and one draw needn't show every extreme that they name: `user_lengths`: the 4 lengths of a group sum to 512, the longest is exactly 256. `neg_ids`: rows may repeat within and across panels. `panel_owner`: several panels may have one owner. `block_mask`: bit k of an entry admits negative columns 128 k to 128 k + 127 for the 128 events of that block.
All inputs are finite; a program needn't handle non-finite values.
Results may differ from a plain program's by a relative error of at most 0.0003.
Values sent between devices are 32-bit elements; how exact they have to be, the bound alone decides.
No kernel may reach another device: no remote copies, remote signals or barrier semaphores. Data moves between devices by JAX's collectives and lax.ppermute only.
A program may use at most 64 MiB of HBM per device.

v0:
```python
import jax
import jax.numpy as jnp
from jax import lax
from jax.sharding import PartitionSpec as P

H = 16


highest = lax.Precision.HIGHEST
beta_weight = 0.75
epsilon = 1e-05


def broadcast(shard, axis, root):
    mine = lax.axis_index(axis) == root
    return lax.psum(jnp.where(mine, shard, jnp.zeros_like(shard)), axis)


def user_index(lengths, positions):
    user_ends = jnp.cumsum(lengths)
    return jnp.sum((positions[:, None] >= user_ends[None, :]).astype(jnp.int32), axis=1)


def pointwise(query_rows, key_rows, value_rows, query_pos, key_pos, query_user, key_user):
    scores = jnp.einsum("qhd,khd->hqk", query_rows, key_rows, precision=highest)
    allowed = (query_user[:, None] == key_user[None, :]) & (query_pos[:, None] >= key_pos[None, :])
    weights = jax.nn.silu(scores) * allowed[None, :, :].astype(jnp.float32)
    return jnp.einsum("hqk,khd->qhd", weights, value_rows, precision=highest)


def loss_terms(outputs, negatives, mask_words, target_cols):
    logits = jnp.einsum("td,nd->tn", outputs, negatives, precision=highest)
    columns = jnp.arange(negatives.shape[0], dtype=jnp.int32)
    mask_bits = jnp.repeat(mask_words, 128)
    live_cols = jnp.bitwise_and(
        jnp.right_shift(mask_bits[:, None], columns[None, :] // 128), 1
    ).astype(jnp.float32)
    is_target = (columns[None, :] == target_cols[:, None]).astype(jnp.float32)
    neg_weight = live_cols * (1.0 - is_target)
    loss_part = jnp.sum(
        beta_weight * is_target * jax.nn.softplus(-logits) + neg_weight * jax.nn.softplus(logits)
    )
    grad_logits = neg_weight * jax.nn.sigmoid(logits) - beta_weight * is_target * jax.nn.sigmoid(
        -logits
    )
    grad_rows = jnp.dot(grad_logits, negatives, precision=highest)
    panel_part = jnp.einsum("tn,td->nd", grad_logits, outputs, precision=highest)
    return (loss_part, grad_rows, panel_part)


def per_device(
    events,
    w_uvqk,
    out_gain,
    w_out,
    item_table,
    user_lengths,
    neg_ids,
    panel_owner,
    block_mask,
    targets,
):
    rows_in = events[0]
    tok_rows, width = rows_in.shape
    head_size = width // H
    lengths = user_lengths[0]
    projected = jax.nn.silu(jnp.dot(rows_in, w_uvqk, precision=highest))
    gates_u = projected[:, :width]
    packed = projected[:, width:].reshape(tok_rows, 3, H, head_size)
    spread = lax.all_to_all(packed, "seq", split_axis=2, concat_axis=0, tiled=True)
    group_len = spread.shape[0]
    positions = jnp.arange(group_len, dtype=jnp.int32)
    user_ids = user_index(lengths, positions)
    block_rows = 512

    def one_block(first_row):
        query_rows = lax.dynamic_slice_in_dim(spread[:, 1], first_row, block_rows, 0)
        query_pos = first_row + jnp.arange(block_rows, dtype=jnp.int32)
        query_user = lax.dynamic_slice_in_dim(user_ids, first_row, block_rows, 0)
        return pointwise(
            query_rows, spread[:, 2], spread[:, 0], query_pos, positions, query_user, user_ids
        )

    firsts = jnp.arange(group_len // block_rows, dtype=jnp.int32) * block_rows
    attended = lax.map(one_block, firsts).reshape(group_len, spread.shape[2], head_size)
    attended = lax.all_to_all(attended, "seq", split_axis=0, concat_axis=1, tiled=True)
    attended = attended.reshape(tok_rows, width)
    row_mean = jnp.mean(attended, axis=1, keepdims=True)
    centered = attended - row_mean
    variance = jnp.mean(centered * centered, axis=1, keepdims=True)
    normed = centered * lax.rsqrt(variance + epsilon) * out_gain
    outputs = rows_in + jnp.dot(normed * gates_u, w_out, precision=highest)
    panel_list = []
    for panel_index in range(neg_ids.shape[0]):
        local_rows = item_table[neg_ids[panel_index]]
        panel_list.append(broadcast(local_rows, "item", panel_owner[panel_index]))
    negatives = jnp.concatenate(panel_list, axis=0)
    loss_part, grad_rows, panel_part = loss_terms(outputs, negatives, block_mask[0], targets[0])
    panel_total, loss_total = lax.psum((panel_part, loss_part), ("seq", "item"))
    owned_panels = (panel_owner == lax.axis_index("item")).astype(jnp.float32)
    owned_rows = jnp.repeat(owned_panels, neg_ids.shape[1])
    table_grad = (
        jnp.zeros_like(item_table).at[neg_ids.reshape(-1)].add(panel_total * owned_rows[:, None])
    )
    event_total = tok_rows * lax.axis_size("seq") * lax.axis_size("item")
    return (loss_total / event_total, grad_rows[None], table_grad)


def solution(mesh):
    placed = (
        P("item", "seq", None),
        P(),
        P(),
        P(),
        P("item", None),
        P("item", None),
        P(),
        P(),
        P("item", "seq"),
        P("item", "seq"),
    )
    return jax.shard_map(
        per_device,
        mesh=mesh,
        in_specs=placed,
        out_specs=(P(), P("item", "seq", None), P("item", None)),
        check_vma=False,
    )
```

profile of v0, /device:TPU:0, one launch (start us, length us, event | category | flops | bytes accessed | tf_op | source)
XLA Modules:
  0.0 368.0 jit_solution(10556521376840838242)
XLA Ops:
  7.2 0.0 copy-start
  7.2 0.0 all-reduce.6.cloned.1.call-start
  7.2 0.9 compare_select_fusion.3
  8.1 1.5 fusion.45
  9.6 0.0 copy-done
  9.6 1.6 gather_fusion
  11.3 2.3 gather_fusion.1
  14.9 2.3 gather_fusion.2
  17.9 2.3 gather_fusion.3
  20.9 0.0 copy-start.1
  20.9 0.0 copy-start.2
  20.9 1.1 broadcast_select_fusion.3
  22.0 1.1 broadcast_select_fusion.2
  23.1 0.0 copy-done.1
  23.1 1.1 broadcast_select_fusion.1
  24.2 1.1 broadcast_select_fusion
  25.2 0.0 all-reduce.6.cloned.1.call-update
  25.3 4.6 %divide_multiply_fusion = f32[128,2048]{1,0:T(8,128)S(1)} fusion(f32[512,2048]{1,0:T(8,128)} %param.11, f32[1,128,512]{2,1,0:T(8,128)S(1)} %copy-done.7), kind=kOutput, calls=%fused_computation.32 | convolution fusion | flops 1611661312 | bytes 5505024 | tf_op jit(solution)/shard_map/dot_general | solution.py:67
  29.9 0.0 copy-start.3
  29.9 1.0 copy-done.3
  30.8 1.0 slice.63
  31.8 1.4 copy.31
  33.2 0.9 copy.32
  34.2 4.2 %all-to-all-start = ((f32[128,3,16,32]{0,3,1,2:T(8,128)}), f32[128,3,16,32]{0,3,1,2:T(8,128)S(1)}, u32[]{:S(2)}, u32[]{:S(2)}) async-start(f32[128,3,16,32]{0,3,1,2:T(8,128)} %copy.32), calls=%async_computation | async-start | bytes 1572864 | tf_op jit(solution)/shard_map/all_to_all | solution.py:70
  38.4 0.2 reduce-window.8
  38.6 0.1 convert_reduce_fusion
  38.7 1.3 fusion.21
  40.0 10.2 %all-to-all-done = f32[128,3,16,32]{0,3,1,2:T(8,128)S(1)} async-done(((f32[128,3,16,32]{0,3,1,2:T(8,128)}), f32[128,3,16,32]{0,3,1,2:T(8,128)S(1)}, u32[]{:S(2)}, u32[]{:S(2)}) %all-to-all-start) | async-done | bytes 786464 | tf_op jit(solution)/shard_map/all_to_all | solution.py:70
  50.1 1.4 copy.43
  51.5 1.4 all_to_all.27
  53.0 0.0 copy-start.6
  53.0 3.5 fusion.22
  56.5 4.4 %fusion.12 = f32[512,4,32]{0,2,1:T(8,128)S(1)} fusion(f32[4,512,512]{2,1,0:T(8,128)S(1)} %fusion.22, f32[512,512]{1,0:T(8,128)S(1)} %copy-done.6, f32[512,3,4,32]{0,3,2,1:T(8,128)S(1)} %all_to_all.27), kind=kOutput, calls=%fused_computation.22 | convolution fusion | flops 407896064 | bytes 5767168 | tf_op jit(solution)/shard_map/while/body/eval_jaxpr/hqk,khd->qhd/dot_general | solution.py:28
  60.9 0.4 copy.34
  61.3 0.0 copy-start.11
  61.3 1.4 reshape.336
  62.7 3.4 all-to-all-start.1
  66.1 0.3 all-reduce.4.cloned.1.call-start
  67.0 5.1 %all-to-all-done.1 = f32[4,1,16384]{2,1,0:T(1,128)S(1)} async-done(((f32[4,1,16384]{2,1,0:T(1,128)}), f32[4,1,16384]{2,1,0:T(1,128)S(1)}, u32[]{:S(2)}, u32[]{:S(2)}) %all-to-all-start.1) | async-done | bytes 262176 | tf_op jit(solution)/shard_map/all_to_all | solution.py:86
  72.1 0.5 broadcast.229
  72.6 1.4 reduce.5
  74.0 0.6 reshape.337
  74.5 1.0 copy.36
  75.5 1.1 copy.37
  76.6 1.0 copy.38
  77.7 1.0 reduce_sum.44
  78.7 1.1 fusion.24
  79.8 2.1 convolution_add_fusion
  81.9 104.8 %all-reduce.6.cloned.1.call-done = (f32[512,512]{1,0:T(8,128)}, f32[512,512]{1,0:T(8,128)}, f32[512,512]{1,0:T(8,128)}, f32[512,512]{1,0:T(8,128)}) async-done(((f32[512,512]{1,0:T(8,128)}, f32[512,512]{1,0:T(8,128)}, f32[512,512]{1,0:T(8,128)}, f32[512,512]{1,0:T(8,128)}), (f32[512,512]{1,0:T(8,128)}, f32[512,512]{1,0:T(8,128)}, f32[512,512]{1,0:T(8,128)}, ...) | async-done | bytes 4194320 | tf_op jit(solution)/shard_map/psum | solution.py:16
  186.7 1.4 constant_dynamic-update-slice_fusion.3
  188.1 1.3 constant_dynamic-update-slice_fusion.2
  189.5 0.1 constant_dynamic-update-slice_fusion.1
  189.5 0.1 constant_dynamic-update-slice_fusion
  189.6 2.0 copy-done.8
  191.6 0.0 copy-done.13
  191.6 6.1 %fusion.16 = (f32[]{:T(128)}, f32[128,2048]{1,0:T(8,128)S(1)}) fusion(f32[2048]{0:T(1024)S(1)} %fusion.37, s32[128]{0:T(128)S(1)} %bitcast.89, f32[128,512]{1,0:T(8,128)S(1)} %convolution_add_fusion, f32[2048,512]{1,0:T(8,128)S(1)} %constant_dynamic-update-slice_fusion), kind=kOutput, calls=%fused_computation.25 | convolution fusion | flops 1616379904 | bytes 5513732 | tf_op jit(solution)/shard_map/td,nd->tn/dot_general | solution.py:32
  197.7 5.4 %fusion.42 = f32[2048,512]{1,0:T(8,128)} fusion(f32[128,512]{1,0:T(8,128)S(1)} %convolution_add_fusion, f32[128,2048]{1,0:T(8,128)S(1)} %get-tuple-element.31, f32[2048]{0:T(1024)S(1)} %fusion.37, s32[128]{0:T(128)S(1)} %bitcast.90), kind=kOutput, calls=%fused_computation.88 | convolution fusion | flops 1614020608 | bytes 5513728 | tf_op jit(solution)/shard_map/tn,td->nd/dot_general | solution.py:47
  203.2 0.0 all-reduce.4.cloned.1.call-update
  203.2 0.7 copy-done.9
  203.9 0.1 broadcast_bitcast_fusion
  204.0 39.9 %psum.46 = f32[]{:T(128)} all-reduce(f32[]{:T(128)} %get-tuple-element.30), channel_id=1, replica_groups=mesh['seq'=4,'item'=8] {'seq','item'}, use_global_device_ids=true, to_apply=%region_10.11 | all-reduce | flops 1 | bytes 8 | tf_op jit(solution)/shard_map/psum | solution.py:99
  244.6 5.8 %convolution_bitcast_fusion = f32[1,128,512]{2,1,0:T(8,128)} fusion(f32[2048,512]{1,0:T(8,128)} %copy-done.8, f32[128,2048]{1,0:T(8,128)S(1)} %get-tuple-element.31, f32[2048]{0:T(1024)S(1)} %fusion.37, s32[128]{0:T(128)S(1)} %bitcast.91), kind=kOutput, calls=%fused_computation.21 | convolution fusion | flops 1614020608 | bytes 5513728 | tf_op jit(solution)/shard_map/dot_general | solution.py:46
  250.4 93.9 %all-reduce.4.cloned.1.call-done = f32[2048,512]{1,0:T(8,128)} async-done(((f32[2048,512]{1,0:T(8,128)}), f32[2048,512]{1,0:T(8,128)}) %all-reduce.4.cloned.1.call-update) | async-done | bytes 4194320 | tf_op jit(solution)/shard_map/psum | solution.py:99
  344.3 15.7 %scatter_custom_fusion = f32[1024,512]{1,0:T(8,128)} fusion(s32[2048]{0:T(1024)S(1)} %bitcast.82, f32[2048,512]{1,0:T(8,128)} %all-reduce.4.cloned.1.call-done, f32[2048]{0:T(1024)S(1)} %bitcast.79, f32[]{:T(128)} %constant.40.clone.1), kind=kCustom, calls=%fused_computation.5 | custom fusion | flops 2097152 | bytes 6299652 | tf_op jit(solution)/shard_map/scatter-add | solution.py:103
  (26 shorter events, 0.1 us)
Async XLA Ops:
  7.2 2.5 copy-start
  7.2 179.5 %all-reduce.6.cloned.1.call-start = ((), (), s32[]{:S(2)}) async-start(), calls=%async_computation.3 | async-start | bytes 8388608 | tf_op jit(solution)/shard_map/psum | solution.py:16
  20.9 2.2 copy-start.1
  20.9 3.3 copy-start.2
  23.1 2.2 copy-start.7
  29.9 1.0 copy-start.3
  30.8 7.6 %copy-start.12 = (s32[1,4]{1,0:T(1,128)S(1)}, s32[1,4]{1,0:T(1,128)}, u32[]{:S(2)}) copy-start(s32[1,4]{1,0:T(1,128)} %param.15) | copy-start | bytes 52
  34.2 15.9 %all-to-all-start = ((f32[128,3,16,32]{0,3,1,2:T(8,128)}), f32[128,3,16,32]{0,3,1,2:T(8,128)S(1)}, u32[]{:S(2)}, u32[]{:S(2)}) async-start(f32[128,3,16,32]{0,3,1,2:T(8,128)} %copy.32), calls=%async_computation | async-start | bytes 1572864 | tf_op jit(solution)/shard_map/all_to_all | solution.py:70
  53.0 3.5 copy-start.6
  61.3 18.6 %copy-start.11 = (f32[512]{0:T(512)S(1)}, f32[512]{0:T(512)}, u32[]{:S(2)}) copy-start(f32[512]{0:T(512)} %param.12) | copy-start | bytes 6148
  62.7 9.4 %all-to-all-start.1 = ((f32[4,1,16384]{2,1,0:T(1,128)}), f32[4,1,16384]{2,1,0:T(1,128)S(1)}, u32[]{:S(2)}, u32[]{:S(2)}) async-start(f32[4,1,16384]{2,1,0:T(1,128)} %reshape.336), calls=%async_computation.1 | async-start | bytes 524288 | tf_op jit(solution)/shard_map/all_to_all | solution.py:86
  66.1 278.3 %all-reduce.4.cloned.1.call-start = ((), (), s32[]{:S(2)}) async-start(), calls=%async_computation.2 | async-start | bytes 8388608 | tf_op jit(solution)/shard_map/psum | solution.py:99
  186.7 2.8 copy-start.5
  186.7 2.8 copy-start.4
  186.7 4.9 %copy-start.13 = (s32[1,128]{1,0:T(1,128)S(1)}, s32[1,128]{1,0:T(1,128)}, u32[]{:S(2)}) copy-start(s32[1,128]{1,0:T(1,128)} %param.19) | copy-start | bytes 1540
  189.6 2.0 copy-start.8
  203.1 0.7 copy-start.9
  203.2 0.7 copy-start.10
Sparse Core Ops, SparseCore 0:
  25.4 161.2 all-reduce.5
  203.3 140.9 all-reduce.3
where the time goes:
time: 368 us
  waiting for transfers between devices  214 us (58%)
  blocking collectives  39.9 us (11%)
  matrix products  32 us (9%)
  local copies, waits for them, and re-layouts  28.8 us (8%)
  other arithmetic  26.1 us (7%)
  between operations  19.3 us (5%)
  starting transfers between devices  7.94 us (2%)
    psum x1, waiting for transfers between devices, broadcast(): return lax.psum(jnp.where(mine, shard, jnp.zeros_like(shard)), axis)  105 us
    psum x1, waiting for transfers between devices, per_device(): panel_total, loss_total = lax.psum((panel_part, loss_part), ('seq', 'item'))  93.9 us
    psum x1, blocking collectives, per_device(): panel_total, loss_total = lax.psum((panel_part, loss_part), ('seq', 'item'))  39.9 us
    scatter-add x1, other arithmetic, per_device(): jnp.zeros_like(item_table).at[neg_ids.reshape(-1)]  15.7 us
    all_to_all x1, waiting for transfers between devices, per_device(): lax.all_to_all(packed, 'seq', split_axis=2, concat_axis=0, tiled=True)  10.2 us
    gather x4, local copies, waits for them, and re-layouts, per_device(): local_rows = item_table[neg_ids[panel_index]]  8.64 us
    unnamed x36, local copies, waits for them, and re-layouts  8.46 us
  transfers between devices with their start and end apart: 4, of which 4 were waited for; matrix products, arithmetic and copies ran while one was open for 10% of the time, Pallas kernels for 0%

commit v1 on v0

v1 whole, which is shorter than its diff:
```python
import jax
import jax.numpy as jnp
from jax import lax
from jax.sharding import PartitionSpec as P

H = 16


high = lax.Precision.HIGH
beta_weight = 0.75
epsilon = 1e-05


def swap(block, axis, bit):
    size = lax.axis_size(axis)
    return lax.ppermute(block, axis, [(i, i ^ (1 << bit)) for i in range(size)])


def bits_of(size):
    return list(range(size.bit_length() - 1))[::-1]


def gather_steps(block, axis, bits):
    stacked, order = block[None], [0]
    for bit in bits:
        stacked = jnp.concatenate([stacked, swap(stacked, axis, bit)], axis=0)
        order = order + [r ^ (1 << bit) for r in order]
    return stacked, order


def reduce_steps(stacked, axis, bits):
    for bit in bits:
        half = stacked.shape[0] // 2
        stacked = stacked[:half] + swap(stacked[half:], axis, bit)
    return stacked[0]


def orders(bits):
    order = [0]
    for bit in bits:
        order = order + [r ^ (1 << bit) for r in order]
    return order


def per_device(
    events,
    w_uvqk,
    out_gain,
    w_out,
    item_table,
    user_lengths,
    neg_ids,
    panel_owner,
    block_mask,
    targets,
):
    rows_in = events[0]
    tok, width = rows_in.shape
    n_seq, n_item = lax.axis_size("seq"), lax.axis_size("item")
    s, i = lax.axis_index("seq"), lax.axis_index("item")
    group_len = tok * n_seq
    head_size = width // H
    seq_bits, item_bits = bits_of(n_seq), bits_of(n_item)
    seq_order, item_order = orders(seq_bits), orders(item_bits)
    seq_rel = s ^ jnp.array(seq_order, jnp.int32)
    item_rel = i ^ jnp.array(item_order, jnp.int32)

    flat_ids = neg_ids.reshape(-1)
    n_neg = flat_ids.shape[0] // n_seq
    per_panel = neg_ids.shape[1] // n_neg
    n_part = n_neg // n_item
    ids_by_seq = flat_ids.reshape(n_seq, n_neg)
    own_ids = ids_by_seq[s]
    root = panel_owner[s // per_panel]
    ids_rel = own_ids.reshape(n_item, n_part)[item_rel]
    part = item_table[ids_rel.reshape(-1)].reshape(n_item, n_part, width)
    for bit in item_bits[::-1]:
        half = part.shape[0] // 2
        other = swap(part[half:], "item", bit)
        part = jnp.where(((i ^ root) >> bit) & 1 == 0, part[:half], other)
    negatives, _ = gather_steps(part[0], "item", item_bits)
    negatives = negatives[item_rel_inverse(item_order, i)].reshape(n_neg, width)

    extra = jnp.zeros((8, width), jnp.float32)
    extra = extra.at[0, :tok].set(targets[0].astype(jnp.float32))
    extra = extra.at[1, : block_mask.shape[1]].set(block_mask[0].astype(jnp.float32))
    with_extra = jnp.concatenate([rows_in, extra], axis=0)
    group, _ = gather_steps(with_extra, "seq", seq_bits)
    group_events = group[:, :tok].reshape(group_len, width)
    group_targets = group[:, tok, :tok].astype(jnp.int32).reshape(-1)
    mask_words = group[:, tok + 1, : block_mask.shape[1]].astype(jnp.int32).reshape(-1)

    positions = (seq_rel[:, None] * tok + jnp.arange(tok, dtype=jnp.int32)[None, :]).reshape(-1)
    user_ends = jnp.cumsum(user_lengths[0])
    user_ids = jnp.sum((positions[:, None] >= user_ends[None, :]).astype(jnp.int32), axis=1)

    own = jax.nn.silu(
        jnp.dot(
            rows_in,
            jnp.concatenate([w_uvqk[:, :width], w_uvqk[:, 2 * width : 3 * width]], axis=1),
            precision=high,
        )
    )
    gates_u, queries = own[:, :width], own[:, width:].reshape(tok, H, head_size)
    values = jax.nn.silu(jnp.dot(group_events, w_uvqk[:, width : 2 * width], precision=high))
    keys = jax.nn.silu(jnp.dot(group_events, w_uvqk[:, 3 * width :], precision=high))
    values = values.reshape(group_len, H, head_size)
    keys = keys.reshape(group_len, H, head_size)
    scores = jnp.einsum("qhd,khd->hqk", queries, keys, precision=high)
    allowed = (user_ids[:tok, None] == user_ids[None, :]) & (
        positions[:tok, None] >= positions[None, :]
    )
    weights = jax.nn.silu(scores) * allowed[None, :, :].astype(jnp.float32)
    attended = jnp.einsum("hqk,khd->qhd", weights, values, precision=high).reshape(tok, width)
    row_mean = jnp.mean(attended, axis=1, keepdims=True)
    centered = attended - row_mean
    variance = jnp.mean(centered * centered, axis=1, keepdims=True)
    normed = centered * lax.rsqrt(variance + epsilon) * out_gain
    own_outputs = rows_in + jnp.dot(normed * gates_u, w_out, precision=high)
    outputs, _ = gather_steps(own_outputs, "seq", seq_bits)
    outputs = outputs.reshape(group_len, width)

    logits = jnp.einsum("td,nd->tn", outputs, negatives, precision=high)
    columns = s * n_neg + jnp.arange(n_neg, dtype=jnp.int32)
    mask_bits = jnp.repeat(mask_words, 128)
    live_cols = jnp.bitwise_and(
        jnp.right_shift(mask_bits[:, None], columns[None, :] // 128), 1
    ).astype(jnp.float32)
    is_target = (columns[None, :] == group_targets[:, None]).astype(jnp.float32)
    neg_weight = live_cols * (1.0 - is_target)
    loss_part = jnp.sum(
        beta_weight * is_target * jax.nn.softplus(-logits) + neg_weight * jax.nn.softplus(logits)
    )
    grad_logits = neg_weight * jax.nn.sigmoid(logits) - beta_weight * is_target * jax.nn.sigmoid(
        -logits
    )
    panel_part = jnp.einsum("td,tn->dn", outputs, grad_logits, precision=high)
    grad_rows = jnp.dot(grad_logits, negatives, precision=high)
    event_grad = reduce_steps(grad_rows.reshape(n_seq, tok, width), "seq", seq_bits[::-1])

    n_dim = width // (n_seq * n_item)
    panel_part = panel_part.reshape(n_seq, n_item, n_dim, n_neg)
    panel_part = panel_part.transpose(1, 0, 2, 3)[item_rel]
    panel_sum = reduce_steps(panel_part, "item", item_bits[::-1])
    panel_sum = panel_sum[seq_rel]
    moved = panel_sum[:, None]
    for bit in seq_bits[::-1]:
        half = moved.shape[0] // 2
        moved = jnp.concatenate([moved[:half], swap(moved[half:], "seq", bit)], axis=1)
    moved = moved[0]
    moved_order = orders(seq_bits[::-1])
    source_seq = s ^ jnp.array(moved_order, jnp.int32)
    rows = jnp.arange(item_table.shape[0], dtype=jnp.int32)
    hot = (ids_by_seq[source_seq][:, :, None] == rows[None, None, :]).astype(jnp.float32)
    spread = jnp.einsum("pdc,pcr->pdr", moved, hot, precision=high)
    owner = panel_owner[source_seq // per_panel]
    mine = (owner[None, :] == jnp.arange(n_item, dtype=jnp.int32)[:, None]).astype(jnp.float32)
    sent = jnp.sum(mine[:, :, None, None] * spread[None], axis=1)
    taken = lax.all_to_all(sent, "item", split_axis=0, concat_axis=0, tiled=True)
    quarter = taken.reshape(n_item * n_dim, -1).T
    table, _ = gather_steps(quarter, "seq", seq_bits)
    table_grad = jnp.concatenate(
        [table[k] for k in range(n_seq)], axis=1
    ).reshape(-1, n_seq, n_item * n_dim)[:, item_rel_inverse(seq_order, s)].reshape(-1, width)

    losses = lax.all_gather(jnp.full((8, 128), loss_part), ("seq", "item"))
    loss_total = jnp.sum(losses[:, 0, 0])
    return (loss_total / (group_len * n_item), event_grad[None], table_grad)


def item_rel_inverse(order, index):
    place = [0] * len(order)
    for k, r in enumerate(order):
        place[r] = k
    return jnp.array(place, jnp.int32)[index ^ jnp.arange(len(order), dtype=jnp.int32)]


def solution(mesh):
    placed = (
        P("item", "seq", None),
        P(),
        P(),
        P(),
        P("item", None),
        P("item", None),
        P(),
        P(),
        P("item", "seq"),
        P("item", "seq"),
    )
    return jax.shard_map(
        per_device,
        mesh=mesh,
        in_specs=placed,
        out_specs=(P(), P("item", "seq", None), P("item", None)),
        check_vma=False,
    )
```

time: 368 us -> 219 us (0.60)
  waiting for transfers between devices: 214 us -> 56.5 us
  blocking collectives: 39.9 us -> 57.9 us
  starting transfers between devices: 7.94 us -> 23.8 us
  between operations: 19.3 us -> 4.22 us
  other arithmetic: 26.1 us -> 16.9 us
  matrix products: 32 us -> 24.7 us
  local copies, waits for them, and re-layouts: 28.8 us -> 34.6 us
    psum x2 -> x0, waiting for transfers between devices: 199 us -> none  [the longest x1 105 us: broadcast(): return lax.psum(jnp.where(mine, shard, jnp.zeros_like(shard)), axis)]
    ppermute x0 -> x19, waiting for transfers between devices: none -> 56.5 us  [swap(): return lax.ppermute(block, axis, [(i, i ^ 1 << bit) for i in range(size)])]
    unnamed x0 -> x1, blocking collectives: none -> 40.3 us
    psum x1 -> x0, blocking collectives: 39.9 us -> none  [per_device(): panel_total, loss_total = lax.psum((panel_part, loss_part), ('seq', 'item'))]
    ppermute x0 -> x19, starting transfers between devices: none -> 23.8 us  [swap(): return lax.ppermute(block, axis, [(i, i ^ 1 << bit) for i in range(size)])]
    all_to_all x0 -> x1, blocking collectives: none -> 17.7 us  [per_device(): lax.all_to_all(sent, 'item', split_axis=0, concat_axis=0, tiled=True)]
    scatter-add x1 -> x0, other arithmetic: 15.7 us -> none  [per_device(): jnp.zeros_like(item_table).at[neg_ids.reshape(-1)]]
    all_to_all x2 -> x0, waiting for transfers between devices: 15.2 us -> none  [the longest x1 10.2 us: per_device(): lax.all_to_all(packed, 'seq', split_axis=2, concat_axis=0, tiled=True)]
  transfers between devices with their start and end apart: 4 -> 19, of which waited for: 4 -> 12; matrix products, arithmetic and copies ran while one was open for 10% -> 20% of each run, Pallas kernels for 0% -> 0%
where the time goes in v1:
time: 219 us
  blocking collectives  57.9 us (26%)
  waiting for transfers between devices  56.5 us (26%)
  local copies, waits for them, and re-layouts  34.6 us (16%)
  matrix products  24.7 us (11%)
  starting transfers between devices  23.8 us (11%)
  other arithmetic  16.9 us (8%)
  between operations  4.22 us (2%)
    ppermute x19, waiting for transfers between devices, swap(): return lax.ppermute(block, axis, [(i, i ^ 1 << bit) for i in range(size)])  56.5 us
    unnamed x1, blocking collectives  40.3 us
    ppermute x19, starting transfers between devices, swap(): return lax.ppermute(block, axis, [(i, i ^ 1 << bit) for i in range(size)])  23.8 us
    all_to_all x1, blocking collectives, per_device(): lax.all_to_all(sent, 'item', split_axis=0, concat_axis=0, tiled=True)  17.7 us
    concatenate x8, other arithmetic, gather_steps(): stacked = jnp.concatenate([stacked, swap(stacked, axis, bit)], axis=0)  7.96 us
    unnamed x47, local copies, waits for them, and re-layouts  7.09 us
    gather x2, local copies, waits for them, and re-layouts, per_device(): jnp.concatenate([table[k] for k in range(n_seq)], axis=1)  6.49 us
    dot_general x1, matrix products, per_device(): logits = jnp.einsum('td,nd->tn', outputs, negatives, precision=high)  4.95 us
  transfers between devices with their start and end apart: 19, of which 12 were waited for; matrix products, arithmetic and copies ran while one was open for 20% of the time, Pallas kernels for 0%

profile of v1, /device:TPU:0, one launch (start us, length us, event | category | flops | bytes accessed | tf_op | source)
XLA Modules:
  0.0 218.7 jit_solution(13659009521187345925)
XLA Ops:
  0.6 0.8 convert_element_type.52
  2.2 1.0 maximum_bitcast_fusion
  3.2 3.0 %collective-permute-start = (f32[1,136,512]{2,1,0:T(8,128)S(1)}, f32[1,136,512]{2,1,0:T(8,128)S(1)}, u32[]{:S(2)}, u32[]{:S(2)}) collective-permute-start(f32[1,136,512]{2,1,0:T(8,128)S(1)} %maximum_bitcast_fusion), channel_id=1, source_target_pairs={{0,16},{8,24},{16,0},{24,8},{1,17},{9,25},{17,1},{25,9},{2,18},{10... | collective-permute-start | bytes 835592 | tf_op jit(solution)/shard_map/ppermute | solution.py:16
  6.2 0.7 dynamic-slice_reduce_fusion
  7.0 0.7 compare_select_fusion.9
  8.3 2.3 %gather_fusion.1 = f32[512,512]{1,0:T(8,128)} fusion(f32[1024,512]{1,0:T(8,128)S(1)} %copy-done, s32[1024]{0:T(1024)S(1)} %pad_clamp_fusion.6), kind=kCustom, calls=%fused_computation.1 | custom fusion | bytes 2099200 | tf_op jit(solution)/shard_map/gather | solution.py:76
  10.7 2.2 %fusion.63 = (f32[256,512]{1,0:T(8,128)}, f32[256,512]{1,0:T(8,128)}) fusion(f32[512,512]{1,0:T(8,128)} %gather_fusion.1), kind=kLoop, calls=%fused_computation.138 | loop fusion | bytes 2097152 | tf_op jit(solution)/shard_map/slice | solution.py:79
  12.9 1.6 collective-permute-start.4
  14.5 3.0 %fusion.61 = (f32[512,512]{1,0:T(8,128)}, f32[512,512]{1,0:T(8,128)}) fusion(f32[512,2048]{1,0:T(8,128)} %param.20), kind=kLoop, calls=%fused_computation.136 | loop fusion | bytes 4194304 | tf_op jit(solution)/shard_map/slice | solution.py:100
  19.2 4.2 %divide_multiply_fusion.2 = f32[128,1024]{0,1:T(8,128)} fusion(f32[512,512]{1,0:T(8,128)} %get-tuple-element.34, f32[512,512]{1,0:T(8,128)} %get-tuple-element.33, f32[1,128,512]{2,1,0:T(8,128)S(1)} %copy-done.14), kind=kOutput, calls=%fused_computation.61 | convolution fusion | flops 403701760 | bytes 2883584 | tf_op jit(solution)/shard_map/dot_general | solution.py:98
  23.4 0.8 pad_maximum_fusion.5
  24.2 2.5 %collective-permute-done.4 = f32[4,64,512]{2,1,0:T(8,128)} collective-permute-done((f32[4,64,512]{2,1,0:T(8,128)}, f32[4,64,512]{2,1,0:T(8,128)}, u32[]{:S(2)}, u32[]{:S(2)}) %collective-permute-start.4) | collective-permute-done | bytes 524320 | tf_op jit(solution)/shard_map/ppermute | solution.py:16
  26.8 0.8 copy-done.5
  27.6 1.6 collective-permute-start.5
  29.3 0.6 gather_fusion.2
  30.0 5.7 %collective-permute-done.5 = f32[2,64,512]{2,1,0:T(8,128)} collective-permute-done((f32[2,64,512]{2,1,0:T(8,128)S(1)}, f32[2,64,512]{2,1,0:T(8,128)}, u32[]{:S(2)}, u32[]{:S(2)}) %collective-permute-start.5) | collective-permute-done | bytes 262176 | tf_op jit(solution)/shard_map/ppermute | solution.py:16
  35.7 1.0 slice_select_fusion
  36.7 2.7 %collective-permute-start.6 = (f32[1,64,512]{2,1,0:T(8,128)S(1)}, f32[1,64,512]{2,1,0:T(8,128)S(1)}, u32[]{:S(2)}, u32[]{:S(2)}) collective-permute-start(f32[1,64,512]{2,1,0:T(8,128)S(1)} %slice.224), channel_id=1, source_target_pairs={{0,4},{1,5},{2,6},{3,7},{4,0},{5,1},{6,2},{7,3},{8,12},{9,13},{10,... | collective-permute-start | bytes 393224 | tf_op jit(solution)/shard_map/ppermute | solution.py:16
  39.6 1.2 divide_multiply_fusion.1
  40.8 1.2 divide_multiply_fusion
  42.0 1.9 fusion.65
  43.9 2.8 %fusion.64 = (f32[128]{0:T(128)S(1)}, f32[16,32,128]{2,1,0:T(8,128)S(1)}) fusion(f32[512,16,32]{0,2,1:T(8,128)S(1)} %bitcast.124, f32[16,128,512]{2,1,0:T(8,128)S(1)} %fusion.65, f32[128,512]{1,0:T(8,128)S(1)} %and_convert_fusion), kind=kOutput, calls=%fused_computation.139 | convolution fusion | flops 206634880 | bytes 5767680 | tf_op jit(solution)/shard_map/hqk,khd->qhd/dot_general | solution.py:114
  47.0 2.0 collective-permute-start.7
  49.5 5.2 %collective-permute-done.7 = f32[1,64,512]{2,1,0:T(8,128)S(1)} collective-permute-done((f32[1,64,512]{2,1,0:T(8,128)S(1)}, f32[1,64,512]{2,1,0:T(8,128)S(1)}, u32[]{:S(2)}, u32[]{:S(2)}) %collective-permute-start.7) | collective-permute-done | bytes 131104 | tf_op jit(solution)/shard_map/ppermute | solution.py:16
  54.7 0.7 pad_maximum_fusion.8
  56.4 1.0 pad_maximum_fusion.6
  57.5 4.7 %collective-permute-done.8 = f32[2,64,512]{2,1,0:T(8,128)} collective-permute-done((f32[2,64,512]{2,1,0:T(8,128)}, f32[2,64,512]{2,1,0:T(8,128)}, u32[]{:S(2)}, u32[]{:S(2)}) %collective-permute-start.8) | collective-permute-done | bytes 262176 | tf_op jit(solution)/shard_map/ppermute | solution.py:16
  62.2 1.9 pad_maximum_fusion.7
  64.0 0.7 collective-permute-start.9
  65.0 1.1 pad_maximum_fusion.2
  66.1 1.3 copy.55
  67.4 8.0 %collective-permute-done.9 = f32[4,64,512]{2,1,0:T(8,128)} collective-permute-done((f32[4,64,512]{2,1,0:T(8,128)}, f32[4,64,512]{2,1,0:T(8,128)}, u32[]{:S(2)}, u32[]{:S(2)}) %collective-permute-start.9) | collective-permute-done | bytes 524320 | tf_op jit(solution)/shard_map/ppermute | solution.py:16
  75.4 1.3 pad_maximum_fusion.3
  76.7 1.6 gather_fusion.3
  78.3 4.9 %fusion.22 = (f32[]{:T(128)}, f32[512,512]{0,1:T(8,128)S(1)}) fusion(s32[512]{0:T(512)S(1)} %get-tuple-element.54, s32[512]{0:T(512)S(1)} %broadcast_bitcast_fusion, s32[512]{0:T(512)S(1)} %bitcast.119, s32[512]{0:T(512)S(1)} %get-tuple-element.55, f32[512,512]{1,0:T(8,128)} %bitcast.105, f32[512,512]{1,0:T(8,128)} %bitcast.110), kind=kOutput, calls=%fused_computation.41 | convolution fusion | flops 811859968 | bytes 3153924 | tf_op jit(solution)/shard_map/td,nd->tn/dot_general | solution.py:123
  83.2 1.0 copy-done.21
  84.2 2.7 %convolution_bitcast_fusion = f32[8,4,16,512]{3,2,0,1:T(8,128)} fusion(f32[4,8,16,512]{3,2,1,0:T(8,128)S(1)} %bitcast.112, f32[512,512]{0,1:T(8,128)S(1)} %get-tuple-element.52, s32[512]{0:T(512)S(1)} %get-tuple-element.54, s32[512]{0:T(512)S(1)} %broadcast_bitcast_fusion, s32[512]{0:T(512)S(1)} %bitcast.120, s32[512]{0:T(512)S(1)} %get-tuple-element.55), kind=kOutput, calls=%fused_computation.33 | convolution fusion | flops 809500672 | bytes 3153920 | tf_op jit(solution)/shard_map/td,tn->dn/dot_general | solution.py:137
  86.9 1.8 gather_fusion.5
  89.1 9.8 %collective-permute-done.12 = f32[4,4,16,512]{3,2,1,0:T(8,128)S(1)} collective-permute-done((f32[4,4,16,512]{3,2,1,0:T(8,128)S(1)}, f32[4,4,16,512]{3,2,1,0:T(8,128)S(1)}, u32[]{:S(2)}, u32[]{:S(2)}) %collective-permute-start.12) | collective-permute-done | bytes 524320 | tf_op jit(solution)/shard_map/ppermute | solution.py:16
  99.1 3.7 %collective-permute-start.13 = (f32[2,4,16,512]{3,2,1,0:T(8,128)S(1)}, f32[2,4,16,512]{3,2,1,0:T(8,128)S(1)}, u32[]{:S(2)}, u32[]{:S(2)}) collective-permute-start(f32[2,4,16,512]{3,2,1,0:T(8,128)S(1)} %slice.232), channel_id=1, source_target_pairs={{0,2},{1,3},{2,0},{3,1},{4,6},{5,7},{6,4},{7,5},{8,10},{9,11},{10,... | collective-permute-start | bytes 786440 | tf_op jit(solution)/shard_map/ppermute | solution.py:16
  102.8 4.4 %collective-permute-done.13 = f32[2,4,16,512]{3,2,1,0:T(8,128)S(1)} collective-permute-done((f32[2,4,16,512]{3,2,1,0:T(8,128)S(1)}, f32[2,4,16,512]{3,2,1,0:T(8,128)S(1)}, u32[]{:S(2)}, u32[]{:S(2)}) %collective-permute-start.13) | collective-permute-done | bytes 262176 | tf_op jit(solution)/shard_map/ppermute | solution.py:16
  107.2 5.7 %collective-permute-start.14 = (f32[1,4,16,512]{3,2,1,0:T(8,128)S(1)}, f32[1,4,16,512]{3,2,1,0:T(8,128)S(1)}, u32[]{:S(2)}, u32[]{:S(2)}) collective-permute-start(f32[1,4,16,512]{3,2,1,0:T(8,128)S(1)} %slice.234), channel_id=1, source_target_pairs={{0,4},{1,5},{2,6},{3,7},{4,0},{5,1},{6,2},{7,3},{8,12},{9,13},{10,... | collective-permute-start | bytes 393224 | tf_op jit(solution)/shard_map/ppermute | solution.py:16
  112.9 4.2 %collective-permute-done.14 = f32[1,4,16,512]{3,2,1,0:T(8,128)S(1)} collective-permute-done((f32[1,4,16,512]{3,2,1,0:T(8,128)S(1)}, f32[1,4,16,512]{3,2,1,0:T(8,128)S(1)}, u32[]{:S(2)}, u32[]{:S(2)}) %collective-permute-start.14) | collective-permute-done | bytes 131104 | tf_op jit(solution)/shard_map/ppermute | solution.py:16
  119.7 3.7 %collective-permute-done.16 = f32[1,2,16,512]{3,2,0,1:T(8,128)S(1)} collective-permute-done((f32[1,2,16,512]{3,2,0,1:T(8,128)S(1)}, f32[1,2,16,512]{3,2,0,1:T(8,128)S(1)}, u32[]{:S(2)}, u32[]{:S(2)}) %collective-permute-start.16) | collective-permute-done | bytes 65568 | tf_op jit(solution)/shard_map/ppermute | solution.py:16
  123.4 2.2 %fusion = f32[4,16,1024]{2,1,0:T(8,128)S(1)} fusion(s32[4,512]{1,0:T(4,128)S(1)} %gather_fusion.7, f32[1,2,16,512]{3,2,0,1:T(8,128)S(1)} %collective-permute-done.16, f32[1,2,16,512]{3,2,0,1:T(8,128)S(1)} %get-tuple-element.41), kind=kOutput, calls=%fused_computation.11 | convolution fusion | flops 203456512 | bytes 401408 | tf_op jit(solution)/shard_map/pdc,pcr->pdr/dot_general | solution.py:155
  125.8 17.7 %all_to_all.5 = f32[8,16,1024]{2,1,0:T(8,128)S(1)} all-to-all(f32[8,16,1024]{2,1,0:T(8,128)S(1)} %multiply_reduce_fusion), channel_id=1, replica_groups=mesh['seq'=4,'item'=8] {'item'}, dimensions={0} | all-to-all | bytes 1048576 | tf_op jit(solution)/shard_map/all_to_all | solution.py:159
  143.7 0.9 collective-permute-start.17
  144.5 3.2 %fusion.59 = f32[512,512]{1,0:T(8,128)S(1)} fusion(f32[512,512]{1,0:T(8,128)} %bitcast.111, f32[512,512]{0,1:T(8,128)} %copy-done.21, s32[512]{0:T(512)S(1)} %get-tuple-element.54, s32[512]{0:T(512)S(1)} %broadcast_bitcast_fusion, s32[512]{0:T(512)S(1)} %bitcast.121, s32[512]{0:T(512)S(1)} %get-tuple-element.55), kind=kOutput, calls=%fused_computation.135 | convolution fusion | flops 809500672 | bytes 3153920 | tf_op jit(solution)/shard_map/dot_general | solution.py:138
  147.7 1.1 fusion.62
  148.8 7.2 %collective-permute-done.17 = f32[1,1024,128]{2,1,0:T(8,128)S(1)} collective-permute-done((f32[1,1024,128]{2,1,0:T(8,128)S(1)}, f32[1,1024,128]{2,1,0:T(8,128)S(1)}, u32[]{:S(2)}, u32[]{:S(2)}) %collective-permute-start.17) | collective-permute-done | bytes 524320 | tf_op jit(solution)/shard_map/ppermute | solution.py:16
  156.0 0.8 copy-done.8
  156.8 1.0 pad_maximum_fusion.4
  158.5 0.8 copy-done.18
  159.3 1.3 add.203
  160.6 0.7 slice.228
  161.3 1.1 collective-permute-start.11
  162.4 0.8 dynamic-update-slice.4
  163.1 40.3 %all-reduce.1 = f32[32]{0:T(128)S(1)} all-reduce(f32[32]{0:T(128)S(1)} %dynamic-update-slice.4), channel_id=2, replica_groups=mesh['seq'=4,'item'=8] {'seq','item'}, use_global_device_ids=true, to_apply=%add.1 | all-reduce | flops 32 | bytes 256
  204.7 0.7 slice_add_fusion.2
  205.4 1.3 slice_bitcast_fusion.1
  206.7 1.5 pad_maximum_fusion
  208.1 3.6 %gather_fusion.9 = f32[4,1024,128]{2,1,0:T(8,128)} fusion(f32[1024,4,128]{2,0,1:T(8,128)} %pad_maximum_fusion, s32[1024]{0:T(1024)S(1)} %pad_clamp_fusion), kind=kCustom, calls=%fused_computation.9 | custom fusion | bytes 4194320 | tf_op jit(solution)/shard_map/gather | solution.py:162
  211.8 2.9 %copy.58 = f32[1024,4,128]{0,2,1:T(8,128)} copy(f32[1024,4,128]{2,0,1:T(8,128)} %bitcast.99) | data formatting | bytes 4194304 | tf_op jit(solution)/shard_map/gather | solution.py:162
  214.6 2.9 %copy.59 = f32[1024,512]{1,0:T(8,128)} copy(f32[1024,512]{0,1:T(8,128)} %bitcast.100) | data formatting | bytes 4194304
  (118 shorter events, 9.1 us)
Async XLA Ops:
  0.6 7.7 %copy-start = (f32[1024,512]{1,0:T(8,128)S(1)}, f32[1024,512]{1,0:T(8,128)}, u32[]{:S(2)}) copy-start(f32[1024,512]{1,0:T(8,128)} %param.23) | copy-start | bytes 6291460
  3.2 20.2 %collective-permute-start = (f32[1,136,512]{2,1,0:T(8,128)S(1)}, f32[1,136,512]{2,1,0:T(8,128)S(1)}, u32[]{:S(2)}, u32[]{:S(2)}) collective-permute-start(f32[1,136,512]{2,1,0:T(8,128)S(1)} %maximum_bitcast_fusion), channel_id=1, source_target_pairs={{0,16},{8,24},{16,0},{24,8},{1,17},{9,25},{17,1},{25,9},{2,18},{10... | collective-permute-start | bytes 835592 | tf_op jit(solution)/shard_map/ppermute | solution.py:16
  12.9 4.6 %copy-start.1 = (s32[4]{0:T(128)S(1)}, s32[4]{0:T(128)}, u32[]{:S(2)}) copy-start(s32[4]{0:T(128)} %constant.151.clone) | copy-start | bytes 52
  12.9 4.7 %copy-start.20 = (s32[1,4]{1,0:T(1,128)S(1)}, s32[1,4]{1,0:T(1,128)}, u32[]{:S(2)}) copy-start(s32[1,4]{1,0:T(1,128)} %param.24) | copy-start | bytes 52
  12.9 5.0 %copy-start.2 = (s32[4]{0:T(128)S(1)}, s32[4]{0:T(128)}, u32[]{:S(2)}) copy-start(s32[4]{0:T(128)} %param.26) | copy-start | bytes 52
  12.9 6.2 %copy-start.14 = (f32[1,128,512]{2,1,0:T(8,128)S(1)}, f32[1,128,512]{2,1,0:T(8,128)}, u32[]{:S(2)}) copy-start(f32[1,128,512]{2,1,0:T(8,128)} %param.19) | copy-start | bytes 786436
  12.9 13.8 %collective-permute-start.4 = (f32[4,64,512]{2,1,0:T(8,128)}, f32[4,64,512]{2,1,0:T(8,128)}, u32[]{:S(2)}, u32[]{:S(2)}) collective-permute-start(f32[4,64,512]{2,1,0:T(8,128)} %bitcast.19), channel_id=1, source_target_pairs={{0,1},{1,0},{2,3},{3,2},{4,5},{5,4},{6,7},{7,6},{8,9},{9,8},{10,11... | collective-permute-start | bytes 1572872 | tf_op jit(solution)/shard_map/ppermute | solution.py:16
  19.1 7.5 %copy-start.6 = (f32[256,512]{1,0:T(8,128)S(1)}, f32[256,512]{1,0:T(8,128)}, u32[]{:S(2)}) copy-start(f32[256,512]{1,0:T(8,128)} %get-tuple-element.40) | copy-start | bytes 1572868
  23.4 5.9 %copy-start.3 = (s32[8]{0:T(128)S(1)}, s32[8]{0:T(128)}, u32[]{:S(2)}) copy-start(s32[8]{0:T(128)} %constant.152.clone) | copy-start | bytes 100
  24.2 15.2 %collective-permute-start.1 = (f32[2,136,512]{2,1,0:T(8,128)}, f32[2,136,512]{2,1,0:T(8,128)S(1)}, u32[]{:S(2)}, u32[]{:S(2)}) collective-permute-start(f32[2,136,512]{2,1,0:T(8,128)} %pad_maximum_fusion.5), channel_id=1, source_target_pairs={{0,8},{8,0},{16,24},{24,16},{1,9},{9,1},{17,25},{25,17},{2,10},{10... | collective-permute-start | bytes 1671176 | tf_op jit(solution)/shard_map/ppermute | solution.py:16
  26.8 0.8 copy-start.5
  27.6 8.1 %collective-permute-start.5 = (f32[2,64,512]{2,1,0:T(8,128)S(1)}, f32[2,64,512]{2,1,0:T(8,128)}, u32[]{:S(2)}, u32[]{:S(2)}) collective-permute-start(f32[2,64,512]{2,1,0:T(8,128)S(1)} %slice.222), channel_id=1, source_target_pairs={{0,2},{1,3},{2,0},{3,1},{4,6},{5,7},{6,4},{7,5},{8,10},{9,11},{10,... | collective-permute-start | bytes 786440 | tf_op jit(solution)/shard_map/ppermute | solution.py:16
  36.7 2.8 %copy-start.11 = (f32[512,2048]{1,0:T(8,128)S(1)}, f32[512,2048]{1,0:T(8,128)}, u32[]{:S(2)}) copy-start(f32[512,2048]{1,0:T(8,128)} %param.20) | copy-start | bytes 12582916
  36.7 10.2 %collective-permute-start.6 = (f32[1,64,512]{2,1,0:T(8,128)S(1)}, f32[1,64,512]{2,1,0:T(8,128)S(1)}, u32[]{:S(2)}, u32[]{:S(2)}) collective-permute-start(f32[1,64,512]{2,1,0:T(8,128)S(1)} %slice.224), channel_id=1, source_target_pairs={{0,4},{1,5},{2,6},{3,7},{4,0},{5,1},{6,2},{7,3},{8,12},{9,13},{10,... | collective-permute-start | bytes 393224 | tf_op jit(solution)/shard_map/ppermute | solution.py:16
  40.8 1.2 slice-start
  43.8 2.9 %copy-start.19 = (f32[512]{0:T(512)S(1)}, f32[512]{0:T(512)}, u32[]{:S(2)}) copy-start(f32[512]{0:T(512)} %param.21) | copy-start | bytes 6148
  43.8 5.1 %copy-start.12 = (f32[512,512]{1,0:T(8,128)S(1)}, f32[512,512]{1,0:T(8,128)}, u32[]{:S(2)}) copy-start(f32[512,512]{1,0:T(8,128)} %param.22) | copy-start | bytes 3145732
  43.8 5.1 %copy-start.15 = (f32[1,128,512]{2,1,0:T(8,128)S(1)}, f32[1,128,512]{2,1,0:T(8,128)}, u32[]{:S(2)}) copy-start(f32[1,128,512]{2,1,0:T(8,128)} %param.19) | copy-start | bytes 786436
  43.9 5.1 %copy-start.16 = (f32[128,1024]{0,1:T(8,128)S(1)}, f32[128,1024]{0,1:T(8,128)}, u32[]{:S(2)}) copy-start(f32[128,1024]{0,1:T(8,128)} %divide_multiply_fusion.2) | copy-start | bytes 1572868
  46.9 7.8 %copy-start.7 = (f32[1,64,512]{2,1,0:T(8,128)}, f32[1,64,512]{2,1,0:T(8,128)S(1)}, u32[]{:S(2)}) copy-start(f32[1,64,512]{2,1,0:T(8,128)S(1)} %slice_select_fusion.1) | copy-start | bytes 393220
  47.0 7.8 %collective-permute-start.7 = (f32[1,64,512]{2,1,0:T(8,128)S(1)}, f32[1,64,512]{2,1,0:T(8,128)S(1)}, u32[]{:S(2)}, u32[]{:S(2)}) collective-permute-start(f32[1,64,512]{2,1,0:T(8,128)S(1)} %slice_select_fusion.1), channel_id=1, source_target_pairs={{0,4},{1,5},{2,6},{3,7},{4,0},{5,1},{6,2},{7,3},{8,12},{9,13},{10,... | collective-permute-start | bytes 393224 | tf_op jit(solution)/shard_map/ppermute | solution.py:16
  49.4 7.0 %collective-permute-start.2 = (f32[1,128,512]{2,1,0:T(8,128)S(1)}, f32[1,128,512]{2,1,0:T(8,128)}, u32[]{:S(2)}, u32[]{:S(2)}) collective-permute-start(f32[1,128,512]{2,1,0:T(8,128)S(1)} %fusion.18), channel_id=1, source_target_pairs={{0,16},{8,24},{16,0},{24,8},{1,17},{9,25},{17,1},{25,9},{2,18},{10... | collective-permute-start | bytes 786440 | tf_op jit(solution)/shard_map/ppermute | solution.py:16
  54.7 0.7 copy-start.10
  55.5 6.7 %collective-permute-start.8 = (f32[2,64,512]{2,1,0:T(8,128)}, f32[2,64,512]{2,1,0:T(8,128)}, u32[]{:S(2)}, u32[]{:S(2)}) collective-permute-start(f32[2,64,512]{2,1,0:T(8,128)} %pad_maximum_fusion.8), channel_id=1, source_target_pairs={{0,2},{1,3},{2,0},{3,1},{4,6},{5,7},{6,4},{7,5},{8,10},{9,11},{10,... | collective-permute-start | bytes 786440 | tf_op jit(solution)/shard_map/ppermute | solution.py:16
  57.4 7.6 %collective-permute-start.3 = (f32[2,128,512]{2,1,0:T(8,128)S(1)}, f32[2,128,512]{2,1,0:T(8,128)S(1)}, u32[]{:S(2)}, u32[]{:S(2)}) collective-permute-start(f32[2,128,512]{2,1,0:T(8,128)S(1)} %pad_maximum_fusion.6), channel_id=1, source_target_pairs={{0,8},{8,0},{16,24},{24,16},{1,9},{9,1},{17,25},{25,17},{2,10},{10... | collective-permute-start | bytes 1572872 | tf_op jit(solution)/shard_map/ppermute | solution.py:16
  64.0 11.4 %collective-permute-start.9 = (f32[4,64,512]{2,1,0:T(8,128)}, f32[4,64,512]{2,1,0:T(8,128)}, u32[]{:S(2)}, u32[]{:S(2)}) collective-permute-start(f32[4,64,512]{2,1,0:T(8,128)} %pad_maximum_fusion.7), channel_id=1, source_target_pairs={{0,1},{1,0},{2,3},{3,2},{4,5},{5,4},{6,7},{7,6},{8,9},{9,8},{10,11... | collective-permute-start | bytes 1572872 | tf_op jit(solution)/shard_map/ppermute | solution.py:16
  66.1 1.3 copy-start.4
  78.3 5.9 %copy-start.13 = (f32[512,512]{1,0:T(8,128)S(1)}, f32[512,512]{1,0:T(8,128)}, u32[]{:S(2)}) copy-start(f32[512,512]{1,0:T(8,128)} %copy.55) | copy-start | bytes 3145732
  83.2 1.0 copy-start.21
  88.8 30.3 %copy-start.17 = (s32[4,512]{1,0:T(4,128)S(1)}, s32[4,512]{1,0:T(4,128)}, u32[]{:S(2)}) copy-start(s32[4,512]{1,0:T(4,128)} %param.25) | copy-start | bytes 24580
  88.8 10.2 %collective-permute-start.12 = (f32[4,4,16,512]{3,2,1,0:T(8,128)S(1)}, f32[4,4,16,512]{3,2,1,0:T(8,128)S(1)}, u32[]{:S(2)}, u32[]{:S(2)}) collective-permute-start(f32[4,4,16,512]{3,2,1,0:T(8,128)S(1)} %slice.230), channel_id=1, source_target_pairs={{0,1},{1,0},{2,3},{3,2},{4,5},{5,4},{6,7},{7,6},{8,9},{9,8},{10,11... | collective-permute-start | bytes 1572872 | tf_op jit(solution)/shard_map/ppermute | solution.py:16
  99.1 8.0 %collective-permute-start.13 = (f32[2,4,16,512]{3,2,1,0:T(8,128)S(1)}, f32[2,4,16,512]{3,2,1,0:T(8,128)S(1)}, u32[]{:S(2)}, u32[]{:S(2)}) collective-permute-start(f32[2,4,16,512]{3,2,1,0:T(8,128)S(1)} %slice.232), channel_id=1, source_target_pairs={{0,2},{1,3},{2,0},{3,1},{4,6},{5,7},{6,4},{7,5},{8,10},{9,11},{10,... | collective-permute-start | bytes 786440 | tf_op jit(solution)/shard_map/ppermute | solution.py:16
  107.2 9.9 %collective-permute-start.14 = (f32[1,4,16,512]{3,2,1,0:T(8,128)S(1)}, f32[1,4,16,512]{3,2,1,0:T(8,128)S(1)}, u32[]{:S(2)}, u32[]{:S(2)}) collective-permute-start(f32[1,4,16,512]{3,2,1,0:T(8,128)S(1)} %slice.234), channel_id=1, source_target_pairs={{0,4},{1,5},{2,6},{3,7},{4,0},{5,1},{6,2},{7,3},{8,12},{9,13},{10,... | collective-permute-start | bytes 393224 | tf_op jit(solution)/shard_map/ppermute | solution.py:16
  117.7 1.3 collective-permute-start.15
  119.0 4.3 %collective-permute-start.16 = (f32[1,2,16,512]{3,2,0,1:T(8,128)S(1)}, f32[1,2,16,512]{3,2,0,1:T(8,128)S(1)}, u32[]{:S(2)}, u32[]{:S(2)}) collective-permute-start(f32[1,2,16,512]{3,2,0,1:T(8,128)S(1)} %get-tuple-element.42), channel_id=1, source_target_pairs={{0,16},{8,24},{16,0},{24,8},{1,17},{9,25},{17,1},{25,9},{2,18},{10... | collective-permute-start | bytes 196616 | tf_op jit(solution)/shard_map/ppermute | solution.py:16
  143.7 12.3 %collective-permute-start.17 = (f32[1,1024,128]{2,1,0:T(8,128)S(1)}, f32[1,1024,128]{2,1,0:T(8,128)S(1)}, u32[]{:S(2)}, u32[]{:S(2)}) collective-permute-start(f32[1,1024,128]{2,1,0:T(8,128)S(1)} %bitcast.101), channel_id=1, source_target_pairs={{0,16},{8,24},{16,0},{24,8},{1,17},{9,25},{17,1},{25,9},{2,18},{10... | collective-permute-start | bytes 1572872 | tf_op jit(solution)/shard_map/ppermute | solution.py:16
  148.8 9.7 %collective-permute-start.10 = (f32[2,128,512]{2,1,0:T(8,128)}, f32[2,128,512]{2,1,0:T(8,128)S(1)}, u32[]{:S(2)}, u32[]{:S(2)}) collective-permute-start(f32[2,128,512]{2,1,0:T(8,128)} %bitcast.27), channel_id=1, source_target_pairs={{0,8},{8,0},{16,24},{24,16},{1,9},{9,1},{17,25},{25,17},{2,10},{10... | collective-permute-start | bytes 1572872 | tf_op jit(solution)/shard_map/ppermute | solution.py:16
  156.0 0.8 copy-start.8
  157.8 47.6 %collective-permute-start.18 = (f32[2,1024,128]{2,1,0:T(8,128)}, f32[2,1024,128]{2,1,0:T(8,128)}, u32[]{:S(2)}, u32[]{:S(2)}) collective-permute-start(f32[2,1024,128]{2,1,0:T(8,128)} %pad_maximum_fusion.4), channel_id=1, source_target_pairs={{0,8},{8,0},{16,24},{24,16},{1,9},{9,1},{17,25},{25,17},{2,10},{10... | collective-permute-start | bytes 3145736 | tf_op jit(solution)/shard_map/ppermute | solution.py:16
  158.5 0.8 copy-start.18
  161.3 43.4 %collective-permute-start.11 = (f32[1,128,512]{2,1,0:T(8,128)}, f32[1,128,512]{2,1,0:T(8,128)S(1)}, u32[]{:S(2)}, u32[]{:S(2)}) collective-permute-start(f32[1,128,512]{2,1,0:T(8,128)} %slice.228), channel_id=1, source_target_pairs={{0,16},{8,24},{16,0},{24,8},{1,17},{9,25},{17,1},{25,9},{2,18},{10... | collective-permute-start | bytes 786440 | tf_op jit(solution)/shard_map/ppermute | solution.py:16
  204.6 2.0 copy-start.9

commit v2 on v1

--- a/solution.py
+++ b/solution.py
@@ -18,6 +18,11 @@
 
 def bits_of(size):
     return list(range(size.bit_length() - 1))[::-1]
+
+
+def two_orders(size):
+    up = bits_of(size)
+    return [up, up[:-2] + up[:-3:-1]]
 
 
 def gather_steps(block, axis, bits):
@@ -60,26 +65,34 @@
     s, i = lax.axis_index("seq"), lax.axis_index("item")
     group_len = tok * n_seq
     head_size = width // H
-    seq_bits, item_bits = bits_of(n_seq), bits_of(n_item)
-    seq_order, item_order = orders(seq_bits), orders(item_bits)
+    seq_bits = bits_of(n_seq)
+    seq_order = orders(seq_bits)
     seq_rel = s ^ jnp.array(seq_order, jnp.int32)
-    item_rel = i ^ jnp.array(item_order, jnp.int32)
 
     flat_ids = neg_ids.reshape(-1)
     n_neg = flat_ids.shape[0] // n_seq
     per_panel = neg_ids.shape[1] // n_neg
-    n_part = n_neg // n_item
+    n_part = n_neg // (2 * n_item)
     ids_by_seq = flat_ids.reshape(n_seq, n_neg)
-    own_ids = ids_by_seq[s]
+    own_ids = ids_by_seq[s].reshape(2, n_item, n_part)
     root = panel_owner[s // per_panel]
-    ids_rel = own_ids.reshape(n_item, n_part)[item_rel]
-    part = item_table[ids_rel.reshape(-1)].reshape(n_item, n_part, width)
-    for bit in item_bits[::-1]:
-        half = part.shape[0] // 2
-        other = swap(part[half:], "item", bit)
-        part = jnp.where(((i ^ root) >> bit) & 1 == 0, part[:half], other)
-    negatives, _ = gather_steps(part[0], "item", item_bits)
-    negatives = negatives[item_rel_inverse(item_order, i)].reshape(n_neg, width)
+    bit_lists = two_orders(n_item)
+    negatives = []
+    for half, bits in enumerate(bit_lists):
+        order = orders(bits)
+        rel = i ^ jnp.array(order, jnp.int32)
+        part = item_table[own_ids[half][rel].reshape(-1)].reshape(n_item, n_part, width)
+        for bit in bits[:0:-1]:
+            cut = part.shape[0] // 2
+            other = swap(part[cut:], "item", bit)
+            part = jnp.where(((i ^ root) >> bit) & 1 == 0, part[:cut], other)
+        other = swap(part, "item", bits[0])
+        same = ((i ^ root) >> bits[0]) & 1 == 0
+        part = jnp.where(same, part, jnp.concatenate([other[1:], other[:1]], axis=0))
+        for bit in bits[1:]:
+            part = jnp.concatenate([part, swap(part, "item", bit)], axis=0)
+        negatives.append(part[item_rel_inverse(order, i)].reshape(n_neg // 2, width))
+    negatives = jnp.concatenate(negatives, axis=0)
 
     extra = jnp.zeros((8, width), jnp.float32)
     extra = extra.at[0, :tok].set(targets[0].astype(jnp.float32))
@@ -139,9 +152,12 @@
     event_grad = reduce_steps(grad_rows.reshape(n_seq, tok, width), "seq", seq_bits[::-1])
 
     n_dim = width // (n_seq * n_item)
-    panel_part = panel_part.reshape(n_seq, n_item, n_dim, n_neg)
-    panel_part = panel_part.transpose(1, 0, 2, 3)[item_rel]
-    panel_sum = reduce_steps(panel_part, "item", item_bits[::-1])
+    panel_part = panel_part.reshape(n_seq, n_item, 2, n_dim // 2, n_neg).transpose(2, 1, 0, 3, 4)
+    sums = []
+    for half, bits in enumerate(bit_lists):
+        rel = i ^ jnp.array(orders(bits), jnp.int32)
+        sums.append(reduce_steps(panel_part[half][rel], "item", bits[::-1]))
+    panel_sum = jnp.concatenate(sums, axis=1)
     panel_sum = panel_sum[seq_rel]
     moved = panel_sum[:, None]
     for bit in seq_bits[::-1]:
@@ -163,8 +179,11 @@
         [table[k] for k in range(n_seq)], axis=1
     ).reshape(-1, n_seq, n_item * n_dim)[:, item_rel_inverse(seq_order, s)].reshape(-1, width)
 
-    losses = lax.all_gather(jnp.full((8, 128), loss_part), ("seq", "item"))
-    loss_total = jnp.sum(losses[:, 0, 0])
+    loss_total = jnp.full((8, 128), loss_part)
+    for axis, size in (("seq", n_seq), ("item", n_item)):
+        for bit in bits_of(size):
+            loss_total = loss_total + swap(loss_total, axis, bit)
+    loss_total = loss_total[0, 0]
     return (loss_total / (group_len * n_item), event_grad[None], table_grad)
 
 

time: 219 us -> 179 us (0.82)
  blocking collectives: 57.9 us -> 0 us
  starting transfers between devices: 23.8 us -> 36.1 us
  local copies, waits for them, and re-layouts: 34.6 us -> 37.8 us
  other arithmetic: 16.9 us -> 19.1 us
    unnamed x1 -> x0, blocking collectives: 40.3 us -> none
    all_to_all x1 -> x0, blocking collectives: 17.7 us -> none  [per_device(): lax.all_to_all(sent, 'item', split_axis=0, concat_axis=0, tiled=True)]
    all_to_all x0 -> x1, waiting for transfers between devices: none -> 12.7 us  [per_device(): lax.all_to_all(sent, 'item', split_axis=0, concat_axis=0, tiled=True)]
    ppermute x19 -> x31, waiting for transfers between devices: 56.5 us -> 45 us  [swap(): return lax.ppermute(block, axis, [(i, i ^ 1 << bit) for i in range(size)])]
    ppermute x19 -> x31, starting transfers between devices: 23.8 us -> 31.6 us  [swap(): return lax.ppermute(block, axis, [(i, i ^ 1 << bit) for i in range(size)])]
    concatenate x8 -> x5, other arithmetic: 7.96 us -> 3.25 us  [gather_steps(): stacked = jnp.concatenate([stacked, swap(stacked, axis, bit)], axis=0)]
    all_to_all x0 -> x1, starting transfers between devices: none -> 4.55 us  [per_device(): lax.all_to_all(sent, 'item', split_axis=0, concat_axis=0, tiled=True)]
    gather x4 -> x8, local copies, waits for them, and re-layouts: 6.3 us -> 8.16 us  [the longest x2 2.9 us: per_device(): part[item_rel_inverse(order, i)].reshape(n_neg // 2, width)]
  transfers between devices with their start and end apart: 19 -> 32, of which waited for: 12 -> 16; matrix products, arithmetic and copies ran while one was open for 20% -> 27% of each run, Pallas kernels for 0% -> 0%
where the time goes in v2:
time: 179 us
  waiting for transfers between devices  57.7 us (32%)
  local copies, waits for them, and re-layouts  37.8 us (21%)
  starting transfers between devices  36.1 us (20%)
  matrix products  23.4 us (13%)
  other arithmetic  19.1 us (11%)
  between operations  4.46 us (2%)
    ppermute x31, waiting for transfers between devices, swap(): return lax.ppermute(block, axis, [(i, i ^ 1 << bit) for i in range(size)])  45 us
    ppermute x31, starting transfers between devices, swap(): return lax.ppermute(block, axis, [(i, i ^ 1 << bit) for i in range(size)])  31.6 us
    all_to_all x1, waiting for transfers between devices, per_device(): lax.all_to_all(sent, 'item', split_axis=0, concat_axis=0, tiled=True)  12.7 us
    gather x2, local copies, waits for them, and re-layouts, per_device(): jnp.concatenate([table[k] for k in range(n_seq)], axis=1)  6.5 us
    unnamed x55, local copies, waits for them, and re-layouts  5.76 us
    all_to_all x1, starting transfers between devices, per_device(): lax.all_to_all(sent, 'item', split_axis=0, concat_axis=0, tiled=True)  4.55 us
    dot_general x1, matrix products, per_device(): logits = jnp.einsum('td,nd->tn', outputs, negatives, precision=high)  4.49 us
    dot_general x1, matrix products, per_device(): jnp.dot(rows_in, jnp.concatenate([w_uvqk[:, :width], w_uvqk[:, 2 * width:...  4.24 us
  transfers between devices with their start and end apart: 32, of which 16 were waited for; matrix products, arithmetic and copies ran while one was open for 27% of the time, Pallas kernels for 0%

profile of v2, /device:TPU:0, one launch (start us, length us, event | category | flops | bytes accessed | tf_op | source)
XLA Modules:
  0.0 178.5 jit_solution(11148007534833035458)
XLA Ops:
  2.2 1.0 maximum_bitcast_fusion
  3.2 3.0 %collective-permute-start = (f32[1,136,512]{2,1,0:T(8,128)S(1)}, f32[1,136,512]{2,1,0:T(8,128)S(1)}, u32[]{:S(2)}, u32[]{:S(2)}) collective-permute-start(f32[1,136,512]{2,1,0:T(8,128)S(1)} %maximum_bitcast_fusion), channel_id=1, source_target_pairs={{0,16},{8,24},{16,0},{24,8},{1,17},{9,25},{17,1},{25,9},{2,18},{10... | collective-permute-start | bytes 835592 | tf_op jit(solution)/shard_map/ppermute | solution.py:16
  8.4 1.0 gather_fusion.5
  10.1 1.6 collective-permute-start.9
  12.4 1.0 gather_fusion.1
  13.4 0.8 fusion.68
  14.2 1.5 collective-permute-start.4
  15.8 3.1 %fusion.66 = (f32[512,512]{1,0:T(8,128)}, f32[512,512]{1,0:T(8,128)}) fusion(f32[512,2048]{1,0:T(8,128)} %param.24), kind=kLoop, calls=%fused_computation.165 | loop fusion | bytes 4194304 | tf_op jit(solution)/shard_map/slice | solution.py:113
  21.2 4.2 %divide_multiply_fusion.2 = f32[128,1024]{0,1:T(8,128)} fusion(f32[512,512]{1,0:T(8,128)} %get-tuple-element.36, f32[512,512]{1,0:T(8,128)} %get-tuple-element.35, f32[1,128,512]{2,1,0:T(8,128)S(1)} %copy-done.11), kind=kOutput, calls=%fused_computation.70 | convolution fusion | flops 403701760 | bytes 2883584 | tf_op jit(solution)/shard_map/dot_general | solution.py:111
  29.2 1.0 broadcast_select_fusion
  31.1 4.2 %collective-permute-done.10 = f32[2,32,512]{2,1,0:T(8,128)S(1)} collective-permute-done((f32[2,32,512]{2,1,0:T(8,128)S(1)}, f32[2,32,512]{2,1,0:T(8,128)S(1)}, u32[]{:S(2)}, u32[]{:S(2)}) %collective-permute-start.10) | collective-permute-done | bytes 131104 | tf_op jit(solution)/shard_map/ppermute | solution.py:16
  35.3 2.7 %collective-permute-start.11 = (f32[2,32,512]{2,1,0:T(8,128)S(1)}, f32[2,32,512]{2,1,0:T(8,128)S(1)}, u32[]{:S(2)}, u32[]{:S(2)}) collective-permute-start(f32[2,32,512]{2,1,0:T(8,128)S(1)} %slice_select_fusion), channel_id=1, source_target_pairs={{0,4},{1,5},{2,6},{3,7},{4,0},{5,1},{6,2},{7,3},{8,12},{9,13},{10,... | collective-permute-start | bytes 393224 | tf_op jit(solution)/shard_map/ppermute | solution.py:16
  38.0 1.4 collective-permute-start.6
  39.4 6.7 %collective-permute-done.11 = f32[2,32,512]{2,1,0:T(8,128)S(1)} collective-permute-done((f32[2,32,512]{2,1,0:T(8,128)S(1)}, f32[2,32,512]{2,1,0:T(8,128)S(1)}, u32[]{:S(2)}, u32[]{:S(2)}) %collective-permute-start.11) | collective-permute-done | bytes 131104 | tf_op jit(solution)/shard_map/ppermute | solution.py:16
  46.1 1.9 %collective-permute-start.12 = (f32[2,32,512]{2,1,0:T(8,128)S(1)}, f32[2,32,512]{2,1,0:T(8,128)S(1)}, u32[]{:S(2)}, u32[]{:S(2)}) collective-permute-start(f32[2,32,512]{2,1,0:T(8,128)S(1)} %maximum_select_fusion.1), channel_id=1, source_target_pairs={{0,1},{1,0},{2,3},{3,2},{4,5},{5,4},{6,7},{7,6},{8,9},{9,8},{10,11... | collective-permute-start | bytes 393224 | tf_op jit(solution)/shard_map/ppermute | solution.py:16
  48.4 1.9 %copy-done.7 = f32[512,2048]{1,0:T(8,128)S(1)} copy-done((f32[512,2048]{1,0:T(8,128)S(1)}, f32[512,2048]{1,0:T(8,128)}, u32[]{:S(2)}) %copy-start.7) | copy-done | bytes 4194328
  50.3 1.2 divide_multiply_fusion.1
  51.5 1.2 divide_multiply_fusion
  52.8 1.9 %fusion.73 = f32[16,128,512]{2,1,0:T(8,128)S(1)} fusion(f32[128,16,32]{0,2,1:T(8,128)S(1)} %bitcast.128, f32[512,16,32]{0,2,1:T(8,128)S(1)} %bitcast.124), kind=kOutput, calls=%fused_computation.172 | convolution fusion | flops 201326592 | bytes 5505024 | tf_op jit(solution)/shard_map/qhd,khd->hqk/dot_general | solution.py:122
  54.7 2.8 %fusion.72 = (f32[128]{0:T(128)S(1)}, f32[16,32,128]{2,1,0:T(8,128)S(1)}) fusion(f32[512,16,32]{0,2,1:T(8,128)S(1)} %bitcast.140, f32[16,128,512]{2,1,0:T(8,128)S(1)} %fusion.73, f32[128,512]{1,0:T(8,128)S(1)} %copy-done.16), kind=kOutput, calls=%fused_computation.171 | convolution fusion | flops 206634880 | bytes 5767680 | tf_op jit(solution)/shard_map/hqk,khd->qhd/dot_general | solution.py:127
  58.3 1.1 collective-permute-start.2
  61.4 3.7 %collective-permute-done.2 = f32[1,128,512]{2,1,0:T(8,128)S(1)} collective-permute-done((f32[1,128,512]{2,1,0:T(8,128)S(1)}, f32[1,128,512]{2,1,0:T(8,128)S(1)}, u32[]{:S(2)}, u32[]{:S(2)}) %collective-permute-start.2) | collective-permute-done | bytes 262176 | tf_op jit(solution)/shard_map/ppermute | solution.py:16
  65.1 0.9 pad_maximum_fusion.8
  67.3 1.5 gather_fusion.7
  68.8 1.0 pad_maximum_fusion.9
  69.8 1.4 gather_fusion.3
  71.2 1.2 pad_maximum_fusion.2
  72.4 1.3 copy.59
  73.8 4.5 %fusion.22 = (f32[]{:T(128)}, f32[512,512]{0,1:T(8,128)S(1)}) fusion(s32[512]{0:T(512)S(1)} %copy-done.22, s32[512]{0:T(512)S(1)} %copy-done.21, s32[512]{0:T(512)S(1)} %bitcast.135, s32[512]{0:T(512)S(1)} %copy-done.23, f32[512,512]{1,0:T(8,128)S(1)} %bitcast.117, f32[256,512]{1,0:T(8,128)} %bitcast.129, f32[256,512]{1,0:T(8,128)} %bitcast.131), kind=kOutput, calls=%fused_computation.46 | convolution fusion | flops 812122112 | bytes 3153924 | tf_op jit(solution)/shard_map/td,nd->tn/dot_general | solution.py:136
  78.3 1.7 convolution_bitcast_fusion
  80.0 0.9 slice_bitcast_fusion.3
  82.2 1.1 collective-permute-start.24
  83.2 1.6 gather_fusion.9
  84.9 2.0 %collective-permute-start.21 = (f32[4,4,8,512]{3,2,1,0:T(8,128)S(1)}, f32[4,4,8,512]{3,2,1,0:T(8,128)S(1)}, u32[]{:S(2)}, u32[]{:S(2)}) collective-permute-start(f32[4,4,8,512]{3,2,1,0:T(8,128)S(1)} %slice.321), channel_id=1, source_target_pairs={{0,1},{1,0},{2,3},{3,2},{4,5},{5,4},{6,7},{7,6},{8,9},{9,8},{10,11... | collective-permute-start | bytes 786440 | tf_op jit(solution)/shard_map/ppermute | solution.py:16
  86.9 4.2 %collective-permute-done.24 = f32[4,4,8,512]{3,2,1,0:T(8,128)S(1)} collective-permute-done((f32[4,4,8,512]{3,2,1,0:T(8,128)}, f32[4,4,8,512]{3,2,1,0:T(8,128)S(1)}, u32[]{:S(2)}, u32[]{:S(2)}) %collective-permute-start.24) | collective-permute-done | bytes 262176 | tf_op jit(solution)/shard_map/ppermute | solution.py:16
  91.2 1.4 collective-permute-start.25
  92.5 1.0 collective-permute-done.21
  93.6 0.8 collective-permute-start.22
  94.5 1.9 %collective-permute-done.25 = f32[2,4,8,512]{3,2,1,0:T(8,128)S(1)} collective-permute-done((f32[2,4,8,512]{3,2,1,0:T(8,128)S(1)}, f32[2,4,8,512]{3,2,1,0:T(8,128)S(1)}, u32[]{:S(2)}, u32[]{:S(2)}) %collective-permute-start.25) | collective-permute-done | bytes 131104 | tf_op jit(solution)/shard_map/ppermute | solution.py:16
  96.4 3.4 %collective-permute-start.26 = (f32[1,4,8,512]{3,2,1,0:T(8,128)S(1)}, f32[1,4,8,512]{3,2,1,0:T(8,128)S(1)}, u32[]{:S(2)}, u32[]{:S(2)}) collective-permute-start(f32[1,4,8,512]{3,2,1,0:T(8,128)S(1)} %slice.332), channel_id=1, source_target_pairs={{0,4},{1,5},{2,6},{3,7},{4,0},{5,1},{6,2},{7,3},{8,12},{9,13},{10,... | collective-permute-start | bytes 196616 | tf_op jit(solution)/shard_map/ppermute | solution.py:16
  99.9 3.2 %collective-permute-start.23 = (f32[1,4,8,512]{3,2,1,0:T(8,128)S(1)}, f32[1,4,8,512]{3,2,1,0:T(8,128)S(1)}, u32[]{:S(2)}, u32[]{:S(2)}) collective-permute-start(f32[1,4,8,512]{3,2,1,0:T(8,128)S(1)} %slice.325), channel_id=1, source_target_pairs={{0,4},{1,5},{2,6},{3,7},{4,0},{5,1},{6,2},{7,3},{8,12},{9,13},{10,... | collective-permute-start | bytes 196616 | tf_op jit(solution)/shard_map/ppermute | solution.py:16
  103.1 2.9 %collective-permute-done.23 = f32[1,4,8,512]{3,2,1,0:T(8,128)S(1)} collective-permute-done((f32[1,4,8,512]{3,2,1,0:T(8,128)S(1)}, f32[1,4,8,512]{3,2,1,0:T(8,128)S(1)}, u32[]{:S(2)}, u32[]{:S(2)}) %collective-permute-start.23) | collective-permute-done | bytes 65568 | tf_op jit(solution)/shard_map/ppermute | solution.py:16
  108.0 0.9 collective-permute-start.28
  109.5 2.9 %collective-permute-done.28 = f32[1,2,16,512]{3,2,0,1:T(8,128)S(1)} collective-permute-done((f32[1,2,16,512]{3,2,0,1:T(8,128)S(1)}, f32[1,2,16,512]{3,2,0,1:T(8,128)S(1)}, u32[]{:S(2)}, u32[]{:S(2)}) %collective-permute-start.28) | collective-permute-done | bytes 65568 | tf_op jit(solution)/shard_map/ppermute | solution.py:16
  112.3 2.2 %fusion = f32[4,16,1024]{2,1,0:T(8,128)S(1)} fusion(s32[4,512]{1,0:T(4,128)S(1)} %gather_fusion.12, f32[1,2,16,512]{3,2,0,1:T(8,128)S(1)} %collective-permute-done.28, f32[1,2,16,512]{3,2,0,1:T(8,128)S(1)} %get-tuple-element.47), kind=kOutput, calls=%fused_computation.16 | convolution fusion | flops 203456512 | bytes 401408 | tf_op jit(solution)/shard_map/pdc,pcr->pdr/dot_general | solution.py:171
  114.5 1.1 multiply_reduce_fusion
  115.6 4.5 %all-to-all-start = ((f32[8,16,1024]{2,1,0:T(8,128)}), f32[8,16,1024]{2,1,0:T(8,128)S(1)}, u32[]{:S(2)}, u32[]{:S(2)}) async-start(f32[8,16,1024]{2,1,0:T(8,128)} %multiply_reduce_fusion), calls=%async_computation | async-start | bytes 1048576 | tf_op jit(solution)/shard_map/all_to_all | solution.py:175
  121.2 12.7 %all-to-all-done = f32[8,16,1024]{2,1,0:T(8,128)S(1)} async-done(((f32[8,16,1024]{2,1,0:T(8,128)}), f32[8,16,1024]{2,1,0:T(8,128)S(1)}, u32[]{:S(2)}, u32[]{:S(2)}) %all-to-all-start) | async-done | bytes 524320 | tf_op jit(solution)/shard_map/all_to_all | solution.py:175
  134.4 3.2 %fusion.34 = f32[512,512]{1,0:T(8,128)S(1)} fusion(f32[256,512]{1,0:T(8,128)} %bitcast.130, f32[256,512]{1,0:T(8,128)} %bitcast.132, f32[512,512]{0,1:T(8,128)} %copy-done.26, s32[512]{0:T(512)S(1)} %copy-done.22, s32[512]{0:T(512)S(1)} %copy-done.21, s32[512]{0:T(512)S(1)} %bitcast.137, s32[512]{0:T(512)S(1)} %copy-done.23), kind=kOutput, calls=%fused_computation.60 | convolution fusion | flops 809762816 | bytes 3153920 | tf_op jit(solution)/shard_map/dot_general | solution.py:151
  137.6 0.9 fusion.67
  138.4 7.8 %collective-permute-done.29 = f32[1,1024,128]{2,1,0:T(8,128)S(1)} collective-permute-done((f32[1,1024,128]{2,1,0:T(8,128)S(1)}, f32[1,1024,128]{2,1,0:T(8,128)S(1)}, u32[]{:S(2)}, u32[]{:S(2)}) %collective-permute-start.29) | collective-permute-done | bytes 524320 | tf_op jit(solution)/shard_map/ppermute | solution.py:16
  146.3 0.8 copy-done.5
  147.1 1.0 pad_maximum_fusion.4
  149.4 1.4 collective-permute-done.15
  152.9 3.2 %collective-permute-done.16 = f32[8,128]{1,0:T(8,128)S(1)} collective-permute-done((f32[8,128]{1,0:T(8,128)S(1)}, f32[8,128]{1,0:T(8,128)S(1)}, u32[]{:S(2)}, u32[]{:S(2)}) %collective-permute-start.16) | collective-permute-done | bytes 4128 | tf_op jit(solution)/shard_map/ppermute | solution.py:16
  156.1 1.2 add.260
  157.6 2.1 %collective-permute-done.17 = f32[8,128]{1,0:T(8,128)S(1)} collective-permute-done((f32[8,128]{1,0:T(8,128)S(1)}, f32[8,128]{1,0:T(8,128)S(1)}, u32[]{:S(2)}, u32[]{:S(2)}) %collective-permute-start.17) | collective-permute-done | bytes 4128 | tf_op jit(solution)/shard_map/ppermute | solution.py:16
  159.7 1.3 collective-permute-start.18
  161.0 2.3 %collective-permute-done.18 = f32[8,128]{1,0:T(8,128)S(1)} collective-permute-done((f32[8,128]{1,0:T(8,128)S(1)}, f32[8,128]{1,0:T(8,128)S(1)}, u32[]{:S(2)}, u32[]{:S(2)}) %collective-permute-start.18) | collective-permute-done | bytes 4128 | tf_op jit(solution)/shard_map/ppermute | solution.py:16
  165.3 1.3 slice_bitcast_fusion.1
  166.6 1.5 pad_maximum_fusion
  168.0 3.6 %gather_fusion.14 = f32[4,1024,128]{2,1,0:T(8,128)} fusion(f32[1024,4,128]{2,0,1:T(8,128)} %pad_maximum_fusion, s32[1024]{0:T(1024)S(1)} %pad_clamp_fusion), kind=kCustom, calls=%fused_computation.14 | custom fusion | bytes 4194320 | tf_op jit(solution)/shard_map/gather | solution.py:178
  171.6 2.9 %copy.62 = f32[1024,4,128]{0,2,1:T(8,128)} copy(f32[1024,4,128]{2,0,1:T(8,128)} %bitcast.111) | data formatting | bytes 4194304 | tf_op jit(solution)/shard_map/gather | solution.py:178
  174.5 2.9 %copy.63 = f32[1024,512]{1,0:T(8,128)} copy(f32[1024,512]{0,1:T(8,128)} %bitcast.112) | data formatting | bytes 4194304
  (183 shorter events, 25.8 us)
Async XLA Ops:
  0.6 7.8 %copy-start = (f32[1024,512]{1,0:T(8,128)S(1)}, f32[1024,512]{1,0:T(8,128)}, u32[]{:S(2)}) copy-start(f32[1024,512]{1,0:T(8,128)} %param.27) | copy-start | bytes 6291460
  3.2 27.8 %collective-permute-start = (f32[1,136,512]{2,1,0:T(8,128)S(1)}, f32[1,136,512]{2,1,0:T(8,128)S(1)}, u32[]{:S(2)}, u32[]{:S(2)}) collective-permute-start(f32[1,136,512]{2,1,0:T(8,128)S(1)} %maximum_bitcast_fusion), channel_id=1, source_target_pairs={{0,16},{8,24},{16,0},{24,8},{1,17},{9,25},{17,1},{25,9},{2,18},{10... | collective-permute-start | bytes 835592 | tf_op jit(solution)/shard_map/ppermute | solution.py:16
  10.1 19.1 %collective-permute-start.9 = (f32[4,32,512]{2,1,0:T(8,128)}, f32[4,32,512]{2,1,0:T(8,128)}, u32[]{:S(2)}, u32[]{:S(2)}) collective-permute-start(f32[4,32,512]{2,1,0:T(8,128)} %bitcast.26), channel_id=1, source_target_pairs={{0,2},{1,3},{2,0},{3,1},{4,6},{5,7},{6,4},{7,5},{8,10},{9,11},{10,... | collective-permute-start | bytes 786440 | tf_op jit(solution)/shard_map/ppermute | solution.py:16
  14.2 16.6 %collective-permute-start.4 = (f32[4,32,512]{2,1,0:T(8,128)}, f32[4,32,512]{2,1,0:T(8,128)}, u32[]{:S(2)}, u32[]{:S(2)}) collective-permute-start(f32[4,32,512]{2,1,0:T(8,128)} %bitcast.19), channel_id=1, source_target_pairs={{0,1},{1,0},{2,3},{3,2},{4,5},{5,4},{6,7},{7,6},{8,9},{9,8},{10,11... | collective-permute-start | bytes 786440 | tf_op jit(solution)/shard_map/ppermute | solution.py:16
  15.7 3.2 %copy-start.1 = (s32[4]{0:T(128)S(1)}, s32[4]{0:T(128)}, u32[]{:S(2)}) copy-start(s32[4]{0:T(128)} %constant.156.clone) | copy-start | bytes 52
  15.7 3.8 %copy-start.25 = (s32[1,4]{1,0:T(1,128)S(1)}, s32[1,4]{1,0:T(1,128)}, u32[]{:S(2)}) copy-start(s32[1,4]{1,0:T(1,128)} %param.28) | copy-start | bytes 52
  15.7 4.1 %copy-start.2 = (s32[8]{0:T(128)S(1)}, s32[8]{0:T(128)}, u32[]{:S(2)}) copy-start(s32[8]{0:T(128)} %constant.157.clone) | copy-start | bytes 100
  15.8 4.7 %copy-start.4 = (s32[8]{0:T(128)S(1)}, s32[8]{0:T(128)}, u32[]{:S(2)}) copy-start(s32[8]{0:T(128)} %constant.159.clone) | copy-start | bytes 100
  15.8 5.4 %copy-start.11 = (f32[1,128,512]{2,1,0:T(8,128)S(1)}, f32[1,128,512]{2,1,0:T(8,128)}, u32[]{:S(2)}) copy-start(f32[1,128,512]{2,1,0:T(8,128)} %param.23) | copy-start | bytes 786436
  21.1 6.8 %copy-start.3 = (s32[4]{0:T(128)S(1)}, s32[4]{0:T(128)}, u32[]{:S(2)}) copy-start(s32[4]{0:T(128)} %param.30) | copy-start | bytes 52
  21.2 9.7 %copy-start.10 = (f32[128,512]{1,0:T(8,128)S(1)}, f32[128,512]{1,0:T(8,128)}, u32[]{:S(2)}) copy-start(f32[128,512]{1,0:T(8,128)} %get-tuple-element.44) | copy-start | bytes 786436
  30.2 5.0 %collective-permute-start.10 = (f32[2,32,512]{2,1,0:T(8,128)S(1)}, f32[2,32,512]{2,1,0:T(8,128)S(1)}, u32[]{:S(2)}, u32[]{:S(2)}) collective-permute-start(f32[2,32,512]{2,1,0:T(8,128)S(1)} %slice.312), channel_id=1, source_target_pairs={{0,1},{1,0},{2,3},{3,2},{4,5},{5,4},{6,7},{7,6},{8,9},{9,8},{10,11... | collective-permute-start | bytes 393224 | tf_op jit(solution)/shard_map/ppermute | solution.py:16
  30.9 7.1 %collective-permute-start.5 = (f32[2,32,512]{2,1,0:T(8,128)S(1)}, f32[2,32,512]{2,1,0:T(8,128)S(1)}, u32[]{:S(2)}, u32[]{:S(2)}) collective-permute-start(f32[2,32,512]{2,1,0:T(8,128)S(1)} %slice.306), channel_id=1, source_target_pairs={{0,2},{1,3},{2,0},{3,1},{4,6},{5,7},{6,4},{7,5},{8,10},{9,11},{10,... | collective-permute-start | bytes 393224 | tf_op jit(solution)/shard_map/ppermute | solution.py:16
  31.0 17.2 %collective-permute-start.1 = (f32[2,136,512]{2,1,0:T(8,128)S(1)}, f32[2,136,512]{2,1,0:T(8,128)S(1)}, u32[]{:S(2)}, u32[]{:S(2)}) collective-permute-start(f32[2,136,512]{2,1,0:T(8,128)S(1)} %pad_maximum_fusion.7), channel_id=1, source_target_pairs={{0,8},{8,0},{16,24},{24,16},{1,9},{9,1},{17,25},{25,17},{2,10},{10... | collective-permute-start | bytes 1671176 | tf_op jit(solution)/shard_map/ppermute | solution.py:16
  35.3 10.8 %collective-permute-start.11 = (f32[2,32,512]{2,1,0:T(8,128)S(1)}, f32[2,32,512]{2,1,0:T(8,128)S(1)}, u32[]{:S(2)}, u32[]{:S(2)}) collective-permute-start(f32[2,32,512]{2,1,0:T(8,128)S(1)} %slice_select_fusion), channel_id=1, source_target_pairs={{0,4},{1,5},{2,6},{3,7},{4,0},{5,1},{6,2},{7,3},{8,12},{9,13},{10,... | collective-permute-start | bytes 393224 | tf_op jit(solution)/shard_map/ppermute | solution.py:16
  38.0 10.1 %collective-permute-start.6 = (f32[2,32,512]{2,1,0:T(8,128)S(1)}, f32[2,32,512]{2,1,0:T(8,128)S(1)}, u32[]{:S(2)}, u32[]{:S(2)}) collective-permute-start(f32[2,32,512]{2,1,0:T(8,128)S(1)} %slice_select_fusion.1), channel_id=1, source_target_pairs={{0,4},{1,5},{2,6},{3,7},{4,0},{5,1},{6,2},{7,3},{8,12},{9,13},{10,... | collective-permute-start | bytes 393224 | tf_op jit(solution)/shard_map/ppermute | solution.py:16
  46.1 13.2 %collective-permute-start.12 = (f32[2,32,512]{2,1,0:T(8,128)S(1)}, f32[2,32,512]{2,1,0:T(8,128)S(1)}, u32[]{:S(2)}, u32[]{:S(2)}) collective-permute-start(f32[2,32,512]{2,1,0:T(8,128)S(1)} %maximum_select_fusion.1), channel_id=1, source_target_pairs={{0,1},{1,0},{2,3},{3,2},{4,5},{5,4},{6,7},{7,6},{8,9},{9,8},{10,11... | collective-permute-start | bytes 393224 | tf_op jit(solution)/shard_map/ppermute | solution.py:16
  48.1 2.2 %copy-start.7 = (f32[512,2048]{1,0:T(8,128)S(1)}, f32[512,2048]{1,0:T(8,128)}, u32[]{:S(2)}) copy-start(f32[512,2048]{1,0:T(8,128)} %param.24) | copy-start | bytes 12582916
  48.1 11.6 %collective-permute-start.7 = (f32[2,32,512]{2,1,0:T(8,128)S(1)}, f32[2,32,512]{2,1,0:T(8,128)S(1)}, u32[]{:S(2)}, u32[]{:S(2)}) collective-permute-start(f32[2,32,512]{2,1,0:T(8,128)S(1)} %maximum_select_fusion), channel_id=1, source_target_pairs={{0,2},{1,3},{2,0},{3,1},{4,6},{5,7},{6,4},{7,5},{8,10},{9,11},{10,... | collective-permute-start | bytes 393224 | tf_op jit(solution)/shard_map/ppermute | solution.py:16
  51.5 1.2 slice-start
  52.8 1.9 %copy-start.16 = (f32[128,512]{1,0:T(8,128)S(1)}, f32[128,512]{1,0:T(8,128)}, u32[]{:S(2)}) copy-start(f32[128,512]{1,0:T(8,128)} %and_convert_fusion) | copy-start | bytes 786436
  54.7 2.9 %copy-start.17 = (f32[512]{0:T(512)S(1)}, f32[512]{0:T(512)}, u32[]{:S(2)}) copy-start(f32[512]{0:T(512)} %param.25) | copy-start | bytes 6148
  54.7 3.1 %copy-start.8 = (f32[512,512]{1,0:T(8,128)S(1)}, f32[512,512]{1,0:T(8,128)}, u32[]{:S(2)}) copy-start(f32[512,512]{1,0:T(8,128)} %param.26) | copy-start | bytes 3145732
  54.7 3.1 %copy-start.12 = (f32[1,128,512]{2,1,0:T(8,128)S(1)}, f32[1,128,512]{2,1,0:T(8,128)}, u32[]{:S(2)}) copy-start(f32[1,128,512]{2,1,0:T(8,128)} %param.23) | copy-start | bytes 786436
  54.7 3.1 %copy-start.14 = (f32[128,1024]{0,1:T(8,128)S(1)}, f32[128,1024]{0,1:T(8,128)}, u32[]{:S(2)}) copy-start(f32[128,1024]{0,1:T(8,128)} %divide_multiply_fusion.2) | copy-start | bytes 1572868
  57.5 1.9 %copy-start.24 = (s32[8]{0:T(128)S(1)}, s32[8]{0:T(128)}, u32[]{:S(2)}) copy-start(s32[8]{0:T(128)} %fusion.53) | copy-start | bytes 100
  58.3 6.8 %collective-permute-start.2 = (f32[1,128,512]{2,1,0:T(8,128)S(1)}, f32[1,128,512]{2,1,0:T(8,128)S(1)}, u32[]{:S(2)}, u32[]{:S(2)}) collective-permute-start(f32[1,128,512]{2,1,0:T(8,128)S(1)} %fusion.18), channel_id=1, source_target_pairs={{0,16},{8,24},{16,0},{24,8},{1,17},{9,25},{17,1},{25,9},{2,18},{10... | collective-permute-start | bytes 786440 | tf_op jit(solution)/shard_map/ppermute | solution.py:16
  59.4 7.8 %collective-permute-start.13 = (f32[4,32,512]{2,1,0:T(8,128)S(1)}, f32[4,32,512]{2,1,0:T(8,128)S(1)}, u32[]{:S(2)}, u32[]{:S(2)}) collective-permute-start(f32[4,32,512]{2,1,0:T(8,128)S(1)} %pad_maximum_fusion.12), channel_id=1, source_target_pairs={{0,2},{1,3},{2,0},{3,1},{4,6},{5,7},{6,4},{7,5},{8,10},{9,11},{10,... | collective-permute-start | bytes 786440 | tf_op jit(solution)/shard_map/ppermute | solution.py:16
  60.5 8.3 %collective-permute-start.8 = (f32[4,32,512]{2,1,0:T(8,128)}, f32[4,32,512]{2,1,0:T(8,128)}, u32[]{:S(2)}, u32[]{:S(2)}) collective-permute-start(f32[4,32,512]{2,1,0:T(8,128)} %pad_maximum_fusion.11), channel_id=1, source_target_pairs={{0,1},{1,0},{2,3},{3,2},{4,5},{5,4},{6,7},{7,6},{8,9},{9,8},{10,11... | collective-permute-start | bytes 786440 | tf_op jit(solution)/shard_map/ppermute | solution.py:16
  65.1 2.1 %copy-start.13 = (f32[1,128,512]{2,1,0:T(8,128)}, f32[1,128,512]{2,1,0:T(8,128)S(1)}, u32[]{:S(2)}) copy-start(f32[1,128,512]{2,1,0:T(8,128)S(1)} %collective-permute-done.2) | copy-start | bytes 786436
  66.0 5.2 %collective-permute-start.3 = (f32[2,128,512]{2,1,0:T(8,128)}, f32[2,128,512]{2,1,0:T(8,128)}, u32[]{:S(2)}, u32[]{:S(2)}) collective-permute-start(f32[2,128,512]{2,1,0:T(8,128)} %pad_maximum_fusion.8), channel_id=1, source_target_pairs={{0,8},{8,0},{16,24},{24,16},{1,9},{9,1},{17,25},{25,17},{2,10},{10... | collective-permute-start | bytes 1572872 | tf_op jit(solution)/shard_map/ppermute | solution.py:16
  71.2 2.6 %copy-start.18 = (s32[4,1,128]{2,1,0:T(1,128)S(1)}, s32[4,1,128]{2,1,0:T(1,128)}, u32[]{:S(2)}) copy-start(s32[4,1,128]{2,1,0:T(1,128)} %maximum_convert_fusion.1) | copy-start | bytes 6148
  71.2 2.6 %copy-start.21 = (s32[512]{0:T(512)S(1)}, s32[512]{0:T(512)}, u32[]{:S(2)}) copy-start(s32[512]{0:T(512)} %broadcast_bitcast_fusion) | copy-start | bytes 6148
  71.2 2.6 %copy-start.22 = (s32[512]{0:T(512)S(1)}, s32[512]{0:T(512)}, u32[]{:S(2)}) copy-start(s32[512]{0:T(512)} %get-tuple-element.64) | copy-start | bytes 6148
  71.2 2.6 %copy-start.23 = (s32[512]{0:T(512)S(1)}, s32[512]{0:T(512)}, u32[]{:S(2)}) copy-start(s32[512]{0:T(512)} %get-tuple-element.65) | copy-start | bytes 6148
  73.8 4.5 %copy-start.9 = (f32[512,512]{1,0:T(8,128)S(1)}, f32[512,512]{1,0:T(8,128)}, u32[]{:S(2)}) copy-start(f32[512,512]{1,0:T(8,128)} %copy.59) | copy-start | bytes 3145732
  78.3 1.7 copy-start.26
  80.9 6.0 %copy-start.20 = (s32[4]{0:T(128)S(1)}, s32[4]{0:T(128)}, u32[]{:S(2)}) copy-start(s32[4]{0:T(128)} %get-tuple-element.55) | copy-start | bytes 52
  82.2 8.9 %collective-permute-start.24 = (f32[4,4,8,512]{3,2,1,0:T(8,128)}, f32[4,4,8,512]{3,2,1,0:T(8,128)S(1)}, u32[]{:S(2)}, u32[]{:S(2)}) collective-permute-start(f32[4,4,8,512]{3,2,1,0:T(8,128)} %slice.328), channel_id=1, source_target_pairs={{0,2},{1,3},{2,0},{3,1},{4,6},{5,7},{6,4},{7,5},{8,10},{9,11},{10,... | collective-permute-start | bytes 786440 | tf_op jit(solution)/shard_map/ppermute | solution.py:16
  84.9 8.7 %collective-permute-start.21 = (f32[4,4,8,512]{3,2,1,0:T(8,128)S(1)}, f32[4,4,8,512]{3,2,1,0:T(8,128)S(1)}, u32[]{:S(2)}, u32[]{:S(2)}) collective-permute-start(f32[4,4,8,512]{3,2,1,0:T(8,128)S(1)} %slice.321), channel_id=1, source_target_pairs={{0,1},{1,0},{2,3},{3,2},{4,5},{5,4},{6,7},{7,6},{8,9},{9,8},{10,11... | collective-permute-start | bytes 786440 | tf_op jit(solution)/shard_map/ppermute | solution.py:16
  86.9 19.9 %copy-start.19 = (s32[4]{0:T(128)S(1)}, s32[4]{0:T(128)}, u32[]{:S(2)}) copy-start(s32[4]{0:T(128)} %get-tuple-element.63) | copy-start | bytes 52
  91.2 17.7 %copy-start.15 = (s32[4,512]{1,0:T(4,128)S(1)}, s32[4,512]{1,0:T(4,128)}, u32[]{:S(2)}) copy-start(s32[4,512]{1,0:T(4,128)} %param.29) | copy-start | bytes 24580
  91.2 5.2 %collective-permute-start.25 = (f32[2,4,8,512]{3,2,1,0:T(8,128)S(1)}, f32[2,4,8,512]{3,2,1,0:T(8,128)S(1)}, u32[]{:S(2)}, u32[]{:S(2)}) collective-permute-start(f32[2,4,8,512]{3,2,1,0:T(8,128)S(1)} %slice.330), channel_id=1, source_target_pairs={{0,1},{1,0},{2,3},{3,2},{4,5},{5,4},{6,7},{7,6},{8,9},{9,8},{10,11... | collective-permute-start | bytes 393224 | tf_op jit(solution)/shard_map/ppermute | solution.py:16
  93.6 6.2 %collective-permute-start.22 = (f32[2,4,8,512]{3,2,1,0:T(8,128)S(1)}, f32[2,4,8,512]{3,2,1,0:T(8,128)S(1)}, u32[]{:S(2)}, u32[]{:S(2)}) collective-permute-start(f32[2,4,8,512]{3,2,1,0:T(8,128)S(1)} %slice.323), channel_id=1, source_target_pairs={{0,2},{1,3},{2,0},{3,1},{4,6},{5,7},{6,4},{7,5},{8,10},{9,11},{10,... | collective-permute-start | bytes 393224 | tf_op jit(solution)/shard_map/ppermute | solution.py:16
  96.4 6.7 %collective-permute-start.26 = (f32[1,4,8,512]{3,2,1,0:T(8,128)S(1)}, f32[1,4,8,512]{3,2,1,0:T(8,128)S(1)}, u32[]{:S(2)}, u32[]{:S(2)}) collective-permute-start(f32[1,4,8,512]{3,2,1,0:T(8,128)S(1)} %slice.332), channel_id=1, source_target_pairs={{0,4},{1,5},{2,6},{3,7},{4,0},{5,1},{6,2},{7,3},{8,12},{9,13},{10,... | collective-permute-start | bytes 196616 | tf_op jit(solution)/shard_map/ppermute | solution.py:16
  99.9 6.1 %collective-permute-start.23 = (f32[1,4,8,512]{3,2,1,0:T(8,128)S(1)}, f32[1,4,8,512]{3,2,1,0:T(8,128)S(1)}, u32[]{:S(2)}, u32[]{:S(2)}) collective-permute-start(f32[1,4,8,512]{3,2,1,0:T(8,128)S(1)} %slice.325), channel_id=1, source_target_pairs={{0,4},{1,5},{2,6},{3,7},{4,0},{5,1},{6,2},{7,3},{8,12},{9,13},{10,... | collective-permute-start | bytes 196616 | tf_op jit(solution)/shard_map/ppermute | solution.py:16
  106.7 1.3 collective-permute-start.27
  108.0 4.3 %collective-permute-start.28 = (f32[1,2,16,512]{3,2,0,1:T(8,128)S(1)}, f32[1,2,16,512]{3,2,0,1:T(8,128)S(1)}, u32[]{:S(2)}, u32[]{:S(2)}) collective-permute-start(f32[1,2,16,512]{3,2,0,1:T(8,128)S(1)} %get-tuple-element.48), channel_id=1, source_target_pairs={{0,16},{8,24},{16,0},{24,8},{1,17},{9,25},{17,1},{25,9},{2,18},{10... | collective-permute-start | bytes 196616 | tf_op jit(solution)/shard_map/ppermute | solution.py:16
  115.6 18.3 %all-to-all-start = ((f32[8,16,1024]{2,1,0:T(8,128)}), f32[8,16,1024]{2,1,0:T(8,128)S(1)}, u32[]{:S(2)}, u32[]{:S(2)}) async-start(f32[8,16,1024]{2,1,0:T(8,128)} %multiply_reduce_fusion), calls=%async_computation | async-start | bytes 1048576 | tf_op jit(solution)/shard_map/all_to_all | solution.py:175
  120.8 27.3 %collective-permute-start.14 = (f32[8,128]{1,0:T(8,128)S(1)}, f32[8,128]{1,0:T(8,128)S(1)}, u32[]{:S(2)}, u32[]{:S(2)}) collective-permute-start(f32[8,128]{1,0:T(8,128)S(1)} %broadcast_in_dim.27), channel_id=1, source_target_pairs={{0,16},{8,24},{16,0},{24,8},{1,17},{9,25},{17,1},{25,9},{2,18},{10... | collective-permute-start | bytes 12296 | tf_op jit(solution)/shard_map/ppermute | solution.py:16
  134.0 12.2 %collective-permute-start.29 = (f32[1,1024,128]{2,1,0:T(8,128)S(1)}, f32[1,1024,128]{2,1,0:T(8,128)S(1)}, u32[]{:S(2)}, u32[]{:S(2)}) collective-permute-start(f32[1,1024,128]{2,1,0:T(8,128)S(1)} %bitcast.113), channel_id=1, source_target_pairs={{0,16},{8,24},{16,0},{24,8},{1,17},{9,25},{17,1},{25,9},{2,18},{10... | collective-permute-start | bytes 1572872 | tf_op jit(solution)/shard_map/ppermute | solution.py:16
  138.4 17.7 %collective-permute-start.19 = (f32[2,128,512]{2,1,0:T(8,128)}, f32[2,128,512]{2,1,0:T(8,128)}, u32[]{:S(2)}, u32[]{:S(2)}) collective-permute-start(f32[2,128,512]{2,1,0:T(8,128)} %bitcast.33), channel_id=1, source_target_pairs={{0,8},{8,0},{16,24},{24,16},{1,9},{9,1},{17,25},{25,17},{2,10},{10... | collective-permute-start | bytes 1572872 | tf_op jit(solution)/shard_map/ppermute | solution.py:16
  146.3 0.8 copy-start.5
  148.1 17.1 %collective-permute-start.30 = (f32[2,1024,128]{2,1,0:T(8,128)}, f32[2,1024,128]{2,1,0:T(8,128)}, u32[]{:S(2)}, u32[]{:S(2)}) collective-permute-start(f32[2,1024,128]{2,1,0:T(8,128)} %pad_maximum_fusion.4), channel_id=1, source_target_pairs={{0,8},{8,0},{16,24},{24,16},{1,9},{9,1},{17,25},{25,17},{2,10},{10... | collective-permute-start | bytes 3145736 | tf_op jit(solution)/shard_map/ppermute | solution.py:16
  148.8 2.0 %collective-permute-start.15 = (f32[8,128]{1,0:T(8,128)S(1)}, f32[8,128]{1,0:T(8,128)S(1)}, u32[]{:S(2)}, u32[]{:S(2)}) collective-permute-start(f32[8,128]{1,0:T(8,128)S(1)} %broadcast_add_fusion), channel_id=1, source_target_pairs={{0,8},{8,0},{16,24},{24,16},{1,9},{9,1},{17,25},{25,17},{2,10},{10... | collective-permute-start | bytes 12296 | tf_op jit(solution)/shard_map/ppermute | solution.py:16
  151.5 4.6 %collective-permute-start.16 = (f32[8,128]{1,0:T(8,128)S(1)}, f32[8,128]{1,0:T(8,128)S(1)}, u32[]{:S(2)}, u32[]{:S(2)}) collective-permute-start(f32[8,128]{1,0:T(8,128)S(1)} %fusion.82), channel_id=1, source_target_pairs={{0,4},{1,5},{2,6},{3,7},{4,0},{5,1},{6,2},{7,3},{8,12},{9,13},{10,... | collective-permute-start | bytes 12296 | tf_op jit(solution)/shard_map/ppermute | solution.py:16
  156.1 3.6 %collective-permute-start.17 = (f32[8,128]{1,0:T(8,128)S(1)}, f32[8,128]{1,0:T(8,128)S(1)}, u32[]{:S(2)}, u32[]{:S(2)}) collective-permute-start(f32[8,128]{1,0:T(8,128)S(1)} %add.255), channel_id=1, source_target_pairs={{0,2},{1,3},{2,0},{3,1},{4,6},{5,7},{6,4},{7,5},{8,10},{9,11},{10,... | collective-permute-start | bytes 12296 | tf_op jit(solution)/shard_map/ppermute | solution.py:16
  157.2 9.3 %copy-start.6 = (f32[1,1024,128]{2,1,0:T(8,128)S(1)}, f32[1,1024,128]{2,1,0:T(8,128)}, u32[]{:S(2)}) copy-start(f32[1,1024,128]{2,1,0:T(8,128)} %copy-done.5) | copy-start | bytes 1572868
  157.3 7.3 %collective-permute-start.20 = (f32[1,128,512]{2,1,0:T(8,128)S(1)}, f32[1,128,512]{2,1,0:T(8,128)S(1)}, u32[]{:S(2)}, u32[]{:S(2)}) collective-permute-start(f32[1,128,512]{2,1,0:T(8,128)S(1)} %slice.318), channel_id=1, source_target_pairs={{0,16},{8,24},{16,0},{24,8},{1,17},{9,25},{17,1},{25,9},{2,18},{10... | collective-permute-start | bytes 786440 | tf_op jit(solution)/shard_map/ppermute | solution.py:16
  159.7 3.6 %collective-permute-start.18 = (f32[8,128]{1,0:T(8,128)S(1)}, f32[8,128]{1,0:T(8,128)S(1)}, u32[]{:S(2)}, u32[]{:S(2)}) collective-permute-start(f32[8,128]{1,0:T(8,128)S(1)} %add.256), channel_id=1, source_target_pairs={{0,1},{1,0},{2,3},{3,2},{4,5},{5,4},{6,7},{7,6},{8,9},{9,8},{10,11... | collective-permute-start | bytes 12296 | tf_op jit(solution)/shard_map/ppermute | solution.py:16

commit v3 on v0

v3 whole, which is shorter than its diff:
```python
import functools

import jax
import jax.numpy as jnp
from jax import lax
from jax.experimental import pallas as pl
from jax.experimental.pallas import tpu as pltpu
from jax.sharding import PartitionSpec as P

H = 16
LANES = 128
EXTRA = 8

beta_weight = 0.75
epsilon = 1e-05

f32, bf16, i32 = jnp.float32, jnp.bfloat16, jnp.int32
high = lax.Precision.HIGH
NN, NT = ((1,), (0,)), ((1,), (1,))
params = pltpu.CompilerParams(vmem_limit_bytes=40 * 2**20)


def swap(block, axis, bit):
    size = lax.axis_size(axis)
    return lax.ppermute(block, axis, [(i, i ^ (1 << bit)) for i in range(size)])


def bits_of(size):
    return list(range(size.bit_length() - 1))[::-1]


def two_orders(size):
    up = bits_of(size)
    return [up, up[:-2] + up[:-3:-1]]


def orders(bits):
    order = [0]
    for bit in bits:
        order = order + [r ^ (1 << bit) for r in order]
    return order


def gather_pieces(block, axis, bits):
    pieces = [block]
    for bit in bits:
        pieces = pieces + [swap(piece, axis, bit) for piece in pieces]
    return pieces


def reduce_steps(kept, sent, axis, bits):
    for n, bit in enumerate(bits):
        got = swap(sent, axis, bit)
        if n == len(bits) - 1:
            return (kept + got)[0]
        half = kept.shape[0] // 2
        sent = kept[half:] + got[half:]
        kept = kept[:half] + got[:half]


def true_order(stacked, order, index):
    place = [0] * len(order)
    for k, r in enumerate(order):
        place[r] = k
    return stacked[jnp.array(place, i32)[index ^ jnp.arange(len(order), dtype=i32)]]


def split(x):
    top = x.astype(bf16)
    return top, (x - top.astype(f32)).astype(bf16)


def dot(a, b, dims):
    return lax.dot_general(a, b, (dims, ((), ())), preferred_element_type=f32)


def dot3(a, b, dims):
    return dot(a[0], b[0], dims) + (dot(a[0], b[1], dims) + dot(a[1], b[0], dims))


def silu(x):
    return x / (1.0 + jnp.exp(jnp.minimum(-x, 87.0)))


def prepare_kernel(x_ref, u_ref, v_ref, q_ref, k_ref, wo_ref, gates_ref, queries_ref, vk_hi, vk_lo, wo_hi, wo_lo):
    x = split(x_ref[...])
    uq = split(jnp.concatenate([u_ref[...], q_ref[...]], axis=1))
    both = silu(dot3(x, uq, NN))
    gates_ref[...] = both[:, :LANES]
    queries_ref[...] = both[:, LANES:]
    vk_hi[0], vk_lo[0] = split(jnp.concatenate([v_ref[...], k_ref[...]], axis=1))
    wo_hi[...], wo_lo[...] = split(wo_ref[...])


def prepare(rows_in, w_uvqk, w_out):
    tok, width = rows_in.shape
    n = width // LANES

    def column(part):
        return pl.BlockSpec((width, LANES), lambda j: (0, part * n + j))

    own = pl.BlockSpec((tok, LANES), lambda j: (0, j))
    pair = pl.BlockSpec((1, width, 2 * LANES), lambda j: (j, 0, 0))
    rows = pl.BlockSpec((LANES, width), lambda j: (j, 0))
    return pl.pallas_call(
        prepare_kernel,
        grid=(n,),
        in_specs=[pl.BlockSpec((tok, width), lambda j: (0, 0)), *[column(p) for p in range(4)], rows],
        out_specs=[own, own, pair, pair, rows, rows],
        out_shape=[jax.ShapeDtypeStruct((tok, width), f32)] * 2
        + [jax.ShapeDtypeStruct((n, width, 2 * LANES), bf16)] * 2
        + [jax.ShapeDtypeStruct((width, width), bf16)] * 2,
        compiler_params=params,
        cost_estimate=pl.CostEstimate(flops=8 * tok * width * width, bytes_accessed=6 * width * width * 4, transcendentals=0),
        name="prepare",
    )(rows_in, w_uvqk, w_uvqk, w_uvqk, w_uvqk, w_out)


def attend_kernel(order, n_seq, meta, *refs):
    x_refs, (q_ref, vk_hi, vk_lo, out_ref, x_hi, x_lo, allowed) = refs[:n_seq], refs[n_seq:]
    tok = q_ref.shape[0]
    head = x_hi.shape[1] // H

    @pl.when(pl.program_id(0) == 0)
    def _():
        me = meta[0]
        q_pos = me * tok + lax.broadcasted_iota(i32, (tok, tok), 0)
        col = lax.broadcasted_iota(i32, (tok, tok), 1)

        def user(pos):
            ids, end = jnp.zeros_like(pos), 0
            for k in range(meta.shape[0] - 1):
                end = end + meta[1 + k]
                ids = ids + (pos >= end).astype(i32)
            return ids

        q_user = user(q_pos)
        for n in range(n_seq):
            span = pl.ds(n * tok, tok)
            x_hi[span], x_lo[span] = split(x_refs[n][...])
            k_pos = (me ^ order[n]) * tok + col
            seen = (q_user == user(k_pos)) & (q_pos >= k_pos)
            allowed[:, span] = seen.astype(f32)

    x = (x_hi[...], x_lo[...])
    vk = silu(dot3(x, (vk_hi[0], vk_lo[0]), NN))
    v_hi, v_lo = split(vk[:, :LANES])
    k_hi, k_lo = split(vk[:, LANES:])
    k_both = jnp.concatenate([k_hi, k_lo], axis=1)
    v_both = jnp.concatenate([v_hi, v_lo], axis=1)
    queries = q_ref[...]
    of_head = lax.broadcasted_iota(i32, (tok, LANES), 1) // head
    total = jnp.zeros((tok, LANES), f32)
    for h in range(LANES // head):
        q_hi, q_lo = split(jnp.where(of_head == h, queries, 0.0))
        scores = dot(jnp.concatenate([q_hi, q_hi], axis=1), k_both, NT) + dot(q_lo, k_hi, NT)
        w_hi, w_lo = split(silu(scores) * allowed[...])
        wide = dot(w_hi, v_both, NN)
        mine = wide[:, :LANES] + wide[:, LANES:] + dot(w_lo, v_hi, NN)
        total = jnp.where(of_head == h, mine, total)
    out_ref[...] = total


def attend(meta, pieces, order, queries, vk_hi, vk_lo, first, count):
    tok, width = pieces[0].shape
    n_seq = len(pieces)
    whole = pl.BlockSpec((tok, width), lambda j: (0, 0))
    pair = pl.BlockSpec((1, width, 2 * LANES), lambda j: (first + j, 0, 0))
    return pl.pallas_call(
        functools.partial(attend_kernel, order, n_seq),
        grid=(count,),
        in_specs=[pl.BlockSpec(memory_space=pltpu.SMEM)]
        + [whole] * n_seq
        + [pl.BlockSpec((tok, LANES), lambda j: (0, first + j)), pair, pair],
        out_specs=pl.BlockSpec((tok, LANES), lambda j: (0, j)),
        out_shape=jax.ShapeDtypeStruct((tok, count * LANES), f32),
        scratch_shapes=[
            pltpu.VMEM((n_seq * tok, width), bf16),
            pltpu.VMEM((n_seq * tok, width), bf16),
            pltpu.VMEM((tok, n_seq * tok), f32),
        ],
        compiler_params=params,
        cost_estimate=pl.CostEstimate(flops=count * 2000000000, bytes_accessed=2 * width * width * 4, transcendentals=0),
        name="attend",
    )(meta, *pieces, queries, vk_hi, vk_lo)


def project_kernel(n_parts, words, *refs):
    parts, (gates, gain, wo_hi, wo_lo, rows_in, targets, out_ref) = refs[:n_parts], refs[n_parts:]
    tok, width = rows_in.shape
    attended = jnp.concatenate([p[...] for p in parts], axis=1)
    centered = attended - jnp.mean(attended, axis=1, keepdims=True)
    variance = jnp.mean(centered * centered, axis=1, keepdims=True)
    normed = centered * lax.rsqrt(variance + epsilon) * gain[...]
    gated = split(normed * gates[...])
    out_ref[:tok] = rows_in[...] + dot3(gated, (wo_hi[...], wo_lo[...]), NN)
    out_ref[tok:] = jnp.zeros((EXTRA, width), f32)
    out_ref[tok : tok + 1, :tok] = targets[...].astype(f32)
    for k in range(words.shape[1]):
        out_ref[tok + 1 : tok + 2, k * LANES : (k + 1) * LANES] = jnp.full((1, LANES), words[0, k].astype(f32))


def project(words, parts, gates, gain, wo_hi, wo_lo, rows_in, targets):
    tok, width = rows_in.shape
    return pl.pallas_call(
        lambda words, *refs: project_kernel(len(parts), words, *refs),
        in_specs=[pl.BlockSpec(memory_space=pltpu.SMEM)] + [pl.BlockSpec(memory_space=pltpu.VMEM)] * (len(parts) + 6),
        out_specs=pl.BlockSpec(memory_space=pltpu.VMEM),
        out_shape=jax.ShapeDtypeStruct((tok + EXTRA, width), f32),
        compiler_params=params,
        cost_estimate=pl.CostEstimate(flops=6 * tok * width * width, bytes_accessed=2 * width * width * 4, transcendentals=0),
        name="project",
    )(words, *parts, gates, gain, wo_hi, wo_lo, rows_in, targets)


def loss_kernel(plan, meta, *refs):
    n_seq, n_item, seq_order, item_orders, aligned = plan
    o_refs, refs = refs[:n_seq], refs[n_seq:]
    n_refs, refs = refs[: 4 if aligned else 1], refs[4 if aligned else 1 :]
    n_out = 4 if aligned else 1
    panel_refs, (kept_rows, sent_rows, loss_ref, n_hi, n_lo, o_hi, o_lo, g_hi, g_lo, panel) = refs[:n_out], refs[n_out:]
    me, item = meta[0], meta[1]
    n_neg, width = n_hi.shape
    tok = o_refs[0].shape[0] - EXTRA

    if aligned:
        n_part = n_neg // (2 * n_item)
        for half in range(2):
            for m, r in enumerate(item_orders[half]):
                source = n_refs[2 * half + m // (n_item // 2)]
                rows = source[pl.ds((m % (n_item // 2)) * n_part, n_part)]
                place = pl.ds(pl.multiple_of(half * (n_neg // 2) + (item ^ r) * n_part, n_part), n_part)
                n_hi[place], n_lo[place] = split(rows)
    else:
        n_hi[...], n_lo[...] = split(n_refs[0][...])

    negatives = (n_hi[...], n_lo[...])
    loss = jnp.zeros((1, 2 * tok), f32)
    columns = me * n_neg + lax.broadcasted_iota(i32, (n_neg, 2 * tok), 0)
    for p in range(n_seq // 2):
        both = o_refs[2 * p], o_refs[2 * p + 1]
        span = pl.ds(2 * p * tok, 2 * tok)
        outputs = split(jnp.concatenate([b[:tok] for b in both], axis=0).T)
        o_hi[:, span], o_lo[:, span] = outputs
        target = jnp.concatenate([b[tok : tok + 1, :tok] for b in both], axis=1).astype(i32)
        words = jnp.concatenate([b[tok + 1 : tok + 2, :tok] for b in both], axis=1).astype(i32)
        logits = dot3(negatives, outputs, NN)
        is_target = columns == target
        live = jnp.bitwise_and(jnp.right_shift(jnp.broadcast_to(words, columns.shape), columns // LANES), 1).astype(f32)
        weight = jnp.where(is_target, beta_weight, live)
        signed = jnp.where(is_target, -logits, logits)
        small = jnp.exp(-jnp.abs(logits))
        loss = loss + jnp.sum(weight * (jnp.maximum(signed, 0.0) + jnp.log1p(small)), axis=0, keepdims=True)
        chance = jnp.where(signed >= 0.0, 1.0, small) / (1.0 + small)
        grad = jnp.where(is_target, -weight, weight) * chance
        g_hi[:, span], g_lo[:, span] = split(grad)
        rows = dot3(split(grad.T), negatives, NN)
        for k in range(2):
            n = 2 * p + k
            target_ref = kept_rows if n < n_seq // 2 else sent_rows
            target_ref[n % (n_seq // 2)] = rows[k * tok : (k + 1) * tok]
    loss_ref[...] = jnp.full((8, LANES), jnp.sum(loss))
    whole = dot3((o_hi[...], o_lo[...]), (g_hi[...], g_lo[...]), NT)
    if not aligned:
        panel_refs[0][...] = whole
        return
    panel[...] = whole
    n_dim = width // (n_seq * n_item)
    part = n_dim // 2
    for half in range(2):
        for m, r in enumerate(item_orders[half]):
            out = panel_refs[2 * half + m // (n_item // 2)]
            for n, q in enumerate(seq_order):
                first = (me ^ q) * (n_item * n_dim) + (item ^ r) * n_dim + half * part
                out[m % (n_item // 2), n] = panel[pl.ds(pl.multiple_of(first, part), part)]


def loss_terms(meta, outputs, negatives, plan, n_neg):
    n_seq, n_item, _, _, aligned = plan
    tok, width = outputs[0].shape[0] - EXTRA, outputs[0].shape[1]
    group_len = tok * n_seq
    vmem = pl.BlockSpec(memory_space=pltpu.VMEM)
    if aligned:
        panel = [jax.ShapeDtypeStruct((n_item // 2, n_seq, width // (2 * n_seq * n_item), n_neg), f32)] * 4
    else:
        panel = [jax.ShapeDtypeStruct((width, n_neg), f32)]
    rows = [jax.ShapeDtypeStruct((n_seq // 2, tok, width), f32)] * 2
    out_shape = panel + rows + [jax.ShapeDtypeStruct((8, LANES), f32)]
    return pl.pallas_call(
        functools.partial(loss_kernel, plan),
        in_specs=[pl.BlockSpec(memory_space=pltpu.SMEM)] + [vmem] * (n_seq + len(negatives)),
        out_specs=[vmem] * len(out_shape),
        out_shape=out_shape,
        scratch_shapes=[pltpu.VMEM((n_neg, width), bf16)] * 2
        + [pltpu.VMEM((width, group_len), bf16)] * 2
        + [pltpu.VMEM((n_neg, group_len), bf16)] * 2
        + [pltpu.VMEM((width, n_neg), f32)],
        compiler_params=params,
        cost_estimate=pl.CostEstimate(flops=18 * group_len * width * n_neg, bytes_accessed=16 * n_neg * width, transcendentals=0),
        name="loss_terms",
    )(meta, *outputs, *negatives)


def spread_kernel(owner, moved, ids, out_ref):
    n_src, n_dim, n_neg = moved.shape
    n_item, _, n_rows = out_ref.shape
    row = lax.broadcasted_iota(i32, (n_rows, n_neg), 0)
    spread = []
    for p in range(n_src):
        hot = jnp.where(row == ids[p : p + 1], 1.0, 0.0).astype(bf16)
        both = dot(jnp.concatenate(split(moved[p]), axis=0), hot, NT)
        spread.append(both[:n_dim] + both[n_dim:])
    for j in range(n_item):
        total = jnp.where(owner[0] == j, spread[0], 0.0)
        for p in range(1, n_src):
            total = total + jnp.where(owner[p] == j, spread[p], 0.0)
        out_ref[j] = total


def spread_rows(owner, moved, ids, n_item, n_rows):
    vmem = pl.BlockSpec(memory_space=pltpu.VMEM)
    return pl.pallas_call(
        spread_kernel,
        in_specs=[pl.BlockSpec(memory_space=pltpu.SMEM), vmem, vmem],
        out_specs=vmem,
        out_shape=jax.ShapeDtypeStruct((n_item, moved.shape[1], n_rows), f32),
        compiler_params=params,
        cost_estimate=pl.CostEstimate(flops=4 * moved.size * n_rows, bytes_accessed=2**21, transcendentals=0),
        name="spread_rows",
    )(owner, moved, ids)


def assemble_kernel(order, meta, *refs):
    pieces, out_ref = refs[:-1], refs[-1]
    cols = pieces[0].shape[0]
    for piece, r in zip(pieces, order):
        place = pl.ds(pl.multiple_of((meta[0] ^ r) * cols, cols), cols)
        out_ref[:, place] = piece[...].T


def assemble(meta, pieces, order):
    cols, n_rows = pieces[0].shape
    width = cols * len(pieces)
    step = min(n_rows, 256)
    return pl.pallas_call(
        functools.partial(assemble_kernel, order),
        grid=(n_rows // step,),
        in_specs=[pl.BlockSpec(memory_space=pltpu.SMEM)] + [pl.BlockSpec((cols, step), lambda j: (0, j))] * len(pieces),
        out_specs=pl.BlockSpec((step, width), lambda j: (j, 0)),
        out_shape=jax.ShapeDtypeStruct((n_rows, width), f32),
        compiler_params=params,
        cost_estimate=pl.CostEstimate(flops=0, bytes_accessed=8 * n_rows * width, transcendentals=0),
        name="assemble",
    )(meta, *pieces)


def per_device(
    events,
    w_uvqk,
    out_gain,
    w_out,
    item_table,
    user_lengths,
    neg_ids,
    panel_owner,
    block_mask,
    targets,
):
    rows_in = events[0]
    tok, width = rows_in.shape
    n_rows = item_table.shape[0]
    n_seq, n_item = lax.axis_size("seq"), lax.axis_size("item")
    s, i = lax.axis_index("seq").astype(i32), lax.axis_index("item").astype(i32)
    group_len = tok * n_seq
    seq_bits = bits_of(n_seq)
    seq_order = orders(seq_bits)
    bit_lists = two_orders(n_item)
    item_orders = [orders(bits) for bits in bit_lists]
    flat_ids = neg_ids.reshape(-1)
    n_neg = flat_ids.shape[0] // n_seq
    per_panel = neg_ids.shape[1] // n_neg
    n_part = n_neg // (2 * n_item)
    n_dim = width // (n_seq * n_item)
    aligned = n_part % 16 == 0 and n_dim % 16 == 0 and (n_item * n_dim) % LANES == 0
    plan = (n_seq, n_item, tuple(seq_order), tuple(tuple(o) for o in item_orders), aligned)

    rel = i ^ jnp.array(item_orders, i32)
    spot = s * n_neg + rel[:, :, None] * n_part + jnp.arange(n_part, dtype=i32)
    spot = spot + jnp.array([0, n_neg // 2], i32)[:, None, None]
    own_ids = flat_ids.at[spot.reshape(2, -1)].get(mode="promise_in_bounds")
    root = panel_owner[s // per_panel]
    parts = [
        item_table.at[own_ids[half]].get(mode="promise_in_bounds").reshape(n_item, n_part, width) for half in range(2)
    ]
    for step in range(len(bit_lists[0]) - 1):
        for half, bits in enumerate(bit_lists):
            bit, part = bits[-1 - step], parts[half]
            cut = part.shape[0] // 2
            other = swap(part[cut:], "item", bit)
            parts[half] = jnp.where(((i ^ root) >> bit) & 1 == 0, part[:cut], other)
    for half, bits in enumerate(bit_lists):
        other = swap(parts[half], "item", bits[0])
        same = ((i ^ root) >> bits[0]) & 1 == 0
        parts[half] = jnp.where(same, parts[half], jnp.concatenate([other[1:], other[:1]], axis=0))
    for step in range(1, len(bit_lists[0]) - 1):
        for half, bits in enumerate(bit_lists):
            parts[half] = jnp.concatenate([parts[half], swap(parts[half], "item", bits[step])], axis=0)
    negatives = []
    for half, bits in enumerate(bit_lists):
        negatives += [parts[half], swap(parts[half], "item", bits[-1])]
    if aligned:
        negatives = [n.reshape(-1, width) for n in negatives]
    else:
        negatives = [
            true_order(jnp.concatenate(negatives[2 * half : 2 * half + 2], axis=0), item_orders[half], i)
            for half in range(2)
        ]
        negatives = [jnp.concatenate([n.reshape(-1, width) for n in negatives], axis=0)]

    meta = jnp.concatenate([s[None], user_lengths[0]])
    pieces = gather_pieces(rows_in, "seq", seq_bits)
    gates, queries, vk_hi, vk_lo, wo_hi, wo_lo = prepare(rows_in, w_uvqk, w_out)
    groups = width // LANES
    attended = [attend(meta, pieces, seq_order, queries, vk_hi, vk_lo, 0, groups)]
    own_outputs = project(block_mask, attended, gates, out_gain[None], wo_hi, wo_lo, rows_in, targets)
    outputs = gather_pieces(own_outputs, "seq", seq_bits)

    place = jnp.stack([s, i])
    *panel, kept_rows, sent_rows, loss_total = loss_terms(place, outputs, negatives, plan, n_neg)
    if not aligned:
        blocks = panel[0].reshape(n_seq, n_item, 2, n_dim // 2, n_neg).transpose(2, 1, 0, 3, 4)
        panel = []
        for half in range(2):
            mine = blocks[half][rel[half]][:, s ^ jnp.array(seq_order, i32)]
            panel += [mine[: n_item // 2], mine[n_item // 2 :]]
    event_grad = reduce_steps(kept_rows, sent_rows, "seq", seq_bits[::-1])
    for axis, size in (("seq", n_seq), ("item", n_item)):
        for bit in bits_of(size):
            loss_total = loss_total + swap(loss_total, axis, bit)
    loss_total = loss_total[0, 0]

    sums = [
        reduce_steps(panel[2 * half], panel[2 * half + 1], "item", bits[::-1]) for half, bits in enumerate(bit_lists)
    ]
    moved = jnp.concatenate(sums, axis=1)[:, None]
    for bit in seq_bits[::-1]:
        half = moved.shape[0] // 2
        moved = jnp.concatenate([moved[:half], swap(moved[half:], "seq", bit)], axis=1)
    moved = moved[0]
    source = s ^ jnp.array(orders(seq_bits[::-1]), i32)
    ids = flat_ids.reshape(n_seq, n_neg)[source]
    owner = panel_owner[source // per_panel]
    if aligned:
        sent = spread_rows(owner, moved, ids, n_item, n_rows)
    else:
        hot = (ids[:, :, None] == jnp.arange(n_rows, dtype=i32)).astype(f32)
        spread = jnp.einsum("pdc,pcr->pdr", moved, hot, precision=high)
        mine = (owner[None, :] == jnp.arange(n_item, dtype=i32)[:, None]).astype(f32)
        sent = jnp.sum(mine[:, :, None, None] * spread[None], axis=1)
    taken = lax.all_to_all(sent, "item", split_axis=0, concat_axis=0, tiled=True)
    table = gather_pieces(taken.reshape(n_item * n_dim, n_rows), "seq", seq_bits)
    if aligned:
        table_grad = assemble(place, table, seq_order)
    else:
        table_grad = true_order(jnp.stack(table), seq_order, s).reshape(width, n_rows).T
    return (loss_total / (group_len * n_item), event_grad[None], table_grad)


def solution(mesh):
    placed = (
        P("item", "seq", None),
        P(),
        P(),
        P(),
        P("item", None),
        P("item", None),
        P(),
        P(),
        P("item", "seq"),
        P("item", "seq"),
    )
    return jax.shard_map(
        per_device,
        mesh=mesh,
        in_specs=placed,
        out_specs=(P(), P("item", "seq", None), P("item", None)),
        check_vma=False,
    )
```

time: 368 us -> 155 us (0.42)
  waiting for transfers between devices: 214 us -> 62.1 us
  matrix products: 32 us -> 0 us
  Pallas kernels: 0 us -> 25.1 us
  other arithmetic: 26.1 us -> 2.13 us
  blocking collectives: 39.9 us -> 16.9 us
  starting transfers between devices: 7.94 us -> 30 us
  between operations: 19.3 us -> 4.12 us
  local copies, waits for them, and re-layouts: 28.8 us -> 14.1 us
    psum x2 -> x0, waiting for transfers between devices: 199 us -> none  [the longest x1 105 us: broadcast(): return lax.psum(jnp.where(mine, shard, jnp.zeros_like(shard)), axis)]
    ppermute x0 -> x34, waiting for transfers between devices: none -> 62.1 us  [swap(): return lax.ppermute(block, axis, [(i, i ^ 1 << bit) for i in range(size)])]
    psum x1 -> x0, blocking collectives: 39.9 us -> none  [per_device(): panel_total, loss_total = lax.psum((panel_part, loss_part), ('seq', 'item'))]
    dot_general x7 -> x0, matrix products: 32 us -> none  [the longest x1 6.12 us: loss_terms(): logits = jnp.einsum('td,nd->tn', outputs, negatives, precision=highest)]
    ppermute x0 -> x34, starting transfers between devices: none -> 30 us  [swap(): return lax.ppermute(block, axis, [(i, i ^ 1 << bit) for i in range(size)])]
    pallas_call x0 -> x6, Pallas kernels: none -> 25.1 us  [the longest x1 12 us: attend(): pl.pallas_call(functools.partial(attend_kernel, order, n_seq), grid=(coun...]
    all_to_all x0 -> x1, blocking collectives: none -> 16.9 us  [per_device(): lax.all_to_all(sent, 'item', split_axis=0, concat_axis=0, tiled=True)]
    scatter-add x1 -> x0, other arithmetic: 15.7 us -> none  [per_device(): jnp.zeros_like(item_table).at[neg_ids.reshape(-1)]]
  transfers between devices with their start and end apart: 4 -> 34, of which waited for: 4 -> 19; matrix products, arithmetic and copies ran while one was open for 10% -> 9% of each run, Pallas kernels for 0% -> 10%
where the time goes in v3:
time: 155 us
  waiting for transfers between devices  62.1 us (40%)
  starting transfers between devices  30 us (19%)
  Pallas kernels  25.1 us (16%)
  blocking collectives  16.9 us (11%)
  local copies, waits for them, and re-layouts  14.1 us (9%)
  between operations  4.12 us (3%)
  other arithmetic  2.13 us (1%)
    ppermute x34, waiting for transfers between devices, swap(): return lax.ppermute(block, axis, [(i, i ^ 1 << bit) for i in range(size)])  62.1 us
    ppermute x34, starting transfers between devices, swap(): return lax.ppermute(block, axis, [(i, i ^ 1 << bit) for i in range(size)])  30 us
    all_to_all x1, blocking collectives, per_device(): lax.all_to_all(sent, 'item', split_axis=0, concat_axis=0, tiled=True)  16.9 us
    pallas_call x1, Pallas kernels, attend(): pl.pallas_call(functools.partial(attend_kernel, order, n_seq), grid=(coun...  12 us
    pallas_call x1, Pallas kernels, loss_terms(): pl.pallas_call(functools.partial(loss_kernel, plan), in_specs=[pl.BlockSp...  5.16 us
    gather x1, local copies, waits for them, and re-layouts, per_device(): own_ids = flat_ids.at[spot.reshape(2, -1)].get(mode='promise_in_bounds')  3.14 us
  transfers between devices with their start and end apart: 34, of which 19 were waited for; matrix products, arithmetic and copies ran while one was open for 9% of the time, Pallas kernels for 10%

profile of v3, /device:TPU:0, one launch (start us, length us, event | category | flops | bytes accessed | tf_op | source)
XLA Modules:
  0.0 154.6 jit_solution(3215206054846483567)
XLA Ops:
  0.6 3.0 %collective-permute-start = (f32[128,512]{1,0:T(8,128)}, f32[128,512]{1,0:T(8,128)}, u32[]{:S(2)}, u32[]{:S(2)}) collective-permute-start(f32[128,512]{1,0:T(8,128)} %bitcast.41), channel_id=1, source_target_pairs={{0,16},{8,24},{16,0},{24,8},{1,17},{9,25},{17,1},{25,9},{2,18},{10... | collective-permute-start | bytes 786440 | tf_op jit(solution)/shard_map/ppermute | solution.py:25
  3.7 0.7 copy.18
  4.4 0.7 multiply_add_fusion
  5.1 0.1 add.150
  5.2 0.1 add.152
  5.4 3.1 %gather_fusion = s32[512]{0:T(512)S(1)} fusion(s32[2048]{0:T(1024)S(1)} %bitcast.51, s32[1024]{0:T(1024)S(1)} %pad_clamp_fusion.3), kind=kCustom, calls=%fused_computation | custom fusion | bytes 6144 | tf_op jit(solution)/shard_map/gather | solution.py:390
  8.6 1.0 gather_fusion.1
  9.6 0.8 fusion.11
  10.4 1.5 collective-permute-start.6
  11.9 1.8 %gather_fusion.2 = f32[256,512]{1,0:T(8,128)} fusion(f32[1024,512]{1,0:T(8,128)S(1)} %copy-done, s32[1024]{0:T(1024)S(1)} %pad_clamp_fusion.1), kind=kCustom, calls=%fused_computation.2 | custom fusion | bytes 1049600 | tf_op jit(solution)/shard_map/gather | solution.py:393
  13.7 1.9 %fusion.10 = (f32[128,512]{1,0:T(8,128)}, f32[128,512]{1,0:T(8,128)}) fusion(f32[256,512]{1,0:T(8,128)} %gather_fusion.2), kind=kLoop, calls=%fused_computation.52 | loop fusion | bytes 1048576 | tf_op jit(solution)/shard_map/slice | solution.py:399
  15.6 1.6 %collective-permute-start.11 = (f32[4,32,512]{2,1,0:T(8,128)}, f32[4,32,512]{2,1,0:T(8,128)}, u32[]{:S(2)}, u32[]{:S(2)}) collective-permute-start(f32[4,32,512]{2,1,0:T(8,128)} %bitcast.15), channel_id=1, source_target_pairs={{0,2},{1,3},{2,0},{3,1},{4,6},{5,7},{6,4},{7,5},{8,10},{9,11},{10,... | collective-permute-start | bytes 786440 | tf_op jit(solution)/shard_map/ppermute | solution.py:25
  17.8 0.6 dynamic_slice.3
  19.1 2.2 %copy-done.1 = f32[512,2048]{1,0:T(8,128)S(1)} copy-done((f32[512,2048]{1,0:T(8,128)S(1)}, f32[512,2048]{1,0:T(8,128)}, u32[]{:S(2)}) %copy-start.1) | copy-done | bytes 4194328
  21.3 2.6 %prepare.1 = (f32[128,512]{1,0:T(8,128)S(1)}, f32[128,512]{1,0:T(8,128)S(1)}, bf16[4,512,256]{2,1,0:T(8,128)(2,1)S(1)}, bf16[4,512,256]{2,1,0:T(8,128)(2,1)S(1)}...) custom-call(f32[128,512]{1,0:T(8,128)S(1)} %bitcast.43, f32[512,2048]{1,0:T(8,128)S(1)} %copy-done.1, ...), custom_call_target="tpu_custom_call" | custom-call | flops 268435456 | bytes 6291456 | tf_op jit(solution)/shard_map/prepare/pallas_call | solution.py:105
  24.0 0.5 collective-permute-start.7
  24.6 1.5 collective-permute-start.12
  26.2 0.2 collective-permute-start.2
  26.3 4.1 %collective-permute-done.7 = f32[2,32,512]{2,1,0:T(8,128)S(1)} collective-permute-done((f32[2,32,512]{2,1,0:T(8,128)S(1)}, f32[2,32,512]{2,1,0:T(8,128)S(1)}, u32[]{:S(2)}, u32[]{:S(2)}) %collective-permute-start.7) | collective-permute-done | bytes 131104 | tf_op jit(solution)/shard_map/ppermute | solution.py:25
  30.4 2.7 %collective-permute-start.8 = (f32[2,32,512]{2,1,0:T(8,128)S(1)}, f32[2,32,512]{2,1,0:T(8,128)S(1)}, u32[]{:S(2)}, u32[]{:S(2)}) collective-permute-start(f32[2,32,512]{2,1,0:T(8,128)S(1)} %slice_select_fusion.1), channel_id=1, source_target_pairs={{0,4},{1,5},{2,6},{3,7},{4,0},{5,1},{6,2},{7,3},{8,12},{9,13},{10,... | collective-permute-start | bytes 393224 | tf_op jit(solution)/shard_map/ppermute | solution.py:25
  33.1 0.4 collective-permute-start.13
  33.5 12.0 %attend.1.refs_0_ = f32[128,512]{1,0:T(8,128)S(1)} custom-call(s32[5]{0:T(128)S(1)} %pad_add_fusion.1.meta, f32[128,512]{1,0:T(8,128)S(1)} %bitcast.44, f32[128,512]{1,0:T(8,128)} %collective-permute-done.refs_1_, f32[128,512]{1,0:T(8,128)} %collective-permute-done.1.refs_2_, f32[128,512]{1,0:T(8,128)S(1)} %collective-permute-done.2.refs_3_, ...), custom_call_target="tpu_custom_call" | custom-call | flops 8000000000 | bytes 2097152 | tf_op jit(solution)/shard_map/attend/pallas_call | solution.py:169
  45.6 0.5 project.1.refs_0_
  46.1 0.4 collective-permute-start.3
  46.6 2.5 %collective-permute-start.9 = (f32[2,32,512]{2,1,0:T(8,128)S(1)}, f32[2,32,512]{2,1,0:T(8,128)S(1)}, u32[]{:S(2)}, u32[]{:S(2)}) collective-permute-start(f32[2,32,512]{2,1,0:T(8,128)S(1)} %maximum_select_fusion), channel_id=1, source_target_pairs={{0,2},{1,3},{2,0},{3,1},{4,6},{5,7},{6,4},{7,5},{8,10},{9,11},{10,... | collective-permute-start | bytes 393224 | tf_op jit(solution)/shard_map/ppermute | solution.py:25
  49.3 2.7 %collective-permute-done.9 = f32[2,32,512]{2,1,0:T(8,128)S(1)} collective-permute-done((f32[2,32,512]{2,1,0:T(8,128)S(1)}, f32[2,32,512]{2,1,0:T(8,128)S(1)}, u32[]{:S(2)}, u32[]{:S(2)}) %collective-permute-start.9) | collective-permute-done | bytes 131104 | tf_op jit(solution)/shard_map/ppermute | solution.py:25
  52.1 0.8 collective-permute-start.10
  52.9 1.6 %collective-permute-done.3.refs_1_ = f32[136,512]{1,0:T(8,128)S(1)} collective-permute-done((f32[136,512]{1,0:T(8,128)S(1)}, f32[136,512]{1,0:T(8,128)S(1)}, u32[]{:S(2)}, u32[]{:S(2)}) %collective-permute-start.3) | collective-permute-done | bytes 278560 | tf_op jit(solution)/shard_map/ppermute | solution.py:25
  54.5 1.0 collective-permute-done.14
  55.7 4.1 %collective-permute-done.10 = f32[4,32,512]{2,1,0:T(8,128)S(1)} collective-permute-done((f32[4,32,512]{2,1,0:T(8,128)S(1)}, f32[4,32,512]{2,1,0:T(8,128)S(1)}, u32[]{:S(2)}, u32[]{:S(2)}) %collective-permute-start.10) | collective-permute-done | bytes 262176 | tf_op jit(solution)/shard_map/ppermute | solution.py:25
  59.8 3.5 %collective-permute-done.15 = f32[4,32,512]{2,1,0:T(8,128)S(1)} collective-permute-done((f32[4,32,512]{2,1,0:T(8,128)S(1)}, f32[4,32,512]{2,1,0:T(8,128)S(1)}, u32[]{:S(2)}, u32[]{:S(2)}) %collective-permute-start.15) | collective-permute-done | bytes 262176 | tf_op jit(solution)/shard_map/ppermute | solution.py:25
  63.3 5.2 %loss_terms.1 = (f32[4,4,8,512]{3,2,1,0:T(8,128)S(1)}, f32[4,4,8,512]{3,2,1,0:T(8,128)S(1)}, f32[4,4,8,512]{3,2,1,0:T(8,128)S(1)}, f32[4,4,8,512]{3,2,1,0:T(8,12...) custom-call(s32[2]{0:T(128)S(1)} %pad_add_fusion.meta, ...), custom_call_target="tpu_custom_call" | custom-call | flops 2415919104 | bytes 4194304 | tf_op jit(solution)/shard_map/loss_terms/pallas_call | solution.py:289
  68.5 0.7 collective-permute-start.23
  69.2 1.1 collective-permute-start.26
  70.3 5.1 %collective-permute-done.23 = f32[4,4,8,512]{3,2,1,0:T(8,128)S(1)} collective-permute-done((f32[4,4,8,512]{3,2,1,0:T(8,128)S(1)}, f32[4,4,8,512]{3,2,1,0:T(8,128)S(1)}, u32[]{:S(2)}, u32[]{:S(2)}) %collective-permute-start.23) | collective-permute-done | bytes 262176 | tf_op jit(solution)/shard_map/ppermute | solution.py:25
  75.4 1.1 collective-permute-start.24
  76.6 0.9 collective-permute-done.26
  77.5 0.9 collective-permute-start.27
  78.4 2.0 %collective-permute-done.24 = f32[2,4,8,512]{3,2,1,0:T(8,128)S(1)} collective-permute-done((f32[2,4,8,512]{3,2,1,0:T(8,128)S(1)}, f32[2,4,8,512]{3,2,1,0:T(8,128)S(1)}, u32[]{:S(2)}, u32[]{:S(2)}) %collective-permute-start.24) | collective-permute-done | bytes 131104 | tf_op jit(solution)/shard_map/ppermute | solution.py:25
  80.5 4.2 %collective-permute-start.25 = (f32[1,4,8,512]{3,2,1,0:T(8,128)S(1)}, f32[1,4,8,512]{3,2,1,0:T(8,128)S(1)}, u32[]{:S(2)}, u32[]{:S(2)}) collective-permute-start(f32[1,4,8,512]{3,2,1,0:T(8,128)S(1)} %slice_add_fusion.8), channel_id=1, source_target_pairs={{0,4},{1,5},{2,6},{3,7},{4,0},{5,1},{6,2},{7,3},{8,12},{9,13},{10,... | collective-permute-start | bytes 196616 | tf_op jit(solution)/shard_map/ppermute | solution.py:25
  84.7 0.1 collective-permute-start.28
  84.8 2.7 %collective-permute-done.25 = f32[1,4,8,512]{3,2,1,0:T(8,128)S(1)} collective-permute-done((f32[1,4,8,512]{3,2,1,0:T(8,128)S(1)}, f32[1,4,8,512]{3,2,1,0:T(8,128)S(1)}, u32[]{:S(2)}, u32[]{:S(2)}) %collective-permute-start.25) | collective-permute-done | bytes 65568 | tf_op jit(solution)/shard_map/ppermute | solution.py:25
  87.5 2.4 %collective-permute-done.28 = f32[1,4,8,512]{3,2,1,0:T(8,128)S(1)} collective-permute-done((f32[1,4,8,512]{3,2,1,0:T(8,128)S(1)}, f32[1,4,8,512]{3,2,1,0:T(8,128)S(1)}, u32[]{:S(2)}, u32[]{:S(2)}) %collective-permute-start.28) | collective-permute-done | bytes 65568 | tf_op jit(solution)/shard_map/ppermute | solution.py:25
  90.0 1.2 collective-permute-done.29
  91.4 0.6 gather_fusion.3
  92.0 0.6 gather_fusion.4
  92.6 3.0 %collective-permute-done.30 = f32[1,2,16,512]{3,2,1,0:T(8,128)S(1)} collective-permute-done((f32[1,2,16,512]{3,2,1,0:T(8,128)S(1)}, f32[1,2,16,512]{3,2,1,0:T(8,128)S(1)}, u32[]{:S(2)}, u32[]{:S(2)}) %collective-permute-start.30) | collective-permute-done | bytes 65568 | tf_op jit(solution)/shard_map/ppermute | solution.py:25
  95.6 2.0 %spread_rows.1 = f32[8,16,1024]{2,1,0:T(8,128)S(1)} custom-call(s32[4]{0:T(128)S(1)} %gather_fusion.3, f32[4,16,512]{2,1,0:T(8,128)S(1)} %maximum_bitcast_fusion.moved, s32[4,512]{1,0:T(4,128)S(1)} %gather_fusion.4), custom_call_target="tpu_custom_call" | custom-call | flops 134217728 | bytes 2097152 | tf_op jit(solution)/shard_map/spread_rows/pallas_call | solution.py:322
  97.6 16.9 %all_to_all.5 = f32[8,16,1024]{2,1,0:T(8,128)S(1)} all-to-all(f32[8,16,1024]{2,1,0:T(8,128)S(1)} %spread_rows.1), channel_id=1, replica_groups=mesh['seq'=4,'item'=8] {'item'}, dimensions={0} | all-to-all | bytes 1048576 | tf_op jit(solution)/shard_map/all_to_all | solution.py:460
  114.5 0.8 collective-permute-start.31
  115.3 0.5 collective-permute-start.32
  115.8 10.9 %collective-permute-done.31.refs_1_ = f32[128,1024]{1,0:T(8,128)S(1)} collective-permute-done((f32[128,1024]{1,0:T(8,128)S(1)}, f32[128,1024]{1,0:T(8,128)S(1)}, u32[]{:S(2)}, u32[]{:S(2)}) %collective-permute-start.31) | collective-permute-done | bytes 524320 | tf_op jit(solution)/shard_map/ppermute | solution.py:25
  126.8 1.1 collective-permute-start.22
  128.0 1.0 collective-permute-start.16
  128.9 6.8 %collective-permute-done.16 = f32[8,128]{1,0:T(8,128)S(1)} collective-permute-done((f32[8,128]{1,0:T(8,128)S(1)}, f32[8,128]{1,0:T(8,128)S(1)}, u32[]{:S(2)}, u32[]{:S(2)}) %collective-permute-start.16) | collective-permute-done | bytes 4128 | tf_op jit(solution)/shard_map/ppermute | solution.py:25
  135.7 1.2 collective-permute-done.17
  136.9 1.4 collective-permute-start.18
  138.3 3.1 %collective-permute-done.18 = f32[8,128]{1,0:T(8,128)S(1)} collective-permute-done((f32[8,128]{1,0:T(8,128)S(1)}, f32[8,128]{1,0:T(8,128)S(1)}, u32[]{:S(2)}, u32[]{:S(2)}) %collective-permute-start.18) | collective-permute-done | bytes 4128 | tf_op jit(solution)/shard_map/ppermute | solution.py:25
  141.4 3.6 %collective-permute-done.19 = f32[8,128]{1,0:T(8,128)S(1)} collective-permute-done((f32[8,128]{1,0:T(8,128)S(1)}, f32[8,128]{1,0:T(8,128)S(1)}, u32[]{:S(2)}, u32[]{:S(2)}) %collective-permute-start.19) | collective-permute-done | bytes 4128 | tf_op jit(solution)/shard_map/ppermute | solution.py:25
  145.0 1.6 %collective-permute-start.20 = (f32[8,128]{1,0:T(8,128)S(1)}, f32[8,128]{1,0:T(8,128)S(1)}, u32[]{:S(2)}, u32[]{:S(2)}) collective-permute-start(f32[8,128]{1,0:T(8,128)S(1)} %add.164), channel_id=1, source_target_pairs={{0,1},{1,0},{2,3},{3,2},{4,5},{5,4},{6,7},{7,6},{8,9},{9,8},{10,11... | collective-permute-start | bytes 12296 | tf_op jit(solution)/shard_map/ppermute | solution.py:25
  146.6 2.0 %collective-permute-done.20 = f32[8,128]{1,0:T(8,128)S(1)} collective-permute-done((f32[8,128]{1,0:T(8,128)S(1)}, f32[8,128]{1,0:T(8,128)S(1)}, u32[]{:S(2)}, u32[]{:S(2)}) %collective-permute-start.20) | collective-permute-done | bytes 4128 | tf_op jit(solution)/shard_map/ppermute | solution.py:25
  148.6 0.5 slice.153
  149.8 0.8 fusion
  150.6 2.9 %assemble.1 = f32[1024,512]{1,0:T(8,128)} custom-call(s32[2]{0:T(128)S(1)} %pad_add_fusion.meta, f32[128,1024]{1,0:T(8,128)S(1)} %bitcast.40, f32[128,1024]{1,0:T(8,128)S(1)} %collective-permute-done.31.refs_1_, f32[128,1024]{1,0:T(8,128)S(1)} %collective-permute-done.32.refs_2_, f32[128,1024]{1,0:T(8,128)S(1)} %collective-permute-done.33.refs_3_), custom_call_target="tpu_custom_call" | custom-call | bytes 4194304 | tf_op jit(solution)/shard_map/assemble/pallas_call | solution.py:345
  (89 shorter events, 1.3 us)
Async XLA Ops:
  0.6 8.0 %copy-start = (f32[1024,512]{1,0:T(8,128)S(1)}, f32[1024,512]{1,0:T(8,128)}, u32[]{:S(2)}) copy-start(f32[1024,512]{1,0:T(8,128)} %param.17) | copy-start | bytes 6291460
  0.6 25.5 %collective-permute-start = (f32[128,512]{1,0:T(8,128)}, f32[128,512]{1,0:T(8,128)}, u32[]{:S(2)}, u32[]{:S(2)}) collective-permute-start(f32[128,512]{1,0:T(8,128)} %bitcast.41), channel_id=1, source_target_pairs={{0,16},{8,24},{16,0},{24,8},{1,17},{9,25},{17,1},{25,9},{2,18},{10... | collective-permute-start | bytes 786440 | tf_op jit(solution)/shard_map/ppermute | solution.py:25
  3.7 29.8 %collective-permute-start.1 = (f32[128,512]{1,0:T(8,128)}, f32[128,512]{1,0:T(8,128)}, u32[]{:S(2)}, u32[]{:S(2)}) collective-permute-start(f32[128,512]{1,0:T(8,128)} %bitcast.42), channel_id=1, source_target_pairs={{0,8},{8,0},{16,24},{24,16},{1,9},{9,1},{17,25},{25,17},{2,10},{10... | collective-permute-start | bytes 786440 | tf_op jit(solution)/shard_map/ppermute | solution.py:25
  10.4 13.6 %collective-permute-start.6 = (f32[4,32,512]{2,1,0:T(8,128)}, f32[4,32,512]{2,1,0:T(8,128)}, u32[]{:S(2)}, u32[]{:S(2)}) collective-permute-start(f32[4,32,512]{2,1,0:T(8,128)} %bitcast.9), channel_id=1, source_target_pairs={{0,1},{1,0},{2,3},{3,2},{4,5},{5,4},{6,7},{7,6},{8,9},{9,8},{10,11... | collective-permute-start | bytes 786440 | tf_op jit(solution)/shard_map/ppermute | solution.py:25
  11.9 5.9 %copy-start.6 = (s32[4]{0:T(128)S(1)}, s32[4]{0:T(128)}, u32[]{:S(2)}) copy-start(s32[4]{0:T(128)} %param.20) | copy-start | bytes 52
  11.9 7.2 %copy-start.10 = (s32[1,4]{1,0:T(1,128)S(1)}, s32[1,4]{1,0:T(1,128)}, u32[]{:S(2)}) copy-start(s32[1,4]{1,0:T(1,128)} %param.18) | copy-start | bytes 52
  11.9 7.2 %copy-start.2 = (f32[1,128,512]{2,1,0:T(8,128)S(1)}, f32[1,128,512]{2,1,0:T(8,128)}, u32[]{:S(2)}) copy-start(f32[1,128,512]{2,1,0:T(8,128)} %param.13) | copy-start | bytes 786436
  11.9 7.2 %copy-start.3 = (f32[512,512]{1,0:T(8,128)S(1)}, f32[512,512]{1,0:T(8,128)}, u32[]{:S(2)}) copy-start(f32[512,512]{1,0:T(8,128)} %wo_ref.1) | copy-start | bytes 3145732
  15.6 9.0 %collective-permute-start.11 = (f32[4,32,512]{2,1,0:T(8,128)}, f32[4,32,512]{2,1,0:T(8,128)}, u32[]{:S(2)}, u32[]{:S(2)}) collective-permute-start(f32[4,32,512]{2,1,0:T(8,128)} %bitcast.15), channel_id=1, source_target_pairs={{0,2},{1,3},{2,0},{3,1},{4,6},{5,7},{6,4},{7,5},{8,10},{9,11},{10,... | collective-permute-start | bytes 786440 | tf_op jit(solution)/shard_map/ppermute | solution.py:25
  19.1 2.2 %copy-start.1 = (f32[512,2048]{1,0:T(8,128)S(1)}, f32[512,2048]{1,0:T(8,128)}, u32[]{:S(2)}) copy-start(f32[512,2048]{1,0:T(8,128)} %k_ref.1) | copy-start | bytes 12582916
  21.3 2.6 %copy-start.7 = (f32[128,512]{1,0:T(8,128)S(1)}, f32[128,512]{1,0:T(8,128)}, u32[]{:S(2)}) copy-start(f32[128,512]{1,0:T(8,128)} %get-tuple-element.36) | copy-start | bytes 786436
  21.3 3.2 %copy-start.8 = (f32[128,512]{1,0:T(8,128)S(1)}, f32[128,512]{1,0:T(8,128)}, u32[]{:S(2)}) copy-start(f32[128,512]{1,0:T(8,128)} %get-tuple-element.34) | copy-start | bytes 786436
  24.0 6.4 %collective-permute-start.7 = (f32[2,32,512]{2,1,0:T(8,128)S(1)}, f32[2,32,512]{2,1,0:T(8,128)S(1)}, u32[]{:S(2)}, u32[]{:S(2)}) collective-permute-start(f32[2,32,512]{2,1,0:T(8,128)S(1)} %slice.195), channel_id=1, source_target_pairs={{0,2},{1,3},{2,0},{3,1},{4,6},{5,7},{6,4},{7,5},{8,10},{9,11},{10,... | collective-permute-start | bytes 393224 | tf_op jit(solution)/shard_map/ppermute | solution.py:25
  24.6 8.5 %collective-permute-start.12 = (f32[2,32,512]{2,1,0:T(8,128)S(1)}, f32[2,32,512]{2,1,0:T(8,128)S(1)}, u32[]{:S(2)}, u32[]{:S(2)}) collective-permute-start(f32[2,32,512]{2,1,0:T(8,128)S(1)} %slice.201), channel_id=1, source_target_pairs={{0,1},{1,0},{2,3},{3,2},{4,5},{5,4},{6,7},{7,6},{8,9},{9,8},{10,11... | collective-permute-start | bytes 393224 | tf_op jit(solution)/shard_map/ppermute | solution.py:25
  26.2 7.3 %collective-permute-start.2 = (f32[128,512]{1,0:T(8,128)}, f32[128,512]{1,0:T(8,128)S(1)}, u32[]{:S(2)}, u32[]{:S(2)}) collective-permute-start(f32[128,512]{1,0:T(8,128)} %collective-permute-done.refs_1_), channel_id=1, source_target_pairs={{0,8},{8,0},{16,24},{24,16},{1,9},{9,1},{17,25},{25,17},{2,10},{10... | collective-permute-start | bytes 786440 | tf_op jit(solution)/shard_map/ppermute | solution.py:25
  30.4 16.1 %collective-permute-start.8 = (f32[2,32,512]{2,1,0:T(8,128)S(1)}, f32[2,32,512]{2,1,0:T(8,128)S(1)}, u32[]{:S(2)}, u32[]{:S(2)}) collective-permute-start(f32[2,32,512]{2,1,0:T(8,128)S(1)} %slice_select_fusion.1), channel_id=1, source_target_pairs={{0,4},{1,5},{2,6},{3,7},{4,0},{5,1},{6,2},{7,3},{8,12},{9,13},{10,... | collective-permute-start | bytes 393224 | tf_op jit(solution)/shard_map/ppermute | solution.py:25
  33.1 16.0 %collective-permute-start.13 = (f32[2,32,512]{2,1,0:T(8,128)S(1)}, f32[2,32,512]{2,1,0:T(8,128)S(1)}, u32[]{:S(2)}, u32[]{:S(2)}) collective-permute-start(f32[2,32,512]{2,1,0:T(8,128)S(1)} %slice_select_fusion), channel_id=1, source_target_pairs={{0,4},{1,5},{2,6},{3,7},{4,0},{5,1},{6,2},{7,3},{8,12},{9,13},{10,... | collective-permute-start | bytes 393224 | tf_op jit(solution)/shard_map/ppermute | solution.py:25
  33.5 12.0 %copy-start.4 = (f32[512]{0:T(512)S(1)}, f32[512]{0:T(512)}, u32[]{:S(2)}) copy-start(f32[512]{0:T(512)} %param.15) | copy-start | bytes 6148
  33.5 12.0 %copy-start.5 = (s32[1,128]{1,0:T(1,128)S(1)}, s32[1,128]{1,0:T(1,128)}, u32[]{:S(2)}) copy-start(s32[1,128]{1,0:T(1,128)} %refs_6_.1) | copy-start | bytes 1540
  46.1 8.4 %collective-permute-start.3 = (f32[136,512]{1,0:T(8,128)S(1)}, f32[136,512]{1,0:T(8,128)S(1)}, u32[]{:S(2)}, u32[]{:S(2)}) collective-permute-start(f32[136,512]{1,0:T(8,128)S(1)} %project.1.refs_0_), channel_id=1, source_target_pairs={{0,16},{8,24},{16,0},{24,8},{1,17},{9,25},{17,1},{25,9},{2,18},{10... | collective-permute-start | bytes 835592 | tf_op jit(solution)/shard_map/ppermute | solution.py:25
  46.6 5.5 %collective-permute-start.9 = (f32[2,32,512]{2,1,0:T(8,128)S(1)}, f32[2,32,512]{2,1,0:T(8,128)S(1)}, u32[]{:S(2)}, u32[]{:S(2)}) collective-permute-start(f32[2,32,512]{2,1,0:T(8,128)S(1)} %maximum_select_fusion), channel_id=1, source_target_pairs={{0,2},{1,3},{2,0},{3,1},{4,6},{5,7},{6,4},{7,5},{8,10},{9,11},{10,... | collective-permute-start | bytes 393224 | tf_op jit(solution)/shard_map/ppermute | solution.py:25
  49.2 6.4 %collective-permute-start.14 = (f32[2,32,512]{2,1,0:T(8,128)S(1)}, f32[2,32,512]{2,1,0:T(8,128)S(1)}, u32[]{:S(2)}, u32[]{:S(2)}) collective-permute-start(f32[2,32,512]{2,1,0:T(8,128)S(1)} %maximum_select_fusion.1), channel_id=1, source_target_pairs={{0,1},{1,0},{2,3},{3,2},{4,5},{5,4},{6,7},{7,6},{8,9},{9,8},{10,11... | collective-permute-start | bytes 393224 | tf_op jit(solution)/shard_map/ppermute | solution.py:25
  49.3 6.5 %collective-permute-start.4 = (f32[136,512]{1,0:T(8,128)S(1)}, f32[136,512]{1,0:T(8,128)S(1)}, u32[]{:S(2)}, u32[]{:S(2)}) collective-permute-start(f32[136,512]{1,0:T(8,128)S(1)} %project.1.refs_0_), channel_id=1, source_target_pairs={{0,8},{8,0},{16,24},{24,16},{1,9},{9,1},{17,25},{25,17},{2,10},{10... | collective-permute-start | bytes 835592 | tf_op jit(solution)/shard_map/ppermute | solution.py:25
  52.1 7.7 %collective-permute-start.10 = (f32[4,32,512]{2,1,0:T(8,128)S(1)}, f32[4,32,512]{2,1,0:T(8,128)S(1)}, u32[]{:S(2)}, u32[]{:S(2)}) collective-permute-start(f32[4,32,512]{2,1,0:T(8,128)S(1)} %pad_maximum_fusion), channel_id=1, source_target_pairs={{0,1},{1,0},{2,3},{3,2},{4,5},{5,4},{6,7},{7,6},{8,9},{9,8},{10,11... | collective-permute-start | bytes 786440 | tf_op jit(solution)/shard_map/ppermute | solution.py:25
  54.5 8.8 %collective-permute-start.5 = (f32[136,512]{1,0:T(8,128)S(1)}, f32[136,512]{1,0:T(8,128)S(1)}, u32[]{:S(2)}, u32[]{:S(2)}) collective-permute-start(f32[136,512]{1,0:T(8,128)S(1)} %collective-permute-done.3.refs_1_), channel_id=1, source_target_pairs={{0,8},{8,0},{16,24},{24,16},{1,9},{9,1},{17,25},{25,17},{2,10},{10... | collective-permute-start | bytes 835592 | tf_op jit(solution)/shard_map/ppermute | solution.py:25
  55.5 7.8 %collective-permute-start.15 = (f32[4,32,512]{2,1,0:T(8,128)S(1)}, f32[4,32,512]{2,1,0:T(8,128)S(1)}, u32[]{:S(2)}, u32[]{:S(2)}) collective-permute-start(f32[4,32,512]{2,1,0:T(8,128)S(1)} %pad_maximum_fusion.1), channel_id=1, source_target_pairs={{0,2},{1,3},{2,0},{3,1},{4,6},{5,7},{6,4},{7,5},{8,10},{9,11},{10,... | collective-permute-start | bytes 786440 | tf_op jit(solution)/shard_map/ppermute | solution.py:25
  68.5 23.5 %copy-start.9 = (s32[4,512]{1,0:T(4,128)S(1)}, s32[4,512]{1,0:T(4,128)}, u32[]{:S(2)}) copy-start(s32[4,512]{1,0:T(4,128)} %param.19) | copy-start | bytes 24580
  68.5 6.9 %collective-permute-start.23 = (f32[4,4,8,512]{3,2,1,0:T(8,128)S(1)}, f32[4,4,8,512]{3,2,1,0:T(8,128)S(1)}, u32[]{:S(2)}, u32[]{:S(2)}) collective-permute-start(f32[4,4,8,512]{3,2,1,0:T(8,128)S(1)} %get-tuple-element.26), channel_id=1, source_target_pairs={{0,1},{1,0},{2,3},{3,2},{4,5},{5,4},{6,7},{7,6},{8,9},{9,8},{10,11... | collective-permute-start | bytes 786440 | tf_op jit(solution)/shard_map/ppermute | solution.py:25
  69.2 8.3 %collective-permute-start.26 = (f32[4,4,8,512]{3,2,1,0:T(8,128)S(1)}, f32[4,4,8,512]{3,2,1,0:T(8,128)S(1)}, u32[]{:S(2)}, u32[]{:S(2)}) collective-permute-start(f32[4,4,8,512]{3,2,1,0:T(8,128)S(1)} %get-tuple-element.28), channel_id=1, source_target_pairs={{0,2},{1,3},{2,0},{3,1},{4,6},{5,7},{6,4},{7,5},{8,10},{9,11},{10,... | collective-permute-start | bytes 786440 | tf_op jit(solution)/shard_map/ppermute | solution.py:25
  75.4 5.0 %collective-permute-start.24 = (f32[2,4,8,512]{3,2,1,0:T(8,128)S(1)}, f32[2,4,8,512]{3,2,1,0:T(8,128)S(1)}, u32[]{:S(2)}, u32[]{:S(2)}) collective-permute-start(f32[2,4,8,512]{3,2,1,0:T(8,128)S(1)} %get-tuple-element.30), channel_id=1, source_target_pairs={{0,2},{1,3},{2,0},{3,1},{4,6},{5,7},{6,4},{7,5},{8,10},{9,11},{10,... | collective-permute-start | bytes 393224 | tf_op jit(solution)/shard_map/ppermute | solution.py:25
  77.5 7.2 %collective-permute-start.27 = (f32[2,4,8,512]{3,2,1,0:T(8,128)S(1)}, f32[2,4,8,512]{3,2,1,0:T(8,128)S(1)}, u32[]{:S(2)}, u32[]{:S(2)}) collective-permute-start(f32[2,4,8,512]{3,2,1,0:T(8,128)S(1)} %get-tuple-element.32), channel_id=1, source_target_pairs={{0,1},{1,0},{2,3},{3,2},{4,5},{5,4},{6,7},{7,6},{8,9},{9,8},{10,11... | collective-permute-start | bytes 393224 | tf_op jit(solution)/shard_map/ppermute | solution.py:25
  80.5 7.0 %collective-permute-start.25 = (f32[1,4,8,512]{3,2,1,0:T(8,128)S(1)}, f32[1,4,8,512]{3,2,1,0:T(8,128)S(1)}, u32[]{:S(2)}, u32[]{:S(2)}) collective-permute-start(f32[1,4,8,512]{3,2,1,0:T(8,128)S(1)} %slice_add_fusion.8), channel_id=1, source_target_pairs={{0,4},{1,5},{2,6},{3,7},{4,0},{5,1},{6,2},{7,3},{8,12},{9,13},{10,... | collective-permute-start | bytes 196616 | tf_op jit(solution)/shard_map/ppermute | solution.py:25
  84.7 5.2 %collective-permute-start.28 = (f32[1,4,8,512]{3,2,1,0:T(8,128)S(1)}, f32[1,4,8,512]{3,2,1,0:T(8,128)S(1)}, u32[]{:S(2)}, u32[]{:S(2)}) collective-permute-start(f32[1,4,8,512]{3,2,1,0:T(8,128)S(1)} %slice_add_fusion.6), channel_id=1, source_target_pairs={{0,4},{1,5},{2,6},{3,7},{4,0},{5,1},{6,2},{7,3},{8,12},{9,13},{10,... | collective-permute-start | bytes 196616 | tf_op jit(solution)/shard_map/ppermute | solution.py:25
  89.9 1.3 collective-permute-start.29
  91.3 4.3 %collective-permute-start.30 = (f32[1,2,16,512]{3,2,1,0:T(8,128)S(1)}, f32[1,2,16,512]{3,2,1,0:T(8,128)S(1)}, u32[]{:S(2)}, u32[]{:S(2)}) collective-permute-start(f32[1,2,16,512]{3,2,1,0:T(8,128)S(1)} %get-tuple-element.38), channel_id=1, source_target_pairs={{0,16},{8,24},{16,0},{24,8},{1,17},{9,25},{17,1},{25,9},{2,18},{10... | collective-permute-start | bytes 196616 | tf_op jit(solution)/shard_map/ppermute | solution.py:25
  114.5 12.3 %collective-permute-start.31 = (f32[128,1024]{1,0:T(8,128)S(1)}, f32[128,1024]{1,0:T(8,128)S(1)}, u32[]{:S(2)}, u32[]{:S(2)}) collective-permute-start(f32[128,1024]{1,0:T(8,128)S(1)} %bitcast.38), channel_id=1, source_target_pairs={{0,16},{8,24},{16,0},{24,8},{1,17},{9,25},{17,1},{25,9},{2,18},{10... | collective-permute-start | bytes 1572872 | tf_op jit(solution)/shard_map/ppermute | solution.py:25
  115.3 11.5 %collective-permute-start.21 = (f32[2,128,512]{2,1,0:T(8,128)S(1)}, f32[2,128,512]{2,1,0:T(8,128)S(1)}, u32[]{:S(2)}, u32[]{:S(2)}) collective-permute-start(f32[2,128,512]{2,1,0:T(8,128)S(1)} %get-tuple-element.24), channel_id=1, source_target_pairs={{0,8},{8,0},{16,24},{24,16},{1,9},{9,1},{17,25},{25,17},{2,10},{10... | collective-permute-start | bytes 1572872 | tf_op jit(solution)/shard_map/ppermute | solution.py:25
  115.3 35.2 %collective-permute-start.32 = (f32[128,1024]{1,0:T(8,128)S(1)}, f32[128,1024]{1,0:T(8,128)S(1)}, u32[]{:S(2)}, u32[]{:S(2)}) collective-permute-start(f32[128,1024]{1,0:T(8,128)S(1)} %bitcast.39), channel_id=1, source_target_pairs={{0,8},{8,0},{16,24},{24,16},{1,9},{9,1},{17,25},{25,17},{2,10},{10... | collective-permute-start | bytes 1572872 | tf_op jit(solution)/shard_map/ppermute | solution.py:25
  126.8 23.8 %collective-permute-start.33 = (f32[128,1024]{1,0:T(8,128)S(1)}, f32[128,1024]{1,0:T(8,128)S(1)}, u32[]{:S(2)}, u32[]{:S(2)}) collective-permute-start(f32[128,1024]{1,0:T(8,128)S(1)} %collective-permute-done.31.refs_1_), channel_id=1, source_target_pairs={{0,8},{8,0},{16,24},{24,16},{1,9},{9,1},{17,25},{25,17},{2,10},{10... | collective-permute-start | bytes 1572872 | tf_op jit(solution)/shard_map/ppermute | solution.py:25
  126.8 22.9 %collective-permute-start.22 = (f32[1,128,512]{2,1,0:T(8,128)S(1)}, f32[1,128,512]{2,1,0:T(8,128)S(1)}, u32[]{:S(2)}, u32[]{:S(2)}) collective-permute-start(f32[1,128,512]{2,1,0:T(8,128)S(1)} %slice_add_fusion), channel_id=1, source_target_pairs={{0,16},{8,24},{16,0},{24,8},{1,17},{9,25},{17,1},{25,9},{2,18},{10... | collective-permute-start | bytes 786440 | tf_op jit(solution)/shard_map/ppermute | solution.py:25
  128.0 7.7 %collective-permute-start.16 = (f32[8,128]{1,0:T(8,128)S(1)}, f32[8,128]{1,0:T(8,128)S(1)}, u32[]{:S(2)}, u32[]{:S(2)}) collective-permute-start(f32[8,128]{1,0:T(8,128)S(1)} %get-tuple-element.22), channel_id=1, source_target_pairs={{0,16},{8,24},{16,0},{24,8},{1,17},{9,25},{17,1},{25,9},{2,18},{10... | collective-permute-start | bytes 12296 | tf_op jit(solution)/shard_map/ppermute | solution.py:25
  135.7 1.2 collective-permute-start.17
  136.9 4.5 %collective-permute-start.18 = (f32[8,128]{1,0:T(8,128)S(1)}, f32[8,128]{1,0:T(8,128)S(1)}, u32[]{:S(2)}, u32[]{:S(2)}) collective-permute-start(f32[8,128]{1,0:T(8,128)S(1)} %add.162), channel_id=1, source_target_pairs={{0,4},{1,5},{2,6},{3,7},{4,0},{5,1},{6,2},{7,3},{8,12},{9,13},{10,... | collective-permute-start | bytes 12296 | tf_op jit(solution)/shard_map/ppermute | solution.py:25
  141.4 3.6 %collective-permute-start.19 = (f32[8,128]{1,0:T(8,128)S(1)}, f32[8,128]{1,0:T(8,128)S(1)}, u32[]{:S(2)}, u32[]{:S(2)}) collective-permute-start(f32[8,128]{1,0:T(8,128)S(1)} %add.163), channel_id=1, source_target_pairs={{0,2},{1,3},{2,0},{3,1},{4,6},{5,7},{6,4},{7,5},{8,10},{9,11},{10,... | collective-permute-start | bytes 12296 | tf_op jit(solution)/shard_map/ppermute | solution.py:25
  145.0 3.6 %collective-permute-start.20 = (f32[8,128]{1,0:T(8,128)S(1)}, f32[8,128]{1,0:T(8,128)S(1)}, u32[]{:S(2)}, u32[]{:S(2)}) collective-permute-start(f32[8,128]{1,0:T(8,128)S(1)} %add.164), channel_id=1, source_target_pairs={{0,1},{1,0},{2,3},{3,2},{4,5},{5,4},{6,7},{7,6},{8,9},{9,8},{10,11... | collective-permute-start | bytes 12296 | tf_op jit(solution)/shard_map/ppermute | solution.py:25

commit v4 on v3

--- a/solution.py
+++ b/solution.py
@@ -18,11 +18,17 @@
 high = lax.Precision.HIGH
 NN, NT = ((1,), (0,)), ((1,), (1,))
 params = pltpu.CompilerParams(vmem_limit_bytes=40 * 2**20)
+alone = pltpu.CompilerParams(vmem_limit_bytes=62 * 2**20)
 
 
 def swap(block, axis, bit):
     size = lax.axis_size(axis)
     return lax.ppermute(block, axis, [(i, i ^ (1 << bit)) for i in range(size)])
+
+
+def send(block, axis, r):
+    size = lax.axis_size(axis)
+    return lax.ppermute(block, axis, [(i, i ^ r) for i in range(size)])
 
 
 def bits_of(size):
@@ -82,55 +88,127 @@
     return x / (1.0 + jnp.exp(jnp.minimum(-x, 87.0)))
 
 
-def prepare_kernel(x_ref, u_ref, v_ref, q_ref, k_ref, wo_ref, gates_ref, queries_ref, vk_hi, vk_lo, wo_hi, wo_lo):
+def pick_kernel(plan, ids_hbm, table_hbm, *refs):
+    _, n_item, _, item_orders, _ = plan
+    outs, (ids, table, picked, sems) = refs[:4], refs[4:]
+    n_neg = ids.shape[1]
+    n_step, step = table.shape[:2]
+    me, item = lax.axis_index("seq"), lax.axis_index("item")
+    copies = [pltpu.make_async_copy(ids_hbm, ids, sems.at[n_step])]
+    copies += [
+        pltpu.make_async_copy(table_hbm.at[pl.ds(k * step, step)], table.at[k], sems.at[k]) for k in range(n_step)
+    ]
+    for copy in copies:
+        copy.start()
+    copies[0].wait()
+    row = ids[pl.ds(me, 1), :].astype(f32)
+    col = jnp.broadcast_to(row, (LANES, n_neg)).T
+    lane = lax.broadcasted_iota(i32, (n_neg, LANES), 1)
+    for k in range(n_step):
+        hot = [
+            jnp.where(col == (lane + (k * step + c)).astype(f32), 1.0, 0.0).astype(bf16) for c in range(0, step, LANES)
+        ]
+        hot = jnp.concatenate(hot, axis=1)
+        copies[1 + k].wait()
+        t_hi, t_lo = split(table[k])
+        part = dot(hot, t_hi, NN) + dot(hot, t_lo, NN)
+        picked[...] = part if k == 0 else picked[...] + part
+    n_part = n_neg // (2 * n_item)
+    for half in range(2):
+        for m, r in enumerate(item_orders[half]):
+            first = half * (n_neg // 2) + (item ^ r) * n_part
+            out = outs[2 * half + m // (n_item // 2)]
+            out[m % (n_item // 2)] = picked[pl.ds(pl.multiple_of(first, n_part), n_part)]
+
+
+def pick_rows(plan, ids, table):
+    n_rows, width = table.shape
+    n_item, n_neg = plan[1], ids.shape[1]
+    step = 256
+    out = (n_item // 2, n_neg // (2 * n_item), width)
+    return pl.pallas_call(
+        functools.partial(pick_kernel, plan),
+        in_specs=[pl.BlockSpec(memory_space=pltpu.HBM)] * 2,
+        out_specs=[pl.BlockSpec(memory_space=pltpu.VMEM)] * 4,
+        out_shape=[jax.ShapeDtypeStruct(out, f32)] * 4,
+        scratch_shapes=[
+            pltpu.VMEM(ids.shape, i32),
+            pltpu.VMEM((n_rows // step, step, width), f32),
+            pltpu.VMEM((n_neg, width), f32),
+            pltpu.SemaphoreType.DMA((n_rows // step + 1,)),
+        ],
+        compiler_params=alone,
+        cost_estimate=pl.CostEstimate(flops=4 * n_neg * n_rows * width, bytes_accessed=4 * n_rows * width, transcendentals=0),
+        name="pick_rows",
+    )(ids, table)
+
+
+def prepare_kernel(x_ref, w_hbm, wo_hbm, gates_ref, queries_ref, vk_hi, vk_lo, wo_hi, wo_lo, w_buf, wo_buf, w_sems, wo_sem):
+    n = w_buf.shape[0]
+    copies = [
+        [
+            pltpu.make_async_copy(
+                w_hbm.at[:, pl.ds((part * n + j) * LANES, LANES)], w_buf.at[j, part], w_sems.at[j, part]
+            )
+            for part in range(4)
+        ]
+        for j in range(n)
+    ]
+    last = pltpu.make_async_copy(wo_hbm, wo_buf, wo_sem)
+    for copy in sum(copies, []) + [last]:
+        copy.start()
     x = split(x_ref[...])
-    uq = split(jnp.concatenate([u_ref[...], q_ref[...]], axis=1))
-    both = silu(dot3(x, uq, NN))
-    gates_ref[...] = both[:, :LANES]
-    queries_ref[...] = both[:, LANES:]
-    vk_hi[0], vk_lo[0] = split(jnp.concatenate([v_ref[...], k_ref[...]], axis=1))
-    wo_hi[...], wo_lo[...] = split(wo_ref[...])
+    for j in range(n):
+        for copy in copies[j]:
+            copy.wait()
+        span = pl.ds(j * LANES, LANES)
+        uq = split(jnp.concatenate([w_buf[j, 0], w_buf[j, 2]], axis=1))
+        both = silu(dot3(x, uq, NN))
+        gates_ref[:, span] = both[:, :LANES]
+        queries_ref[:, span] = both[:, LANES:]
+        vk_hi[j], vk_lo[j] = split(jnp.concatenate([w_buf[j, 1], w_buf[j, 3]], axis=1))
+    last.wait()
+    wo_hi[...], wo_lo[...] = split(wo_buf[...])
 
 
 def prepare(rows_in, w_uvqk, w_out):
     tok, width = rows_in.shape
     n = width // LANES
-
-    def column(part):
-        return pl.BlockSpec((width, LANES), lambda j: (0, part * n + j))
-
-    own = pl.BlockSpec((tok, LANES), lambda j: (0, j))
-    pair = pl.BlockSpec((1, width, 2 * LANES), lambda j: (j, 0, 0))
-    rows = pl.BlockSpec((LANES, width), lambda j: (j, 0))
+    hbm, vmem = pl.BlockSpec(memory_space=pltpu.HBM), pl.BlockSpec(memory_space=pltpu.VMEM)
     return pl.pallas_call(
         prepare_kernel,
-        grid=(n,),
-        in_specs=[pl.BlockSpec((tok, width), lambda j: (0, 0)), *[column(p) for p in range(4)], rows],
-        out_specs=[own, own, pair, pair, rows, rows],
+        in_specs=[vmem, hbm, hbm],
+        out_specs=[vmem] * 6,
         out_shape=[jax.ShapeDtypeStruct((tok, width), f32)] * 2
         + [jax.ShapeDtypeStruct((n, width, 2 * LANES), bf16)] * 2
         + [jax.ShapeDtypeStruct((width, width), bf16)] * 2,
+        scratch_shapes=[
+            pltpu.VMEM((n, 4, width, LANES), f32),
+            pltpu.VMEM((width, width), f32),
+            pltpu.SemaphoreType.DMA((n, 4)),
+            pltpu.SemaphoreType.DMA,
+        ],
         compiler_params=params,
         cost_estimate=pl.CostEstimate(flops=8 * tok * width * width, bytes_accessed=6 * width * width * 4, transcendentals=0),
         name="prepare",
-    )(rows_in, w_uvqk, w_uvqk, w_uvqk, w_uvqk, w_out)
-
-
-def attend_kernel(order, n_seq, meta, *refs):
+    )(rows_in, w_uvqk, w_out)
+
+
+def attend_kernel(order, n_seq, lengths, *refs):
     x_refs, (q_ref, vk_hi, vk_lo, out_ref, x_hi, x_lo, allowed) = refs[:n_seq], refs[n_seq:]
     tok = q_ref.shape[0]
     head = x_hi.shape[1] // H
 
     @pl.when(pl.program_id(0) == 0)
     def _():
-        me = meta[0]
+        me = lax.axis_index("seq")
         q_pos = me * tok + lax.broadcasted_iota(i32, (tok, tok), 0)
         col = lax.broadcasted_iota(i32, (tok, tok), 1)
 
         def user(pos):
             ids, end = jnp.zeros_like(pos), 0
-            for k in range(meta.shape[0] - 1):
-                end = end + meta[1 + k]
+            for k in range(lengths.shape[1]):
+                end = end + lengths[0, k]
                 ids = ids + (pos >= end).astype(i32)
             return ids
 
@@ -149,19 +227,23 @@
     k_both = jnp.concatenate([k_hi, k_lo], axis=1)
     v_both = jnp.concatenate([v_hi, v_lo], axis=1)
     queries = q_ref[...]
+    n_heads = LANES // head
     of_head = lax.broadcasted_iota(i32, (tok, LANES), 1) // head
-    total = jnp.zeros((tok, LANES), f32)
-    for h in range(LANES // head):
-        q_hi, q_lo = split(jnp.where(of_head == h, queries, 0.0))
-        scores = dot(jnp.concatenate([q_hi, q_hi], axis=1), k_both, NT) + dot(q_lo, k_hi, NT)
-        w_hi, w_lo = split(silu(scores) * allowed[...])
-        wide = dot(w_hi, v_both, NN)
-        mine = wide[:, :LANES] + wide[:, LANES:] + dot(w_lo, v_hi, NN)
-        total = jnp.where(of_head == h, mine, total)
+    stacked = jnp.concatenate([jnp.where(of_head == h, queries, 0.0) for h in range(n_heads)], axis=0)
+    q_hi, q_lo = split(stacked)
+    scores = dot(jnp.concatenate([q_hi, q_hi], axis=1), k_both, NT) + dot(q_lo, k_hi, NT)
+    seen = allowed[...]
+    weights = silu(scores) * jnp.concatenate([seen] * n_heads, axis=0)
+    w_hi, w_lo = split(weights)
+    wide = dot(w_hi, v_both, NN)
+    mine = wide[:, :LANES] + wide[:, LANES:] + dot(w_lo, v_hi, NN)
+    total = mine[:tok]
+    for h in range(1, n_heads):
+        total = jnp.where(of_head == h, mine[h * tok : (h + 1) * tok], total)
     out_ref[...] = total
 
 
-def attend(meta, pieces, order, queries, vk_hi, vk_lo, first, count):
+def attend(lengths, pieces, order, queries, vk_hi, vk_lo, first, count):
     tok, width = pieces[0].shape
     n_seq = len(pieces)
     whole = pl.BlockSpec((tok, width), lambda j: (0, 0))
@@ -182,7 +264,7 @@
         compiler_params=params,
         cost_estimate=pl.CostEstimate(flops=count * 2000000000, bytes_accessed=2 * width * width * 4, transcendentals=0),
         name="attend",
-    )(meta, *pieces, queries, vk_hi, vk_lo)
+    )(lengths, *pieces, queries, vk_hi, vk_lo)
 
 
 def project_kernel(n_parts, words, *refs):
@@ -213,13 +295,13 @@
     )(words, *parts, gates, gain, wo_hi, wo_lo, rows_in, targets)
 
 
-def loss_kernel(plan, meta, *refs):
+def loss_kernel(plan, *refs):
     n_seq, n_item, seq_order, item_orders, aligned = plan
     o_refs, refs = refs[:n_seq], refs[n_seq:]
     n_refs, refs = refs[: 4 if aligned else 1], refs[4 if aligned else 1 :]
-    n_out = 4 if aligned else 1
-    panel_refs, (kept_rows, sent_rows, loss_ref, n_hi, n_lo, o_hi, o_lo, g_hi, g_lo, panel) = refs[:n_out], refs[n_out:]
-    me, item = meta[0], meta[1]
+    n_out = 4 if aligned else 2
+    panel_refs, (kept_rows, sent_rows, n_hi, n_lo, o_hi, o_lo, g_hi, g_lo, panel) = refs[:n_out], refs[n_out:]
+    me, item = lax.axis_index("seq"), lax.axis_index("item")
     n_neg, width = n_hi.shape
     tok = o_refs[0].shape[0] - EXTRA
 
@@ -259,10 +341,11 @@
             n = 2 * p + k
             target_ref = kept_rows if n < n_seq // 2 else sent_rows
             target_ref[n % (n_seq // 2)] = rows[k * tok : (k + 1) * tok]
-    loss_ref[...] = jnp.full((8, LANES), jnp.sum(loss))
+    loss = jnp.full((EXTRA, n_neg), jnp.sum(loss))
     whole = dot3((o_hi[...], o_lo[...]), (g_hi[...], g_lo[...]), NT)
     if not aligned:
         panel_refs[0][...] = whole
+        panel_refs[1][...] = loss
         return
     panel[...] = whole
     n_dim = width // (n_seq * n_item)
@@ -270,25 +353,29 @@
     for half in range(2):
         for m, r in enumerate(item_orders[half]):
             out = panel_refs[2 * half + m // (n_item // 2)]
+            k = m % (n_item // 2)
             for n, q in enumerate(seq_order):
                 first = (me ^ q) * (n_item * n_dim) + (item ^ r) * n_dim + half * part
-                out[m % (n_item // 2), n] = panel[pl.ds(pl.multiple_of(first, part), part)]
-
-
-def loss_terms(meta, outputs, negatives, plan, n_neg):
+                out[k, n * part : (n + 1) * part] = panel[pl.ds(pl.multiple_of(first, part), part)]
+            if half == 0:
+                out[k, n_seq * part :] = loss
+
+
+def loss_terms(outputs, negatives, plan, n_neg):
     n_seq, n_item, _, _, aligned = plan
     tok, width = outputs[0].shape[0] - EXTRA, outputs[0].shape[1]
     group_len = tok * n_seq
     vmem = pl.BlockSpec(memory_space=pltpu.VMEM)
     if aligned:
-        panel = [jax.ShapeDtypeStruct((n_item // 2, n_seq, width // (2 * n_seq * n_item), n_neg), f32)] * 4
+        part = width // (2 * n_item)
+        panel = [jax.ShapeDtypeStruct((n_item // 2, part + e, n_neg), f32) for e in (EXTRA, EXTRA, 0, 0)]
     else:
-        panel = [jax.ShapeDtypeStruct((width, n_neg), f32)]
+        panel = [jax.ShapeDtypeStruct((width, n_neg), f32), jax.ShapeDtypeStruct((EXTRA, n_neg), f32)]
     rows = [jax.ShapeDtypeStruct((n_seq // 2, tok, width), f32)] * 2
-    out_shape = panel + rows + [jax.ShapeDtypeStruct((8, LANES), f32)]
+    out_shape = panel + rows
     return pl.pallas_call(
         functools.partial(loss_kernel, plan),
-        in_specs=[pl.BlockSpec(memory_space=pltpu.SMEM)] + [vmem] * (n_seq + len(negatives)),
+        in_specs=[vmem] * (n_seq + len(negatives)),
         out_specs=[vmem] * len(out_shape),
         out_shape=out_shape,
         scratch_shapes=[pltpu.VMEM((n_neg, width), bf16)] * 2
@@ -298,60 +385,76 @@
         compiler_params=params,
         cost_estimate=pl.CostEstimate(flops=18 * group_len * width * n_neg, bytes_accessed=16 * n_neg * width, transcendentals=0),
         name="loss_terms",
-    )(meta, *outputs, *negatives)
-
-
-def spread_kernel(owner, moved, ids, out_ref):
-    n_src, n_dim, n_neg = moved.shape
-    n_item, _, n_rows = out_ref.shape
+    )(*outputs, *negatives)
+
+
+def spread_kernel(order, per_panel, n_item, owner, ids, *refs):
+    moved, (*outs, loss_ref) = refs[: len(order)], refs[len(order) :]
+    n_dim, n_rows = outs[0].shape
+    n_neg = ids.shape[1]
+    me, item = lax.axis_index("seq"), lax.axis_index("item")
     row = lax.broadcasted_iota(i32, (n_rows, n_neg), 0)
-    spread = []
-    for p in range(n_src):
-        hot = jnp.where(row == ids[p : p + 1], 1.0, 0.0).astype(bf16)
-        both = dot(jnp.concatenate(split(moved[p]), axis=0), hot, NT)
+    spread, owners = [], []
+    for p, r in enumerate(order):
+        source = me ^ r
+        owners.append(owner[source // per_panel])
+        hot = jnp.where(row == ids[pl.ds(source, 1), :], 1.0, 0.0).astype(bf16)
+        both = dot(jnp.concatenate(split(moved[p][:n_dim]), axis=0), hot, NT)
         spread.append(both[:n_dim] + both[n_dim:])
-    for j in range(n_item):
-        total = jnp.where(owner[0] == j, spread[0], 0.0)
-        for p in range(1, n_src):
-            total = total + jnp.where(owner[p] == j, spread[p], 0.0)
-        out_ref[j] = total
-
-
-def spread_rows(owner, moved, ids, n_item, n_rows):
+    for r in range(n_item):
+        total = jnp.where(owners[0] == item ^ r, spread[0], 0.0)
+        for p in range(1, len(order)):
+            total = total + jnp.where(owners[p] == item ^ r, spread[p], 0.0)
+        outs[r][...] = total
+    loss_ref[...] = sum(m[n_dim:, :LANES] for m in moved)
+
+
+def spread_rows(order, per_panel, owner, moved, ids, n_item, n_rows):
     vmem = pl.BlockSpec(memory_space=pltpu.VMEM)
+    smem = pl.BlockSpec(memory_space=pltpu.SMEM)
+    n_dim = moved[0].shape[0] - EXTRA
     return pl.pallas_call(
-        spread_kernel,
-        in_specs=[pl.BlockSpec(memory_space=pltpu.SMEM), vmem, vmem],
-        out_specs=vmem,
-        out_shape=jax.ShapeDtypeStruct((n_item, moved.shape[1], n_rows), f32),
+        functools.partial(spread_kernel, order, per_panel, n_item),
+        in_specs=[smem, vmem] + [vmem] * len(moved),
+        out_specs=[vmem] * (n_item + 1),
+        out_shape=[jax.ShapeDtypeStruct((n_dim, n_rows), f32)] * n_item + [jax.ShapeDtypeStruct((EXTRA, LANES), f32)],
         compiler_params=params,
-        cost_estimate=pl.CostEstimate(flops=4 * moved.size * n_rows, bytes_accessed=2**21, transcendentals=0),
+        cost_estimate=pl.CostEstimate(flops=4 * len(moved) * moved[0].size * n_rows, bytes_accessed=2**21, transcendentals=0),
         name="spread_rows",
-    )(owner, moved, ids)
-
-
-def assemble_kernel(order, meta, *refs):
-    pieces, out_ref = refs[:-1], refs[-1]
-    cols = pieces[0].shape[0]
-    for piece, r in zip(pieces, order):
-        place = pl.ds(pl.multiple_of((meta[0] ^ r) * cols, cols), cols)
-        out_ref[:, place] = piece[...].T
-
-
-def assemble(meta, pieces, order):
-    cols, n_rows = pieces[0].shape
-    width = cols * len(pieces)
+    )(owner, ids, *moved)
+
+
+def assemble_kernel(order, n_item, *refs):
+    n_seq = len(order)
+    near, far, (out_ref, quarter) = refs[:n_seq], refs[n_seq : 2 * n_seq], refs[2 * n_seq :]
+    me, item = lax.axis_index("seq"), lax.axis_index("item")
+    cols = quarter.shape[0]
+    part = cols // n_item
+    for k, q in enumerate(order):
+        for r in range(n_item):
+            source = near[k] if r < n_item // 2 else far[k]
+            rows = source[pl.ds(r % (n_item // 2) * part, part)]
+            quarter[pl.ds(pl.multiple_of((item ^ r) * part, part), part)] = rows
+        out_ref[:, pl.ds(pl.multiple_of((me ^ q) * cols, cols), cols)] = quarter[...].T
+
+
+def assemble(table, order, n_item):
+    half, n_rows = table[0][0].shape
+    cols = 2 * half
+    width = cols * len(order)
     step = min(n_rows, 256)
+    pieces = table[0] + table[1]
     return pl.pallas_call(
-        functools.partial(assemble_kernel, order),
+        functools.partial(assemble_kernel, order, n_item),
         grid=(n_rows // step,),
-        in_specs=[pl.BlockSpec(memory_space=pltpu.SMEM)] + [pl.BlockSpec((cols, step), lambda j: (0, j))] * len(pieces),
+        in_specs=[pl.BlockSpec((half, step), lambda j: (0, j))] * len(pieces),
         out_specs=pl.BlockSpec((step, width), lambda j: (j, 0)),
         out_shape=jax.ShapeDtypeStruct((n_rows, width), f32),
+        scratch_shapes=[pltpu.VMEM((cols, step), f32)],
         compiler_params=params,
         cost_estimate=pl.CostEstimate(flops=0, bytes_accessed=8 * n_rows * width, transcendentals=0),
         name="assemble",
-    )(meta, *pieces)
+    )(*pieces)
 
 
 def per_device(
@@ -375,6 +478,7 @@
     seq_bits = bits_of(n_seq)
     seq_order = orders(seq_bits)
     bit_lists = two_orders(n_item)
+    shared = bit_lists[0][:-2]
     item_orders = [orders(bits) for bits in bit_lists]
     flat_ids = neg_ids.reshape(-1)
     n_neg = flat_ids.shape[0] // n_seq
@@ -384,24 +488,34 @@
     aligned = n_part % 16 == 0 and n_dim % 16 == 0 and (n_item * n_dim) % LANES == 0
     plan = (n_seq, n_item, tuple(seq_order), tuple(tuple(o) for o in item_orders), aligned)
 
+    ids_by_seq = flat_ids.reshape(n_seq, n_neg)
     rel = i ^ jnp.array(item_orders, i32)
-    spot = s * n_neg + rel[:, :, None] * n_part + jnp.arange(n_part, dtype=i32)
-    spot = spot + jnp.array([0, n_neg // 2], i32)[:, None, None]
-    own_ids = flat_ids.at[spot.reshape(2, -1)].get(mode="promise_in_bounds")
     root = panel_owner[s // per_panel]
+    if aligned:
+        parts = pick_rows(plan, ids_by_seq, item_table)
+        parts = [parts[:2], parts[2:]]
+    else:
+        spot = s * n_neg + rel[:, :, None] * n_part + jnp.arange(n_part, dtype=i32)
+        spot = spot + jnp.array([0, n_neg // 2], i32)[:, None, None]
+        rows = item_table[flat_ids[spot.reshape(-1)]].reshape(2, n_item, n_part, width)
+        parts = [(part[: n_item // 2], part[n_item // 2 :]) for part in rows]
+    for step in range(2):
+        for half, bits in enumerate(bit_lists):
+            bit, (kept, sent) = bits[-1 - step], parts[half]
+            other = swap(sent, "item", bit)
+            same = ((i ^ root) >> bit) & 1 == 0
+            cut = kept.shape[0] if step == 1 else kept.shape[0] // 2
+            parts[half] = (jnp.where(same, kept[:cut], other[:cut]), jnp.where(same, kept[cut:], other[cut:]))
+    both = jnp.stack([part[0] for part in parts])
+    for bit in shared[:0:-1]:
+        cut = both.shape[1] // 2
+        other = swap(both[:, cut:], "item", bit)
+        both = jnp.where(((i ^ root) >> bit) & 1 == 0, both[:, :cut], other)
+    other = swap(both, "item", shared[0])
+    same = ((i ^ root) >> shared[0]) & 1 == 0
     parts = [
-        item_table.at[own_ids[half]].get(mode="promise_in_bounds").reshape(n_item, n_part, width) for half in range(2)
+        jnp.where(same, both[half], jnp.concatenate([other[half, 1:], other[half, :1]], axis=0)) for half in range(2)
     ]
-    for step in range(len(bit_lists[0]) - 1):
-        for half, bits in enumerate(bit_lists):
-            bit, part = bits[-1 - step], parts[half]
-            cut = part.shape[0] // 2
-            other = swap(part[cut:], "item", bit)
-            parts[half] = jnp.where(((i ^ root) >> bit) & 1 == 0, part[:cut], other)
-    for half, bits in enumerate(bit_lists):
-        other = swap(parts[half], "item", bits[0])
-        same = ((i ^ root) >> bits[0]) & 1 == 0
-        parts[half] = jnp.where(same, parts[half], jnp.concatenate([other[1:], other[:1]], axis=0))
     for step in range(1, len(bit_lists[0]) - 1):
         for half, bits in enumerate(bit_lists):
             parts[half] = jnp.concatenate([parts[half], swap(parts[half], "item", bits[step])], axis=0)
@@ -417,53 +531,74 @@
         ]
         negatives = [jnp.concatenate([n.reshape(-1, width) for n in negatives], axis=0)]
 
-    meta = jnp.concatenate([s[None], user_lengths[0]])
     pieces = gather_pieces(rows_in, "seq", seq_bits)
     gates, queries, vk_hi, vk_lo, wo_hi, wo_lo = prepare(rows_in, w_uvqk, w_out)
     groups = width // LANES
-    attended = [attend(meta, pieces, seq_order, queries, vk_hi, vk_lo, 0, groups)]
+    calls = 2
+    attended = [
+        attend(user_lengths, pieces, seq_order, queries, vk_hi, vk_lo, c * groups // calls, groups // calls)
+        for c in range(calls)
+    ]
     own_outputs = project(block_mask, attended, gates, out_gain[None], wo_hi, wo_lo, rows_in, targets)
     outputs = gather_pieces(own_outputs, "seq", seq_bits)
 
-    place = jnp.stack([s, i])
-    *panel, kept_rows, sent_rows, loss_total = loss_terms(place, outputs, negatives, plan, n_neg)
+    *panel, kept_rows, sent_rows = loss_terms(outputs, negatives, plan, n_neg)
     if not aligned:
         blocks = panel[0].reshape(n_seq, n_item, 2, n_dim // 2, n_neg).transpose(2, 1, 0, 3, 4)
+        loss = jnp.broadcast_to(panel[1], (n_item, EXTRA, n_neg))
         panel = []
         for half in range(2):
-            mine = blocks[half][rel[half]][:, s ^ jnp.array(seq_order, i32)]
+            mine = blocks[half][rel[half]][:, s ^ jnp.array(seq_order, i32)].reshape(n_item, -1, n_neg)
+            if half == 0:
+                mine = jnp.concatenate([mine, loss], axis=1)
             panel += [mine[: n_item // 2], mine[n_item // 2 :]]
     event_grad = reduce_steps(kept_rows, sent_rows, "seq", seq_bits[::-1])
-    for axis, size in (("seq", n_seq), ("item", n_item)):
-        for bit in bits_of(size):
-            loss_total = loss_total + swap(loss_total, axis, bit)
-    loss_total = loss_total[0, 0]
-
-    sums = [
-        reduce_steps(panel[2 * half], panel[2 * half + 1], "item", bits[::-1]) for half, bits in enumerate(bit_lists)
-    ]
-    moved = jnp.concatenate(sums, axis=1)[:, None]
-    for bit in seq_bits[::-1]:
-        half = moved.shape[0] // 2
-        moved = jnp.concatenate([moved[:half], swap(moved[half:], "seq", bit)], axis=1)
-    moved = moved[0]
-    source = s ^ jnp.array(orders(seq_bits[::-1]), i32)
-    ids = flat_ids.reshape(n_seq, n_neg)[source]
-    owner = panel_owner[source // per_panel]
+
+    kept, sent = [], []
+    for half, bits in enumerate(bit_lists):
+        k, t = panel[2 * half], panel[2 * half + 1]
+        for bit in bits[:-3:-1]:
+            got = swap(t, "item", bit)
+            cut = k.shape[0] // 2
+            k, t = k[:cut] + got[:cut], k[cut:] + got[cut:]
+        kept.append(k)
+        sent.append(t)
+    total = reduce_steps(jnp.concatenate(kept, axis=1), jnp.concatenate(sent, axis=1), "item", shared[::-1])
+    total, event_grad = lax.optimization_barrier((total, event_grad))
+    part = n_dim // 2
+    loss = total[n_seq * part : n_seq * part + EXTRA]
+    halves = total[: n_seq * part], total[n_seq * part + EXTRA :]
+    moved = []
+    for k, r in enumerate(seq_order):
+        block = jnp.concatenate([half[k * part : (k + 1) * part] for half in halves] + [loss], axis=0)
+        moved.append(send(block, "seq", r) if r else block)
     if aligned:
-        sent = spread_rows(owner, moved, ids, n_item, n_rows)
+        *sent, loss_total = spread_rows(seq_order, per_panel, panel_owner, moved, ids_by_seq, n_item, n_rows)
     else:
+        source = s ^ jnp.array(seq_order, i32)
+        ids, owner = ids_by_seq[source], panel_owner[source // per_panel]
         hot = (ids[:, :, None] == jnp.arange(n_rows, dtype=i32)).astype(f32)
-        spread = jnp.einsum("pdc,pcr->pdr", moved, hot, precision=high)
-        mine = (owner[None, :] == jnp.arange(n_item, dtype=i32)[:, None]).astype(f32)
+        moved = jnp.stack(moved)
+        loss_total = jnp.sum(moved[:, n_dim:], axis=0)
+        spread = jnp.einsum("pdc,pcr->pdr", moved[:, :n_dim], hot, precision=high)
+        mine = (owner[None, :] == (i ^ jnp.arange(n_item, dtype=i32))[:, None]).astype(f32)
         sent = jnp.sum(mine[:, :, None, None] * spread[None], axis=1)
-    taken = lax.all_to_all(sent, "item", split_axis=0, concat_axis=0, tiled=True)
-    table = gather_pieces(taken.reshape(n_item * n_dim, n_rows), "seq", seq_bits)
+        sent = [sent[r] for r in range(n_item)]
+
+    taken = {r: send(sent[r], "item", r) if r else sent[r] for r in list(range(n_item // 2, n_item)) + list(range(n_item // 2))}
+    table = []
+    for first in (0, n_item // 2):
+        group = jnp.concatenate([taken[r] for r in range(first, first + n_item // 2)], axis=0)
+        table.append([group, swap(group, "seq", seq_bits[0])])
+    for bit in seq_bits[1:]:
+        table = [group + [swap(piece, "seq", bit) for piece in group] for group in table]
     if aligned:
-        table_grad = assemble(place, table, seq_order)
+        table_grad = assemble(table, seq_order, n_item)
     else:
-        table_grad = true_order(jnp.stack(table), seq_order, s).reshape(width, n_rows).T
-    return (loss_total / (group_len * n_item), event_grad[None], table_grad)
+        table = jnp.stack([jnp.concatenate([near, far], axis=0) for near, far in zip(*table)])
+        table = table.reshape(n_seq, n_item, n_dim, n_rows)[:, i ^ jnp.arange(n_item, dtype=i32)]
+        table_grad = true_order(table, seq_order, s).reshape(width, n_rows).T
+    return (loss_total[0, 0] / (group_len * n_item), event_grad[None], table_grad)
 
 
 def solution(mesh):

time: 155 us -> 123 us (0.79)
  blocking collectives: 16.9 us -> 0 us
  waiting for transfers between devices: 62.1 us -> 49.6 us
  local copies, waits for them, and re-layouts: 14.1 us -> 3.41 us
  starting transfers between devices: 30 us -> 37.7 us
    ppermute x34 -> x28, waiting for transfers between devices: 62.1 us -> 43.9 us  [swap(): return lax.ppermute(block, axis, [(i, i ^ 1 << bit) for i in range(size)])]
    all_to_all x1 -> x0, blocking collectives: 16.9 us -> none  [per_device(): lax.all_to_all(sent, 'item', split_axis=0, concat_axis=0, tiled=True)]
    ppermute x0 -> x10, starting transfers between devices: none -> 13.5 us  [send(): return lax.ppermute(block, axis, [(i, i ^ r) for i in range(size)])]
    gather x5 -> x0, local copies, waits for them, and re-layouts: 7.07 us -> none  [the longest x1 3.14 us: per_device(): own_ids = flat_ids.at[spot.reshape(2, -1)].get(mode='promise_in_bounds')]
    ppermute x34 -> x28, starting transfers between devices: 30 us -> 24.2 us  [swap(): return lax.ppermute(block, axis, [(i, i ^ 1 << bit) for i in range(size)])]
    ppermute x0 -> x10, waiting for transfers between devices: none -> 5.7 us  [send(): return lax.ppermute(block, axis, [(i, i ^ r) for i in range(size)])]
    pallas_call x4 -> x5, Pallas kernels: 12.6 us -> 15.8 us  [the longest x1 4.64 us: loss_terms(): pl.pallas_call(functools.partial(loss_kernel, plan), in_specs=[vmem] * (n...]
    slice x8 -> x2, local copies, waits for them, and re-layouts: 3.25 us -> 0.52 us  [the longest x1 0.51 us: per_device(): loss_total[0, 0] / (group_len * n_item)]
  transfers between devices with their start and end apart: 34 -> 38, of which waited for: 19 -> 18; matrix products, arithmetic and copies ran while one was open for 9% -> 1% of each run, Pallas kernels for 10% -> 11%
where the time goes in v4:
time: 123 us
  waiting for transfers between devices  49.6 us (40%)
  starting transfers between devices  37.7 us (31%)
  Pallas kernels  26.6 us (22%)
  between operations  4.13 us (3%)
  local copies, waits for them, and re-layouts  3.41 us (3%)
    ppermute x28, waiting for transfers between devices, swap(): return lax.ppermute(block, axis, [(i, i ^ 1 << bit) for i in range(size)])  43.9 us
    ppermute x28, starting transfers between devices, swap(): return lax.ppermute(block, axis, [(i, i ^ 1 << bit) for i in range(size)])  24.2 us
    ppermute x10, starting transfers between devices, send(): return lax.ppermute(block, axis, [(i, i ^ r) for i in range(size)])  13.5 us
    pallas_call x2, Pallas kernels, attend(): pl.pallas_call(functools.partial(attend_kernel, order, n_seq), grid=(coun...  10.2 us
    ppermute x10, waiting for transfers between devices, send(): return lax.ppermute(block, axis, [(i, i ^ r) for i in range(size)])  5.7 us
    pallas_call x1, Pallas kernels, loss_terms(): pl.pallas_call(functools.partial(loss_kernel, plan), in_specs=[vmem] * (n...  4.64 us
    pallas_call x1, Pallas kernels, pick_rows(): pl.pallas_call(functools.partial(pick_kernel, plan), in_specs=[pl.BlockSp...  3.68 us
    pallas_call x1, Pallas kernels, prepare(): pl.pallas_call(prepare_kernel, in_specs=[vmem, hbm, hbm], out_specs=[vmem...  3.04 us
  transfers between devices with their start and end apart: 38, of which 18 were waited for; matrix products, arithmetic and copies ran while one was open for 1% of the time, Pallas kernels for 11%

profile of v4, /device:TPU:0, one launch (start us, length us, event | category | flops | bytes accessed | tf_op | source)
XLA Modules:
  0.0 122.5 jit_solution(7520234902647594323)
XLA Ops:
  0.7 3.7 %pick_rows.1 = (f32[4,32,512]{2,1,0:T(8,128)}, f32[4,32,512]{2,1,0:T(8,128)}, f32[4,32,512]{2,1,0:T(8,128)}, f32[4,32,512]{2,1,0:T(8,128)}) custom-call(s32[4,512]{1,0:T(4,128)} %ids.1, f32[1024,512]{1,0:T(8,128)} %table_hbm.1), custom_call_target="tpu_custom_call" | custom-call | flops 1073741824 | bytes 2097152 | tf_op jit(solution)/shard_map/pick_rows/pallas_call | solution.py:129
  4.4 3.0 %collective-permute-start.6 = (f32[4,32,512]{2,1,0:T(8,128)}, f32[4,32,512]{2,1,0:T(8,128)S(1)}, u32[]{:S(2)}, u32[]{:S(2)}) collective-permute-start(f32[4,32,512]{2,1,0:T(8,128)} %get-tuple-element.37), channel_id=1, source_target_pairs={{0,1},{1,0},{2,3},{3,2},{4,5},{5,4},{6,7},{7,6},{8,9},{9,8},{10,11... | collective-permute-start | bytes 786440 | tf_op jit(solution)/shard_map/ppermute | solution.py:26
  7.4 1.6 %collective-permute-start.8 = (f32[4,32,512]{2,1,0:T(8,128)}, f32[4,32,512]{2,1,0:T(8,128)S(1)}, u32[]{:S(2)}, u32[]{:S(2)}) collective-permute-start(f32[4,32,512]{2,1,0:T(8,128)} %get-tuple-element.39), channel_id=1, source_target_pairs={{0,2},{1,3},{2,0},{3,1},{4,6},{5,7},{6,4},{7,5},{8,10},{9,11},{10,... | collective-permute-start | bytes 786440 | tf_op jit(solution)/shard_map/ppermute | solution.py:26
  8.9 1.5 %collective-permute-start = (f32[128,512]{1,0:T(8,128)S(1)}, f32[128,512]{1,0:T(8,128)S(1)}, u32[]{:S(2)}, u32[]{:S(2)}) collective-permute-start(f32[128,512]{1,0:T(8,128)S(1)} %bitcast.23), channel_id=1, source_target_pairs={{0,16},{8,24},{16,0},{24,8},{1,17},{9,25},{17,1},{25,9},{2,18},{10... | collective-permute-start | bytes 786440 | tf_op jit(solution)/shard_map/ppermute | solution.py:26
  10.5 0.0 collective-permute-start.1
  11.1 0.6 dynamic_slice.3
  12.4 0.0 copy-start
  12.4 2.2 %copy-done = f32[512,2048]{1,0:T(8,128)S(1)} copy-done((f32[512,2048]{1,0:T(8,128)S(1)}, f32[512,2048]{1,0:T(8,128)}, u32[]{:S(2)}) %copy-start) | copy-done | bytes 4194328
  14.6 3.0 %prepare.1 = (f32[128,512]{1,0:T(8,128)S(1)}, f32[128,512]{1,0:T(8,128)S(1)}, bf16[4,512,256]{2,1,0:T(8,128)(2,1)S(1)}, bf16[4,512,256]{2,1,0:T(8,128)(2,1)S(1)}...) custom-call(f32[128,512]{1,0:T(8,128)S(1)} %bitcast.25, f32[512,2048]{1,0:T(8,128)S(1)} %copy-done, ...), custom_call_target="tpu_custom_call" | custom-call | flops 268435456 | bytes 6291456 | tf_op jit(solution)/shard_map/prepare/pallas_call | solution.py:178
  17.6 0.0 copy-start.6
  17.7 0.5 collective-permute-start.7
  18.2 0.6 collective-permute-start.9
  18.8 4.8 %collective-permute-done.7 = f32[2,32,512]{2,1,0:T(8,128)S(1)} collective-permute-done((f32[2,32,512]{2,1,0:T(8,128)S(1)}, f32[2,32,512]{2,1,0:T(8,128)S(1)}, u32[]{:S(2)}, u32[]{:S(2)}) %collective-permute-start.7) | collective-permute-done | bytes 131104 | tf_op jit(solution)/shard_map/ppermute | solution.py:26
  23.7 0.2 collective-permute-done.9
  24.0 2.7 %collective-permute-start.10 = (f32[2,2,32,512]{3,2,1,0:T(8,128)S(1)}, f32[2,2,32,512]{3,2,1,0:T(8,128)S(1)}, u32[]{:S(2)}, u32[]{:S(2)}) collective-permute-start(f32[2,2,32,512]{3,2,1,0:T(8,128)S(1)} %pad_maximum_fusion), channel_id=1, source_target_pairs={{0,4},{1,5},{2,6},{3,7},{4,0},{5,1},{6,2},{7,3},{8,12},{9,13},{10,... | collective-permute-start | bytes 786440 | tf_op jit(solution)/shard_map/ppermute | solution.py:26
  26.6 5.0 %attend.2.refs_0_ = f32[128,256]{1,0:T(8,128)S(1)} custom-call(s32[1,4]{1,0:T(1,128)S(1)} %copy-done.6, f32[128,512]{1,0:T(8,128)S(1)} %bitcast.26, f32[128,512]{1,0:T(8,128)S(1)} %collective-permute-done.refs_1_, f32[128,512]{1,0:T(8,128)S(1)} %collective-permute-done.1.refs_2_, f32[128,512]{1,0:T(8,128)S(1)} %collective-permute-done.2.refs_3_, ...), custom_call_target="tpu_custom_call" | custom-call | flops 4000000000 | bytes 2097152 | tf_op jit(solution)/shard_map/attend/pallas_call | solution.py:251
  31.6 0.0 copy-start.3
  31.7 0.0 copy-start.4
  31.7 5.2 %attend.3.refs_1_ = f32[128,256]{1,0:T(8,128)S(1)} custom-call(s32[1,4]{1,0:T(1,128)S(1)} %copy-done.6, f32[128,512]{1,0:T(8,128)S(1)} %bitcast.27, f32[128,512]{1,0:T(8,128)S(1)} %collective-permute-done.refs_1_, f32[128,512]{1,0:T(8,128)S(1)} %collective-permute-done.1.refs_2_, f32[128,512]{1,0:T(8,128)S(1)} %collective-permute-done.2.refs_3_, ...), custom_call_target="tpu_custom_call" | custom-call | flops 4000000000 | bytes 2097152 | tf_op jit(solution)/shard_map/attend/pallas_call | solution.py:251
  36.9 0.5 project.1.refs_0_
  37.4 0.6 collective-permute-start.3
  38.0 0.3 collective-permute-done.10
  38.3 1.4 %collective-permute-start.11 = (f32[2,32,512]{2,1,0:T(8,128)S(1)}, f32[2,32,512]{2,1,0:T(8,128)S(1)}, u32[]{:S(2)}, u32[]{:S(2)}) collective-permute-start(f32[2,32,512]{2,1,0:T(8,128)S(1)} %maximum_select_fusion), channel_id=1, source_target_pairs={{0,2},{1,3},{2,0},{3,1},{4,6},{5,7},{6,4},{7,5},{8,10},{9,11},{10,... | collective-permute-start | bytes 393224 | tf_op jit(solution)/shard_map/ppermute | solution.py:26
  39.7 0.6 collective-permute-start.13
  40.3 3.0 %collective-permute-done.11 = f32[2,32,512]{2,1,0:T(8,128)S(1)} collective-permute-done((f32[2,32,512]{2,1,0:T(8,128)S(1)}, f32[2,32,512]{2,1,0:T(8,128)S(1)}, u32[]{:S(2)}, u32[]{:S(2)}) %collective-permute-start.11) | collective-permute-done | bytes 131104 | tf_op jit(solution)/shard_map/ppermute | solution.py:26
  43.4 0.6 collective-permute-start.12
  44.0 1.3 %collective-permute-done.3.refs_1_ = f32[136,512]{1,0:T(8,128)S(1)} collective-permute-done((f32[136,512]{1,0:T(8,128)S(1)}, f32[136,512]{1,0:T(8,128)S(1)}, u32[]{:S(2)}, u32[]{:S(2)}) %collective-permute-start.3) | collective-permute-done | bytes 278560 | tf_op jit(solution)/shard_map/ppermute | solution.py:26
  45.3 1.5 %collective-permute-start.14 = (f32[4,32,512]{2,1,0:T(8,128)S(1)}, f32[4,32,512]{2,1,0:T(8,128)S(1)}, u32[]{:S(2)}, u32[]{:S(2)}) collective-permute-start(f32[4,32,512]{2,1,0:T(8,128)S(1)} %pad_maximum_fusion.2), channel_id=1, source_target_pairs={{0,2},{1,3},{2,0},{3,1},{4,6},{5,7},{6,4},{7,5},{8,10},{9,11},{10,... | collective-permute-start | bytes 786440 | tf_op jit(solution)/shard_map/ppermute | solution.py:26
  46.9 3.5 %collective-permute-done.12 = f32[4,32,512]{2,1,0:T(8,128)S(1)} collective-permute-done((f32[4,32,512]{2,1,0:T(8,128)S(1)}, f32[4,32,512]{2,1,0:T(8,128)S(1)}, u32[]{:S(2)}, u32[]{:S(2)}) %collective-permute-start.12) | collective-permute-done | bytes 262176 | tf_op jit(solution)/shard_map/ppermute | solution.py:26
  50.4 3.7 %collective-permute-done.14 = f32[4,32,512]{2,1,0:T(8,128)S(1)} collective-permute-done((f32[4,32,512]{2,1,0:T(8,128)S(1)}, f32[4,32,512]{2,1,0:T(8,128)S(1)}, u32[]{:S(2)}, u32[]{:S(2)}) %collective-permute-start.14) | collective-permute-done | bytes 262176 | tf_op jit(solution)/shard_map/ppermute | solution.py:26
  54.1 4.6 %loss_terms.1 = (f32[4,40,512]{2,1,0:T(8,128)S(1)}, f32[4,40,512]{2,1,0:T(8,128)S(1)}, f32[4,32,512]{2,1,0:T(8,128)S(1)}, f32[4,32,512]{2,1,0:T(8,128)S(1)}, f32...) custom-call(f32[136,512]{1,0:T(8,128)S(1)} %project.1.refs_0_, f32[136,512]{1,0:T(8,128)S(1)} %collective-permute-done.3.refs_1_, ...), custom_call_target="tpu_custom_call" | custom-call | flops 2415919104 | bytes 4194304 | tf_op jit(solution)/shard_map/loss_terms/pallas_call | solution.py:376
  58.7 1.5 %collective-permute-start.17 = (f32[4,32,512]{2,1,0:T(8,128)S(1)}, f32[4,32,512]{2,1,0:T(8,128)S(1)}, u32[]{:S(2)}, u32[]{:S(2)}) collective-permute-start(f32[4,32,512]{2,1,0:T(8,128)S(1)} %get-tuple-element.43), channel_id=1, source_target_pairs={{0,2},{1,3},{2,0},{3,1},{4,6},{5,7},{6,4},{7,5},{8,10},{9,11},{10,... | collective-permute-start | bytes 786440 | tf_op jit(solution)/shard_map/ppermute | solution.py:26
  60.3 0.5 collective-permute-start.15
  60.8 5.9 %collective-permute-done.17 = f32[4,32,512]{2,1,0:T(8,128)S(1)} collective-permute-done((f32[4,32,512]{2,1,0:T(8,128)S(1)}, f32[4,32,512]{2,1,0:T(8,128)S(1)}, u32[]{:S(2)}, u32[]{:S(2)}) %collective-permute-start.17) | collective-permute-done | bytes 262176 | tf_op jit(solution)/shard_map/ppermute | solution.py:26
  66.8 0.6 collective-permute-start.18
  67.4 3.0 %collective-permute-done.15 = f32[4,40,512]{2,1,0:T(8,128)S(1)} collective-permute-done((f32[4,40,512]{2,1,0:T(8,128)S(1)}, f32[4,40,512]{2,1,0:T(8,128)S(1)}, u32[]{:S(2)}, u32[]{:S(2)}) %collective-permute-start.15) | collective-permute-done | bytes 327712 | tf_op jit(solution)/shard_map/ppermute | solution.py:26
  70.4 0.0 copy-start.5
  70.4 0.1 collective-permute-start.16
  70.5 1.7 %collective-permute-done.18 = f32[2,32,512]{2,1,0:T(8,128)S(1)} collective-permute-done((f32[2,32,512]{2,1,0:T(8,128)S(1)}, f32[2,32,512]{2,1,0:T(8,128)S(1)}, u32[]{:S(2)}, u32[]{:S(2)}) %collective-permute-start.18) | collective-permute-done | bytes 131104 | tf_op jit(solution)/shard_map/ppermute | solution.py:26
  72.2 3.6 %collective-permute-done.16 = f32[2,40,512]{2,1,0:T(8,128)S(1)} collective-permute-done((f32[2,40,512]{2,1,0:T(8,128)S(1)}, f32[2,40,512]{2,1,0:T(8,128)S(1)}, u32[]{:S(2)}, u32[]{:S(2)}) %collective-permute-start.16) | collective-permute-done | bytes 163872 | tf_op jit(solution)/shard_map/ppermute | solution.py:26
  75.8 3.3 %collective-permute-start.19 = (f32[1,72,512]{2,1,0:T(8,128)S(1)}, f32[1,72,512]{2,1,0:T(8,128)S(1)}, u32[]{:S(2)}, u32[]{:S(2)}) collective-permute-start(f32[1,72,512]{2,1,0:T(8,128)S(1)} %pad_maximum_fusion.3), channel_id=1, source_target_pairs={{0,4},{1,5},{2,6},{3,7},{4,0},{5,1},{6,2},{7,3},{8,12},{9,13},{10,... | collective-permute-start | bytes 442376 | tf_op jit(solution)/shard_map/ppermute | solution.py:26
  79.2 0.8 collective-permute-start.21
  80.0 3.0 %collective-permute-done.19 = f32[1,72,512]{2,1,0:T(8,128)S(1)} collective-permute-done((f32[1,72,512]{2,1,0:T(8,128)S(1)}, f32[1,72,512]{2,1,0:T(8,128)S(1)}, u32[]{:S(2)}, u32[]{:S(2)}) %collective-permute-start.19) | collective-permute-done | bytes 147488 | tf_op jit(solution)/shard_map/ppermute | solution.py:26
  83.0 3.0 %collective-permute-done.21 = f32[1,128,512]{2,1,0:T(8,128)S(1)} collective-permute-done((f32[1,128,512]{2,1,0:T(8,128)S(1)}, f32[1,128,512]{2,1,0:T(8,128)S(1)}, u32[]{:S(2)}, u32[]{:S(2)}) %collective-permute-start.21) | collective-permute-done | bytes 262176 | tf_op jit(solution)/shard_map/ppermute | solution.py:26
  86.0 0.8 fusion.1
  86.8 0.6 collective-permute-start.22
  87.4 1.6 %collective-permute-start.24 = (f32[24,512]{1,0:T(8,128)S(1)}, f32[24,512]{1,0:T(8,128)S(1)}, u32[]{:S(2)}, u32[]{:S(2)}) collective-permute-start(f32[24,512]{1,0:T(8,128)S(1)} %get-tuple-element.78), channel_id=1, source_target_pairs={{0,24},{8,16},{16,8},{24,0},{1,25},{9,17},{17,9},{25,1},{2,26},{10... | collective-permute-start | bytes 147464 | tf_op jit(solution)/shard_map/ppermute | solution.py:31
  89.0 2.4 %collective-permute-done.22.refs_1_ = f32[24,512]{1,0:T(8,128)S(1)} collective-permute-done((f32[24,512]{1,0:T(8,128)S(1)}, f32[24,512]{1,0:T(8,128)S(1)}, u32[]{:S(2)}, u32[]{:S(2)}) %collective-permute-start.22) | collective-permute-done | bytes 49184 | tf_op jit(solution)/shard_map/ppermute | solution.py:31
  91.4 2.0 %spread_rows.1 = (f32[16,1024]{1,0:T(8,128)S(1)}, f32[16,1024]{1,0:T(8,128)S(1)}, f32[16,1024]{1,0:T(8,128)S(1)}, f32[16,1024]{1,0:T(8,128)S(1)}, f32[16,1024]{1...) custom-call(s32[4]{0:T(128)S(1)} %copy-done.7, ...), custom_call_target="tpu_custom_call" | custom-call | flops 201326592 | bytes 2097152 | tf_op jit(solution)/shard_map/spread_rows/pallas_call | solution.py:416
  93.4 1.6 %collective-permute-start.25 = (f32[16,1024]{1,0:T(8,128)S(1)}, f32[16,1024]{1,0:T(8,128)S(1)}, u32[]{:S(2)}, u32[]{:S(2)}) collective-permute-start(f32[16,1024]{1,0:T(8,128)S(1)} %get-tuple-element.50), channel_id=1, source_target_pairs={{0,1},{1,0},{2,3},{3,2},{4,5},{5,4},{6,7},{7,6},{8,9},{9,8},{10,11... | collective-permute-start | bytes 196616 | tf_op jit(solution)/shard_map/ppermute | solution.py:31
  95.0 2.0 %collective-permute-start.27 = (f32[16,1024]{1,0:T(8,128)S(1)}, f32[16,1024]{1,0:T(8,128)S(1)}, u32[]{:S(2)}, u32[]{:S(2)}) collective-permute-start(f32[16,1024]{1,0:T(8,128)S(1)} %get-tuple-element.52), channel_id=1, source_target_pairs={{0,3},{1,2},{2,1},{3,0},{4,7},{5,6},{6,5},{7,4},{8,11},{9,10},{10,... | collective-permute-start | bytes 196616 | tf_op jit(solution)/shard_map/ppermute | solution.py:31
  97.0 0.3 collective-permute-start.31
  97.3 3.5 %collective-permute-start.32 = (f32[16,1024]{1,0:T(8,128)S(1)}, f32[16,1024]{1,0:T(8,128)S(1)}, u32[]{:S(2)}, u32[]{:S(2)}) collective-permute-start(f32[16,1024]{1,0:T(8,128)S(1)} %get-tuple-element.54), channel_id=1, source_target_pairs={{0,5},{1,4},{2,7},{3,6},{4,1},{5,0},{6,3},{7,2},{8,13},{9,12},{10,... | collective-permute-start | bytes 196616 | tf_op jit(solution)/shard_map/ppermute | solution.py:31
  100.8 0.1 collective-permute-start.33
  100.9 3.8 %collective-permute-start.34 = (f32[16,1024]{1,0:T(8,128)S(1)}, f32[16,1024]{1,0:T(8,128)S(1)}, u32[]{:S(2)}, u32[]{:S(2)}) collective-permute-start(f32[16,1024]{1,0:T(8,128)S(1)} %get-tuple-element.56), channel_id=1, source_target_pairs={{0,7},{1,6},{2,5},{3,4},{4,3},{5,2},{6,1},{7,0},{8,15},{9,14},{10,... | collective-permute-start | bytes 196616 | tf_op jit(solution)/shard_map/ppermute | solution.py:31
  104.8 1.0 collective-permute-start.28
  105.8 3.3 %collective-permute-done.32 = f32[16,1024]{1,0:T(8,128)S(1)} collective-permute-done((f32[16,1024]{1,0:T(8,128)S(1)}, f32[16,1024]{1,0:T(8,128)S(1)}, u32[]{:S(2)}, u32[]{:S(2)}) %collective-permute-start.32) | collective-permute-done | bytes 65568 | tf_op jit(solution)/shard_map/ppermute | solution.py:31
  109.2 1.2 collective-permute-start.35
  110.4 0.5 collective-permute-start.36
  110.9 0.5 collective-permute-done.28.refs_1_
  111.4 5.9 %collective-permute-done.35.refs_5_ = f32[64,1024]{1,0:T(8,128)S(1)} collective-permute-done((f32[64,1024]{1,0:T(8,128)S(1)}, f32[64,1024]{1,0:T(8,128)S(1)}, u32[]{:S(2)}, u32[]{:S(2)}) %collective-permute-start.35) | collective-permute-done | bytes 262176 | tf_op jit(solution)/shard_map/ppermute | solution.py:26
  117.4 0.5 slice.177
  118.6 0.3 collective-permute-done.37.refs_7_
  118.9 2.5 %assemble.1 = f32[1024,512]{1,0:T(8,128)} custom-call(f32[64,1024]{1,0:T(8,128)S(1)} %constant_dynamic-update-slice_fusion.refs_0_, f32[64,1024]{1,0:T(8,128)S(1)} %collective-permute-done.28.refs_1_, f32[64,1024]{1,0:T(8,128)S(1)} %collective-permute-done.29.refs_2_, f32[64,1024]{1,0:T(8,128)S(1)} %collective-permute-done.30.refs_3_, ...), custom_call_target="tpu_custom_call" | custom-call | bytes 4194304 | tf_op jit(solution)/shard_map/assemble/pallas_call | solution.py:447
  (70 shorter events, 0.6 us)
Async XLA Ops:
  0.6 8.3 %copy-start.2 = (f32[1,128,512]{2,1,0:T(8,128)S(1)}, f32[1,128,512]{2,1,0:T(8,128)}, u32[]{:S(2)}) copy-start(f32[1,128,512]{2,1,0:T(8,128)} %param.10) | copy-start | bytes 786436
  0.6 10.5 %copy-start.7 = (s32[4]{0:T(128)S(1)}, s32[4]{0:T(128)}, u32[]{:S(2)}) copy-start(s32[4]{0:T(128)} %owner.1) | copy-start | bytes 52
  0.7 11.7 %copy-start.1 = (f32[512,512]{1,0:T(8,128)S(1)}, f32[512,512]{1,0:T(8,128)}, u32[]{:S(2)}) copy-start(f32[512,512]{1,0:T(8,128)} %wo_hbm.1) | copy-start | bytes 3145732
  4.4 13.3 %collective-permute-start.6 = (f32[4,32,512]{2,1,0:T(8,128)}, f32[4,32,512]{2,1,0:T(8,128)S(1)}, u32[]{:S(2)}, u32[]{:S(2)}) collective-permute-start(f32[4,32,512]{2,1,0:T(8,128)} %get-tuple-element.37), channel_id=1, source_target_pairs={{0,1},{1,0},{2,3},{3,2},{4,5},{5,4},{6,7},{7,6},{8,9},{9,8},{10,11... | collective-permute-start | bytes 786440 | tf_op jit(solution)/shard_map/ppermute | solution.py:26
  7.4 10.8 %collective-permute-start.8 = (f32[4,32,512]{2,1,0:T(8,128)}, f32[4,32,512]{2,1,0:T(8,128)S(1)}, u32[]{:S(2)}, u32[]{:S(2)}) collective-permute-start(f32[4,32,512]{2,1,0:T(8,128)} %get-tuple-element.39), channel_id=1, source_target_pairs={{0,2},{1,3},{2,0},{3,1},{4,6},{5,7},{6,4},{7,5},{8,10},{9,11},{10,... | collective-permute-start | bytes 786440 | tf_op jit(solution)/shard_map/ppermute | solution.py:26
  8.9 9.9 %collective-permute-start = (f32[128,512]{1,0:T(8,128)S(1)}, f32[128,512]{1,0:T(8,128)S(1)}, u32[]{:S(2)}, u32[]{:S(2)}) collective-permute-start(f32[128,512]{1,0:T(8,128)S(1)} %bitcast.23), channel_id=1, source_target_pairs={{0,16},{8,24},{16,0},{24,8},{1,17},{9,25},{17,1},{25,9},{2,18},{10... | collective-permute-start | bytes 786440 | tf_op jit(solution)/shard_map/ppermute | solution.py:26
  10.5 16.2 %collective-permute-start.1 = (f32[128,512]{1,0:T(8,128)S(1)}, f32[128,512]{1,0:T(8,128)S(1)}, u32[]{:S(2)}, u32[]{:S(2)}) collective-permute-start(f32[128,512]{1,0:T(8,128)S(1)} %bitcast.24), channel_id=1, source_target_pairs={{0,8},{8,0},{16,24},{24,16},{1,9},{9,1},{17,25},{25,17},{2,10},{10... | collective-permute-start | bytes 786440 | tf_op jit(solution)/shard_map/ppermute | solution.py:26
  12.4 2.2 %copy-start = (f32[512,2048]{1,0:T(8,128)S(1)}, f32[512,2048]{1,0:T(8,128)}, u32[]{:S(2)}) copy-start(f32[512,2048]{1,0:T(8,128)} %w_hbm.1) | copy-start | bytes 12582916
  14.6 3.1 %copy-start.9 = (f32[4,32,512]{2,1,0:T(8,128)S(1)}, f32[4,32,512]{2,1,0:T(8,128)}, u32[]{:S(2)}) copy-start(f32[4,32,512]{2,1,0:T(8,128)} %get-tuple-element.36) | copy-start | bytes 786436
  14.6 3.6 %copy-start.8 = (f32[4,32,512]{2,1,0:T(8,128)S(1)}, f32[4,32,512]{2,1,0:T(8,128)}, u32[]{:S(2)}) copy-start(f32[4,32,512]{2,1,0:T(8,128)} %get-tuple-element.38) | copy-start | bytes 786436
  17.6 9.0 %copy-start.6 = (s32[1,4]{1,0:T(1,128)S(1)}, s32[1,4]{1,0:T(1,128)}, u32[]{:S(2)}) copy-start(s32[1,4]{1,0:T(1,128)} %lengths.3) | copy-start | bytes 52
  17.7 6.0 %collective-permute-start.7 = (f32[2,32,512]{2,1,0:T(8,128)S(1)}, f32[2,32,512]{2,1,0:T(8,128)S(1)}, u32[]{:S(2)}, u32[]{:S(2)}) collective-permute-start(f32[2,32,512]{2,1,0:T(8,128)S(1)} %slice_select_fusion.2), channel_id=1, source_target_pairs={{0,2},{1,3},{2,0},{3,1},{4,6},{5,7},{6,4},{7,5},{8,10},{9,11},{10,... | collective-permute-start | bytes 393224 | tf_op jit(solution)/shard_map/ppermute | solution.py:26
  18.2 5.7 %collective-permute-start.9 = (f32[2,32,512]{2,1,0:T(8,128)S(1)}, f32[2,32,512]{2,1,0:T(8,128)S(1)}, u32[]{:S(2)}, u32[]{:S(2)}) collective-permute-start(f32[2,32,512]{2,1,0:T(8,128)S(1)} %slice_select_fusion), channel_id=1, source_target_pairs={{0,1},{1,0},{2,3},{3,2},{4,5},{5,4},{6,7},{7,6},{8,9},{9,8},{10,11... | collective-permute-start | bytes 393224 | tf_op jit(solution)/shard_map/ppermute | solution.py:26
  18.8 7.8 %collective-permute-start.2 = (f32[128,512]{1,0:T(8,128)S(1)}, f32[128,512]{1,0:T(8,128)S(1)}, u32[]{:S(2)}, u32[]{:S(2)}) collective-permute-start(f32[128,512]{1,0:T(8,128)S(1)} %collective-permute-done.refs_1_), channel_id=1, source_target_pairs={{0,8},{8,0},{16,24},{24,16},{1,9},{9,1},{17,25},{25,17},{2,10},{10... | collective-permute-start | bytes 786440 | tf_op jit(solution)/shard_map/ppermute | solution.py:26
  24.0 14.3 %collective-permute-start.10 = (f32[2,2,32,512]{3,2,1,0:T(8,128)S(1)}, f32[2,2,32,512]{3,2,1,0:T(8,128)S(1)}, u32[]{:S(2)}, u32[]{:S(2)}) collective-permute-start(f32[2,2,32,512]{3,2,1,0:T(8,128)S(1)} %pad_maximum_fusion), channel_id=1, source_target_pairs={{0,4},{1,5},{2,6},{3,7},{4,0},{5,1},{6,2},{7,3},{8,12},{9,13},{10,... | collective-permute-start | bytes 786440 | tf_op jit(solution)/shard_map/ppermute | solution.py:26
  31.6 5.2 %copy-start.3 = (f32[512]{0:T(512)S(1)}, f32[512]{0:T(512)}, u32[]{:S(2)}) copy-start(f32[512]{0:T(512)} %param.12) | copy-start | bytes 6148
  31.7 5.2 %copy-start.4 = (s32[1,128]{1,0:T(1,128)S(1)}, s32[1,128]{1,0:T(1,128)}, u32[]{:S(2)}) copy-start(s32[1,128]{1,0:T(1,128)} %refs_7_.1) | copy-start | bytes 1540
  37.4 7.8 %collective-permute-start.3 = (f32[136,512]{1,0:T(8,128)S(1)}, f32[136,512]{1,0:T(8,128)S(1)}, u32[]{:S(2)}, u32[]{:S(2)}) collective-permute-start(f32[136,512]{1,0:T(8,128)S(1)} %project.1.refs_0_), channel_id=1, source_target_pairs={{0,16},{8,24},{16,0},{24,8},{1,17},{9,25},{17,1},{25,9},{2,18},{10... | collective-permute-start | bytes 835592 | tf_op jit(solution)/shard_map/ppermute | solution.py:26
  38.3 5.0 %collective-permute-start.11 = (f32[2,32,512]{2,1,0:T(8,128)S(1)}, f32[2,32,512]{2,1,0:T(8,128)S(1)}, u32[]{:S(2)}, u32[]{:S(2)}) collective-permute-start(f32[2,32,512]{2,1,0:T(8,128)S(1)} %maximum_select_fusion), channel_id=1, source_target_pairs={{0,2},{1,3},{2,0},{3,1},{4,6},{5,7},{6,4},{7,5},{8,10},{9,11},{10,... | collective-permute-start | bytes 393224 | tf_op jit(solution)/shard_map/ppermute | solution.py:26
  39.7 5.6 %collective-permute-start.13 = (f32[2,32,512]{2,1,0:T(8,128)S(1)}, f32[2,32,512]{2,1,0:T(8,128)S(1)}, u32[]{:S(2)}, u32[]{:S(2)}) collective-permute-start(f32[2,32,512]{2,1,0:T(8,128)S(1)} %maximum_select_fusion.1), channel_id=1, source_target_pairs={{0,1},{1,0},{2,3},{3,2},{4,5},{5,4},{6,7},{7,6},{8,9},{9,8},{10,11... | collective-permute-start | bytes 393224 | tf_op jit(solution)/shard_map/ppermute | solution.py:26
  40.3 6.5 %collective-permute-start.4 = (f32[136,512]{1,0:T(8,128)S(1)}, f32[136,512]{1,0:T(8,128)S(1)}, u32[]{:S(2)}, u32[]{:S(2)}) collective-permute-start(f32[136,512]{1,0:T(8,128)S(1)} %project.1.refs_0_), channel_id=1, source_target_pairs={{0,8},{8,0},{16,24},{24,16},{1,9},{9,1},{17,25},{25,17},{2,10},{10... | collective-permute-start | bytes 835592 | tf_op jit(solution)/shard_map/ppermute | solution.py:26
  43.4 7.0 %collective-permute-start.12 = (f32[4,32,512]{2,1,0:T(8,128)S(1)}, f32[4,32,512]{2,1,0:T(8,128)S(1)}, u32[]{:S(2)}, u32[]{:S(2)}) collective-permute-start(f32[4,32,512]{2,1,0:T(8,128)S(1)} %pad_maximum_fusion.1), channel_id=1, source_target_pairs={{0,1},{1,0},{2,3},{3,2},{4,5},{5,4},{6,7},{7,6},{8,9},{9,8},{10,11... | collective-permute-start | bytes 786440 | tf_op jit(solution)/shard_map/ppermute | solution.py:26
  45.3 8.8 %collective-permute-start.5 = (f32[136,512]{1,0:T(8,128)S(1)}, f32[136,512]{1,0:T(8,128)S(1)}, u32[]{:S(2)}, u32[]{:S(2)}) collective-permute-start(f32[136,512]{1,0:T(8,128)S(1)} %collective-permute-done.3.refs_1_), channel_id=1, source_target_pairs={{0,8},{8,0},{16,24},{24,16},{1,9},{9,1},{17,25},{25,17},{2,10},{10... | collective-permute-start | bytes 835592 | tf_op jit(solution)/shard_map/ppermute | solution.py:26
  45.3 8.8 %collective-permute-start.14 = (f32[4,32,512]{2,1,0:T(8,128)S(1)}, f32[4,32,512]{2,1,0:T(8,128)S(1)}, u32[]{:S(2)}, u32[]{:S(2)}) collective-permute-start(f32[4,32,512]{2,1,0:T(8,128)S(1)} %pad_maximum_fusion.2), channel_id=1, source_target_pairs={{0,2},{1,3},{2,0},{3,1},{4,6},{5,7},{6,4},{7,5},{8,10},{9,11},{10,... | collective-permute-start | bytes 786440 | tf_op jit(solution)/shard_map/ppermute | solution.py:26
  58.7 8.0 %collective-permute-start.17 = (f32[4,32,512]{2,1,0:T(8,128)S(1)}, f32[4,32,512]{2,1,0:T(8,128)S(1)}, u32[]{:S(2)}, u32[]{:S(2)}) collective-permute-start(f32[4,32,512]{2,1,0:T(8,128)S(1)} %get-tuple-element.43), channel_id=1, source_target_pairs={{0,2},{1,3},{2,0},{3,1},{4,6},{5,7},{6,4},{7,5},{8,10},{9,11},{10,... | collective-permute-start | bytes 786440 | tf_op jit(solution)/shard_map/ppermute | solution.py:26
  60.3 10.1 %collective-permute-start.15 = (f32[4,40,512]{2,1,0:T(8,128)S(1)}, f32[4,40,512]{2,1,0:T(8,128)S(1)}, u32[]{:S(2)}, u32[]{:S(2)}) collective-permute-start(f32[4,40,512]{2,1,0:T(8,128)S(1)} %get-tuple-element.41), channel_id=1, source_target_pairs={{0,1},{1,0},{2,3},{3,2},{4,5},{5,4},{6,7},{7,6},{8,9},{9,8},{10,11... | collective-permute-start | bytes 983048 | tf_op jit(solution)/shard_map/ppermute | solution.py:26
  60.8 18.3 %collective-permute-start.20 = (f32[2,128,512]{2,1,0:T(8,128)S(1)}, f32[2,128,512]{2,1,0:T(8,128)S(1)}, u32[]{:S(2)}, u32[]{:S(2)}) collective-permute-start(f32[2,128,512]{2,1,0:T(8,128)S(1)} %get-tuple-element.45), channel_id=1, source_target_pairs={{0,8},{8,0},{16,24},{24,16},{1,9},{9,1},{17,25},{25,17},{2,10},{10... | collective-permute-start | bytes 1572872 | tf_op jit(solution)/shard_map/ppermute | solution.py:26
  66.8 5.4 %collective-permute-start.18 = (f32[2,32,512]{2,1,0:T(8,128)S(1)}, f32[2,32,512]{2,1,0:T(8,128)S(1)}, u32[]{:S(2)}, u32[]{:S(2)}) collective-permute-start(f32[2,32,512]{2,1,0:T(8,128)S(1)} %get-tuple-element.60), channel_id=1, source_target_pairs={{0,1},{1,0},{2,3},{3,2},{4,5},{5,4},{6,7},{7,6},{8,9},{9,8},{10,11... | collective-permute-start | bytes 393224 | tf_op jit(solution)/shard_map/ppermute | solution.py:26
  70.4 21.0 %copy-start.5 = (s32[4,512]{1,0:T(4,128)S(1)}, s32[4,512]{1,0:T(4,128)}, u32[]{:S(2)}) copy-start(s32[4,512]{1,0:T(4,128)} %ids.1) | copy-start | bytes 24580
  70.4 5.4 %collective-permute-start.16 = (f32[2,40,512]{2,1,0:T(8,128)S(1)}, f32[2,40,512]{2,1,0:T(8,128)S(1)}, u32[]{:S(2)}, u32[]{:S(2)}) collective-permute-start(f32[2,40,512]{2,1,0:T(8,128)S(1)} %get-tuple-element.58), channel_id=1, source_target_pairs={{0,2},{1,3},{2,0},{3,1},{4,6},{5,7},{6,4},{7,5},{8,10},{9,11},{10,... | collective-permute-start | bytes 491528 | tf_op jit(solution)/shard_map/ppermute | solution.py:26
  75.8 7.1 %collective-permute-start.19 = (f32[1,72,512]{2,1,0:T(8,128)S(1)}, f32[1,72,512]{2,1,0:T(8,128)S(1)}, u32[]{:S(2)}, u32[]{:S(2)}) collective-permute-start(f32[1,72,512]{2,1,0:T(8,128)S(1)} %pad_maximum_fusion.3), channel_id=1, source_target_pairs={{0,4},{1,5},{2,6},{3,7},{4,0},{5,1},{6,2},{7,3},{8,12},{9,13},{10,... | collective-permute-start | bytes 442376 | tf_op jit(solution)/shard_map/ppermute | solution.py:26
  79.2 6.8 %collective-permute-start.21 = (f32[1,128,512]{2,1,0:T(8,128)S(1)}, f32[1,128,512]{2,1,0:T(8,128)S(1)}, u32[]{:S(2)}, u32[]{:S(2)}) collective-permute-start(f32[1,128,512]{2,1,0:T(8,128)S(1)} %slice_add_fusion), channel_id=1, source_target_pairs={{0,16},{8,24},{16,0},{24,8},{1,17},{9,25},{17,1},{25,9},{2,18},{10... | collective-permute-start | bytes 786440 | tf_op jit(solution)/shard_map/ppermute | solution.py:26
  86.8 4.6 %collective-permute-start.22 = (f32[24,512]{1,0:T(8,128)S(1)}, f32[24,512]{1,0:T(8,128)S(1)}, u32[]{:S(2)}, u32[]{:S(2)}) collective-permute-start(f32[24,512]{1,0:T(8,128)S(1)} %get-tuple-element.79), channel_id=1, source_target_pairs={{0,16},{8,24},{16,0},{24,8},{1,17},{9,25},{17,1},{25,9},{2,18},{10... | collective-permute-start | bytes 147464 | tf_op jit(solution)/shard_map/ppermute | solution.py:31
  87.4 4.0 %collective-permute-start.23 = (f32[24,512]{1,0:T(8,128)S(1)}, f32[24,512]{1,0:T(8,128)S(1)}, u32[]{:S(2)}, u32[]{:S(2)}) collective-permute-start(f32[24,512]{1,0:T(8,128)S(1)} %get-tuple-element.80), channel_id=1, source_target_pairs={{0,8},{8,0},{16,24},{24,16},{1,9},{9,1},{17,25},{25,17},{2,10},{10... | collective-permute-start | bytes 147464 | tf_op jit(solution)/shard_map/ppermute | solution.py:31
  87.4 4.0 %collective-permute-start.24 = (f32[24,512]{1,0:T(8,128)S(1)}, f32[24,512]{1,0:T(8,128)S(1)}, u32[]{:S(2)}, u32[]{:S(2)}) collective-permute-start(f32[24,512]{1,0:T(8,128)S(1)} %get-tuple-element.78), channel_id=1, source_target_pairs={{0,24},{8,16},{16,8},{24,0},{1,25},{9,17},{17,9},{25,1},{2,26},{10... | collective-permute-start | bytes 147464 | tf_op jit(solution)/shard_map/ppermute | solution.py:31
  93.4 7.4 %collective-permute-start.25 = (f32[16,1024]{1,0:T(8,128)S(1)}, f32[16,1024]{1,0:T(8,128)S(1)}, u32[]{:S(2)}, u32[]{:S(2)}) collective-permute-start(f32[16,1024]{1,0:T(8,128)S(1)} %get-tuple-element.50), channel_id=1, source_target_pairs={{0,1},{1,0},{2,3},{3,2},{4,5},{5,4},{6,7},{7,6},{8,9},{9,8},{10,11... | collective-permute-start | bytes 196616 | tf_op jit(solution)/shard_map/ppermute | solution.py:31
  95.0 6.0 %collective-permute-start.26 = (f32[16,1024]{1,0:T(8,128)S(1)}, f32[16,1024]{1,0:T(8,128)S(1)}, u32[]{:S(2)}, u32[]{:S(2)}) collective-permute-start(f32[16,1024]{1,0:T(8,128)S(1)} %get-tuple-element.51), channel_id=1, source_target_pairs={{0,2},{1,3},{2,0},{3,1},{4,6},{5,7},{6,4},{7,5},{8,10},{9,11},{10,... | collective-permute-start | bytes 196616 | tf_op jit(solution)/shard_map/ppermute | solution.py:31
  95.0 9.8 %collective-permute-start.27 = (f32[16,1024]{1,0:T(8,128)S(1)}, f32[16,1024]{1,0:T(8,128)S(1)}, u32[]{:S(2)}, u32[]{:S(2)}) collective-permute-start(f32[16,1024]{1,0:T(8,128)S(1)} %get-tuple-element.52), channel_id=1, source_target_pairs={{0,3},{1,2},{2,1},{3,0},{4,7},{5,6},{6,5},{7,4},{8,11},{9,10},{10,... | collective-permute-start | bytes 196616 | tf_op jit(solution)/shard_map/ppermute | solution.py:31
  97.0 8.9 %collective-permute-start.31 = (f32[16,1024]{1,0:T(8,128)S(1)}, f32[16,1024]{1,0:T(8,128)S(1)}, u32[]{:S(2)}, u32[]{:S(2)}) collective-permute-start(f32[16,1024]{1,0:T(8,128)S(1)} %get-tuple-element.53), channel_id=1, source_target_pairs={{0,4},{1,5},{2,6},{3,7},{4,0},{5,1},{6,2},{7,3},{8,12},{9,13},{10,... | collective-permute-start | bytes 196616 | tf_op jit(solution)/shard_map/ppermute | solution.py:31
  97.3 11.8 %collective-permute-start.32 = (f32[16,1024]{1,0:T(8,128)S(1)}, f32[16,1024]{1,0:T(8,128)S(1)}, u32[]{:S(2)}, u32[]{:S(2)}) collective-permute-start(f32[16,1024]{1,0:T(8,128)S(1)} %get-tuple-element.54), channel_id=1, source_target_pairs={{0,5},{1,4},{2,7},{3,6},{4,1},{5,0},{6,3},{7,2},{8,13},{9,12},{10,... | collective-permute-start | bytes 196616 | tf_op jit(solution)/shard_map/ppermute | solution.py:31
  100.8 8.3 %collective-permute-start.33 = (f32[16,1024]{1,0:T(8,128)S(1)}, f32[16,1024]{1,0:T(8,128)S(1)}, u32[]{:S(2)}, u32[]{:S(2)}) collective-permute-start(f32[16,1024]{1,0:T(8,128)S(1)} %get-tuple-element.55), channel_id=1, source_target_pairs={{0,6},{1,7},{2,4},{3,5},{4,2},{5,3},{6,0},{7,1},{8,14},{9,15},{10,... | collective-permute-start | bytes 196616 | tf_op jit(solution)/shard_map/ppermute | solution.py:31
  100.9 8.2 %collective-permute-start.34 = (f32[16,1024]{1,0:T(8,128)S(1)}, f32[16,1024]{1,0:T(8,128)S(1)}, u32[]{:S(2)}, u32[]{:S(2)}) collective-permute-start(f32[16,1024]{1,0:T(8,128)S(1)} %get-tuple-element.56), channel_id=1, source_target_pairs={{0,7},{1,6},{2,5},{3,4},{4,3},{5,2},{6,1},{7,0},{8,15},{9,14},{10,... | collective-permute-start | bytes 196616 | tf_op jit(solution)/shard_map/ppermute | solution.py:31
  104.8 6.6 %collective-permute-start.28 = (f32[64,1024]{1,0:T(8,128)S(1)}, f32[64,1024]{1,0:T(8,128)S(1)}, u32[]{:S(2)}, u32[]{:S(2)}) collective-permute-start(f32[64,1024]{1,0:T(8,128)S(1)} %constant_dynamic-update-slice_fusion.refs_0_), channel_id=1, source_target_pairs={{0,16},{8,24},{16,0},{24,8},{1,17},{9,25},{17,1},{25,9},{2,18},{10... | collective-permute-start | bytes 786440 | tf_op jit(solution)/shard_map/ppermute | solution.py:26
  109.2 8.2 %collective-permute-start.35 = (f32[64,1024]{1,0:T(8,128)S(1)}, f32[64,1024]{1,0:T(8,128)S(1)}, u32[]{:S(2)}, u32[]{:S(2)}) collective-permute-start(f32[64,1024]{1,0:T(8,128)S(1)} %constant_dynamic-update-slice_fusion.4.refs_4_), channel_id=1, source_target_pairs={{0,16},{8,24},{16,0},{24,8},{1,17},{9,25},{17,1},{25,9},{2,18},{10... | collective-permute-start | bytes 786440 | tf_op jit(solution)/shard_map/ppermute | solution.py:26
  110.4 8.2 %collective-permute-start.29 = (f32[64,1024]{1,0:T(8,128)S(1)}, f32[64,1024]{1,0:T(8,128)S(1)}, u32[]{:S(2)}, u32[]{:S(2)}) collective-permute-start(f32[64,1024]{1,0:T(8,128)S(1)} %constant_dynamic-update-slice_fusion.refs_0_), channel_id=1, source_target_pairs={{0,8},{8,0},{16,24},{24,16},{1,9},{9,1},{17,25},{25,17},{2,10},{10... | collective-permute-start | bytes 786440 | tf_op jit(solution)/shard_map/ppermute | solution.py:26
  110.4 8.2 %collective-permute-start.36 = (f32[64,1024]{1,0:T(8,128)S(1)}, f32[64,1024]{1,0:T(8,128)S(1)}, u32[]{:S(2)}, u32[]{:S(2)}) collective-permute-start(f32[64,1024]{1,0:T(8,128)S(1)} %constant_dynamic-update-slice_fusion.4.refs_4_), channel_id=1, source_target_pairs={{0,8},{8,0},{16,24},{24,16},{1,9},{9,1},{17,25},{25,17},{2,10},{10... | collective-permute-start | bytes 786440 | tf_op jit(solution)/shard_map/ppermute | solution.py:26
  111.4 7.1 %collective-permute-start.30 = (f32[64,1024]{1,0:T(8,128)S(1)}, f32[64,1024]{1,0:T(8,128)S(1)}, u32[]{:S(2)}, u32[]{:S(2)}) collective-permute-start(f32[64,1024]{1,0:T(8,128)S(1)} %collective-permute-done.28.refs_1_), channel_id=1, source_target_pairs={{0,8},{8,0},{16,24},{24,16},{1,9},{9,1},{17,25},{25,17},{2,10},{10... | collective-permute-start | bytes 786440 | tf_op jit(solution)/shard_map/ppermute | solution.py:26
  117.4 1.5 %collective-permute-start.37 = (f32[64,1024]{1,0:T(8,128)S(1)}, f32[64,1024]{1,0:T(8,128)S(1)}, u32[]{:S(2)}, u32[]{:S(2)}) collective-permute-start(f32[64,1024]{1,0:T(8,128)S(1)} %collective-permute-done.35.refs_5_), channel_id=1, source_target_pairs={{0,8},{8,0},{16,24},{24,16},{1,9},{9,1},{17,25},{25,17},{2,10},{10... | collective-permute-start | bytes 786440 | tf_op jit(solution)/shard_map/ppermute | solution.py:26

commit v5 on v4

--- a/solution.py
+++ b/solution.py
@@ -18,6 +18,7 @@
 high = lax.Precision.HIGH
 NN, NT = ((1,), (0,)), ((1,), (1,))
 params = pltpu.CompilerParams(vmem_limit_bytes=40 * 2**20)
+almost = pltpu.CompilerParams(vmem_limit_bytes=55 * 2**20)
 alone = pltpu.CompilerParams(vmem_limit_bytes=62 * 2**20)
 
 
@@ -143,37 +144,35 @@
     )(ids, table)
 
 
-def prepare_kernel(x_ref, w_hbm, wo_hbm, gates_ref, queries_ref, vk_hi, vk_lo, wo_hi, wo_lo, w_buf, wo_buf, w_sems, wo_sem):
-    n = w_buf.shape[0]
-    copies = [
-        [
-            pltpu.make_async_copy(
-                w_hbm.at[:, pl.ds((part * n + j) * LANES, LANES)], w_buf.at[j, part], w_sems.at[j, part]
-            )
-            for part in range(4)
-        ]
-        for j in range(n)
-    ]
-    last = pltpu.make_async_copy(wo_hbm, wo_buf, wo_sem)
-    for copy in sum(copies, []) + [last]:
+def prepare_kernel(x_ref, w_hbm, wo_hbm, gates_ref, queries_ref, vk_hi, vk_lo, wo_hi, wo_lo, w_buf, wo_buf, sems):
+    n, depth, _ = w_buf.shape
+    width = x_ref.shape[1]
+    copies = [pltpu.make_async_copy(w_hbm.at[pl.ds(k * depth, depth)], w_buf.at[k], sems.at[k]) for k in range(n)]
+    copies.append(pltpu.make_async_copy(wo_hbm, wo_buf, sems.at[n]))
+    for copy in copies:
         copy.start()
     x = split(x_ref[...])
-    for j in range(n):
-        for copy in copies[j]:
-            copy.wait()
-        span = pl.ds(j * LANES, LANES)
-        uq = split(jnp.concatenate([w_buf[j, 0], w_buf[j, 2]], axis=1))
-        both = silu(dot3(x, uq, NN))
-        gates_ref[:, span] = both[:, :LANES]
-        queries_ref[:, span] = both[:, LANES:]
-        vk_hi[j], vk_lo[j] = split(jnp.concatenate([w_buf[j, 1], w_buf[j, 3]], axis=1))
-    last.wait()
+    gates = queries = 0.0
+    for k in range(n):
+        copies[k].wait()
+        span = pl.ds(k * depth, depth)
+        mine = x[0][:, k * depth : (k + 1) * depth], x[1][:, k * depth : (k + 1) * depth]
+        w = w_buf[k]
+        gates = gates + dot3(mine, split(w[:, :width]), NN)
+        queries = queries + dot3(mine, split(w[:, 2 * width : 3 * width]), NN)
+        for j in range(width // LANES):
+            v = w[:, width + j * LANES : width + (j + 1) * LANES]
+            key = w[:, 3 * width + j * LANES : 3 * width + (j + 1) * LANES]
+            vk_hi[j, span], vk_lo[j, span] = split(jnp.concatenate([v, key], axis=1))
+    gates_ref[...] = silu(gates)
+    queries_ref[...] = silu(queries)
+    copies[n].wait()
     wo_hi[...], wo_lo[...] = split(wo_buf[...])
 
 
 def prepare(rows_in, w_uvqk, w_out):
     tok, width = rows_in.shape
-    n = width // LANES
+    n, depth = width // LANES, 256
     hbm, vmem = pl.BlockSpec(memory_space=pltpu.HBM), pl.BlockSpec(memory_space=pltpu.VMEM)
     return pl.pallas_call(
         prepare_kernel,
@@ -183,12 +182,11 @@
         + [jax.ShapeDtypeStruct((n, width, 2 * LANES), bf16)] * 2
         + [jax.ShapeDtypeStruct((width, width), bf16)] * 2,
         scratch_shapes=[
-            pltpu.VMEM((n, 4, width, LANES), f32),
+            pltpu.VMEM((width // depth, depth, w_uvqk.shape[1]), f32),
             pltpu.VMEM((width, width), f32),
-            pltpu.SemaphoreType.DMA((n, 4)),
-            pltpu.SemaphoreType.DMA,
+            pltpu.SemaphoreType.DMA((width // depth + 1,)),
         ],
-        compiler_params=params,
+        compiler_params=almost,
         cost_estimate=pl.CostEstimate(flops=8 * tok * width * width, bytes_accessed=6 * width * width * 4, transcendentals=0),
         name="prepare",
     )(rows_in, w_uvqk, w_out)
@@ -299,8 +297,8 @@
     n_seq, n_item, seq_order, item_orders, aligned = plan
     o_refs, refs = refs[:n_seq], refs[n_seq:]
     n_refs, refs = refs[: 4 if aligned else 1], refs[4 if aligned else 1 :]
-    n_out = 4 if aligned else 2
-    panel_refs, (kept_rows, sent_rows, n_hi, n_lo, o_hi, o_lo, g_hi, g_lo, panel) = refs[:n_out], refs[n_out:]
+    n_out = 4 if aligned else 1
+    panel_refs, (kept_rows, sent_rows, loss_ref, n_hi, n_lo, o_hi, o_lo, g_hi, g_lo, panel) = refs[:n_out], refs[n_out:]
     me, item = lax.axis_index("seq"), lax.axis_index("item")
     n_neg, width = n_hi.shape
     tok = o_refs[0].shape[0] - EXTRA
@@ -341,11 +339,10 @@
             n = 2 * p + k
             target_ref = kept_rows if n < n_seq // 2 else sent_rows
             target_ref[n % (n_seq // 2)] = rows[k * tok : (k + 1) * tok]
-    loss = jnp.full((EXTRA, n_neg), jnp.sum(loss))
+    loss_ref[...] = jnp.full((EXTRA, LANES), jnp.sum(loss))
     whole = dot3((o_hi[...], o_lo[...]), (g_hi[...], g_lo[...]), NT)
     if not aligned:
         panel_refs[0][...] = whole
-        panel_refs[1][...] = loss
         return
     panel[...] = whole
     n_dim = width // (n_seq * n_item)
@@ -357,8 +354,6 @@
             for n, q in enumerate(seq_order):
                 first = (me ^ q) * (n_item * n_dim) + (item ^ r) * n_dim + half * part
                 out[k, n * part : (n + 1) * part] = panel[pl.ds(pl.multiple_of(first, part), part)]
-            if half == 0:
-                out[k, n_seq * part :] = loss
 
 
 def loss_terms(outputs, negatives, plan, n_neg):
@@ -368,11 +363,11 @@
     vmem = pl.BlockSpec(memory_space=pltpu.VMEM)
     if aligned:
         part = width // (2 * n_item)
-        panel = [jax.ShapeDtypeStruct((n_item // 2, part + e, n_neg), f32) for e in (EXTRA, EXTRA, 0, 0)]
+        panel = [jax.ShapeDtypeStruct((n_item // 2, part, n_neg), f32)] * 4
     else:
-        panel = [jax.ShapeDtypeStruct((width, n_neg), f32), jax.ShapeDtypeStruct((EXTRA, n_neg), f32)]
+        panel = [jax.ShapeDtypeStruct((width, n_neg), f32)]
     rows = [jax.ShapeDtypeStruct((n_seq // 2, tok, width), f32)] * 2
-    out_shape = panel + rows
+    out_shape = panel + rows + [jax.ShapeDtypeStruct((EXTRA, LANES), f32)]
     return pl.pallas_call(
         functools.partial(loss_kernel, plan),
         in_specs=[vmem] * (n_seq + len(negatives)),
@@ -388,69 +383,83 @@
     )(*outputs, *negatives)
 
 
-def spread_kernel(order, per_panel, n_item, owner, ids, *refs):
-    moved, (*outs, loss_ref) = refs[: len(order)], refs[len(order) :]
-    n_dim, n_rows = outs[0].shape
-    n_neg = ids.shape[1]
+def spread_kernel(order, per_panel, n_item, owner, ids, loss, *refs):
+    moved, outs = refs[: len(order)], refs[len(order) :]
+    n_dim, n_neg = moved[0].shape
+    n_tiles = (outs[0].shape[0] - EXTRA) // n_dim
     me, item = lax.axis_index("seq"), lax.axis_index("item")
-    row = lax.broadcasted_iota(i32, (n_rows, n_neg), 0)
+    row = lax.broadcasted_iota(i32, (n_tiles * LANES, n_neg), 0)
     spread, owners = [], []
     for p, r in enumerate(order):
         source = me ^ r
         owners.append(owner[source // per_panel])
         hot = jnp.where(row == ids[pl.ds(source, 1), :], 1.0, 0.0).astype(bf16)
-        both = dot(jnp.concatenate(split(moved[p][:n_dim]), axis=0), hot, NT)
+        both = dot(jnp.concatenate(split(moved[p][...]), axis=0), hot, NT)
         spread.append(both[:n_dim] + both[n_dim:])
     for r in range(n_item):
         total = jnp.where(owners[0] == item ^ r, spread[0], 0.0)
         for p in range(1, len(order)):
             total = total + jnp.where(owners[p] == item ^ r, spread[p], 0.0)
-        outs[r][...] = total
-    loss_ref[...] = sum(m[n_dim:, :LANES] for m in moved)
-
-
-def spread_rows(order, per_panel, owner, moved, ids, n_item, n_rows):
+        for c in range(n_tiles):
+            outs[r][c * n_dim : (c + 1) * n_dim] = total[:, c * LANES : (c + 1) * LANES]
+        outs[r][n_tiles * n_dim :] = loss[...]
+
+
+def spread_rows(order, per_panel, owner, moved, ids, loss, n_item, n_rows):
     vmem = pl.BlockSpec(memory_space=pltpu.VMEM)
     smem = pl.BlockSpec(memory_space=pltpu.SMEM)
-    n_dim = moved[0].shape[0] - EXTRA
+    n_dim = moved[0].shape[0]
+    out = jax.ShapeDtypeStruct((n_rows // LANES * n_dim + EXTRA, LANES), f32)
     return pl.pallas_call(
         functools.partial(spread_kernel, order, per_panel, n_item),
-        in_specs=[smem, vmem] + [vmem] * len(moved),
-        out_specs=[vmem] * (n_item + 1),
-        out_shape=[jax.ShapeDtypeStruct((n_dim, n_rows), f32)] * n_item + [jax.ShapeDtypeStruct((EXTRA, LANES), f32)],
+        in_specs=[smem, vmem, vmem] + [vmem] * len(moved),
+        out_specs=[vmem] * n_item,
+        out_shape=[out] * n_item,
         compiler_params=params,
         cost_estimate=pl.CostEstimate(flops=4 * len(moved) * moved[0].size * n_rows, bytes_accessed=2**21, transcendentals=0),
         name="spread_rows",
-    )(owner, ids, *moved)
-
-
-def assemble_kernel(order, n_item, *refs):
+    )(owner, ids, loss, *moved)
+
+
+def assemble_kernel(order, n_item, n_dim, events, *refs):
+    groups, (out_ref, loss_ref, quarter) = refs[:-3], refs[-3:]
     n_seq = len(order)
-    near, far, (out_ref, quarter) = refs[:n_seq], refs[n_seq : 2 * n_seq], refs[2 * n_seq :]
     me, item = lax.axis_index("seq"), lax.axis_index("item")
-    cols = quarter.shape[0]
-    part = cols // n_item
-    for k, q in enumerate(order):
-        for r in range(n_item):
-            source = near[k] if r < n_item // 2 else far[k]
-            rows = source[pl.ds(r % (n_item // 2) * part, part)]
-            quarter[pl.ds(pl.multiple_of((item ^ r) * part, part), part)] = rows
-        out_ref[:, pl.ds(pl.multiple_of((me ^ q) * cols, cols), cols)] = quarter[...].T
-
-
-def assemble(table, order, n_item):
-    half, n_rows = table[0][0].shape
-    cols = 2 * half
-    width = cols * len(order)
+    cols = n_item * n_dim
+    n_tiles = out_ref.shape[0] // LANES
+    block = pl.program_id(0)
+
+    def places(k):
+        return [(groups[g], m) for g in range(k, len(groups), n_seq) for m in range(groups[g].shape[0])]
+
+    for c in range(n_tiles):
+        rows = pl.ds(pl.multiple_of((block * n_tiles + c) * n_dim, n_dim), n_dim)
+        for k, q in enumerate(order):
+            for r, (group, m) in enumerate(places(k)):
+                quarter[pl.ds(pl.multiple_of((item ^ r) * n_dim, n_dim), n_dim)] = group[m, rows]
+            place = pl.ds(pl.multiple_of((me ^ q) * cols, cols), cols)
+            out_ref[c * LANES : (c + 1) * LANES, place] = quarter[...].T
+
+    @pl.when(block == 0)
+    def _():
+        total = jnp.zeros((EXTRA, LANES), f32)
+        for k in range(n_seq):
+            for group, m in places(k):
+                total = total + group[m, group.shape[1] - EXTRA :]
+        loss_ref[0, 0] = jnp.sum(total) / (EXTRA * LANES * events)
+
+
+def assemble(table, order, n_item, n_dim, n_rows, events):
+    width = n_item * n_dim * len(order)
     step = min(n_rows, 256)
-    pieces = table[0] + table[1]
+    pieces = sum(table, [])
     return pl.pallas_call(
-        functools.partial(assemble_kernel, order, n_item),
+        functools.partial(assemble_kernel, order, n_item, n_dim, events),
         grid=(n_rows // step,),
-        in_specs=[pl.BlockSpec((half, step), lambda j: (0, j))] * len(pieces),
-        out_specs=pl.BlockSpec((step, width), lambda j: (j, 0)),
-        out_shape=jax.ShapeDtypeStruct((n_rows, width), f32),
-        scratch_shapes=[pltpu.VMEM((cols, step), f32)],
+        in_specs=[pl.BlockSpec(memory_space=pltpu.VMEM)] * len(pieces),
+        out_specs=[pl.BlockSpec((step, width), lambda j: (j, 0)), pl.BlockSpec(memory_space=pltpu.SMEM)],
+        out_shape=[jax.ShapeDtypeStruct((n_rows, width), f32), jax.ShapeDtypeStruct((1, 1), f32)],
+        scratch_shapes=[pltpu.VMEM((n_item * n_dim, LANES), f32)],
         compiler_params=params,
         cost_estimate=pl.CostEstimate(flops=0, bytes_accessed=8 * n_rows * width, transcendentals=0),
         name="assemble",
@@ -542,15 +551,12 @@
     own_outputs = project(block_mask, attended, gates, out_gain[None], wo_hi, wo_lo, rows_in, targets)
     outputs = gather_pieces(own_outputs, "seq", seq_bits)
 
-    *panel, kept_rows, sent_rows = loss_terms(outputs, negatives, plan, n_neg)
+    *panel, kept_rows, sent_rows, loss = loss_terms(outputs, negatives, plan, n_neg)
     if not aligned:
         blocks = panel[0].reshape(n_seq, n_item, 2, n_dim // 2, n_neg).transpose(2, 1, 0, 3, 4)
-        loss = jnp.broadcast_to(panel[1], (n_item, EXTRA, n_neg))
         panel = []
         for half in range(2):
             mine = blocks[half][rel[half]][:, s ^ jnp.array(seq_order, i32)].reshape(n_item, -1, n_neg)
-            if half == 0:
-                mine = jnp.concatenate([mine, loss], axis=1)
             panel += [mine[: n_item // 2], mine[n_item // 2 :]]
     event_grad = reduce_steps(kept_rows, sent_rows, "seq", seq_bits[::-1])
 
@@ -564,41 +570,43 @@
         kept.append(k)
         sent.append(t)
     total = reduce_steps(jnp.concatenate(kept, axis=1), jnp.concatenate(sent, axis=1), "item", shared[::-1])
-    total, event_grad = lax.optimization_barrier((total, event_grad))
     part = n_dim // 2
-    loss = total[n_seq * part : n_seq * part + EXTRA]
-    halves = total[: n_seq * part], total[n_seq * part + EXTRA :]
+    halves = total[: n_seq * part], total[n_seq * part :]
     moved = []
     for k, r in enumerate(seq_order):
-        block = jnp.concatenate([half[k * part : (k + 1) * part] for half in halves] + [loss], axis=0)
+        block = jnp.concatenate([half[k * part : (k + 1) * part] for half in halves], axis=0)
         moved.append(send(block, "seq", r) if r else block)
     if aligned:
-        *sent, loss_total = spread_rows(seq_order, per_panel, panel_owner, moved, ids_by_seq, n_item, n_rows)
+        sent = spread_rows(seq_order, per_panel, panel_owner, moved, ids_by_seq, loss, n_item, n_rows)
     else:
         source = s ^ jnp.array(seq_order, i32)
         ids, owner = ids_by_seq[source], panel_owner[source // per_panel]
         hot = (ids[:, :, None] == jnp.arange(n_rows, dtype=i32)).astype(f32)
-        moved = jnp.stack(moved)
-        loss_total = jnp.sum(moved[:, n_dim:], axis=0)
-        spread = jnp.einsum("pdc,pcr->pdr", moved[:, :n_dim], hot, precision=high)
+        spread = jnp.einsum("pdc,pcr->pdr", jnp.stack(moved), hot, precision=high)
         mine = (owner[None, :] == (i ^ jnp.arange(n_item, dtype=i32))[:, None]).astype(f32)
         sent = jnp.sum(mine[:, :, None, None] * spread[None], axis=1)
-        sent = [sent[r] for r in range(n_item)]
-
-    taken = {r: send(sent[r], "item", r) if r else sent[r] for r in list(range(n_item // 2, n_item)) + list(range(n_item // 2))}
+        sent = sent.reshape(n_item, n_dim, -1, LANES).transpose(0, 2, 1, 3).reshape(n_item, -1, LANES)
+        sent = [jnp.concatenate([sent[r], loss], axis=0) for r in range(n_item)]
+
+    taken = [send(sent[r], "item", r) if r else sent[r] for r in range(n_item)]
+    cuts = [0, n_item // 2, 3 * n_item // 4, n_item]
     table = []
-    for first in (0, n_item // 2):
-        group = jnp.concatenate([taken[r] for r in range(first, first + n_item // 2)], axis=0)
+    for first, end in zip(cuts, cuts[1:]):
+        group = jnp.stack(taken[first:end])
+        if first == 0:
+            group, event_grad = lax.optimization_barrier((group, event_grad))
         table.append([group, swap(group, "seq", seq_bits[0])])
     for bit in seq_bits[1:]:
         table = [group + [swap(piece, "seq", bit) for piece in group] for group in table]
     if aligned:
-        table_grad = assemble(table, seq_order, n_item)
+        table_grad, mean_loss = assemble(table, seq_order, n_item, n_dim, n_rows, group_len * n_item)
+        mean_loss = mean_loss.reshape(())
     else:
-        table = jnp.stack([jnp.concatenate([near, far], axis=0) for near, far in zip(*table)])
-        table = table.reshape(n_seq, n_item, n_dim, n_rows)[:, i ^ jnp.arange(n_item, dtype=i32)]
-        table_grad = true_order(table, seq_order, s).reshape(width, n_rows).T
-    return (loss_total[0, 0] / (group_len * n_item), event_grad[None], table_grad)
+        table = jnp.stack([jnp.concatenate(groups, axis=0) for groups in zip(*table)])
+        mean_loss = jnp.sum(table[:, :, -1, 0]) / (group_len * n_item)
+        table = table[:, :, :-EXTRA].reshape(n_seq, n_item, -1, n_dim, LANES)[:, i ^ jnp.arange(n_item, dtype=i32)]
+        table_grad = true_order(table, seq_order, s).transpose(2, 4, 0, 1, 3).reshape(n_rows, width)
+    return (mean_loss, event_grad[None], table_grad)
 
 
 def solution(mesh):

time: 123 us -> 115 us (0.935)
  waiting for transfers between devices: 49.6 us -> 44.8 us
  Pallas kernels: 26.6 us -> 29.1 us
  starting transfers between devices: 37.7 us -> 35.6 us
  local copies, waits for them, and re-layouts: 3.41 us -> 1.64 us
  between operations: 4.13 us -> 2.37 us
    ppermute x28 -> x31, waiting for transfers between devices: 43.9 us -> 38.8 us  [swap(): return lax.ppermute(block, axis, [(i, i ^ 1 << bit) for i in range(size)])]
    ppermute x10, starting transfers between devices: 13.5 us -> 10.7 us  [send(): return lax.ppermute(block, axis, [(i, i ^ r) for i in range(size)])]
    pallas_call x1, Pallas kernels: 3.04 us -> 5.82 us  [prepare(): pl.pallas_call(prepare_kernel, in_specs=[vmem, hbm, hbm], out_specs=[vmem...]
    unnamed x26 -> x32, local copies, waits for them, and re-layouts: 2.27 us -> 1.02 us
    ppermute x28 -> x31, starting transfers between devices: 24.2 us -> 24.9 us  [swap(): return lax.ppermute(block, axis, [(i, i ^ 1 << bit) for i in range(size)])]
  transfers between devices with their start and end apart: 38 -> 41, of which waited for: 18 -> 20; matrix products, arithmetic and copies ran while one was open for 1% -> 2% of each run, Pallas kernels for 11% -> 16%
where the time goes in v5:
time: 115 us
  waiting for transfers between devices  44.8 us (39%)
  starting transfers between devices  35.6 us (31%)
  Pallas kernels  29.1 us (25%)
  between operations  2.37 us (2%)
  local copies, waits for them, and re-layouts  1.64 us (1%)
  other arithmetic  1.19 us (1%)
    ppermute x31, waiting for transfers between devices, swap(): return lax.ppermute(block, axis, [(i, i ^ 1 << bit) for i in range(size)])  38.8 us
    ppermute x31, starting transfers between devices, swap(): return lax.ppermute(block, axis, [(i, i ^ 1 << bit) for i in range(size)])  24.9 us
    ppermute x10, starting transfers between devices, send(): return lax.ppermute(block, axis, [(i, i ^ r) for i in range(size)])  10.7 us
    pallas_call x2, Pallas kernels, attend(): pl.pallas_call(functools.partial(attend_kernel, order, n_seq), grid=(coun...  9.98 us
    ppermute x10, waiting for transfers between devices, send(): return lax.ppermute(block, axis, [(i, i ^ r) for i in range(size)])  6.04 us
    pallas_call x1, Pallas kernels, prepare(): pl.pallas_call(prepare_kernel, in_specs=[vmem, hbm, hbm], out_specs=[vmem...  5.82 us
    pallas_call x1, Pallas kernels, loss_terms(): pl.pallas_call(functools.partial(loss_kernel, plan), in_specs=[vmem] * (n...  4.64 us
    pallas_call x1, Pallas kernels, pick_rows(): pl.pallas_call(functools.partial(pick_kernel, plan), in_specs=[pl.BlockSp...  3.67 us
  transfers between devices with their start and end apart: 41, of which 20 were waited for; matrix products, arithmetic and copies ran while one was open for 2% of the time, Pallas kernels for 16%

profile of v5, /device:TPU:0, one launch (start us, length us, event | category | flops | bytes accessed | tf_op | source)
XLA Modules:
  0.0 114.7 jit_solution(14217843443314791175)
XLA Ops:
  0.6 0.0 copy-start
  0.7 3.7 %pick_rows.1 = (f32[4,32,512]{2,1,0:T(8,128)}, f32[4,32,512]{2,1,0:T(8,128)}, f32[4,32,512]{2,1,0:T(8,128)}, f32[4,32,512]{2,1,0:T(8,128)}) custom-call(s32[4,512]{1,0:T(4,128)} %ids.1, f32[1024,512]{1,0:T(8,128)} %table_hbm.1), custom_call_target="tpu_custom_call" | custom-call | flops 1073741824 | bytes 2097152 | tf_op jit(solution)/shard_map/pick_rows/pallas_call | solution.py:130
  4.3 3.0 %collective-permute-start.6 = (f32[4,32,512]{2,1,0:T(8,128)}, f32[4,32,512]{2,1,0:T(8,128)S(1)}, u32[]{:S(2)}, u32[]{:S(2)}) collective-permute-start(f32[4,32,512]{2,1,0:T(8,128)} %get-tuple-element.39), channel_id=1, source_target_pairs={{0,1},{1,0},{2,3},{3,2},{4,5},{5,4},{6,7},{7,6},{8,9},{9,8},{10,11... | collective-permute-start | bytes 786440 | tf_op jit(solution)/shard_map/ppermute | solution.py:27
  7.3 1.6 %collective-permute-start.8 = (f32[4,32,512]{2,1,0:T(8,128)}, f32[4,32,512]{2,1,0:T(8,128)S(1)}, u32[]{:S(2)}, u32[]{:S(2)}) collective-permute-start(f32[4,32,512]{2,1,0:T(8,128)} %get-tuple-element.41), channel_id=1, source_target_pairs={{0,2},{1,3},{2,0},{3,1},{4,6},{5,7},{6,4},{7,5},{8,10},{9,11},{10,... | collective-permute-start | bytes 786440 | tf_op jit(solution)/shard_map/ppermute | solution.py:27
  8.9 1.5 %collective-permute-start = (f32[128,512]{1,0:T(8,128)S(1)}, f32[128,512]{1,0:T(8,128)S(1)}, u32[]{:S(2)}, u32[]{:S(2)}) collective-permute-start(f32[128,512]{1,0:T(8,128)S(1)} %bitcast.46), channel_id=1, source_target_pairs={{0,16},{8,24},{16,0},{24,8},{1,17},{9,25},{17,1},{25,9},{2,18},{10... | collective-permute-start | bytes 786440 | tf_op jit(solution)/shard_map/ppermute | solution.py:27
  11.1 0.6 dynamic_slice.3
  12.4 5.8 %prepare.1 = (f32[128,512]{1,0:T(8,128)}, f32[128,512]{1,0:T(8,128)}, bf16[4,512,256]{2,1,0:T(8,128)(2,1)}, bf16[4,512,256]{2,1,0:T(8,128)(2,1)}, bf16[512,512]{1,0:T(8,128)(2,1)}, /*index=5*/bf16[512,512]{1,0:T(8,128)(2,1)}) custom-call(f32[128,512]{1,0:T(8,128)} %bitcast.45, f32[512,2048]{1,0:T(8,128)} %w_hbm.1, f32[512,512]{1,0:T(8,128)} %wo_hbm.1), custom_call_target="tpu_custom_call" | custom-call | flops 268435456 | bytes 6291456 | tf_op jit(solution)/shard_map/prepare/pallas_call | solution.py:177
  18.3 0.5 collective-permute-start.7
  18.8 0.6 collective-permute-start.9
  19.4 4.8 %collective-permute-done.7 = f32[2,32,512]{2,1,0:T(8,128)S(1)} collective-permute-done((f32[2,32,512]{2,1,0:T(8,128)S(1)}, f32[2,32,512]{2,1,0:T(8,128)S(1)}, u32[]{:S(2)}, u32[]{:S(2)}) %collective-permute-start.7) | collective-permute-done | bytes 131104 | tf_op jit(solution)/shard_map/ppermute | solution.py:27
  24.3 0.2 collective-permute-done.9
  24.6 2.7 %collective-permute-start.10 = (f32[2,2,32,512]{3,2,1,0:T(8,128)S(1)}, f32[2,2,32,512]{3,2,1,0:T(8,128)S(1)}, u32[]{:S(2)}, u32[]{:S(2)}) collective-permute-start(f32[2,2,32,512]{3,2,1,0:T(8,128)S(1)} %pad_maximum_fusion.1), channel_id=1, source_target_pairs={{0,4},{1,5},{2,6},{3,7},{4,0},{5,1},{6,2},{7,3},{8,12},{9,13},{10,... | collective-permute-start | bytes 786440 | tf_op jit(solution)/shard_map/ppermute | solution.py:27
  27.3 0.9 copy-done.9
  28.2 5.0 %attend.2.refs_0_ = f32[128,256]{1,0:T(8,128)S(1)} custom-call(s32[1,4]{1,0:T(1,128)S(1)} %copy-done.12, f32[128,512]{1,0:T(8,128)S(1)} %bitcast.48, f32[128,512]{1,0:T(8,128)S(1)} %collective-permute-done.refs_1_, f32[128,512]{1,0:T(8,128)S(1)} %collective-permute-done.1.refs_2_, f32[128,512]{1,0:T(8,128)S(1)} %collective-permute-done.2.refs_3_, ...), custom_call_target="tpu_custom_call" | custom-call | flops 4000000000 | bytes 2097152 | tf_op jit(solution)/shard_map/attend/pallas_call | solution.py:249
  33.3 5.0 %attend.3.refs_1_ = f32[128,256]{1,0:T(8,128)S(1)} custom-call(s32[1,4]{1,0:T(1,128)S(1)} %copy-done.12, f32[128,512]{1,0:T(8,128)S(1)} %bitcast.49, f32[128,512]{1,0:T(8,128)S(1)} %collective-permute-done.refs_1_, f32[128,512]{1,0:T(8,128)S(1)} %collective-permute-done.1.refs_2_, f32[128,512]{1,0:T(8,128)S(1)} %collective-permute-done.2.refs_3_, ...), custom_call_target="tpu_custom_call" | custom-call | flops 4000000000 | bytes 2097152 | tf_op jit(solution)/shard_map/attend/pallas_call | solution.py:249
  38.4 0.5 project.1.refs_0_
  38.9 0.6 collective-permute-start.3
  39.5 1.6 %collective-permute-start.11 = (f32[2,32,512]{2,1,0:T(8,128)S(1)}, f32[2,32,512]{2,1,0:T(8,128)S(1)}, u32[]{:S(2)}, u32[]{:S(2)}) collective-permute-start(f32[2,32,512]{2,1,0:T(8,128)S(1)} %maximum_select_fusion), channel_id=1, source_target_pairs={{0,2},{1,3},{2,0},{3,1},{4,6},{5,7},{6,4},{7,5},{8,10},{9,11},{10,... | collective-permute-start | bytes 393224 | tf_op jit(solution)/shard_map/ppermute | solution.py:27
  41.2 0.6 collective-permute-start.13
  41.8 2.8 %collective-permute-done.11 = f32[2,32,512]{2,1,0:T(8,128)S(1)} collective-permute-done((f32[2,32,512]{2,1,0:T(8,128)S(1)}, f32[2,32,512]{2,1,0:T(8,128)S(1)}, u32[]{:S(2)}, u32[]{:S(2)}) %collective-permute-start.11) | collective-permute-done | bytes 131104 | tf_op jit(solution)/shard_map/ppermute | solution.py:27
  44.6 0.6 collective-permute-start.12
  45.2 1.6 %collective-permute-done.3.refs_1_ = f32[136,512]{1,0:T(8,128)S(1)} collective-permute-done((f32[136,512]{1,0:T(8,128)S(1)}, f32[136,512]{1,0:T(8,128)S(1)}, u32[]{:S(2)}, u32[]{:S(2)}) %collective-permute-start.3) | collective-permute-done | bytes 278560 | tf_op jit(solution)/shard_map/ppermute | solution.py:27
  46.8 0.7 collective-permute-done.13
  47.4 0.9 collective-permute-start.14
  48.3 3.5 %collective-permute-done.12 = f32[4,32,512]{2,1,0:T(8,128)S(1)} collective-permute-done((f32[4,32,512]{2,1,0:T(8,128)S(1)}, f32[4,32,512]{2,1,0:T(8,128)S(1)}, u32[]{:S(2)}, u32[]{:S(2)}) %collective-permute-start.12) | collective-permute-done | bytes 262176 | tf_op jit(solution)/shard_map/ppermute | solution.py:27
  51.8 3.7 %collective-permute-done.14 = f32[4,32,512]{2,1,0:T(8,128)S(1)} collective-permute-done((f32[4,32,512]{2,1,0:T(8,128)S(1)}, f32[4,32,512]{2,1,0:T(8,128)S(1)}, u32[]{:S(2)}, u32[]{:S(2)}) %collective-permute-start.14) | collective-permute-done | bytes 262176 | tf_op jit(solution)/shard_map/ppermute | solution.py:27
  55.6 4.6 %loss_terms.1 = (f32[4,32,512]{2,1,0:T(8,128)S(1)}, f32[4,32,512]{2,1,0:T(8,128)S(1)}, f32[4,32,512]{2,1,0:T(8,128)S(1)}, f32[4,32,512]{2,1,0:T(8,128)S(1)}, f32...) custom-call(f32[136,512]{1,0:T(8,128)S(1)} %project.1.refs_0_, ...), custom_call_target="tpu_custom_call" | custom-call | flops 2415919104 | bytes 4194304 | tf_op jit(solution)/shard_map/loss_terms/pallas_call | solution.py:371
  60.2 1.5 %collective-permute-start.17 = (f32[4,32,512]{2,1,0:T(8,128)S(1)}, f32[4,32,512]{2,1,0:T(8,128)S(1)}, u32[]{:S(2)}, u32[]{:S(2)}) collective-permute-start(f32[4,32,512]{2,1,0:T(8,128)S(1)} %get-tuple-element.46), channel_id=1, source_target_pairs={{0,2},{1,3},{2,0},{3,1},{4,6},{5,7},{6,4},{7,5},{8,10},{9,11},{10,... | collective-permute-start | bytes 786440 | tf_op jit(solution)/shard_map/ppermute | solution.py:27
  61.8 0.5 collective-permute-start.15
  62.3 5.7 %collective-permute-done.17 = f32[4,32,512]{2,1,0:T(8,128)S(1)} collective-permute-done((f32[4,32,512]{2,1,0:T(8,128)S(1)}, f32[4,32,512]{2,1,0:T(8,128)S(1)}, u32[]{:S(2)}, u32[]{:S(2)}) %collective-permute-start.17) | collective-permute-done | bytes 262176 | tf_op jit(solution)/shard_map/ppermute | solution.py:27
  68.0 0.9 collective-permute-start.18
  68.9 0.7 collective-permute-done.15
  69.6 0.8 collective-permute-start.16
  70.4 2.6 %collective-permute-done.18 = f32[2,32,512]{2,1,0:T(8,128)S(1)} collective-permute-done((f32[2,32,512]{2,1,0:T(8,128)S(1)}, f32[2,32,512]{2,1,0:T(8,128)S(1)}, u32[]{:S(2)}, u32[]{:S(2)}) %collective-permute-start.18) | collective-permute-done | bytes 131104 | tf_op jit(solution)/shard_map/ppermute | solution.py:27
  73.0 1.6 %collective-permute-done.16 = f32[2,32,512]{2,1,0:T(8,128)S(1)} collective-permute-done((f32[2,32,512]{2,1,0:T(8,128)S(1)}, f32[2,32,512]{2,1,0:T(8,128)S(1)}, u32[]{:S(2)}, u32[]{:S(2)}) %collective-permute-start.16) | collective-permute-done | bytes 131104 | tf_op jit(solution)/shard_map/ppermute | solution.py:27
  74.7 0.9 collective-permute-start.19
  75.6 6.4 %collective-permute-done.19 = f32[1,64,512]{2,1,0:T(8,128)S(1)} collective-permute-done((f32[1,64,512]{2,1,0:T(8,128)S(1)}, f32[1,64,512]{2,1,0:T(8,128)S(1)}, u32[]{:S(2)}, u32[]{:S(2)}) %collective-permute-start.19) | collective-permute-done | bytes 131104 | tf_op jit(solution)/shard_map/ppermute | solution.py:27
  82.1 0.6 collective-permute-start.20
  82.6 1.6 %collective-permute-start.22 = (f32[16,512]{1,0:T(8,128)S(1)}, f32[16,512]{1,0:T(8,128)S(1)}, u32[]{:S(2)}, u32[]{:S(2)}) collective-permute-start(f32[16,512]{1,0:T(8,128)S(1)} %pad_maximum_fusion.10), channel_id=1, source_target_pairs={{0,24},{8,16},{16,8},{24,0},{1,25},{9,17},{17,9},{25,1},{2,26},{10... | collective-permute-start | bytes 98312 | tf_op jit(solution)/shard_map/ppermute | solution.py:32
  84.3 0.6 collective-permute-start.27
  84.9 1.5 %collective-permute-done.20.refs_1_ = f32[16,512]{1,0:T(8,128)S(1)} collective-permute-done((f32[16,512]{1,0:T(8,128)S(1)}, f32[16,512]{1,0:T(8,128)S(1)}, u32[]{:S(2)}, u32[]{:S(2)}) %collective-permute-start.20) | collective-permute-done | bytes 32800 | tf_op jit(solution)/shard_map/ppermute | solution.py:32
  86.4 0.0 collective-permute-done.22.refs_3_
  86.4 2.0 %spread_rows.1 = (f32[136,128]{1,0:T(8,128)S(1)}, f32[136,128]{1,0:T(8,128)S(1)}, f32[136,128]{1,0:T(8,128)S(1)}, f32[136,128]{1,0:T(8,128)S(1)}, f32[136,128]{1...) custom-call(s32[4]{0:T(128)S(1)} %copy-done.13, s32[4,512]{1,0:T(4,128)S(1)} %copy-done.11, ...), custom_call_target="tpu_custom_call" | custom-call | flops 134217728 | bytes 2097152 | tf_op jit(solution)/shard_map/spread_rows/pallas_call | solution.py:413
  88.4 0.5 collective-permute-start.25
  88.8 1.6 %collective-permute-start.24 = (f32[136,128]{1,0:T(8,128)S(1)}, f32[136,128]{1,0:T(8,128)S(1)}, u32[]{:S(2)}, u32[]{:S(2)}) collective-permute-start(f32[136,128]{1,0:T(8,128)S(1)} %get-tuple-element.49), channel_id=1, source_target_pairs={{0,2},{1,3},{2,0},{3,1},{4,6},{5,7},{6,4},{7,5},{8,10},{9,11},{10,... | collective-permute-start | bytes 208904 | tf_op jit(solution)/shard_map/ppermute | solution.py:32
  90.5 1.4 %collective-permute-start.23 = (f32[136,128]{1,0:T(8,128)S(1)}, f32[136,128]{1,0:T(8,128)S(1)}, u32[]{:S(2)}, u32[]{:S(2)}) collective-permute-start(f32[136,128]{1,0:T(8,128)S(1)} %get-tuple-element.48), channel_id=1, source_target_pairs={{0,1},{1,0},{2,3},{3,2},{4,5},{5,4},{6,7},{7,6},{8,9},{9,8},{10,11... | collective-permute-start | bytes 208904 | tf_op jit(solution)/shard_map/ppermute | solution.py:32
  91.9 0.6 collective-permute-start.32
  92.5 1.9 %collective-permute-done.25 = f32[136,128]{1,0:T(8,128)S(1)} collective-permute-done((f32[136,128]{1,0:T(8,128)S(1)}, f32[136,128]{1,0:T(8,128)S(1)}, u32[]{:S(2)}, u32[]{:S(2)}) %collective-permute-start.25) | collective-permute-done | bytes 69664 | tf_op jit(solution)/shard_map/ppermute | solution.py:32
  94.4 0.4 collective-permute-start.31
  94.9 0.3 collective-permute-done.23
  95.2 0.8 fusion.1
  96.0 1.7 %collective-permute-start.28 = (f32[4,136,128]{2,1,0:T(8,128)S(1)}, f32[4,136,128]{2,1,0:T(8,128)S(1)}, u32[]{:S(2)}, u32[]{:S(2)}) collective-permute-start(f32[4,136,128]{2,1,0:T(8,128)S(1)} %pad_maximum_fusion.refs_0_), channel_id=1, source_target_pairs={{0,16},{8,24},{16,0},{24,8},{1,17},{9,25},{17,1},{25,9},{2,18},{10... | collective-permute-start | bytes 835592 | tf_op jit(solution)/shard_map/ppermute | solution.py:27
  97.6 2.0 %collective-permute-start.37 = (f32[136,128]{1,0:T(8,128)S(1)}, f32[136,128]{1,0:T(8,128)S(1)}, u32[]{:S(2)}, u32[]{:S(2)}) collective-permute-start(f32[136,128]{1,0:T(8,128)S(1)} %get-tuple-element.57), channel_id=1, source_target_pairs={{0,7},{1,6},{2,5},{3,4},{4,3},{5,2},{6,1},{7,0},{8,15},{9,14},{10,... | collective-permute-start | bytes 208904 | tf_op jit(solution)/shard_map/ppermute | solution.py:32
  99.6 1.9 %collective-permute-start.36 = (f32[136,128]{1,0:T(8,128)S(1)}, f32[136,128]{1,0:T(8,128)S(1)}, u32[]{:S(2)}, u32[]{:S(2)}) collective-permute-start(f32[136,128]{1,0:T(8,128)S(1)} %get-tuple-element.56), channel_id=1, source_target_pairs={{0,6},{1,7},{2,4},{3,5},{4,2},{5,3},{6,0},{7,1},{8,14},{9,15},{10,... | collective-permute-start | bytes 208904 | tf_op jit(solution)/shard_map/ppermute | solution.py:32
  101.6 1.9 %collective-permute-start.33 = (f32[2,136,128]{2,1,0:T(8,128)S(1)}, f32[2,136,128]{2,1,0:T(8,128)S(1)}, u32[]{:S(2)}, u32[]{:S(2)}) collective-permute-start(f32[2,136,128]{2,1,0:T(8,128)S(1)} %pad_maximum_fusion.4.refs_4_), channel_id=1, source_target_pairs={{0,16},{8,24},{16,0},{24,8},{1,17},{9,25},{17,1},{25,9},{2,18},{10... | collective-permute-start | bytes 417800 | tf_op jit(solution)/shard_map/ppermute | solution.py:27
  103.5 1.7 %collective-permute-done.37 = f32[136,128]{1,0:T(8,128)S(1)} collective-permute-done((f32[136,128]{1,0:T(8,128)S(1)}, f32[136,128]{1,0:T(8,128)S(1)}, u32[]{:S(2)}, u32[]{:S(2)}) %collective-permute-start.37) | collective-permute-done | bytes 69664 | tf_op jit(solution)/shard_map/ppermute | solution.py:32
  105.2 0.5 collective-permute-done.36
  105.8 0.9 collective-permute-start.38
  106.7 0.5 collective-permute-start.30
  107.2 0.5 collective-permute-done.33.refs_5_
  107.7 0.5 collective-permute-start.35
  108.2 2.7 %collective-permute-done.38.refs_9_ = f32[2,136,128]{2,1,0:T(8,128)S(1)} collective-permute-done((f32[2,136,128]{2,1,0:T(8,128)S(1)}, f32[2,136,128]{2,1,0:T(8,128)S(1)}, u32[]{:S(2)}, u32[]{:S(2)}) %collective-permute-start.38) | collective-permute-done | bytes 139296 | tf_op jit(solution)/shard_map/ppermute | solution.py:27
  110.9 1.3 %collective-permute-done.40.refs_11_ = f32[2,136,128]{2,1,0:T(8,128)S(1)} collective-permute-done((f32[2,136,128]{2,1,0:T(8,128)S(1)}, f32[2,136,128]{2,1,0:T(8,128)S(1)}, u32[]{:S(2)}, u32[]{:S(2)}) %collective-permute-start.40) | collective-permute-done | bytes 139296 | tf_op jit(solution)/shard_map/ppermute | solution.py:27
  112.3 2.5 %assemble.1 = (f32[1024,512]{1,0:T(8,128)}, f32[1,1]{1,0:T(1,128)}) custom-call(f32[4,136,128]{2,1,0:T(8,128)S(1)} %pad_maximum_fusion.refs_0_, f32[4,136,128]{2,1,0:T(8,128)S(1)} %collective-permute-done.28.refs_1_, f32[4,136,128]{2,1,0:T(8,128)S(1)} %collective-permute-done.29.refs_2_, f32[4,136,128]{2,1,0:T(8,128)S(1)} %collective-permute-done.30.refs_3_, ...), custom_call_target="tpu_custom_call" | custom-call | bytes 4194304 | tf_op jit(solution)/shard_map/assemble/pallas_call | solution.py:456
  (85 shorter events, 0.6 us)
Async XLA Ops:
  0.6 8.3 %copy-start = (f32[1,128,512]{2,1,0:T(8,128)S(1)}, f32[1,128,512]{2,1,0:T(8,128)}, u32[]{:S(2)}) copy-start(f32[1,128,512]{2,1,0:T(8,128)} %param.10) | copy-start | bytes 786436
  0.6 10.5 %copy-start.13 = (s32[4]{0:T(128)S(1)}, s32[4]{0:T(128)}, u32[]{:S(2)}) copy-start(s32[4]{0:T(128)} %owner.1) | copy-start | bytes 52
  4.3 13.9 %collective-permute-start.6 = (f32[4,32,512]{2,1,0:T(8,128)}, f32[4,32,512]{2,1,0:T(8,128)S(1)}, u32[]{:S(2)}, u32[]{:S(2)}) collective-permute-start(f32[4,32,512]{2,1,0:T(8,128)} %get-tuple-element.39), channel_id=1, source_target_pairs={{0,1},{1,0},{2,3},{3,2},{4,5},{5,4},{6,7},{7,6},{8,9},{9,8},{10,11... | collective-permute-start | bytes 786440 | tf_op jit(solution)/shard_map/ppermute | solution.py:27
  7.3 11.5 %collective-permute-start.8 = (f32[4,32,512]{2,1,0:T(8,128)}, f32[4,32,512]{2,1,0:T(8,128)S(1)}, u32[]{:S(2)}, u32[]{:S(2)}) collective-permute-start(f32[4,32,512]{2,1,0:T(8,128)} %get-tuple-element.41), channel_id=1, source_target_pairs={{0,2},{1,3},{2,0},{3,1},{4,6},{5,7},{6,4},{7,5},{8,10},{9,11},{10,... | collective-permute-start | bytes 786440 | tf_op jit(solution)/shard_map/ppermute | solution.py:27
  8.9 10.5 %collective-permute-start = (f32[128,512]{1,0:T(8,128)S(1)}, f32[128,512]{1,0:T(8,128)S(1)}, u32[]{:S(2)}, u32[]{:S(2)}) collective-permute-start(f32[128,512]{1,0:T(8,128)S(1)} %bitcast.46), channel_id=1, source_target_pairs={{0,16},{8,24},{16,0},{24,8},{1,17},{9,25},{17,1},{25,9},{2,18},{10... | collective-permute-start | bytes 786440 | tf_op jit(solution)/shard_map/ppermute | solution.py:27
  10.4 16.8 %collective-permute-start.1 = (f32[128,512]{1,0:T(8,128)S(1)}, f32[128,512]{1,0:T(8,128)S(1)}, u32[]{:S(2)}, u32[]{:S(2)}) collective-permute-start(f32[128,512]{1,0:T(8,128)S(1)} %bitcast.47), channel_id=1, source_target_pairs={{0,8},{8,0},{16,24},{24,16},{1,9},{9,1},{17,25},{25,17},{2,10},{10... | collective-permute-start | bytes 786440 | tf_op jit(solution)/shard_map/ppermute | solution.py:27
  12.3 5.9 %copy-start.15 = (f32[4,32,512]{2,1,0:T(8,128)S(1)}, f32[4,32,512]{2,1,0:T(8,128)}, u32[]{:S(2)}) copy-start(f32[4,32,512]{2,1,0:T(8,128)} %get-tuple-element.38) | copy-start | bytes 786436
  12.4 6.5 %copy-start.14 = (f32[4,32,512]{2,1,0:T(8,128)S(1)}, f32[4,32,512]{2,1,0:T(8,128)}, u32[]{:S(2)}) copy-start(f32[4,32,512]{2,1,0:T(8,128)} %get-tuple-element.40) | copy-start | bytes 786436
  18.2 9.1 %copy-start.1 = (f32[1,128,512]{2,1,0:T(8,128)S(1)}, f32[1,128,512]{2,1,0:T(8,128)}, u32[]{:S(2)}) copy-start(f32[1,128,512]{2,1,0:T(8,128)} %param.10) | copy-start | bytes 786436
  18.2 9.0 %copy-start.7 = (bf16[4,512,256]{2,1,0:T(8,128)(2,1)S(1)}, bf16[4,512,256]{2,1,0:T(8,128)(2,1)}, u32[]{:S(2)}) copy-start(bf16[4,512,256]{2,1,0:T(8,128)(2,1)} %get-tuple-element.33.refs_5_) | copy-start | bytes 3145732
  18.2 9.0 %copy-start.8 = (bf16[4,512,256]{2,1,0:T(8,128)(2,1)S(1)}, bf16[4,512,256]{2,1,0:T(8,128)(2,1)}, u32[]{:S(2)}) copy-start(bf16[4,512,256]{2,1,0:T(8,128)(2,1)} %get-tuple-element.34.refs_6_) | copy-start | bytes 3145732
  18.2 9.0 %copy-start.12 = (s32[1,4]{1,0:T(1,128)S(1)}, s32[1,4]{1,0:T(1,128)}, u32[]{:S(2)}) copy-start(s32[1,4]{1,0:T(1,128)} %lengths.3) | copy-start | bytes 52
  18.3 6.0 %collective-permute-start.7 = (f32[2,32,512]{2,1,0:T(8,128)S(1)}, f32[2,32,512]{2,1,0:T(8,128)S(1)}, u32[]{:S(2)}, u32[]{:S(2)}) collective-permute-start(f32[2,32,512]{2,1,0:T(8,128)S(1)} %slice_select_fusion.2), channel_id=1, source_target_pairs={{0,2},{1,3},{2,0},{3,1},{4,6},{5,7},{6,4},{7,5},{8,10},{9,11},{10,... | collective-permute-start | bytes 393224 | tf_op jit(solution)/shard_map/ppermute | solution.py:27
  18.8 5.7 %collective-permute-start.9 = (f32[2,32,512]{2,1,0:T(8,128)S(1)}, f32[2,32,512]{2,1,0:T(8,128)S(1)}, u32[]{:S(2)}, u32[]{:S(2)}) collective-permute-start(f32[2,32,512]{2,1,0:T(8,128)S(1)} %slice_select_fusion), channel_id=1, source_target_pairs={{0,1},{1,0},{2,3},{3,2},{4,5},{5,4},{6,7},{7,6},{8,9},{9,8},{10,11... | collective-permute-start | bytes 393224 | tf_op jit(solution)/shard_map/ppermute | solution.py:27
  19.4 7.8 %collective-permute-start.2 = (f32[128,512]{1,0:T(8,128)S(1)}, f32[128,512]{1,0:T(8,128)S(1)}, u32[]{:S(2)}, u32[]{:S(2)}) collective-permute-start(f32[128,512]{1,0:T(8,128)S(1)} %collective-permute-done.refs_1_), channel_id=1, source_target_pairs={{0,8},{8,0},{16,24},{24,16},{1,9},{9,1},{17,25},{25,17},{2,10},{10... | collective-permute-start | bytes 786440 | tf_op jit(solution)/shard_map/ppermute | solution.py:27
  24.6 14.9 %collective-permute-start.10 = (f32[2,2,32,512]{3,2,1,0:T(8,128)S(1)}, f32[2,2,32,512]{3,2,1,0:T(8,128)S(1)}, u32[]{:S(2)}, u32[]{:S(2)}) collective-permute-start(f32[2,2,32,512]{3,2,1,0:T(8,128)S(1)} %pad_maximum_fusion.1), channel_id=1, source_target_pairs={{0,4},{1,5},{2,6},{3,7},{4,0},{5,1},{6,2},{7,3},{8,12},{9,13},{10,... | collective-permute-start | bytes 786440 | tf_op jit(solution)/shard_map/ppermute | solution.py:27
  27.3 1.0 copy-start.9
  28.2 5.0 %copy-start.10 = (f32[128,512]{1,0:T(8,128)S(1)}, f32[128,512]{1,0:T(8,128)}, u32[]{:S(2)}) copy-start(f32[128,512]{1,0:T(8,128)} %get-tuple-element.32.refs_4_) | copy-start | bytes 786436
  33.2 5.1 %copy-start.2 = (bf16[512,512]{1,0:T(8,128)(2,1)S(1)}, bf16[512,512]{1,0:T(8,128)(2,1)}, u32[]{:S(2)}) copy-start(bf16[512,512]{1,0:T(8,128)(2,1)} %get-tuple-element.36.refs_4_) | copy-start | bytes 1572868
  33.2 5.1 %copy-start.3 = (bf16[512,512]{1,0:T(8,128)(2,1)S(1)}, bf16[512,512]{1,0:T(8,128)(2,1)}, u32[]{:S(2)}) copy-start(bf16[512,512]{1,0:T(8,128)(2,1)} %get-tuple-element.37.refs_5_) | copy-start | bytes 1572868
  33.3 5.1 %copy-start.4 = (f32[128,512]{1,0:T(8,128)S(1)}, f32[128,512]{1,0:T(8,128)}, u32[]{:S(2)}) copy-start(f32[128,512]{1,0:T(8,128)} %get-tuple-element.35.refs_2_) | copy-start | bytes 786436
  33.3 5.1 %copy-start.5 = (f32[512]{0:T(512)S(1)}, f32[512]{0:T(512)}, u32[]{:S(2)}) copy-start(f32[512]{0:T(512)} %param.12) | copy-start | bytes 6148
  33.3 5.1 %copy-start.6 = (s32[1,128]{1,0:T(1,128)S(1)}, s32[1,128]{1,0:T(1,128)}, u32[]{:S(2)}) copy-start(s32[1,128]{1,0:T(1,128)} %refs_7_.1) | copy-start | bytes 1540
  38.9 7.9 %collective-permute-start.3 = (f32[136,512]{1,0:T(8,128)S(1)}, f32[136,512]{1,0:T(8,128)S(1)}, u32[]{:S(2)}, u32[]{:S(2)}) collective-permute-start(f32[136,512]{1,0:T(8,128)S(1)} %project.1.refs_0_), channel_id=1, source_target_pairs={{0,16},{8,24},{16,0},{24,8},{1,17},{9,25},{17,1},{25,9},{2,18},{10... | collective-permute-start | bytes 835592 | tf_op jit(solution)/shard_map/ppermute | solution.py:27
  39.5 5.0 %collective-permute-start.11 = (f32[2,32,512]{2,1,0:T(8,128)S(1)}, f32[2,32,512]{2,1,0:T(8,128)S(1)}, u32[]{:S(2)}, u32[]{:S(2)}) collective-permute-start(f32[2,32,512]{2,1,0:T(8,128)S(1)} %maximum_select_fusion), channel_id=1, source_target_pairs={{0,2},{1,3},{2,0},{3,1},{4,6},{5,7},{6,4},{7,5},{8,10},{9,11},{10,... | collective-permute-start | bytes 393224 | tf_op jit(solution)/shard_map/ppermute | solution.py:27
  41.2 6.2 %collective-permute-start.13 = (f32[2,32,512]{2,1,0:T(8,128)S(1)}, f32[2,32,512]{2,1,0:T(8,128)S(1)}, u32[]{:S(2)}, u32[]{:S(2)}) collective-permute-start(f32[2,32,512]{2,1,0:T(8,128)S(1)} %maximum_select_fusion.1), channel_id=1, source_target_pairs={{0,1},{1,0},{2,3},{3,2},{4,5},{5,4},{6,7},{7,6},{8,9},{9,8},{10,11... | collective-permute-start | bytes 393224 | tf_op jit(solution)/shard_map/ppermute | solution.py:27
  41.8 6.5 %collective-permute-start.4 = (f32[136,512]{1,0:T(8,128)S(1)}, f32[136,512]{1,0:T(8,128)S(1)}, u32[]{:S(2)}, u32[]{:S(2)}) collective-permute-start(f32[136,512]{1,0:T(8,128)S(1)} %project.1.refs_0_), channel_id=1, source_target_pairs={{0,8},{8,0},{16,24},{24,16},{1,9},{9,1},{17,25},{25,17},{2,10},{10... | collective-permute-start | bytes 835592 | tf_op jit(solution)/shard_map/ppermute | solution.py:27
  44.6 7.3 %collective-permute-start.12 = (f32[4,32,512]{2,1,0:T(8,128)S(1)}, f32[4,32,512]{2,1,0:T(8,128)S(1)}, u32[]{:S(2)}, u32[]{:S(2)}) collective-permute-start(f32[4,32,512]{2,1,0:T(8,128)S(1)} %pad_maximum_fusion.2), channel_id=1, source_target_pairs={{0,1},{1,0},{2,3},{3,2},{4,5},{5,4},{6,7},{7,6},{8,9},{9,8},{10,11... | collective-permute-start | bytes 786440 | tf_op jit(solution)/shard_map/ppermute | solution.py:27
  46.7 8.8 %collective-permute-start.5 = (f32[136,512]{1,0:T(8,128)S(1)}, f32[136,512]{1,0:T(8,128)S(1)}, u32[]{:S(2)}, u32[]{:S(2)}) collective-permute-start(f32[136,512]{1,0:T(8,128)S(1)} %collective-permute-done.3.refs_1_), channel_id=1, source_target_pairs={{0,8},{8,0},{16,24},{24,16},{1,9},{9,1},{17,25},{25,17},{2,10},{10... | collective-permute-start | bytes 835592 | tf_op jit(solution)/shard_map/ppermute | solution.py:27
  47.4 8.1 %collective-permute-start.14 = (f32[4,32,512]{2,1,0:T(8,128)S(1)}, f32[4,32,512]{2,1,0:T(8,128)S(1)}, u32[]{:S(2)}, u32[]{:S(2)}) collective-permute-start(f32[4,32,512]{2,1,0:T(8,128)S(1)} %pad_maximum_fusion.3), channel_id=1, source_target_pairs={{0,2},{1,3},{2,0},{3,1},{4,6},{5,7},{6,4},{7,5},{8,10},{9,11},{10,... | collective-permute-start | bytes 786440 | tf_op jit(solution)/shard_map/ppermute | solution.py:27
  60.2 7.7 %collective-permute-start.17 = (f32[4,32,512]{2,1,0:T(8,128)S(1)}, f32[4,32,512]{2,1,0:T(8,128)S(1)}, u32[]{:S(2)}, u32[]{:S(2)}) collective-permute-start(f32[4,32,512]{2,1,0:T(8,128)S(1)} %get-tuple-element.46), channel_id=1, source_target_pairs={{0,2},{1,3},{2,0},{3,1},{4,6},{5,7},{6,4},{7,5},{8,10},{9,11},{10,... | collective-permute-start | bytes 786440 | tf_op jit(solution)/shard_map/ppermute | solution.py:27
  61.8 7.8 %collective-permute-start.15 = (f32[4,32,512]{2,1,0:T(8,128)S(1)}, f32[4,32,512]{2,1,0:T(8,128)S(1)}, u32[]{:S(2)}, u32[]{:S(2)}) collective-permute-start(f32[4,32,512]{2,1,0:T(8,128)S(1)} %get-tuple-element.44), channel_id=1, source_target_pairs={{0,1},{1,0},{2,3},{3,2},{4,5},{5,4},{6,7},{7,6},{8,9},{9,8},{10,11... | collective-permute-start | bytes 786440 | tf_op jit(solution)/shard_map/ppermute | solution.py:27
  67.9 18.5 %copy-start.11 = (s32[4,512]{1,0:T(4,128)S(1)}, s32[4,512]{1,0:T(4,128)}, u32[]{:S(2)}) copy-start(s32[4,512]{1,0:T(4,128)} %ids.1) | copy-start | bytes 24580
  68.0 5.0 %collective-permute-start.18 = (f32[2,32,512]{2,1,0:T(8,128)S(1)}, f32[2,32,512]{2,1,0:T(8,128)S(1)}, u32[]{:S(2)}, u32[]{:S(2)}) collective-permute-start(f32[2,32,512]{2,1,0:T(8,128)S(1)} %get-tuple-element.64), channel_id=1, source_target_pairs={{0,1},{1,0},{2,3},{3,2},{4,5},{5,4},{6,7},{7,6},{8,9},{9,8},{10,11... | collective-permute-start | bytes 393224 | tf_op jit(solution)/shard_map/ppermute | solution.py:27
  69.6 5.0 %collective-permute-start.16 = (f32[2,32,512]{2,1,0:T(8,128)S(1)}, f32[2,32,512]{2,1,0:T(8,128)S(1)}, u32[]{:S(2)}, u32[]{:S(2)}) collective-permute-start(f32[2,32,512]{2,1,0:T(8,128)S(1)} %get-tuple-element.62), channel_id=1, source_target_pairs={{0,2},{1,3},{2,0},{3,1},{4,6},{5,7},{6,4},{7,5},{8,10},{9,11},{10,... | collective-permute-start | bytes 393224 | tf_op jit(solution)/shard_map/ppermute | solution.py:27
  74.7 7.3 %collective-permute-start.19 = (f32[1,64,512]{2,1,0:T(8,128)S(1)}, f32[1,64,512]{2,1,0:T(8,128)S(1)}, u32[]{:S(2)}, u32[]{:S(2)}) collective-permute-start(f32[1,64,512]{2,1,0:T(8,128)S(1)} %pad_maximum_fusion.6), channel_id=1, source_target_pairs={{0,4},{1,5},{2,6},{3,7},{4,0},{5,1},{6,2},{7,3},{8,12},{9,13},{10,... | collective-permute-start | bytes 393224 | tf_op jit(solution)/shard_map/ppermute | solution.py:27
  75.6 8.7 %collective-permute-start.26 = (f32[2,128,512]{2,1,0:T(8,128)S(1)}, f32[2,128,512]{2,1,0:T(8,128)S(1)}, u32[]{:S(2)}, u32[]{:S(2)}) collective-permute-start(f32[2,128,512]{2,1,0:T(8,128)S(1)} %get-tuple-element.52), channel_id=1, source_target_pairs={{0,8},{8,0},{16,24},{24,16},{1,9},{9,1},{17,25},{25,17},{2,10},{10... | collective-permute-start | bytes 1572872 | tf_op jit(solution)/shard_map/ppermute | solution.py:27
  82.1 4.3 %collective-permute-start.20 = (f32[16,512]{1,0:T(8,128)S(1)}, f32[16,512]{1,0:T(8,128)S(1)}, u32[]{:S(2)}, u32[]{:S(2)}) collective-permute-start(f32[16,512]{1,0:T(8,128)S(1)} %pad_maximum_fusion.8), channel_id=1, source_target_pairs={{0,16},{8,24},{16,0},{24,8},{1,17},{9,25},{17,1},{25,9},{2,18},{10... | collective-permute-start | bytes 98312 | tf_op jit(solution)/shard_map/ppermute | solution.py:32
  82.6 3.8 %collective-permute-start.21 = (f32[16,512]{1,0:T(8,128)S(1)}, f32[16,512]{1,0:T(8,128)S(1)}, u32[]{:S(2)}, u32[]{:S(2)}) collective-permute-start(f32[16,512]{1,0:T(8,128)S(1)} %pad_maximum_fusion.9), channel_id=1, source_target_pairs={{0,8},{8,0},{16,24},{24,16},{1,9},{9,1},{17,25},{25,17},{2,10},{10... | collective-permute-start | bytes 98312 | tf_op jit(solution)/shard_map/ppermute | solution.py:32
  82.6 3.8 %collective-permute-start.22 = (f32[16,512]{1,0:T(8,128)S(1)}, f32[16,512]{1,0:T(8,128)S(1)}, u32[]{:S(2)}, u32[]{:S(2)}) collective-permute-start(f32[16,512]{1,0:T(8,128)S(1)} %pad_maximum_fusion.10), channel_id=1, source_target_pairs={{0,24},{8,16},{16,8},{24,0},{1,25},{9,17},{17,9},{25,1},{2,26},{10... | collective-permute-start | bytes 98312 | tf_op jit(solution)/shard_map/ppermute | solution.py:32
  84.3 10.9 %collective-permute-start.27 = (f32[1,128,512]{2,1,0:T(8,128)S(1)}, f32[1,128,512]{2,1,0:T(8,128)S(1)}, u32[]{:S(2)}, u32[]{:S(2)}) collective-permute-start(f32[1,128,512]{2,1,0:T(8,128)S(1)} %slice_add_fusion), channel_id=1, source_target_pairs={{0,16},{8,24},{16,0},{24,8},{1,17},{9,25},{17,1},{25,9},{2,18},{10... | collective-permute-start | bytes 786440 | tf_op jit(solution)/shard_map/ppermute | solution.py:27
  88.4 6.1 %collective-permute-start.25 = (f32[136,128]{1,0:T(8,128)S(1)}, f32[136,128]{1,0:T(8,128)S(1)}, u32[]{:S(2)}, u32[]{:S(2)}) collective-permute-start(f32[136,128]{1,0:T(8,128)S(1)} %get-tuple-element.50), channel_id=1, source_target_pairs={{0,3},{1,2},{2,1},{3,0},{4,7},{5,6},{6,5},{7,4},{8,11},{9,10},{10,... | collective-permute-start | bytes 208904 | tf_op jit(solution)/shard_map/ppermute | solution.py:32
  88.8 6.0 %collective-permute-start.24 = (f32[136,128]{1,0:T(8,128)S(1)}, f32[136,128]{1,0:T(8,128)S(1)}, u32[]{:S(2)}, u32[]{:S(2)}) collective-permute-start(f32[136,128]{1,0:T(8,128)S(1)} %get-tuple-element.49), channel_id=1, source_target_pairs={{0,2},{1,3},{2,0},{3,1},{4,6},{5,7},{6,4},{7,5},{8,10},{9,11},{10,... | collective-permute-start | bytes 208904 | tf_op jit(solution)/shard_map/ppermute | solution.py:32
  90.5 4.7 %collective-permute-start.23 = (f32[136,128]{1,0:T(8,128)S(1)}, f32[136,128]{1,0:T(8,128)S(1)}, u32[]{:S(2)}, u32[]{:S(2)}) collective-permute-start(f32[136,128]{1,0:T(8,128)S(1)} %get-tuple-element.48), channel_id=1, source_target_pairs={{0,1},{1,0},{2,3},{3,2},{4,5},{5,4},{6,7},{7,6},{8,9},{9,8},{10,11... | collective-permute-start | bytes 208904 | tf_op jit(solution)/shard_map/ppermute | solution.py:32
  91.9 9.6 %collective-permute-start.32 = (f32[136,128]{1,0:T(8,128)S(1)}, f32[136,128]{1,0:T(8,128)S(1)}, u32[]{:S(2)}, u32[]{:S(2)}) collective-permute-start(f32[136,128]{1,0:T(8,128)S(1)} %get-tuple-element.55), channel_id=1, source_target_pairs={{0,5},{1,4},{2,7},{3,6},{4,1},{5,0},{6,3},{7,2},{8,13},{9,12},{10,... | collective-permute-start | bytes 208904 | tf_op jit(solution)/shard_map/ppermute | solution.py:32
  94.4 7.1 %collective-permute-start.31 = (f32[136,128]{1,0:T(8,128)S(1)}, f32[136,128]{1,0:T(8,128)S(1)}, u32[]{:S(2)}, u32[]{:S(2)}) collective-permute-start(f32[136,128]{1,0:T(8,128)S(1)} %get-tuple-element.54), channel_id=1, source_target_pairs={{0,4},{1,5},{2,6},{3,7},{4,0},{5,1},{6,2},{7,3},{8,12},{9,13},{10,... | collective-permute-start | bytes 208904 | tf_op jit(solution)/shard_map/ppermute | solution.py:32
  96.0 10.7 %collective-permute-start.28 = (f32[4,136,128]{2,1,0:T(8,128)S(1)}, f32[4,136,128]{2,1,0:T(8,128)S(1)}, u32[]{:S(2)}, u32[]{:S(2)}) collective-permute-start(f32[4,136,128]{2,1,0:T(8,128)S(1)} %pad_maximum_fusion.refs_0_), channel_id=1, source_target_pairs={{0,16},{8,24},{16,0},{24,8},{1,17},{9,25},{17,1},{25,9},{2,18},{10... | collective-permute-start | bytes 835592 | tf_op jit(solution)/shard_map/ppermute | solution.py:27
  97.6 7.6 %collective-permute-start.37 = (f32[136,128]{1,0:T(8,128)S(1)}, f32[136,128]{1,0:T(8,128)S(1)}, u32[]{:S(2)}, u32[]{:S(2)}) collective-permute-start(f32[136,128]{1,0:T(8,128)S(1)} %get-tuple-element.57), channel_id=1, source_target_pairs={{0,7},{1,6},{2,5},{3,4},{4,3},{5,2},{6,1},{7,0},{8,15},{9,14},{10,... | collective-permute-start | bytes 208904 | tf_op jit(solution)/shard_map/ppermute | solution.py:32
  99.6 6.1 %collective-permute-start.36 = (f32[136,128]{1,0:T(8,128)S(1)}, f32[136,128]{1,0:T(8,128)S(1)}, u32[]{:S(2)}, u32[]{:S(2)}) collective-permute-start(f32[136,128]{1,0:T(8,128)S(1)} %get-tuple-element.56), channel_id=1, source_target_pairs={{0,6},{1,7},{2,4},{3,5},{4,2},{5,3},{6,0},{7,1},{8,14},{9,15},{10,... | collective-permute-start | bytes 208904 | tf_op jit(solution)/shard_map/ppermute | solution.py:32
  101.6 6.1 %collective-permute-start.33 = (f32[2,136,128]{2,1,0:T(8,128)S(1)}, f32[2,136,128]{2,1,0:T(8,128)S(1)}, u32[]{:S(2)}, u32[]{:S(2)}) collective-permute-start(f32[2,136,128]{2,1,0:T(8,128)S(1)} %pad_maximum_fusion.4.refs_4_), channel_id=1, source_target_pairs={{0,16},{8,24},{16,0},{24,8},{1,17},{9,25},{17,1},{25,9},{2,18},{10... | collective-permute-start | bytes 417800 | tf_op jit(solution)/shard_map/ppermute | solution.py:27
  103.5 4.2 %collective-permute-start.34 = (f32[2,136,128]{2,1,0:T(8,128)S(1)}, f32[2,136,128]{2,1,0:T(8,128)S(1)}, u32[]{:S(2)}, u32[]{:S(2)}) collective-permute-start(f32[2,136,128]{2,1,0:T(8,128)S(1)} %pad_maximum_fusion.4.refs_4_), channel_id=1, source_target_pairs={{0,8},{8,0},{16,24},{24,16},{1,9},{9,1},{17,25},{25,17},{2,10},{10... | collective-permute-start | bytes 417800 | tf_op jit(solution)/shard_map/ppermute | solution.py:27
  105.8 5.1 %collective-permute-start.38 = (f32[2,136,128]{2,1,0:T(8,128)S(1)}, f32[2,136,128]{2,1,0:T(8,128)S(1)}, u32[]{:S(2)}, u32[]{:S(2)}) collective-permute-start(f32[2,136,128]{2,1,0:T(8,128)S(1)} %pad_maximum_fusion.5.refs_8_), channel_id=1, source_target_pairs={{0,16},{8,24},{16,0},{24,8},{1,17},{9,25},{17,1},{25,9},{2,18},{10... | collective-permute-start | bytes 417800 | tf_op jit(solution)/shard_map/ppermute | solution.py:27
  106.7 5.6 %collective-permute-start.29 = (f32[4,136,128]{2,1,0:T(8,128)S(1)}, f32[4,136,128]{2,1,0:T(8,128)S(1)}, u32[]{:S(2)}, u32[]{:S(2)}) collective-permute-start(f32[4,136,128]{2,1,0:T(8,128)S(1)} %pad_maximum_fusion.refs_0_), channel_id=1, source_target_pairs={{0,8},{8,0},{16,24},{24,16},{1,9},{9,1},{17,25},{25,17},{2,10},{10... | collective-permute-start | bytes 835592 | tf_op jit(solution)/shard_map/ppermute | solution.py:27
  106.7 5.6 %collective-permute-start.30 = (f32[4,136,128]{2,1,0:T(8,128)S(1)}, f32[4,136,128]{2,1,0:T(8,128)S(1)}, u32[]{:S(2)}, u32[]{:S(2)}) collective-permute-start(f32[4,136,128]{2,1,0:T(8,128)S(1)} %collective-permute-done.28.refs_1_), channel_id=1, source_target_pairs={{0,8},{8,0},{16,24},{24,16},{1,9},{9,1},{17,25},{25,17},{2,10},{10... | collective-permute-start | bytes 835592 | tf_op jit(solution)/shard_map/ppermute | solution.py:27
  107.6 3.2 %collective-permute-start.39 = (f32[2,136,128]{2,1,0:T(8,128)S(1)}, f32[2,136,128]{2,1,0:T(8,128)S(1)}, u32[]{:S(2)}, u32[]{:S(2)}) collective-permute-start(f32[2,136,128]{2,1,0:T(8,128)S(1)} %pad_maximum_fusion.5.refs_8_), channel_id=1, source_target_pairs={{0,8},{8,0},{16,24},{24,16},{1,9},{9,1},{17,25},{25,17},{2,10},{10... | collective-permute-start | bytes 417800 | tf_op jit(solution)/shard_map/ppermute | solution.py:27
  107.7 3.2 %collective-permute-start.35 = (f32[2,136,128]{2,1,0:T(8,128)S(1)}, f32[2,136,128]{2,1,0:T(8,128)S(1)}, u32[]{:S(2)}, u32[]{:S(2)}) collective-permute-start(f32[2,136,128]{2,1,0:T(8,128)S(1)} %collective-permute-done.33.refs_5_), channel_id=1, source_target_pairs={{0,8},{8,0},{16,24},{24,16},{1,9},{9,1},{17,25},{25,17},{2,10},{10... | collective-permute-start | bytes 417800 | tf_op jit(solution)/shard_map/ppermute | solution.py:27
  110.9 1.4 %collective-permute-start.40 = (f32[2,136,128]{2,1,0:T(8,128)S(1)}, f32[2,136,128]{2,1,0:T(8,128)S(1)}, u32[]{:S(2)}, u32[]{:S(2)}) collective-permute-start(f32[2,136,128]{2,1,0:T(8,128)S(1)} %collective-permute-done.38.refs_9_), channel_id=1, source_target_pairs={{0,8},{8,0},{16,24},{24,16},{1,9},{9,1},{17,25},{25,17},{2,10},{10... | collective-permute-start | bytes 417800 | tf_op jit(solution)/shard_map/ppermute | solution.py:27

commit v6 on v5

--- a/solution.py
+++ b/solution.py
@@ -18,7 +18,6 @@
 high = lax.Precision.HIGH
 NN, NT = ((1,), (0,)), ((1,), (1,))
 params = pltpu.CompilerParams(vmem_limit_bytes=40 * 2**20)
-almost = pltpu.CompilerParams(vmem_limit_bytes=55 * 2**20)
 alone = pltpu.CompilerParams(vmem_limit_bytes=62 * 2**20)
 
 
@@ -144,56 +143,33 @@
     )(ids, table)
 
 
-def prepare_kernel(x_ref, w_hbm, wo_hbm, gates_ref, queries_ref, vk_hi, vk_lo, wo_hi, wo_lo, w_buf, wo_buf, sems):
-    n, depth, _ = w_buf.shape
-    width = x_ref.shape[1]
-    copies = [pltpu.make_async_copy(w_hbm.at[pl.ds(k * depth, depth)], w_buf.at[k], sems.at[k]) for k in range(n)]
-    copies.append(pltpu.make_async_copy(wo_hbm, wo_buf, sems.at[n]))
-    for copy in copies:
-        copy.start()
-    x = split(x_ref[...])
-    gates = queries = 0.0
-    for k in range(n):
-        copies[k].wait()
-        span = pl.ds(k * depth, depth)
-        mine = x[0][:, k * depth : (k + 1) * depth], x[1][:, k * depth : (k + 1) * depth]
-        w = w_buf[k]
-        gates = gates + dot3(mine, split(w[:, :width]), NN)
-        queries = queries + dot3(mine, split(w[:, 2 * width : 3 * width]), NN)
-        for j in range(width // LANES):
-            v = w[:, width + j * LANES : width + (j + 1) * LANES]
-            key = w[:, 3 * width + j * LANES : 3 * width + (j + 1) * LANES]
-            vk_hi[j, span], vk_lo[j, span] = split(jnp.concatenate([v, key], axis=1))
-    gates_ref[...] = silu(gates)
-    queries_ref[...] = silu(queries)
-    copies[n].wait()
-    wo_hi[...], wo_lo[...] = split(wo_buf[...])
-
-
-def prepare(rows_in, w_uvqk, w_out):
+def prepare_kernel(x_ref, u_ref, q_ref, gates_ref, queries_ref):
+    both = silu(dot3(split(x_ref[...]), split(jnp.concatenate([u_ref[...], q_ref[...]], axis=1)), NN))
+    gates_ref[...], queries_ref[...] = both[:, :LANES], both[:, LANES:]
+
+
+def prepare(rows_in, w_uvqk):
     tok, width = rows_in.shape
-    n, depth = width // LANES, 256
-    hbm, vmem = pl.BlockSpec(memory_space=pltpu.HBM), pl.BlockSpec(memory_space=pltpu.VMEM)
+    n = width // LANES
+    own = pl.BlockSpec((tok, LANES), lambda j: (0, j))
     return pl.pallas_call(
         prepare_kernel,
-        in_specs=[vmem, hbm, hbm],
-        out_specs=[vmem] * 6,
-        out_shape=[jax.ShapeDtypeStruct((tok, width), f32)] * 2
-        + [jax.ShapeDtypeStruct((n, width, 2 * LANES), bf16)] * 2
-        + [jax.ShapeDtypeStruct((width, width), bf16)] * 2,
-        scratch_shapes=[
-            pltpu.VMEM((width // depth, depth, w_uvqk.shape[1]), f32),
-            pltpu.VMEM((width, width), f32),
-            pltpu.SemaphoreType.DMA((width // depth + 1,)),
+        grid=(n,),
+        in_specs=[
+            pl.BlockSpec((tok, width), lambda j: (0, 0)),
+            pl.BlockSpec((width, LANES), lambda j: (0, j)),
+            pl.BlockSpec((width, LANES), lambda j: (0, 2 * n + j)),
         ],
-        compiler_params=almost,
-        cost_estimate=pl.CostEstimate(flops=8 * tok * width * width, bytes_accessed=6 * width * width * 4, transcendentals=0),
+        out_specs=[own, own],
+        out_shape=[jax.ShapeDtypeStruct((tok, width), f32)] * 2,
+        compiler_params=params,
+        cost_estimate=pl.CostEstimate(flops=12 * tok * width * width, bytes_accessed=2 * width * width * 4, transcendentals=0),
         name="prepare",
-    )(rows_in, w_uvqk, w_out)
+    )(rows_in, w_uvqk, w_uvqk)
 
 
 def attend_kernel(order, n_seq, lengths, *refs):
-    x_refs, (q_ref, vk_hi, vk_lo, out_ref, x_hi, x_lo, allowed) = refs[:n_seq], refs[n_seq:]
+    x_refs, (q_ref, v_ref, k_ref, out_ref, x_hi, x_lo, allowed) = refs[:n_seq], refs[n_seq:]
     tok = q_ref.shape[0]
     head = x_hi.shape[1] // H
 
@@ -219,7 +195,7 @@
             allowed[:, span] = seen.astype(f32)
 
     x = (x_hi[...], x_lo[...])
-    vk = silu(dot3(x, (vk_hi[0], vk_lo[0]), NN))
+    vk = silu(dot3(x, split(jnp.concatenate([v_ref[...], k_ref[...]], axis=1)), NN))
     v_hi, v_lo = split(vk[:, :LANES])
     k_hi, k_lo = split(vk[:, LANES:])
     k_both = jnp.concatenate([k_hi, k_lo], axis=1)
@@ -241,17 +217,19 @@
     out_ref[...] = total
 
 
-def attend(lengths, pieces, order, queries, vk_hi, vk_lo, first, count):
+def attend(lengths, pieces, order, queries, w_uvqk, first, count):
     tok, width = pieces[0].shape
     n_seq = len(pieces)
     whole = pl.BlockSpec((tok, width), lambda j: (0, 0))
-    pair = pl.BlockSpec((1, width, 2 * LANES), lambda j: (first + j, 0, 0))
+    n = width // LANES
+    v = pl.BlockSpec((width, LANES), lambda j: (0, n + first + j))
+    k = pl.BlockSpec((width, LANES), lambda j: (0, 3 * n + first + j))
     return pl.pallas_call(
         functools.partial(attend_kernel, order, n_seq),
         grid=(count,),
         in_specs=[pl.BlockSpec(memory_space=pltpu.SMEM)]
         + [whole] * n_seq
-        + [pl.BlockSpec((tok, LANES), lambda j: (0, first + j)), pair, pair],
+        + [pl.BlockSpec((tok, LANES), lambda j: (0, first + j)), v, k],
         out_specs=pl.BlockSpec((tok, LANES), lambda j: (0, j)),
         out_shape=jax.ShapeDtypeStruct((tok, count * LANES), f32),
         scratch_shapes=[
@@ -262,43 +240,65 @@
         compiler_params=params,
         cost_estimate=pl.CostEstimate(flops=count * 2000000000, bytes_accessed=2 * width * width * 4, transcendentals=0),
         name="attend",
-    )(lengths, *pieces, queries, vk_hi, vk_lo)
+    )(lengths, *pieces, queries, w_uvqk, w_uvqk)
 
 
 def project_kernel(n_parts, words, *refs):
-    parts, (gates, gain, wo_hi, wo_lo, rows_in, targets, out_ref) = refs[:n_parts], refs[n_parts:]
+    parts, (gates, gain, w_out, rows_in, targets, out_ref) = refs[:n_parts], refs[n_parts:]
     tok, width = rows_in.shape
     attended = jnp.concatenate([p[...] for p in parts], axis=1)
     centered = attended - jnp.mean(attended, axis=1, keepdims=True)
     variance = jnp.mean(centered * centered, axis=1, keepdims=True)
     normed = centered * lax.rsqrt(variance + epsilon) * gain[...]
     gated = split(normed * gates[...])
-    out_ref[:tok] = rows_in[...] + dot3(gated, (wo_hi[...], wo_lo[...]), NN)
+    out_ref[:tok] = rows_in[...] + dot3(gated, split(w_out[...]), NN)
     out_ref[tok:] = jnp.zeros((EXTRA, width), f32)
     out_ref[tok : tok + 1, :tok] = targets[...].astype(f32)
     for k in range(words.shape[1]):
         out_ref[tok + 1 : tok + 2, k * LANES : (k + 1) * LANES] = jnp.full((1, LANES), words[0, k].astype(f32))
 
 
-def project(words, parts, gates, gain, wo_hi, wo_lo, rows_in, targets):
+def project(words, parts, gates, gain, w_out, rows_in, targets):
     tok, width = rows_in.shape
     return pl.pallas_call(
         lambda words, *refs: project_kernel(len(parts), words, *refs),
-        in_specs=[pl.BlockSpec(memory_space=pltpu.SMEM)] + [pl.BlockSpec(memory_space=pltpu.VMEM)] * (len(parts) + 6),
+        in_specs=[pl.BlockSpec(memory_space=pltpu.SMEM)] + [pl.BlockSpec(memory_space=pltpu.VMEM)] * (len(parts) + 5),
         out_specs=pl.BlockSpec(memory_space=pltpu.VMEM),
         out_shape=jax.ShapeDtypeStruct((tok + EXTRA, width), f32),
         compiler_params=params,
         cost_estimate=pl.CostEstimate(flops=6 * tok * width * width, bytes_accessed=2 * width * width * 4, transcendentals=0),
         name="project",
-    )(words, *parts, gates, gain, wo_hi, wo_lo, rows_in, targets)
-
-
-def loss_kernel(plan, *refs):
+    )(words, *parts, gates, gain, w_out, rows_in, targets)
+
+
+def transpose_kernel(*refs):
+    o_refs, (o_hi, o_lo) = refs[:-2], refs[-2:]
+    tok = o_refs[0].shape[0] - EXTRA
+    for n, o_ref in enumerate(o_refs):
+        span = pl.ds(n * tok, tok)
+        o_hi[:, span], o_lo[:, span] = split(o_ref[:tok].T)
+
+
+def transpose_outputs(outputs):
+    tok, width = outputs[0].shape[0] - EXTRA, outputs[0].shape[1]
+    vmem = pl.BlockSpec(memory_space=pltpu.VMEM)
+    return pl.pallas_call(
+        transpose_kernel,
+        in_specs=[vmem] * len(outputs),
+        out_specs=[vmem] * 2,
+        out_shape=[jax.ShapeDtypeStruct((width, tok * len(outputs)), bf16)] * 2,
+        compiler_params=params,
+        cost_estimate=pl.CostEstimate(flops=0, bytes_accessed=2**22, transcendentals=0),
+        name="transpose_outputs",
+    )(*outputs)
+
+
+def loss_kernel(plan, o_hi, o_lo, *refs):
     n_seq, n_item, seq_order, item_orders, aligned = plan
     o_refs, refs = refs[:n_seq], refs[n_seq:]
-    n_refs, refs = refs[: 4 if aligned else 1], refs[4 if aligned else 1 :]
-    n_out = 4 if aligned else 1
-    panel_refs, (kept_rows, sent_rows, loss_ref, n_hi, n_lo, o_hi, o_lo, g_hi, g_lo, panel) = refs[:n_out], refs[n_out:]
+    n_in = 4 if aligned else 1
+    n_refs, panel_refs, refs = refs[:n_in], refs[n_in : 2 * n_in], refs[2 * n_in :]
+    loss_ref, g_ref, n_hi, n_lo, g_hi, g_lo, panel = refs
     me, item = lax.axis_index("seq"), lax.axis_index("item")
     n_neg, width = n_hi.shape
     tok = o_refs[0].shape[0] - EXTRA
@@ -320,11 +320,9 @@
     for p in range(n_seq // 2):
         both = o_refs[2 * p], o_refs[2 * p + 1]
         span = pl.ds(2 * p * tok, 2 * tok)
-        outputs = split(jnp.concatenate([b[:tok] for b in both], axis=0).T)
-        o_hi[:, span], o_lo[:, span] = outputs
         target = jnp.concatenate([b[tok : tok + 1, :tok] for b in both], axis=1).astype(i32)
         words = jnp.concatenate([b[tok + 1 : tok + 2, :tok] for b in both], axis=1).astype(i32)
-        logits = dot3(negatives, outputs, NN)
+        logits = dot3(negatives, (o_hi[:, span], o_lo[:, span]), NN)
         is_target = columns == target
         live = jnp.bitwise_and(jnp.right_shift(jnp.broadcast_to(words, columns.shape), columns // LANES), 1).astype(f32)
         weight = jnp.where(is_target, beta_weight, live)
@@ -333,12 +331,8 @@
         loss = loss + jnp.sum(weight * (jnp.maximum(signed, 0.0) + jnp.log1p(small)), axis=0, keepdims=True)
         chance = jnp.where(signed >= 0.0, 1.0, small) / (1.0 + small)
         grad = jnp.where(is_target, -weight, weight) * chance
+        g_ref[:, span] = grad
         g_hi[:, span], g_lo[:, span] = split(grad)
-        rows = dot3(split(grad.T), negatives, NN)
-        for k in range(2):
-            n = 2 * p + k
-            target_ref = kept_rows if n < n_seq // 2 else sent_rows
-            target_ref[n % (n_seq // 2)] = rows[k * tok : (k + 1) * tok]
     loss_ref[...] = jnp.full((EXTRA, LANES), jnp.sum(loss))
     whole = dot3((o_hi[...], o_lo[...]), (g_hi[...], g_lo[...]), NT)
     if not aligned:
@@ -356,53 +350,84 @@
                 out[k, n * part : (n + 1) * part] = panel[pl.ds(pl.multiple_of(first, part), part)]
 
 
-def loss_terms(outputs, negatives, plan, n_neg):
+def loss_terms(transposed, outputs, negatives, plan, n_neg):
     n_seq, n_item, _, _, aligned = plan
     tok, width = outputs[0].shape[0] - EXTRA, outputs[0].shape[1]
     group_len = tok * n_seq
     vmem = pl.BlockSpec(memory_space=pltpu.VMEM)
     if aligned:
-        part = width // (2 * n_item)
-        panel = [jax.ShapeDtypeStruct((n_item // 2, part, n_neg), f32)] * 4
+        panel = [jax.ShapeDtypeStruct((n_item // 2, width // (2 * n_item), n_neg), f32)] * 4
     else:
         panel = [jax.ShapeDtypeStruct((width, n_neg), f32)]
-    rows = [jax.ShapeDtypeStruct((n_seq // 2, tok, width), f32)] * 2
-    out_shape = panel + rows + [jax.ShapeDtypeStruct((EXTRA, LANES), f32)]
+    loss = jax.ShapeDtypeStruct((EXTRA, LANES), f32)
+    grad = jax.ShapeDtypeStruct((n_neg, group_len), f32)
+    parts = [jax.ShapeDtypeStruct((n_neg, width), bf16)] * 2
+    out_shape = [*panel, loss, grad, *parts]
     return pl.pallas_call(
         functools.partial(loss_kernel, plan),
-        in_specs=[vmem] * (n_seq + len(negatives)),
+        in_specs=[vmem] * (2 + n_seq + len(negatives)),
         out_specs=[vmem] * len(out_shape),
         out_shape=out_shape,
-        scratch_shapes=[pltpu.VMEM((n_neg, width), bf16)] * 2
-        + [pltpu.VMEM((width, group_len), bf16)] * 2
-        + [pltpu.VMEM((n_neg, group_len), bf16)] * 2
-        + [pltpu.VMEM((width, n_neg), f32)],
-        compiler_params=params,
-        cost_estimate=pl.CostEstimate(flops=18 * group_len * width * n_neg, bytes_accessed=16 * n_neg * width, transcendentals=0),
+        scratch_shapes=[pltpu.VMEM((n_neg, group_len), bf16)] * 2 + [pltpu.VMEM((width, n_neg), f32)],
+        compiler_params=params,
+        cost_estimate=pl.CostEstimate(flops=12 * group_len * width * n_neg, bytes_accessed=16 * n_neg * width, transcendentals=0),
         name="loss_terms",
-    )(*outputs, *negatives)
-
-
-def spread_kernel(order, per_panel, n_item, owner, ids, loss, *refs):
+    )(*transposed, *outputs, *negatives)
+
+
+def rows_kernel(n_seq, grad, n_hi, n_lo, kept_rows, sent_rows):
+    tok = grad.shape[1] // n_seq
+    negatives = (n_hi[...], n_lo[...])
+    for p in range(n_seq // 2):
+        rows = dot3(split(grad[:, 2 * p * tok : 2 * (p + 1) * tok].T), negatives, NN)
+        for k in range(2):
+            n = 2 * p + k
+            target_ref = kept_rows if n < n_seq // 2 else sent_rows
+            target_ref[n % (n_seq // 2)] = rows[k * tok : (k + 1) * tok]
+
+
+def event_rows(grad, n_hi, n_lo, n_seq):
+    n_neg, group_len = grad.shape
+    width = n_hi.shape[1]
+    vmem = pl.BlockSpec(memory_space=pltpu.VMEM)
+    return pl.pallas_call(
+        functools.partial(rows_kernel, n_seq),
+        in_specs=[vmem] * 3,
+        out_specs=[vmem] * 2,
+        out_shape=[jax.ShapeDtypeStruct((n_seq // 2, group_len // n_seq, width), f32)] * 2,
+        compiler_params=params,
+        cost_estimate=pl.CostEstimate(flops=6 * group_len * width * n_neg, bytes_accessed=8 * n_neg * width, transcendentals=0),
+        name="event_rows",
+    )(grad, n_hi, n_lo)
+
+
+def pieces_kernel(spread, owners, which, loss, outs):
+    n_dim, n_rows = spread[0].shape
+    item = lax.axis_index("item")
+    for r, out in zip(which, outs):
+        total = jnp.where(owners[0] == item ^ r, spread[0], 0.0)
+        for p in range(1, len(owners)):
+            total = total + jnp.where(owners[p] == item ^ r, spread[p], 0.0)
+        for c in range(n_rows // LANES):
+            out[c * n_dim : (c + 1) * n_dim] = total[:, c * LANES : (c + 1) * LANES]
+        out[n_rows // LANES * n_dim :] = loss[...]
+
+
+def owners_of(order, per_panel, owner):
+    return [owner[(lax.axis_index("seq") ^ r) // per_panel] for r in order]
+
+
+def spread_kernel(order, per_panel, which, owner, ids, loss, *refs):
     moved, outs = refs[: len(order)], refs[len(order) :]
     n_dim, n_neg = moved[0].shape
-    n_tiles = (outs[0].shape[0] - EXTRA) // n_dim
-    me, item = lax.axis_index("seq"), lax.axis_index("item")
-    row = lax.broadcasted_iota(i32, (n_tiles * LANES, n_neg), 0)
-    spread, owners = [], []
+    n_rows = (outs[0].shape[0] - EXTRA) // n_dim * LANES
+    row = lax.broadcasted_iota(i32, (n_rows, n_neg), 0)
+    spread = []
     for p, r in enumerate(order):
-        source = me ^ r
-        owners.append(owner[source // per_panel])
-        hot = jnp.where(row == ids[pl.ds(source, 1), :], 1.0, 0.0).astype(bf16)
+        hot = jnp.where(row == ids[pl.ds(lax.axis_index("seq") ^ r, 1), :], 1.0, 0.0).astype(bf16)
         both = dot(jnp.concatenate(split(moved[p][...]), axis=0), hot, NT)
         spread.append(both[:n_dim] + both[n_dim:])
-    for r in range(n_item):
-        total = jnp.where(owners[0] == item ^ r, spread[0], 0.0)
-        for p in range(1, len(order)):
-            total = total + jnp.where(owners[p] == item ^ r, spread[p], 0.0)
-        for c in range(n_tiles):
-            outs[r][c * n_dim : (c + 1) * n_dim] = total[:, c * LANES : (c + 1) * LANES]
-        outs[r][n_tiles * n_dim :] = loss[...]
+    pieces_kernel(spread, owners_of(order, per_panel, owner), which, loss, outs)
 
 
 def spread_rows(order, per_panel, owner, moved, ids, loss, n_item, n_rows):
@@ -411,7 +436,7 @@
     n_dim = moved[0].shape[0]
     out = jax.ShapeDtypeStruct((n_rows // LANES * n_dim + EXTRA, LANES), f32)
     return pl.pallas_call(
-        functools.partial(spread_kernel, order, per_panel, n_item),
+        functools.partial(spread_kernel, order, per_panel, tuple(range(n_item))),
         in_specs=[smem, vmem, vmem] + [vmem] * len(moved),
         out_specs=[vmem] * n_item,
         out_shape=[out] * n_item,
@@ -421,8 +446,9 @@
     )(owner, ids, loss, *moved)
 
 
-def assemble_kernel(order, n_item, n_dim, events, *refs):
-    groups, (out_ref, loss_ref, quarter) = refs[:-3], refs[-3:]
+def assemble_kernel(order, members, n_item, n_dim, events, kept, got, *refs):
+    groups, (out_ref, loss_ref, event_ref, quarter) = refs[:-4], refs[-4:]
+    event_ref[...] = kept[...] + got[...]
     n_seq = len(order)
     me, item = lax.axis_index("seq"), lax.axis_index("item")
     cols = n_item * n_dim
@@ -435,7 +461,7 @@
     for c in range(n_tiles):
         rows = pl.ds(pl.multiple_of((block * n_tiles + c) * n_dim, n_dim), n_dim)
         for k, q in enumerate(order):
-            for r, (group, m) in enumerate(places(k)):
+            for r, (group, m) in zip(members, places(k)):
                 quarter[pl.ds(pl.multiple_of((item ^ r) * n_dim, n_dim), n_dim)] = group[m, rows]
             place = pl.ds(pl.multiple_of((me ^ q) * cols, cols), cols)
             out_ref[c * LANES : (c + 1) * LANES, place] = quarter[...].T
@@ -449,21 +475,26 @@
         loss_ref[0, 0] = jnp.sum(total) / (EXTRA * LANES * events)
 
 
-def assemble(table, order, n_item, n_dim, n_rows, events):
+def assemble(table, kept, got, order, members, n_item, n_dim, n_rows, events):
     width = n_item * n_dim * len(order)
     step = min(n_rows, 256)
     pieces = sum(table, [])
-    return pl.pallas_call(
-        functools.partial(assemble_kernel, order, n_item, n_dim, events),
+    rows = pl.BlockSpec((1, kept.shape[1] * step // n_rows, width), lambda j: (0, j, 0))
+    return pl.pallas_call(
+        functools.partial(assemble_kernel, order, members, n_item, n_dim, events),
         grid=(n_rows // step,),
-        in_specs=[pl.BlockSpec(memory_space=pltpu.VMEM)] * len(pieces),
-        out_specs=[pl.BlockSpec((step, width), lambda j: (j, 0)), pl.BlockSpec(memory_space=pltpu.SMEM)],
-        out_shape=[jax.ShapeDtypeStruct((n_rows, width), f32), jax.ShapeDtypeStruct((1, 1), f32)],
+        in_specs=[rows, rows] + [pl.BlockSpec(memory_space=pltpu.VMEM)] * len(pieces),
+        out_specs=[pl.BlockSpec((step, width), lambda j: (j, 0)), pl.BlockSpec(memory_space=pltpu.SMEM), rows],
+        out_shape=[
+            jax.ShapeDtypeStruct((n_rows, width), f32),
+            jax.ShapeDtypeStruct((1, 1), f32),
+            jax.ShapeDtypeStruct(kept.shape, f32),
+        ],
         scratch_shapes=[pltpu.VMEM((n_item * n_dim, LANES), f32)],
         compiler_params=params,
         cost_estimate=pl.CostEstimate(flops=0, bytes_accessed=8 * n_rows * width, transcendentals=0),
         name="assemble",
-    )(*pieces)
+    )(kept, got, *pieces)
 
 
 def per_device(
@@ -508,11 +539,20 @@
         spot = spot + jnp.array([0, n_neg // 2], i32)[:, None, None]
         rows = item_table[flat_ids[spot.reshape(-1)]].reshape(2, n_item, n_part, width)
         parts = [(part[: n_item // 2], part[n_item // 2 :]) for part in rows]
+    pieces = gather_pieces(rows_in, "seq", seq_bits)
+    gates, queries = prepare(rows_in, w_uvqk)
+    groups = width // LANES
+    attended = [
+        attend(user_lengths, pieces, seq_order, queries, w_uvqk, first, count)
+        for first, count in ((0, groups // 4), (groups // 4, groups - groups // 4))
+    ]
     for step in range(2):
+        others = [swap(parts[half][1], "item", bits[-1 - step]) for half, bits in enumerate(bit_lists)]
+        if step == 1:
+            *others, attended[0] = lax.optimization_barrier((*others, attended[0]))
         for half, bits in enumerate(bit_lists):
-            bit, (kept, sent) = bits[-1 - step], parts[half]
-            other = swap(sent, "item", bit)
-            same = ((i ^ root) >> bit) & 1 == 0
+            kept, other = parts[half][0], others[half]
+            same = ((i ^ root) >> bits[-1 - step]) & 1 == 0
             cut = kept.shape[0] if step == 1 else kept.shape[0] // 2
             parts[half] = (jnp.where(same, kept[:cut], other[:cut]), jnp.where(same, kept[cut:], other[cut:]))
     both = jnp.stack([part[0] for part in parts])
@@ -540,36 +580,36 @@
         ]
         negatives = [jnp.concatenate([n.reshape(-1, width) for n in negatives], axis=0)]
 
-    pieces = gather_pieces(rows_in, "seq", seq_bits)
-    gates, queries, vk_hi, vk_lo, wo_hi, wo_lo = prepare(rows_in, w_uvqk, w_out)
-    groups = width // LANES
-    calls = 2
-    attended = [
-        attend(user_lengths, pieces, seq_order, queries, vk_hi, vk_lo, c * groups // calls, groups // calls)
-        for c in range(calls)
-    ]
-    own_outputs = project(block_mask, attended, gates, out_gain[None], wo_hi, wo_lo, rows_in, targets)
+    own_outputs = project(block_mask, attended, gates, out_gain[None], w_out, rows_in, targets)
     outputs = gather_pieces(own_outputs, "seq", seq_bits)
 
-    *panel, kept_rows, sent_rows, loss = loss_terms(outputs, negatives, plan, n_neg)
+    *panel, loss, grad, n_hi, n_lo = loss_terms(transpose_outputs(outputs), outputs, negatives, plan, n_neg)
+    kept_rows, sent_rows = event_rows(grad, n_hi, n_lo, n_seq)
     if not aligned:
         blocks = panel[0].reshape(n_seq, n_item, 2, n_dim // 2, n_neg).transpose(2, 1, 0, 3, 4)
         panel = []
         for half in range(2):
             mine = blocks[half][rel[half]][:, s ^ jnp.array(seq_order, i32)].reshape(n_item, -1, n_neg)
             panel += [mine[: n_item // 2], mine[n_item // 2 :]]
-    event_grad = reduce_steps(kept_rows, sent_rows, "seq", seq_bits[::-1])
-
-    kept, sent = [], []
-    for half, bits in enumerate(bit_lists):
-        k, t = panel[2 * half], panel[2 * half + 1]
-        for bit in bits[:-3:-1]:
-            got = swap(t, "item", bit)
-            cut = k.shape[0] // 2
-            k, t = k[:cut] + got[:cut], k[cut:] + got[cut:]
-        kept.append(k)
-        sent.append(t)
+
+    for step in range(2):
+        got = [swap(panel[2 * half + 1], "item", bits[-1 - step]) for half, bits in enumerate(bit_lists)]
+        if step == 0:
+            *got, kept_rows, sent_rows = lax.optimization_barrier((*got, kept_rows, sent_rows))
+        cut = panel[0].shape[0] // 2
+        panel = [
+            k[:cut] + g[:cut] if part == 0 else k[cut:] + g[cut:]
+            for k, g in zip(panel[::2], got)
+            for part in range(2)
+        ]
+    kept, sent = panel[::2], panel[1::2]
     total = reduce_steps(jnp.concatenate(kept, axis=1), jnp.concatenate(sent, axis=1), "item", shared[::-1])
+    for n, bit in enumerate(seq_bits[::-1]):
+        got_rows = swap(sent_rows, "seq", bit)
+        if n < n_seq.bit_length() - 2:
+            half = kept_rows.shape[0] // 2
+            sent_rows = kept_rows[half:] + got_rows[half:]
+            kept_rows = kept_rows[:half] + got_rows[:half]
     part = n_dim // 2
     halves = total[: n_seq * part], total[n_seq * part :]
     moved = []
@@ -589,24 +629,27 @@
         sent = [jnp.concatenate([sent[r], loss], axis=0) for r in range(n_item)]
 
     taken = [send(sent[r], "item", r) if r else sent[r] for r in range(n_item)]
-    cuts = [0, n_item // 2, 3 * n_item // 4, n_item]
+    near, far = list(range(1, n_item // 2)), list(range(n_item // 2, n_item))
+    which = [[0] + far[: len(far) // 2], far[len(far) // 2 :], near]
     table = []
-    for first, end in zip(cuts, cuts[1:]):
-        group = jnp.stack(taken[first:end])
-        if first == 0:
-            group, event_grad = lax.optimization_barrier((group, event_grad))
+    for members in which:
+        group = jnp.stack([taken[r] for r in members])
+        if members[0] == 0:
+            group, got_rows = lax.optimization_barrier((group, got_rows))
         table.append([group, swap(group, "seq", seq_bits[0])])
     for bit in seq_bits[1:]:
         table = [group + [swap(piece, "seq", bit) for piece in group] for group in table]
     if aligned:
-        table_grad, mean_loss = assemble(table, seq_order, n_item, n_dim, n_rows, group_len * n_item)
+        table_grad, mean_loss, event_grad = assemble(table, kept_rows, got_rows, seq_order, sum(which, []), n_item, n_dim, n_rows, group_len * n_item)
         mean_loss = mean_loss.reshape(())
     else:
         table = jnp.stack([jnp.concatenate(groups, axis=0) for groups in zip(*table)])
+        event_grad = kept_rows + got_rows
         mean_loss = jnp.sum(table[:, :, -1, 0]) / (group_len * n_item)
-        table = table[:, :, :-EXTRA].reshape(n_seq, n_item, -1, n_dim, LANES)[:, i ^ jnp.arange(n_item, dtype=i32)]
+        table = table[:, :, :-EXTRA].reshape(n_seq, n_item, -1, n_dim, LANES)
+        table = true_order(table.swapaxes(0, 1), sum(which, []), i).swapaxes(0, 1)
         table_grad = true_order(table, seq_order, s).transpose(2, 4, 0, 1, 3).reshape(n_rows, width)
-    return (mean_loss, event_grad[None], table_grad)
+    return (mean_loss, event_grad, table_grad)
 
 
 def solution(mesh):

time: 115 us -> 113 us (0.983)
  starting transfers between devices: 35.6 us -> 41.8 us
  waiting for transfers between devices: 44.8 us -> 39.7 us
  Pallas kernels: 29.1 us -> 25 us
  local copies, waits for them, and re-layouts: 1.64 us -> 2.85 us
    ppermute x31, waiting for transfers between devices: 38.8 us -> 32.8 us  [swap(): return lax.ppermute(block, axis, [(i, i ^ 1 << bit) for i in range(size)])]
    pallas_call x4 -> x6, Pallas kernels: 14.9 us -> 10.7 us  [the longest x1 3.2 us: loss_terms(): pl.pallas_call(functools.partial(loss_kernel, plan), in_specs=[vmem] * (2...]
    ppermute x10, starting transfers between devices: 10.7 us -> 14.4 us  [send(): return lax.ppermute(block, axis, [(i, i ^ r) for i in range(size)])]
    ppermute x31, starting transfers between devices: 24.9 us -> 27.5 us  [swap(): return lax.ppermute(block, axis, [(i, i ^ 1 << bit) for i in range(size)])]
    unnamed x32 -> x20, local copies, waits for them, and re-layouts: 1.02 us -> 2.23 us
  transfers between devices with their start and end apart: 41 -> 41, of which waited for: 20 -> 20; matrix products, arithmetic and copies ran while one was open for 2% -> 1% of each run, Pallas kernels for 16% -> 17%
where the time goes in v6:
time: 113 us; the launch traced here: 112 us
  starting transfers between devices  41.8 us (37%)
  waiting for transfers between devices  39.7 us (35%)
  Pallas kernels  25 us (22%)
  local copies, waits for them, and re-layouts  2.85 us (3%)
  between operations  2.27 us (2%)
    ppermute x31, waiting for transfers between devices, swap(): return lax.ppermute(block, axis, [(i, i ^ 1 << bit) for i in range(size)])  32.8 us
    ppermute x31, starting transfers between devices, swap(): return lax.ppermute(block, axis, [(i, i ^ 1 << bit) for i in range(size)])  27.5 us
    ppermute x10, starting transfers between devices, send(): return lax.ppermute(block, axis, [(i, i ^ r) for i in range(size)])  14.4 us
    pallas_call x2, Pallas kernels, attend(): pl.pallas_call(functools.partial(attend_kernel, order, n_seq), grid=(coun...  10.1 us
    ppermute x10, waiting for transfers between devices, send(): return lax.ppermute(block, axis, [(i, i ^ r) for i in range(size)])  6.88 us
    pallas_call x1, Pallas kernels, pick_rows(): pl.pallas_call(functools.partial(pick_kernel, plan), in_specs=[pl.BlockSp...  3.59 us
    pallas_call x1, Pallas kernels, loss_terms(): pl.pallas_call(functools.partial(loss_kernel, plan), in_specs=[vmem] * (2...  3.2 us
    pallas_call x1, Pallas kernels, assemble(): pl.pallas_call(functools.partial(assemble_kernel, order, members, n_item,...  2.54 us
  transfers between devices with their start and end apart: 41, of which 20 were waited for; matrix products, arithmetic and copies ran while one was open for 1% of the time, Pallas kernels for 17%

profile of v6, /device:TPU:0, one launch (start us, length us, event | category | flops | bytes accessed | tf_op | source)
XLA Modules:
  0.0 112.1 jit_solution(9935828682258933830)
XLA Ops:
  0.7 3.0 %collective-permute-start.4 = (f32[128,512]{1,0:T(8,128)}, f32[128,512]{1,0:T(8,128)S(1)}, u32[]{:S(2)}, u32[]{:S(2)}) collective-permute-start(f32[128,512]{1,0:T(8,128)} %bitcast.42), channel_id=1, source_target_pairs={{0,16},{8,24},{16,0},{24,8},{1,17},{9,25},{17,1},{25,9},{2,18},{10... | collective-permute-start | bytes 786440 | tf_op jit(solution)/shard_map/ppermute | solution.py:26
  3.7 3.6 %pick_rows.1 = (f32[4,32,512]{2,1,0:T(8,128)}, f32[4,32,512]{2,1,0:T(8,128)}, f32[4,32,512]{2,1,0:T(8,128)}, f32[4,32,512]{2,1,0:T(8,128)}) custom-call(s32[4,512]{1,0:T(4,128)} %ids.1, f32[1024,512]{1,0:T(8,128)} %table_hbm.1), custom_call_target="tpu_custom_call" | custom-call | flops 1073741824 | bytes 2097152 | tf_op jit(solution)/shard_map/pick_rows/pallas_call | solution.py:129
  7.3 1.6 %collective-permute-start = (f32[4,32,512]{2,1,0:T(8,128)}, f32[4,32,512]{2,1,0:T(8,128)S(1)}, u32[]{:S(2)}, u32[]{:S(2)}) collective-permute-start(f32[4,32,512]{2,1,0:T(8,128)} %get-tuple-element.42), channel_id=1, source_target_pairs={{0,1},{1,0},{2,3},{3,2},{4,5},{5,4},{6,7},{7,6},{8,9},{9,8},{10,11... | collective-permute-start | bytes 786440 | tf_op jit(solution)/shard_map/ppermute | solution.py:26
  8.8 1.6 %collective-permute-start.2 = (f32[4,32,512]{2,1,0:T(8,128)}, f32[4,32,512]{2,1,0:T(8,128)S(1)}, u32[]{:S(2)}, u32[]{:S(2)}) collective-permute-start(f32[4,32,512]{2,1,0:T(8,128)} %get-tuple-element.44), channel_id=1, source_target_pairs={{0,2},{1,3},{2,0},{3,1},{4,6},{5,7},{6,4},{7,5},{8,10},{9,11},{10,... | collective-permute-start | bytes 786440 | tf_op jit(solution)/shard_map/ppermute | solution.py:26
  11.1 0.6 dynamic_slice.3
  12.3 2.2 %copy-done = f32[512,2048]{1,0:T(8,128)S(1)} copy-done((f32[512,2048]{1,0:T(8,128)S(1)}, f32[512,2048]{1,0:T(8,128)}, u32[]{:S(2)}) %copy-start) | copy-done | bytes 4194328
  14.5 1.6 %prepare.1 = (f32[128,512]{1,0:T(8,128)S(1)}, f32[128,512]{1,0:T(8,128)S(1)}) custom-call(f32[128,512]{1,0:T(8,128)S(1)} %bitcast.44, f32[512,2048]{1,0:T(8,128)S(1)} %copy-done, f32[512,2048]{1,0:T(8,128)S(1)} %copy-done), custom_call_target="tpu_custom_call" | custom-call | flops 402653184 | bytes 2097152 | tf_op jit(solution)/shard_map/prepare/pallas_call | solution.py:155
  16.2 0.3 collective-permute-start.6
  16.5 0.5 collective-permute-start.1
  17.0 0.8 collective-permute-done.2
  17.8 0.8 collective-permute-start.3
  18.6 2.6 %attend.2.refs_0_ = f32[128,128]{1,0:T(8,128)S(1)} custom-call(s32[1,4]{1,0:T(1,128)S(1)} %copy-done.4, f32[128,512]{1,0:T(8,128)S(1)} %bitcast.45, f32[128,512]{1,0:T(8,128)S(1)} %collective-permute-done.4.refs_1_, f32[128,512]{1,0:T(8,128)S(1)} %collective-permute-done.5.refs_2_, f32[128,512]{1,0:T(8,128)S(1)} %collective-permute-done.6.refs_3_, ...), custom_call_target="tpu_custom_call" | custom-call | flops 2000000000 | bytes 2097152 | tf_op jit(solution)/shard_map/attend/pallas_call | solution.py:227
  21.2 1.0 collective-permute-done.1
  22.3 0.7 collective-permute-done.3
  23.1 2.7 %collective-permute-start.10 = (f32[2,2,32,512]{3,2,1,0:T(8,128)S(1)}, f32[2,2,32,512]{3,2,1,0:T(8,128)S(1)}, u32[]{:S(2)}, u32[]{:S(2)}) collective-permute-start(f32[2,2,32,512]{3,2,1,0:T(8,128)S(1)} %pad_maximum_fusion), channel_id=1, source_target_pairs={{0,4},{1,5},{2,6},{3,7},{4,0},{5,1},{6,2},{7,3},{8,12},{9,13},{10,... | collective-permute-start | bytes 786440 | tf_op jit(solution)/shard_map/ppermute | solution.py:26
  25.8 7.4 %attend.3.refs_1_ = f32[128,384]{1,0:T(8,128)S(1)} custom-call(s32[1,4]{1,0:T(1,128)S(1)} %copy-done.4, f32[128,512]{1,0:T(8,128)S(1)} %bitcast.46, f32[128,512]{1,0:T(8,128)S(1)} %collective-permute-done.4.refs_1_, f32[128,512]{1,0:T(8,128)S(1)} %collective-permute-done.5.refs_2_, f32[128,512]{1,0:T(8,128)S(1)} %collective-permute-done.6.refs_3_, ...), custom_call_target="tpu_custom_call" | custom-call | flops 6000000000 | bytes 2097152 | tf_op jit(solution)/shard_map/attend/pallas_call | solution.py:227
  33.3 0.6 project.1.refs_0_
  33.9 0.6 collective-permute-start.7
  34.4 2.3 %collective-permute-done.10 = f32[2,2,32,512]{3,2,1,0:T(8,128)S(1)} collective-permute-done((f32[2,2,32,512]{3,2,1,0:T(8,128)S(1)}, f32[2,2,32,512]{3,2,1,0:T(8,128)S(1)}, u32[]{:S(2)}, u32[]{:S(2)}) %collective-permute-start.10) | collective-permute-done | bytes 262176 | tf_op jit(solution)/shard_map/ppermute | solution.py:26
  36.8 0.7 collective-permute-start.11
  37.6 0.5 collective-permute-start.13
  38.0 3.0 %collective-permute-done.7.refs_1_ = f32[136,512]{1,0:T(8,128)S(1)} collective-permute-done((f32[136,512]{1,0:T(8,128)S(1)}, f32[136,512]{1,0:T(8,128)S(1)}, u32[]{:S(2)}, u32[]{:S(2)}) %collective-permute-start.7) | collective-permute-done | bytes 278560 | tf_op jit(solution)/shard_map/ppermute | solution.py:26
  41.0 0.8 collective-permute-done.11
  41.9 0.5 collective-permute-start.12
  42.3 0.4 collective-permute-done.13
  42.8 1.2 %collective-permute-start.14 = (f32[4,32,512]{2,1,0:T(8,128)S(1)}, f32[4,32,512]{2,1,0:T(8,128)S(1)}, u32[]{:S(2)}, u32[]{:S(2)}) collective-permute-start(f32[4,32,512]{2,1,0:T(8,128)S(1)} %pad_maximum_fusion.2), channel_id=1, source_target_pairs={{0,2},{1,3},{2,0},{3,1},{4,6},{5,7},{6,4},{7,5},{8,10},{9,11},{10,... | collective-permute-start | bytes 786440 | tf_op jit(solution)/shard_map/ppermute | solution.py:26
  44.0 0.3 transpose_outputs.1
  44.4 5.5 %collective-permute-done.12 = f32[4,32,512]{2,1,0:T(8,128)S(1)} collective-permute-done((f32[4,32,512]{2,1,0:T(8,128)S(1)}, f32[4,32,512]{2,1,0:T(8,128)S(1)}, u32[]{:S(2)}, u32[]{:S(2)}) %collective-permute-start.12) | collective-permute-done | bytes 262176 | tf_op jit(solution)/shard_map/ppermute | solution.py:26
  49.9 0.2 collective-permute-done.14
  50.1 3.2 %loss_terms.1 = (f32[4,32,512]{2,1,0:T(8,128)S(1)}, f32[4,32,512]{2,1,0:T(8,128)S(1)}, f32[4,32,512]{2,1,0:T(8,128)S(1)}, f32[4,32,512]{2,1,0:T(8,128)S(1)}, f32...) custom-call(bf16[512,512]{1,0:T(8,128)(2,1)S(1)} %get-tuple-element.48., ...), custom_call_target="tpu_custom_call" | custom-call | flops 1610612736 | bytes 4194304 | tf_op jit(solution)/shard_map/loss_terms/pallas_call | solution.py:366
  53.3 1.7 %collective-permute-start.15 = (f32[4,32,512]{2,1,0:T(8,128)S(1)}, f32[4,32,512]{2,1,0:T(8,128)S(1)}, u32[]{:S(2)}, u32[]{:S(2)}) collective-permute-start(f32[4,32,512]{2,1,0:T(8,128)S(1)} %get-tuple-element.52), channel_id=1, source_target_pairs={{0,1},{1,0},{2,3},{3,2},{4,5},{5,4},{6,7},{7,6},{8,9},{9,8},{10,11... | collective-permute-start | bytes 786440 | tf_op jit(solution)/shard_map/ppermute | solution.py:26
  55.0 1.6 %collective-permute-start.16 = (f32[4,32,512]{2,1,0:T(8,128)S(1)}, f32[4,32,512]{2,1,0:T(8,128)S(1)}, u32[]{:S(2)}, u32[]{:S(2)}) collective-permute-start(f32[4,32,512]{2,1,0:T(8,128)S(1)} %get-tuple-element.53), channel_id=1, source_target_pairs={{0,2},{1,3},{2,0},{3,1},{4,6},{5,7},{6,4},{7,5},{8,10},{9,11},{10,... | collective-permute-start | bytes 786440 | tf_op jit(solution)/shard_map/ppermute | solution.py:26
  56.5 1.0 event_rows.1
  57.6 2.6 %collective-permute-done.15 = f32[4,32,512]{2,1,0:T(8,128)S(1)} collective-permute-done((f32[4,32,512]{2,1,0:T(8,128)S(1)}, f32[4,32,512]{2,1,0:T(8,128)S(1)}, u32[]{:S(2)}, u32[]{:S(2)}) %collective-permute-start.15) | collective-permute-done | bytes 262176 | tf_op jit(solution)/shard_map/ppermute | solution.py:26
  60.2 1.6 %collective-permute-done.16 = f32[4,32,512]{2,1,0:T(8,128)S(1)} collective-permute-done((f32[4,32,512]{2,1,0:T(8,128)S(1)}, f32[4,32,512]{2,1,0:T(8,128)S(1)}, u32[]{:S(2)}, u32[]{:S(2)}) %collective-permute-start.16) | collective-permute-done | bytes 262176 | tf_op jit(solution)/shard_map/ppermute | solution.py:26
  61.8 0.6 collective-permute-start.19
  62.4 1.8 %collective-permute-start.18 = (f32[2,32,512]{2,1,0:T(8,128)S(1)}, f32[2,32,512]{2,1,0:T(8,128)S(1)}, u32[]{:S(2)}, u32[]{:S(2)}) collective-permute-start(f32[2,32,512]{2,1,0:T(8,128)S(1)} %get-tuple-element.82), channel_id=1, source_target_pairs={{0,2},{1,3},{2,0},{3,1},{4,6},{5,7},{6,4},{7,5},{8,10},{9,11},{10,... | collective-permute-start | bytes 393224 | tf_op jit(solution)/shard_map/ppermute | solution.py:26
  64.2 2.6 %collective-permute-done.19 = f32[2,32,512]{2,1,0:T(8,128)S(1)} collective-permute-done((f32[2,32,512]{2,1,0:T(8,128)S(1)}, f32[2,32,512]{2,1,0:T(8,128)S(1)}, u32[]{:S(2)}, u32[]{:S(2)}) %collective-permute-start.19) | collective-permute-done | bytes 131104 | tf_op jit(solution)/shard_map/ppermute | solution.py:26
  66.9 0.9 collective-permute-done.18
  67.8 3.4 %collective-permute-start.20 = (f32[1,64,512]{2,1,0:T(8,128)S(1)}, f32[1,64,512]{2,1,0:T(8,128)S(1)}, u32[]{:S(2)}, u32[]{:S(2)}) collective-permute-start(f32[1,64,512]{2,1,0:T(8,128)S(1)} %pad_maximum_fusion.6), channel_id=1, source_target_pairs={{0,4},{1,5},{2,6},{3,7},{4,0},{5,1},{6,2},{7,3},{8,12},{9,13},{10,... | collective-permute-start | bytes 393224 | tf_op jit(solution)/shard_map/ppermute | solution.py:26
  71.2 2.9 %collective-permute-done.20 = f32[1,64,512]{2,1,0:T(8,128)S(1)} collective-permute-done((f32[1,64,512]{2,1,0:T(8,128)S(1)}, f32[1,64,512]{2,1,0:T(8,128)S(1)}, u32[]{:S(2)}, u32[]{:S(2)}) %collective-permute-start.20) | collective-permute-done | bytes 131104 | tf_op jit(solution)/shard_map/ppermute | solution.py:26
  74.2 0.6 collective-permute-start.21
  74.8 1.6 %collective-permute-start.23 = (f32[16,512]{1,0:T(8,128)S(1)}, f32[16,512]{1,0:T(8,128)S(1)}, u32[]{:S(2)}, u32[]{:S(2)}) collective-permute-start(f32[16,512]{1,0:T(8,128)S(1)} %pad_maximum_fusion.10), channel_id=1, source_target_pairs={{0,24},{8,16},{16,8},{24,0},{1,25},{9,17},{17,9},{25,1},{2,26},{10... | collective-permute-start | bytes 98312 | tf_op jit(solution)/shard_map/ppermute | solution.py:31
  76.4 2.1 %collective-permute-done.21.refs_1_ = f32[16,512]{1,0:T(8,128)S(1)} collective-permute-done((f32[16,512]{1,0:T(8,128)S(1)}, f32[16,512]{1,0:T(8,128)S(1)}, u32[]{:S(2)}, u32[]{:S(2)}) %collective-permute-start.21) | collective-permute-done | bytes 32800 | tf_op jit(solution)/shard_map/ppermute | solution.py:31
  78.6 2.0 %spread_rows.1 = (f32[136,128]{1,0:T(8,128)S(1)}, f32[136,128]{1,0:T(8,128)S(1)}, f32[136,128]{1,0:T(8,128)S(1)}, f32[136,128]{1,0:T(8,128)S(1)}, f32[136,128]{1...) custom-call(s32[4]{0:T(128)S(1)} %copy-done.7, s32[4,512]{1,0:T(4,128)S(1)} %copy-done.6, ...), custom_call_target="tpu_custom_call" | custom-call | flops 134217728 | bytes 2097152 | tf_op jit(solution)/shard_map/spread_rows/pallas_call | solution.py:438
  80.5 1.3 %collective-permute-start.35 = (f32[136,128]{1,0:T(8,128)S(1)}, f32[136,128]{1,0:T(8,128)S(1)}, u32[]{:S(2)}, u32[]{:S(2)}) collective-permute-start(f32[136,128]{1,0:T(8,128)S(1)} %get-tuple-element.73), channel_id=1, source_target_pairs={{0,1},{1,0},{2,3},{3,2},{4,5},{5,4},{6,7},{7,6},{8,9},{9,8},{10,11... | collective-permute-start | bytes 208904 | tf_op jit(solution)/shard_map/ppermute | solution.py:31
  81.9 2.5 %collective-permute-start.36 = (f32[136,128]{1,0:T(8,128)S(1)}, f32[136,128]{1,0:T(8,128)S(1)}, u32[]{:S(2)}, u32[]{:S(2)}) collective-permute-start(f32[136,128]{1,0:T(8,128)S(1)} %get-tuple-element.74), channel_id=1, source_target_pairs={{0,2},{1,3},{2,0},{3,1},{4,6},{5,7},{6,4},{7,5},{8,10},{9,11},{10,... | collective-permute-start | bytes 208904 | tf_op jit(solution)/shard_map/ppermute | solution.py:31
  84.4 1.2 %collective-permute-start.26 = (f32[1,128,512]{2,1,0:T(8,128)S(1)}, f32[1,128,512]{2,1,0:T(8,128)S(1)}, u32[]{:S(2)}, u32[]{:S(2)}) collective-permute-start(f32[1,128,512]{2,1,0:T(8,128)S(1)} %get-tuple-element.79), channel_id=1, source_target_pairs={{0,16},{8,24},{16,0},{24,8},{1,17},{9,25},{17,1},{25,9},{2,18},{10... | collective-permute-start | bytes 786440 | tf_op jit(solution)/shard_map/ppermute | solution.py:26
  85.7 3.0 %collective-permute-start.24 = (f32[136,128]{1,0:T(8,128)S(1)}, f32[136,128]{1,0:T(8,128)S(1)}, u32[]{:S(2)}, u32[]{:S(2)}) collective-permute-start(f32[136,128]{1,0:T(8,128)S(1)} %get-tuple-element.67), channel_id=1, source_target_pairs={{0,4},{1,5},{2,6},{3,7},{4,0},{5,1},{6,2},{7,3},{8,12},{9,13},{10,... | collective-permute-start | bytes 208904 | tf_op jit(solution)/shard_map/ppermute | solution.py:31
  88.7 0.8 collective-permute-start.25
  89.5 3.8 %collective-permute-start.30 = (f32[136,128]{1,0:T(8,128)S(1)}, f32[136,128]{1,0:T(8,128)S(1)}, u32[]{:S(2)}, u32[]{:S(2)}) collective-permute-start(f32[136,128]{1,0:T(8,128)S(1)} %get-tuple-element.71), channel_id=1, source_target_pairs={{0,6},{1,7},{2,4},{3,5},{4,2},{5,3},{6,0},{7,1},{8,14},{9,15},{10,... | collective-permute-start | bytes 208904 | tf_op jit(solution)/shard_map/ppermute | solution.py:31
  93.3 0.7 collective-permute-start.31
  94.1 0.9 collective-permute-start.38
  95.0 3.9 %collective-permute-done.25 = f32[136,128]{1,0:T(8,128)S(1)} collective-permute-done((f32[136,128]{1,0:T(8,128)S(1)}, f32[136,128]{1,0:T(8,128)S(1)}, u32[]{:S(2)}, u32[]{:S(2)}) %collective-permute-start.25) | collective-permute-done | bytes 69664 | tf_op jit(solution)/shard_map/ppermute | solution.py:31
  98.9 0.7 collective-permute-start.27
  99.6 0.9 collective-permute-done.31
  100.5 0.9 collective-permute-start.32
  101.5 0.2 collective-permute-start.39
  101.6 0.3 collective-permute-start.40
  102.0 0.2 collective-permute-start.28
  102.1 4.6 %collective-permute-done.27.refs_1_ = f32[3,136,128]{2,1,0:T(8,128)S(1)} collective-permute-done((f32[3,136,128]{2,1,0:T(8,128)S(1)}, f32[3,136,128]{2,1,0:T(8,128)S(1)}, u32[]{:S(2)}, u32[]{:S(2)}) %collective-permute-start.27) | collective-permute-done | bytes 208928 | tf_op jit(solution)/shard_map/ppermute | solution.py:26
  106.7 1.5 %collective-permute-done.32.refs_5_ = f32[2,136,128]{2,1,0:T(8,128)S(1)} collective-permute-done((f32[2,136,128]{2,1,0:T(8,128)S(1)}, f32[2,136,128]{2,1,0:T(8,128)S(1)}, u32[]{:S(2)}, u32[]{:S(2)}) %collective-permute-start.32) | collective-permute-done | bytes 139296 | tf_op jit(solution)/shard_map/ppermute | solution.py:26
  108.2 1.4 %collective-permute-done.34.refs_7_ = f32[2,136,128]{2,1,0:T(8,128)S(1)} collective-permute-done((f32[2,136,128]{2,1,0:T(8,128)S(1)}, f32[2,136,128]{2,1,0:T(8,128)S(1)}, u32[]{:S(2)}, u32[]{:S(2)}) %collective-permute-start.34) | collective-permute-done | bytes 139296 | tf_op jit(solution)/shard_map/ppermute | solution.py:26
  109.6 2.5 %assemble.1 = (f32[1024,512]{1,0:T(8,128)}, f32[1,1]{1,0:T(1,128)}, f32[1,128,512]{2,1,0:T(8,128)}) custom-call(f32[1,128,512]{2,1,0:T(8,128)S(1)} %get-tuple-element.80.kept, f32[1,128,512]{2,1,0:T(8,128)S(1)} %collective-permute-done.26.got, f32[3,136,128]{2,1,0:T(8,128)S(1)} %pad_maximum_fusion.3.refs_0_, ...), custom_call_target="tpu_custom_call" | custom-call | bytes 4194304 | tf_op jit(solution)/shard_map/assemble/pallas_call | solution.py:483
  (73 shorter events, 0.7 us)
Async XLA Ops:
  0.6 8.2 %copy-start.1 = (f32[1,128,512]{2,1,0:T(8,128)S(1)}, f32[1,128,512]{2,1,0:T(8,128)}, u32[]{:S(2)}) copy-start(f32[1,128,512]{2,1,0:T(8,128)} %param.10) | copy-start | bytes 786436
  0.6 10.4 %copy-start.7 = (s32[4]{0:T(128)S(1)}, s32[4]{0:T(128)}, u32[]{:S(2)}) copy-start(s32[4]{0:T(128)} %owner.1) | copy-start | bytes 52
  0.7 15.5 %collective-permute-start.4 = (f32[128,512]{1,0:T(8,128)}, f32[128,512]{1,0:T(8,128)S(1)}, u32[]{:S(2)}, u32[]{:S(2)}) collective-permute-start(f32[128,512]{1,0:T(8,128)} %bitcast.42), channel_id=1, source_target_pairs={{0,16},{8,24},{16,0},{24,8},{1,17},{9,25},{17,1},{25,9},{2,18},{10... | collective-permute-start | bytes 786440 | tf_op jit(solution)/shard_map/ppermute | solution.py:26
  7.3 9.2 %collective-permute-start = (f32[4,32,512]{2,1,0:T(8,128)}, f32[4,32,512]{2,1,0:T(8,128)S(1)}, u32[]{:S(2)}, u32[]{:S(2)}) collective-permute-start(f32[4,32,512]{2,1,0:T(8,128)} %get-tuple-element.42), channel_id=1, source_target_pairs={{0,1},{1,0},{2,3},{3,2},{4,5},{5,4},{6,7},{7,6},{8,9},{9,8},{10,11... | collective-permute-start | bytes 786440 | tf_op jit(solution)/shard_map/ppermute | solution.py:26
  8.8 9.7 %collective-permute-start.5 = (f32[128,512]{1,0:T(8,128)S(1)}, f32[128,512]{1,0:T(8,128)S(1)}, u32[]{:S(2)}, u32[]{:S(2)}) collective-permute-start(f32[128,512]{1,0:T(8,128)S(1)} %bitcast.43), channel_id=1, source_target_pairs={{0,8},{8,0},{16,24},{24,16},{1,9},{9,1},{17,25},{25,17},{2,10},{10... | collective-permute-start | bytes 786440 | tf_op jit(solution)/shard_map/ppermute | solution.py:26
  8.8 8.9 %collective-permute-start.2 = (f32[4,32,512]{2,1,0:T(8,128)}, f32[4,32,512]{2,1,0:T(8,128)S(1)}, u32[]{:S(2)}, u32[]{:S(2)}) collective-permute-start(f32[4,32,512]{2,1,0:T(8,128)} %get-tuple-element.44), channel_id=1, source_target_pairs={{0,2},{1,3},{2,0},{3,1},{4,6},{5,7},{6,4},{7,5},{8,10},{9,11},{10,... | collective-permute-start | bytes 786440 | tf_op jit(solution)/shard_map/ppermute | solution.py:26
  12.3 2.2 %copy-start = (f32[512,2048]{1,0:T(8,128)S(1)}, f32[512,2048]{1,0:T(8,128)}, u32[]{:S(2)}) copy-start(f32[512,2048]{1,0:T(8,128)} %refs_6_.4) | copy-start | bytes 12582916
  14.5 1.9 %copy-start.8 = (f32[4,32,512]{2,1,0:T(8,128)S(1)}, f32[4,32,512]{2,1,0:T(8,128)}, u32[]{:S(2)}) copy-start(f32[4,32,512]{2,1,0:T(8,128)} %get-tuple-element.41) | copy-start | bytes 786436
  14.5 3.3 %copy-start.9 = (f32[4,32,512]{2,1,0:T(8,128)S(1)}, f32[4,32,512]{2,1,0:T(8,128)}, u32[]{:S(2)}) copy-start(f32[4,32,512]{2,1,0:T(8,128)} %get-tuple-element.43) | copy-start | bytes 786436
  14.5 4.1 %copy-start.4 = (s32[1,4]{1,0:T(1,128)S(1)}, s32[1,4]{1,0:T(1,128)}, u32[]{:S(2)}) copy-start(s32[1,4]{1,0:T(1,128)} %lengths.3) | copy-start | bytes 52
  16.2 2.4 %collective-permute-start.6 = (f32[128,512]{1,0:T(8,128)S(1)}, f32[128,512]{1,0:T(8,128)S(1)}, u32[]{:S(2)}, u32[]{:S(2)}) collective-permute-start(f32[128,512]{1,0:T(8,128)S(1)} %collective-permute-done.4.refs_1_), channel_id=1, source_target_pairs={{0,8},{8,0},{16,24},{24,16},{1,9},{9,1},{17,25},{25,17},{2,10},{10... | collective-permute-start | bytes 786440 | tf_op jit(solution)/shard_map/ppermute | solution.py:26
  16.5 5.8 %collective-permute-start.1 = (f32[2,32,512]{2,1,0:T(8,128)S(1)}, f32[2,32,512]{2,1,0:T(8,128)S(1)}, u32[]{:S(2)}, u32[]{:S(2)}) collective-permute-start(f32[2,32,512]{2,1,0:T(8,128)S(1)} %slice_select_fusion.3), channel_id=1, source_target_pairs={{0,2},{1,3},{2,0},{3,1},{4,6},{5,7},{6,4},{7,5},{8,10},{9,11},{10,... | collective-permute-start | bytes 393224 | tf_op jit(solution)/shard_map/ppermute | solution.py:26
  17.8 5.2 %collective-permute-start.3 = (f32[2,32,512]{2,1,0:T(8,128)S(1)}, f32[2,32,512]{2,1,0:T(8,128)S(1)}, u32[]{:S(2)}, u32[]{:S(2)}) collective-permute-start(f32[2,32,512]{2,1,0:T(8,128)S(1)} %slice_select_fusion.2), channel_id=1, source_target_pairs={{0,1},{1,0},{2,3},{3,2},{4,5},{5,4},{6,7},{7,6},{8,9},{9,8},{10,11... | collective-permute-start | bytes 393224 | tf_op jit(solution)/shard_map/ppermute | solution.py:26
  23.1 10.1 %copy-start.2 = (f32[512,512]{1,0:T(8,128)S(1)}, f32[512,512]{1,0:T(8,128)}, u32[]{:S(2)}) copy-start(f32[512,512]{1,0:T(8,128)} %refs_4_.1) | copy-start | bytes 3145732
  23.1 10.1 %copy-start.3 = (f32[512]{0:T(512)S(1)}, f32[512]{0:T(512)}, u32[]{:S(2)}) copy-start(f32[512]{0:T(512)} %param.12) | copy-start | bytes 6148
  23.1 10.1 %copy-start.5 = (s32[1,128]{1,0:T(1,128)S(1)}, s32[1,128]{1,0:T(1,128)}, u32[]{:S(2)}) copy-start(s32[1,128]{1,0:T(1,128)} %refs_6_.5) | copy-start | bytes 1540
  23.1 13.6 %collective-permute-start.10 = (f32[2,2,32,512]{3,2,1,0:T(8,128)S(1)}, f32[2,2,32,512]{3,2,1,0:T(8,128)S(1)}, u32[]{:S(2)}, u32[]{:S(2)}) collective-permute-start(f32[2,2,32,512]{3,2,1,0:T(8,128)S(1)} %pad_maximum_fusion), channel_id=1, source_target_pairs={{0,4},{1,5},{2,6},{3,7},{4,0},{5,1},{6,2},{7,3},{8,12},{9,13},{10,... | collective-permute-start | bytes 786440 | tf_op jit(solution)/shard_map/ppermute | solution.py:26
  33.9 7.2 %collective-permute-start.7 = (f32[136,512]{1,0:T(8,128)S(1)}, f32[136,512]{1,0:T(8,128)S(1)}, u32[]{:S(2)}, u32[]{:S(2)}) collective-permute-start(f32[136,512]{1,0:T(8,128)S(1)} %project.1.refs_0_), channel_id=1, source_target_pairs={{0,16},{8,24},{16,0},{24,8},{1,17},{9,25},{17,1},{25,9},{2,18},{10... | collective-permute-start | bytes 835592 | tf_op jit(solution)/shard_map/ppermute | solution.py:26
  36.8 5.0 %collective-permute-start.11 = (f32[2,32,512]{2,1,0:T(8,128)S(1)}, f32[2,32,512]{2,1,0:T(8,128)S(1)}, u32[]{:S(2)}, u32[]{:S(2)}) collective-permute-start(f32[2,32,512]{2,1,0:T(8,128)S(1)} %maximum_select_fusion), channel_id=1, source_target_pairs={{0,2},{1,3},{2,0},{3,1},{4,6},{5,7},{6,4},{7,5},{8,10},{9,11},{10,... | collective-permute-start | bytes 393224 | tf_op jit(solution)/shard_map/ppermute | solution.py:26
  37.6 5.2 %collective-permute-start.13 = (f32[2,32,512]{2,1,0:T(8,128)S(1)}, f32[2,32,512]{2,1,0:T(8,128)S(1)}, u32[]{:S(2)}, u32[]{:S(2)}) collective-permute-start(f32[2,32,512]{2,1,0:T(8,128)S(1)} %maximum_select_fusion.1), channel_id=1, source_target_pairs={{0,1},{1,0},{2,3},{3,2},{4,5},{5,4},{6,7},{7,6},{8,9},{9,8},{10,11... | collective-permute-start | bytes 393224 | tf_op jit(solution)/shard_map/ppermute | solution.py:26
  38.0 6.0 %collective-permute-start.8 = (f32[136,512]{1,0:T(8,128)S(1)}, f32[136,512]{1,0:T(8,128)S(1)}, u32[]{:S(2)}, u32[]{:S(2)}) collective-permute-start(f32[136,512]{1,0:T(8,128)S(1)} %project.1.refs_0_), channel_id=1, source_target_pairs={{0,8},{8,0},{16,24},{24,16},{1,9},{9,1},{17,25},{25,17},{2,10},{10... | collective-permute-start | bytes 835592 | tf_op jit(solution)/shard_map/ppermute | solution.py:26
  41.0 3.0 %collective-permute-start.9 = (f32[136,512]{1,0:T(8,128)S(1)}, f32[136,512]{1,0:T(8,128)S(1)}, u32[]{:S(2)}, u32[]{:S(2)}) collective-permute-start(f32[136,512]{1,0:T(8,128)S(1)} %collective-permute-done.7.refs_1_), channel_id=1, source_target_pairs={{0,8},{8,0},{16,24},{24,16},{1,9},{9,1},{17,25},{25,17},{2,10},{10... | collective-permute-start | bytes 835592 | tf_op jit(solution)/shard_map/ppermute | solution.py:26
  41.9 8.0 %collective-permute-start.12 = (f32[4,32,512]{2,1,0:T(8,128)S(1)}, f32[4,32,512]{2,1,0:T(8,128)S(1)}, u32[]{:S(2)}, u32[]{:S(2)}) collective-permute-start(f32[4,32,512]{2,1,0:T(8,128)S(1)} %pad_maximum_fusion.1), channel_id=1, source_target_pairs={{0,1},{1,0},{2,3},{3,2},{4,5},{5,4},{6,7},{7,6},{8,9},{9,8},{10,11... | collective-permute-start | bytes 786440 | tf_op jit(solution)/shard_map/ppermute | solution.py:26
  42.8 7.3 %collective-permute-start.14 = (f32[4,32,512]{2,1,0:T(8,128)S(1)}, f32[4,32,512]{2,1,0:T(8,128)S(1)}, u32[]{:S(2)}, u32[]{:S(2)}) collective-permute-start(f32[4,32,512]{2,1,0:T(8,128)S(1)} %pad_maximum_fusion.2), channel_id=1, source_target_pairs={{0,2},{1,3},{2,0},{3,1},{4,6},{5,7},{6,4},{7,5},{8,10},{9,11},{10,... | collective-permute-start | bytes 786440 | tf_op jit(solution)/shard_map/ppermute | solution.py:26
  53.3 6.9 %collective-permute-start.15 = (f32[4,32,512]{2,1,0:T(8,128)S(1)}, f32[4,32,512]{2,1,0:T(8,128)S(1)}, u32[]{:S(2)}, u32[]{:S(2)}) collective-permute-start(f32[4,32,512]{2,1,0:T(8,128)S(1)} %get-tuple-element.52), channel_id=1, source_target_pairs={{0,1},{1,0},{2,3},{3,2},{4,5},{5,4},{6,7},{7,6},{8,9},{9,8},{10,11... | collective-permute-start | bytes 786440 | tf_op jit(solution)/shard_map/ppermute | solution.py:26
  55.0 6.8 %collective-permute-start.16 = (f32[4,32,512]{2,1,0:T(8,128)S(1)}, f32[4,32,512]{2,1,0:T(8,128)S(1)}, u32[]{:S(2)}, u32[]{:S(2)}) collective-permute-start(f32[4,32,512]{2,1,0:T(8,128)S(1)} %get-tuple-element.53), channel_id=1, source_target_pairs={{0,2},{1,3},{2,0},{3,1},{4,6},{5,7},{6,4},{7,5},{8,10},{9,11},{10,... | collective-permute-start | bytes 786440 | tf_op jit(solution)/shard_map/ppermute | solution.py:26
  57.6 21.0 %copy-start.6 = (s32[4,512]{1,0:T(4,128)S(1)}, s32[4,512]{1,0:T(4,128)}, u32[]{:S(2)}) copy-start(s32[4,512]{1,0:T(4,128)} %ids.1) | copy-start | bytes 24580
  61.8 5.0 %collective-permute-start.19 = (f32[2,32,512]{2,1,0:T(8,128)S(1)}, f32[2,32,512]{2,1,0:T(8,128)S(1)}, u32[]{:S(2)}, u32[]{:S(2)}) collective-permute-start(f32[2,32,512]{2,1,0:T(8,128)S(1)} %get-tuple-element.84), channel_id=1, source_target_pairs={{0,1},{1,0},{2,3},{3,2},{4,5},{5,4},{6,7},{7,6},{8,9},{9,8},{10,11... | collective-permute-start | bytes 393224 | tf_op jit(solution)/shard_map/ppermute | solution.py:26
  62.4 5.4 %collective-permute-start.18 = (f32[2,32,512]{2,1,0:T(8,128)S(1)}, f32[2,32,512]{2,1,0:T(8,128)S(1)}, u32[]{:S(2)}, u32[]{:S(2)}) collective-permute-start(f32[2,32,512]{2,1,0:T(8,128)S(1)} %get-tuple-element.82), channel_id=1, source_target_pairs={{0,2},{1,3},{2,0},{3,1},{4,6},{5,7},{6,4},{7,5},{8,10},{9,11},{10,... | collective-permute-start | bytes 393224 | tf_op jit(solution)/shard_map/ppermute | solution.py:26
  67.8 6.3 %collective-permute-start.20 = (f32[1,64,512]{2,1,0:T(8,128)S(1)}, f32[1,64,512]{2,1,0:T(8,128)S(1)}, u32[]{:S(2)}, u32[]{:S(2)}) collective-permute-start(f32[1,64,512]{2,1,0:T(8,128)S(1)} %pad_maximum_fusion.6), channel_id=1, source_target_pairs={{0,4},{1,5},{2,6},{3,7},{4,0},{5,1},{6,2},{7,3},{8,12},{9,13},{10,... | collective-permute-start | bytes 393224 | tf_op jit(solution)/shard_map/ppermute | solution.py:26
  71.2 13.1 %collective-permute-start.17 = (f32[2,128,512]{2,1,0:T(8,128)S(1)}, f32[2,128,512]{2,1,0:T(8,128)S(1)}, u32[]{:S(2)}, u32[]{:S(2)}) collective-permute-start(f32[2,128,512]{2,1,0:T(8,128)S(1)} %get-tuple-element.60), channel_id=1, source_target_pairs={{0,8},{8,0},{16,24},{24,16},{1,9},{9,1},{17,25},{25,17},{2,10},{10... | collective-permute-start | bytes 1572872 | tf_op jit(solution)/shard_map/ppermute | solution.py:26
  74.2 4.3 %collective-permute-start.21 = (f32[16,512]{1,0:T(8,128)S(1)}, f32[16,512]{1,0:T(8,128)S(1)}, u32[]{:S(2)}, u32[]{:S(2)}) collective-permute-start(f32[16,512]{1,0:T(8,128)S(1)} %pad_maximum_fusion.8), channel_id=1, source_target_pairs={{0,16},{8,24},{16,0},{24,8},{1,17},{9,25},{17,1},{25,9},{2,18},{10... | collective-permute-start | bytes 98312 | tf_op jit(solution)/shard_map/ppermute | solution.py:31
  74.8 3.7 %collective-permute-start.22 = (f32[16,512]{1,0:T(8,128)S(1)}, f32[16,512]{1,0:T(8,128)S(1)}, u32[]{:S(2)}, u32[]{:S(2)}) collective-permute-start(f32[16,512]{1,0:T(8,128)S(1)} %pad_maximum_fusion.9), channel_id=1, source_target_pairs={{0,8},{8,0},{16,24},{24,16},{1,9},{9,1},{17,25},{25,17},{2,10},{10... | collective-permute-start | bytes 98312 | tf_op jit(solution)/shard_map/ppermute | solution.py:31
  74.8 3.8 %collective-permute-start.23 = (f32[16,512]{1,0:T(8,128)S(1)}, f32[16,512]{1,0:T(8,128)S(1)}, u32[]{:S(2)}, u32[]{:S(2)}) collective-permute-start(f32[16,512]{1,0:T(8,128)S(1)} %pad_maximum_fusion.10), channel_id=1, source_target_pairs={{0,24},{8,16},{16,8},{24,0},{1,25},{9,17},{17,9},{25,1},{2,26},{10... | collective-permute-start | bytes 98312 | tf_op jit(solution)/shard_map/ppermute | solution.py:31
  80.5 8.1 %collective-permute-start.35 = (f32[136,128]{1,0:T(8,128)S(1)}, f32[136,128]{1,0:T(8,128)S(1)}, u32[]{:S(2)}, u32[]{:S(2)}) collective-permute-start(f32[136,128]{1,0:T(8,128)S(1)} %get-tuple-element.73), channel_id=1, source_target_pairs={{0,1},{1,0},{2,3},{3,2},{4,5},{5,4},{6,7},{7,6},{8,9},{9,8},{10,11... | collective-permute-start | bytes 208904 | tf_op jit(solution)/shard_map/ppermute | solution.py:31
  81.9 7.6 %collective-permute-start.36 = (f32[136,128]{1,0:T(8,128)S(1)}, f32[136,128]{1,0:T(8,128)S(1)}, u32[]{:S(2)}, u32[]{:S(2)}) collective-permute-start(f32[136,128]{1,0:T(8,128)S(1)} %get-tuple-element.74), channel_id=1, source_target_pairs={{0,2},{1,3},{2,0},{3,1},{4,6},{5,7},{6,4},{7,5},{8,10},{9,11},{10,... | collective-permute-start | bytes 208904 | tf_op jit(solution)/shard_map/ppermute | solution.py:31
  84.3 9.0 %collective-permute-start.37 = (f32[136,128]{1,0:T(8,128)S(1)}, f32[136,128]{1,0:T(8,128)S(1)}, u32[]{:S(2)}, u32[]{:S(2)}) collective-permute-start(f32[136,128]{1,0:T(8,128)S(1)} %get-tuple-element.75), channel_id=1, source_target_pairs={{0,3},{1,2},{2,1},{3,0},{4,7},{5,6},{6,5},{7,4},{8,11},{9,10},{10,... | collective-permute-start | bytes 208904 | tf_op jit(solution)/shard_map/ppermute | solution.py:31
  84.4 14.4 %collective-permute-start.26 = (f32[1,128,512]{2,1,0:T(8,128)S(1)}, f32[1,128,512]{2,1,0:T(8,128)S(1)}, u32[]{:S(2)}, u32[]{:S(2)}) collective-permute-start(f32[1,128,512]{2,1,0:T(8,128)S(1)} %get-tuple-element.79), channel_id=1, source_target_pairs={{0,16},{8,24},{16,0},{24,8},{1,17},{9,25},{17,1},{25,9},{2,18},{10... | collective-permute-start | bytes 786440 | tf_op jit(solution)/shard_map/ppermute | solution.py:26
  85.7 8.4 %collective-permute-start.24 = (f32[136,128]{1,0:T(8,128)S(1)}, f32[136,128]{1,0:T(8,128)S(1)}, u32[]{:S(2)}, u32[]{:S(2)}) collective-permute-start(f32[136,128]{1,0:T(8,128)S(1)} %get-tuple-element.67), channel_id=1, source_target_pairs={{0,4},{1,5},{2,6},{3,7},{4,0},{5,1},{6,2},{7,3},{8,12},{9,13},{10,... | collective-permute-start | bytes 208904 | tf_op jit(solution)/shard_map/ppermute | solution.py:31
  88.7 10.2 %collective-permute-start.25 = (f32[136,128]{1,0:T(8,128)S(1)}, f32[136,128]{1,0:T(8,128)S(1)}, u32[]{:S(2)}, u32[]{:S(2)}) collective-permute-start(f32[136,128]{1,0:T(8,128)S(1)} %get-tuple-element.68), channel_id=1, source_target_pairs={{0,5},{1,4},{2,7},{3,6},{4,1},{5,0},{6,3},{7,2},{8,13},{9,12},{10,... | collective-permute-start | bytes 208904 | tf_op jit(solution)/shard_map/ppermute | solution.py:31
  89.5 10.1 %collective-permute-start.30 = (f32[136,128]{1,0:T(8,128)S(1)}, f32[136,128]{1,0:T(8,128)S(1)}, u32[]{:S(2)}, u32[]{:S(2)}) collective-permute-start(f32[136,128]{1,0:T(8,128)S(1)} %get-tuple-element.71), channel_id=1, source_target_pairs={{0,6},{1,7},{2,4},{3,5},{4,2},{5,3},{6,0},{7,1},{8,14},{9,15},{10,... | collective-permute-start | bytes 208904 | tf_op jit(solution)/shard_map/ppermute | solution.py:31
  93.3 7.1 %collective-permute-start.31 = (f32[136,128]{1,0:T(8,128)S(1)}, f32[136,128]{1,0:T(8,128)S(1)}, u32[]{:S(2)}, u32[]{:S(2)}) collective-permute-start(f32[136,128]{1,0:T(8,128)S(1)} %get-tuple-element.72), channel_id=1, source_target_pairs={{0,7},{1,6},{2,5},{3,4},{4,3},{5,2},{6,1},{7,0},{8,15},{9,14},{10,... | collective-permute-start | bytes 208904 | tf_op jit(solution)/shard_map/ppermute | solution.py:31
  94.1 7.6 %collective-permute-start.38 = (f32[3,136,128]{2,1,0:T(8,128)S(1)}, f32[3,136,128]{2,1,0:T(8,128)S(1)}, u32[]{:S(2)}, u32[]{:S(2)}) collective-permute-start(f32[3,136,128]{2,1,0:T(8,128)S(1)} %pad_maximum_fusion.4.refs_8_), channel_id=1, source_target_pairs={{0,16},{8,24},{16,0},{24,8},{1,17},{9,25},{17,1},{25,9},{2,18},{10... | collective-permute-start | bytes 626696 | tf_op jit(solution)/shard_map/ppermute | solution.py:26
  98.9 7.8 %collective-permute-start.27 = (f32[3,136,128]{2,1,0:T(8,128)S(1)}, f32[3,136,128]{2,1,0:T(8,128)S(1)}, u32[]{:S(2)}, u32[]{:S(2)}) collective-permute-start(f32[3,136,128]{2,1,0:T(8,128)S(1)} %pad_maximum_fusion.3.refs_0_), channel_id=1, source_target_pairs={{0,16},{8,24},{16,0},{24,8},{1,17},{9,25},{17,1},{25,9},{2,18},{10... | collective-permute-start | bytes 626696 | tf_op jit(solution)/shard_map/ppermute | solution.py:26
  100.5 1.5 %collective-permute-start.33 = (f32[2,136,128]{2,1,0:T(8,128)S(1)}, f32[2,136,128]{2,1,0:T(8,128)S(1)}, u32[]{:S(2)}, u32[]{:S(2)}) collective-permute-start(f32[2,136,128]{2,1,0:T(8,128)S(1)} %pad_maximum_fusion.5.refs_4_), channel_id=1, source_target_pairs={{0,8},{8,0},{16,24},{24,16},{1,9},{9,1},{17,25},{25,17},{2,10},{10... | collective-permute-start | bytes 417800 | tf_op jit(solution)/shard_map/ppermute | solution.py:26
  100.5 7.7 %collective-permute-start.32 = (f32[2,136,128]{2,1,0:T(8,128)S(1)}, f32[2,136,128]{2,1,0:T(8,128)S(1)}, u32[]{:S(2)}, u32[]{:S(2)}) collective-permute-start(f32[2,136,128]{2,1,0:T(8,128)S(1)} %pad_maximum_fusion.5.refs_4_), channel_id=1, source_target_pairs={{0,16},{8,24},{16,0},{24,8},{1,17},{9,25},{17,1},{25,9},{2,18},{10... | collective-permute-start | bytes 417800 | tf_op jit(solution)/shard_map/ppermute | solution.py:26
  101.5 6.8 %collective-permute-start.39 = (f32[3,136,128]{2,1,0:T(8,128)S(1)}, f32[3,136,128]{2,1,0:T(8,128)S(1)}, u32[]{:S(2)}, u32[]{:S(2)}) collective-permute-start(f32[3,136,128]{2,1,0:T(8,128)S(1)} %pad_maximum_fusion.4.refs_8_), channel_id=1, source_target_pairs={{0,8},{8,0},{16,24},{24,16},{1,9},{9,1},{17,25},{25,17},{2,10},{10... | collective-permute-start | bytes 626696 | tf_op jit(solution)/shard_map/ppermute | solution.py:26
  101.6 7.9 %collective-permute-start.40 = (f32[3,136,128]{2,1,0:T(8,128)S(1)}, f32[3,136,128]{2,1,0:T(8,128)S(1)}, u32[]{:S(2)}, u32[]{:S(2)}) collective-permute-start(f32[3,136,128]{2,1,0:T(8,128)S(1)} %collective-permute-done.38.refs_9_), channel_id=1, source_target_pairs={{0,8},{8,0},{16,24},{24,16},{1,9},{9,1},{17,25},{25,17},{2,10},{10... | collective-permute-start | bytes 626696 | tf_op jit(solution)/shard_map/ppermute | solution.py:26
  102.0 7.6 %collective-permute-start.28 = (f32[3,136,128]{2,1,0:T(8,128)S(1)}, f32[3,136,128]{2,1,0:T(8,128)S(1)}, u32[]{:S(2)}, u32[]{:S(2)}) collective-permute-start(f32[3,136,128]{2,1,0:T(8,128)S(1)} %pad_maximum_fusion.3.refs_0_), channel_id=1, source_target_pairs={{0,8},{8,0},{16,24},{24,16},{1,9},{9,1},{17,25},{25,17},{2,10},{10... | collective-permute-start | bytes 626696 | tf_op jit(solution)/shard_map/ppermute | solution.py:26
  106.7 2.9 %collective-permute-start.29 = (f32[3,136,128]{2,1,0:T(8,128)S(1)}, f32[3,136,128]{2,1,0:T(8,128)S(1)}, u32[]{:S(2)}, u32[]{:S(2)}) collective-permute-start(f32[3,136,128]{2,1,0:T(8,128)S(1)} %collective-permute-done.27.refs_1_), channel_id=1, source_target_pairs={{0,8},{8,0},{16,24},{24,16},{1,9},{9,1},{17,25},{25,17},{2,10},{10... | collective-permute-start | bytes 626696 | tf_op jit(solution)/shard_map/ppermute | solution.py:26
  108.2 1.4 %collective-permute-start.34 = (f32[2,136,128]{2,1,0:T(8,128)S(1)}, f32[2,136,128]{2,1,0:T(8,128)S(1)}, u32[]{:S(2)}, u32[]{:S(2)}) collective-permute-start(f32[2,136,128]{2,1,0:T(8,128)S(1)} %collective-permute-done.32.refs_5_), channel_id=1, source_target_pairs={{0,8},{8,0},{16,24},{24,16},{1,9},{9,1},{17,25},{25,17},{2,10},{10... | collective-permute-start | bytes 417800 | tf_op jit(solution)/shard_map/ppermute | solution.py:26

commit v7 on v6

--- a/solution.py
+++ b/solution.py
@@ -459,10 +459,12 @@
         return [(groups[g], m) for g in range(k, len(groups), n_seq) for m in range(groups[g].shape[0])]
 
     for c in range(n_tiles):
-        rows = pl.ds(pl.multiple_of((block * n_tiles + c) * n_dim, n_dim), n_dim)
+        first = (block * n_tiles + c) * 2 * n_dim
         for k, q in enumerate(order):
             for r, (group, m) in zip(members, places(k)):
-                quarter[pl.ds(pl.multiple_of((item ^ r) * n_dim, n_dim), n_dim)] = group[m, rows]
+                for chunk in range(2):
+                    place = pl.ds(pl.multiple_of((item ^ r ^ (chunk * n_item // 2)) * n_dim, n_dim), n_dim)
+                    quarter[place] = group[m, pl.ds(pl.multiple_of(first + chunk * n_dim, n_dim), n_dim)]
             place = pl.ds(pl.multiple_of((me ^ q) * cols, cols), cols)
             out_ref[c * LANES : (c + 1) * LANES, place] = quarter[...].T
 
@@ -603,51 +605,66 @@
             for part in range(2)
         ]
     kept, sent = panel[::2], panel[1::2]
-    total = reduce_steps(jnp.concatenate(kept, axis=1), jnp.concatenate(sent, axis=1), "item", shared[::-1])
+    kept, sent = jnp.concatenate(kept, axis=1), jnp.concatenate(sent, axis=1)
+    for bit in shared[:0:-1]:
+        got = swap(sent, "item", bit)
+        cut = kept.shape[0] // 2
+        kept, sent = kept[:cut] + got[:cut], kept[cut:] + got[cut:]
+    tail = jnp.concatenate([loss] * (n_neg // LANES), axis=1)
+    mine = jnp.concatenate([kept[0], sent[0], tail], axis=0)
+    other = swap(mine, "item", shared[0])
     for n, bit in enumerate(seq_bits[::-1]):
         got_rows = swap(sent_rows, "seq", bit)
         if n < n_seq.bit_length() - 2:
             half = kept_rows.shape[0] // 2
             sent_rows = kept_rows[half:] + got_rows[half:]
             kept_rows = kept_rows[:half] + got_rows[:half]
+    other, got_rows = lax.optimization_barrier((other, got_rows))
+    rows = kept.shape[1]
+    total = [kept[0] + other[rows : 2 * rows], sent[0] + other[:rows]]
+    loss = loss + other[2 * rows :, :LANES]
     part = n_dim // 2
-    halves = total[: n_seq * part], total[n_seq * part :]
     moved = []
     for k, r in enumerate(seq_order):
-        block = jnp.concatenate([half[k * part : (k + 1) * part] for half in halves], axis=0)
+        spans = [slice(h * n_seq * part + k * part, h * n_seq * part + (k + 1) * part) for h in range(2)]
+        block = jnp.concatenate([chunk[span] for chunk in total for span in spans], axis=0)
         moved.append(send(block, "seq", r) if r else block)
+    n_near, top = n_item // 2, 1 << shared[0]
     if aligned:
-        sent = spread_rows(seq_order, per_panel, panel_owner, moved, ids_by_seq, loss, n_item, n_rows)
+        sent = spread_rows(seq_order, per_panel, panel_owner, moved, ids_by_seq, loss, n_near, n_rows)
     else:
         source = s ^ jnp.array(seq_order, i32)
         ids, owner = ids_by_seq[source], panel_owner[source // per_panel]
         hot = (ids[:, :, None] == jnp.arange(n_rows, dtype=i32)).astype(f32)
         spread = jnp.einsum("pdc,pcr->pdr", jnp.stack(moved), hot, precision=high)
-        mine = (owner[None, :] == (i ^ jnp.arange(n_item, dtype=i32))[:, None]).astype(f32)
+        mine = (owner[None, :] == (i ^ jnp.arange(n_near, dtype=i32))[:, None]).astype(f32)
         sent = jnp.sum(mine[:, :, None, None] * spread[None], axis=1)
-        sent = sent.reshape(n_item, n_dim, -1, LANES).transpose(0, 2, 1, 3).reshape(n_item, -1, LANES)
-        sent = [jnp.concatenate([sent[r], loss], axis=0) for r in range(n_item)]
-
-    taken = [send(sent[r], "item", r) if r else sent[r] for r in range(n_item)]
-    near, far = list(range(1, n_item // 2)), list(range(n_item // 2, n_item))
-    which = [[0] + far[: len(far) // 2], far[len(far) // 2 :], near]
-    table = []
-    for members in which:
+        sent = sent.reshape(n_near, 2 * n_dim, -1, LANES).transpose(0, 2, 1, 3).reshape(n_near, -1, LANES)
+        sent = [jnp.concatenate([sent[r], loss], axis=0) for r in range(n_near)]
+
+    sent = list(sent)
+    own = sent[0][None]
+    own = [own, swap(own, "seq", seq_bits[0])]
+    sent[3], own[1] = lax.optimization_barrier((sent[3], own[1]))
+    taken = [send(sent[r], "item", r) if r else sent[r] for r in range(n_near)]
+    which = [[0], [1, 2], list(range(3, n_near))]
+    table = [own]
+    for members in which[1:]:
         group = jnp.stack([taken[r] for r in members])
-        if members[0] == 0:
-            group, got_rows = lax.optimization_barrier((group, got_rows))
         table.append([group, swap(group, "seq", seq_bits[0])])
+    members = sum(which, [])
     for bit in seq_bits[1:]:
         table = [group + [swap(piece, "seq", bit) for piece in group] for group in table]
     if aligned:
-        table_grad, mean_loss, event_grad = assemble(table, kept_rows, got_rows, seq_order, sum(which, []), n_item, n_dim, n_rows, group_len * n_item)
+        table_grad, mean_loss, event_grad = assemble(table, kept_rows, got_rows, seq_order, members, n_item, n_dim, n_rows, group_len * n_item)
         mean_loss = mean_loss.reshape(())
     else:
         table = jnp.stack([jnp.concatenate(groups, axis=0) for groups in zip(*table)])
         event_grad = kept_rows + got_rows
         mean_loss = jnp.sum(table[:, :, -1, 0]) / (group_len * n_item)
-        table = table[:, :, :-EXTRA].reshape(n_seq, n_item, -1, n_dim, LANES)
-        table = true_order(table.swapaxes(0, 1), sum(which, []), i).swapaxes(0, 1)
+        table = table[:, :, :-EXTRA].reshape(n_seq, n_near, -1, 2, n_dim, LANES).transpose(1, 3, 0, 2, 4, 5)
+        table = table.reshape(n_item, n_seq, -1, n_dim, LANES)
+        table = true_order(table, [r ^ chunk for r in members for chunk in (0, top)], i).swapaxes(0, 1)
         table_grad = true_order(table, seq_order, s).transpose(2, 4, 0, 1, 3).reshape(n_rows, width)
     return (mean_loss, event_grad, table_grad)
 

time: 113 us -> 111 us (0.982)
  starting transfers between devices: 41.8 us -> 32.4 us
  waiting for transfers between devices: 39.7 us -> 47.5 us
    ppermute x10 -> x6, starting transfers between devices: 14.4 us -> 4.55 us  [send(): return lax.ppermute(block, axis, [(i, i ^ r) for i in range(size)])]
    ppermute x10 -> x6, waiting for transfers between devices: 6.88 us -> 12.2 us  [send(): return lax.ppermute(block, axis, [(i, i ^ r) for i in range(size)])]
    ppermute x31, waiting for transfers between devices: 32.8 us -> 35.3 us  [swap(): return lax.ppermute(block, axis, [(i, i ^ 1 << bit) for i in range(size)])]
  transfers between devices with their start and end apart: 41 -> 37, of which waited for: 20 -> 21; matrix products, arithmetic and copies ran while one was open for 1% -> 1% of each run, Pallas kernels for 17% -> 16%
where the time goes in v7:
time: 111 us
  waiting for transfers between devices  47.5 us (43%)
  starting transfers between devices  32.4 us (29%)
  Pallas kernels  25 us (23%)
  local copies, waits for them, and re-layouts  2.86 us (3%)
  between operations  2.28 us (2%)
    ppermute x31, waiting for transfers between devices, swap(): return lax.ppermute(block, axis, [(i, i ^ 1 << bit) for i in range(size)])  35.3 us
    ppermute x31, starting transfers between devices, swap(): return lax.ppermute(block, axis, [(i, i ^ 1 << bit) for i in range(size)])  27.9 us
    ppermute x6, waiting for transfers between devices, send(): return lax.ppermute(block, axis, [(i, i ^ r) for i in range(size)])  12.2 us
    pallas_call x2, Pallas kernels, attend(): pl.pallas_call(functools.partial(attend_kernel, order, n_seq), grid=(coun...  10.1 us
    ppermute x6, starting transfers between devices, send(): return lax.ppermute(block, axis, [(i, i ^ r) for i in range(size)])  4.55 us
    pallas_call x1, Pallas kernels, pick_rows(): pl.pallas_call(functools.partial(pick_kernel, plan), in_specs=[pl.BlockSp...  3.59 us
    pallas_call x1, Pallas kernels, loss_terms(): pl.pallas_call(functools.partial(loss_kernel, plan), in_specs=[vmem] * (2...  3.21 us
    pallas_call x1, Pallas kernels, assemble(): pl.pallas_call(functools.partial(assemble_kernel, order, members, n_item,...  2.48 us
  transfers between devices with their start and end apart: 37, of which 21 were waited for; matrix products, arithmetic and copies ran while one was open for 1% of the time, Pallas kernels for 16%

profile of v7, /device:TPU:0, one launch (start us, length us, event | category | flops | bytes accessed | tf_op | source)
XLA Modules:
  0.0 110.6 jit_solution(2937531958062309552)
XLA Ops:
  0.7 3.0 %collective-permute-start.4 = (f32[128,512]{1,0:T(8,128)}, f32[128,512]{1,0:T(8,128)S(1)}, u32[]{:S(2)}, u32[]{:S(2)}) collective-permute-start(f32[128,512]{1,0:T(8,128)} %bitcast.30), channel_id=1, source_target_pairs={{0,16},{8,24},{16,0},{24,8},{1,17},{9,25},{17,1},{25,9},{2,18},{10... | collective-permute-start | bytes 786440 | tf_op jit(solution)/shard_map/ppermute | solution.py:26
  3.7 3.6 %pick_rows.1 = (f32[4,32,512]{2,1,0:T(8,128)}, f32[4,32,512]{2,1,0:T(8,128)}, f32[4,32,512]{2,1,0:T(8,128)}, f32[4,32,512]{2,1,0:T(8,128)}) custom-call(s32[4,512]{1,0:T(4,128)} %ids.1, f32[1024,512]{1,0:T(8,128)} %table_hbm.1), custom_call_target="tpu_custom_call" | custom-call | flops 1073741824 | bytes 2097152 | tf_op jit(solution)/shard_map/pick_rows/pallas_call | solution.py:129
  7.3 1.6 %collective-permute-start = (f32[4,32,512]{2,1,0:T(8,128)}, f32[4,32,512]{2,1,0:T(8,128)S(1)}, u32[]{:S(2)}, u32[]{:S(2)}) collective-permute-start(f32[4,32,512]{2,1,0:T(8,128)} %get-tuple-element.40), channel_id=1, source_target_pairs={{0,1},{1,0},{2,3},{3,2},{4,5},{5,4},{6,7},{7,6},{8,9},{9,8},{10,11... | collective-permute-start | bytes 786440 | tf_op jit(solution)/shard_map/ppermute | solution.py:26
  8.8 1.6 %collective-permute-start.2 = (f32[4,32,512]{2,1,0:T(8,128)}, f32[4,32,512]{2,1,0:T(8,128)S(1)}, u32[]{:S(2)}, u32[]{:S(2)}) collective-permute-start(f32[4,32,512]{2,1,0:T(8,128)} %get-tuple-element.42), channel_id=1, source_target_pairs={{0,2},{1,3},{2,0},{3,1},{4,6},{5,7},{6,4},{7,5},{8,10},{9,11},{10,... | collective-permute-start | bytes 786440 | tf_op jit(solution)/shard_map/ppermute | solution.py:26
  11.1 0.6 dynamic_slice.3
  12.3 0.0 copy-start
  12.3 2.2 %copy-done = f32[512,2048]{1,0:T(8,128)S(1)} copy-done((f32[512,2048]{1,0:T(8,128)S(1)}, f32[512,2048]{1,0:T(8,128)}, u32[]{:S(2)}) %copy-start) | copy-done | bytes 4194328
  14.5 1.6 %prepare.1 = (f32[128,512]{1,0:T(8,128)S(1)}, f32[128,512]{1,0:T(8,128)S(1)}) custom-call(f32[128,512]{1,0:T(8,128)S(1)} %bitcast.32, f32[512,2048]{1,0:T(8,128)S(1)} %copy-done, f32[512,2048]{1,0:T(8,128)S(1)} %copy-done), custom_call_target="tpu_custom_call" | custom-call | flops 402653184 | bytes 2097152 | tf_op jit(solution)/shard_map/prepare/pallas_call | solution.py:155
  16.2 0.3 collective-permute-start.6
  16.5 0.5 collective-permute-start.1
  17.0 0.8 collective-permute-done.2
  17.8 0.8 collective-permute-start.3
  18.6 2.6 %attend.2.refs_0_ = f32[128,128]{1,0:T(8,128)S(1)} custom-call(s32[1,4]{1,0:T(1,128)S(1)} %copy-done.4, f32[128,512]{1,0:T(8,128)S(1)} %bitcast.33, f32[128,512]{1,0:T(8,128)S(1)} %collective-permute-done.4.refs_1_, f32[128,512]{1,0:T(8,128)S(1)} %collective-permute-done.5.refs_2_, f32[128,512]{1,0:T(8,128)S(1)} %collective-permute-done.6.refs_3_, ...), custom_call_target="tpu_custom_call" | custom-call | flops 2000000000 | bytes 2097152 | tf_op jit(solution)/shard_map/attend/pallas_call | solution.py:227
  21.2 1.0 collective-permute-done.1
  22.3 0.7 collective-permute-done.3
  23.0 0.1 fusion
  23.1 2.7 %collective-permute-start.10 = (f32[2,2,32,512]{3,2,1,0:T(8,128)S(1)}, f32[2,2,32,512]{3,2,1,0:T(8,128)S(1)}, u32[]{:S(2)}, u32[]{:S(2)}) collective-permute-start(f32[2,2,32,512]{3,2,1,0:T(8,128)S(1)} %pad_maximum_fusion.1), channel_id=1, source_target_pairs={{0,4},{1,5},{2,6},{3,7},{4,0},{5,1},{6,2},{7,3},{8,12},{9,13},{10,... | collective-permute-start | bytes 786440 | tf_op jit(solution)/shard_map/ppermute | solution.py:26
  25.8 7.4 %attend.3.refs_1_ = f32[128,384]{1,0:T(8,128)S(1)} custom-call(s32[1,4]{1,0:T(1,128)S(1)} %copy-done.4, f32[128,512]{1,0:T(8,128)S(1)} %bitcast.34, f32[128,512]{1,0:T(8,128)S(1)} %collective-permute-done.4.refs_1_, f32[128,512]{1,0:T(8,128)S(1)} %collective-permute-done.5.refs_2_, f32[128,512]{1,0:T(8,128)S(1)} %collective-permute-done.6.refs_3_, ...), custom_call_target="tpu_custom_call" | custom-call | flops 6000000000 | bytes 2097152 | tf_op jit(solution)/shard_map/attend/pallas_call | solution.py:227
  33.3 0.6 project.1.refs_0_
  33.9 0.6 collective-permute-start.7
  34.4 2.3 %collective-permute-done.10 = f32[2,2,32,512]{3,2,1,0:T(8,128)S(1)} collective-permute-done((f32[2,2,32,512]{3,2,1,0:T(8,128)S(1)}, f32[2,2,32,512]{3,2,1,0:T(8,128)S(1)}, u32[]{:S(2)}, u32[]{:S(2)}) %collective-permute-start.10) | collective-permute-done | bytes 262176 | tf_op jit(solution)/shard_map/ppermute | solution.py:26
  36.8 0.7 collective-permute-start.11
  37.6 0.5 collective-permute-start.13
  38.0 3.0 %collective-permute-done.7.refs_1_ = f32[136,512]{1,0:T(8,128)S(1)} collective-permute-done((f32[136,512]{1,0:T(8,128)S(1)}, f32[136,512]{1,0:T(8,128)S(1)}, u32[]{:S(2)}, u32[]{:S(2)}) %collective-permute-start.7) | collective-permute-done | bytes 278560 | tf_op jit(solution)/shard_map/ppermute | solution.py:26
  41.0 0.8 collective-permute-done.11
  41.9 0.5 collective-permute-start.12
  42.3 0.4 collective-permute-done.13
  42.8 1.2 %collective-permute-start.14 = (f32[4,32,512]{2,1,0:T(8,128)S(1)}, f32[4,32,512]{2,1,0:T(8,128)S(1)}, u32[]{:S(2)}, u32[]{:S(2)}) collective-permute-start(f32[4,32,512]{2,1,0:T(8,128)S(1)} %pad_maximum_fusion.3), channel_id=1, source_target_pairs={{0,2},{1,3},{2,0},{3,1},{4,6},{5,7},{6,4},{7,5},{8,10},{9,11},{10,... | collective-permute-start | bytes 786440 | tf_op jit(solution)/shard_map/ppermute | solution.py:26
  44.0 0.3 transpose_outputs.1
  44.4 5.5 %collective-permute-done.12 = f32[4,32,512]{2,1,0:T(8,128)S(1)} collective-permute-done((f32[4,32,512]{2,1,0:T(8,128)S(1)}, f32[4,32,512]{2,1,0:T(8,128)S(1)}, u32[]{:S(2)}, u32[]{:S(2)}) %collective-permute-start.12) | collective-permute-done | bytes 262176 | tf_op jit(solution)/shard_map/ppermute | solution.py:26
  49.9 0.2 collective-permute-done.14
  50.1 3.2 %loss_terms.1 = (f32[4,32,512]{2,1,0:T(8,128)S(1)}, f32[4,32,512]{2,1,0:T(8,128)S(1)}, f32[4,32,512]{2,1,0:T(8,128)S(1)}, f32[4,32,512]{2,1,0:T(8,128)S(1)}, f32...) custom-call(bf16[512,512]{1,0:T(8,128)(2,1)S(1)} %get-tuple-element.46., ...), custom_call_target="tpu_custom_call" | custom-call | flops 1610612736 | bytes 4194304 | tf_op jit(solution)/shard_map/loss_terms/pallas_call | solution.py:366
  53.3 1.7 %collective-permute-start.15 = (f32[4,32,512]{2,1,0:T(8,128)S(1)}, f32[4,32,512]{2,1,0:T(8,128)S(1)}, u32[]{:S(2)}, u32[]{:S(2)}) collective-permute-start(f32[4,32,512]{2,1,0:T(8,128)S(1)} %get-tuple-element.50), channel_id=1, source_target_pairs={{0,1},{1,0},{2,3},{3,2},{4,5},{5,4},{6,7},{7,6},{8,9},{9,8},{10,11... | collective-permute-start | bytes 786440 | tf_op jit(solution)/shard_map/ppermute | solution.py:26
  55.0 1.6 %collective-permute-start.16 = (f32[4,32,512]{2,1,0:T(8,128)S(1)}, f32[4,32,512]{2,1,0:T(8,128)S(1)}, u32[]{:S(2)}, u32[]{:S(2)}) collective-permute-start(f32[4,32,512]{2,1,0:T(8,128)S(1)} %get-tuple-element.51), channel_id=1, source_target_pairs={{0,2},{1,3},{2,0},{3,1},{4,6},{5,7},{6,4},{7,5},{8,10},{9,11},{10,... | collective-permute-start | bytes 786440 | tf_op jit(solution)/shard_map/ppermute | solution.py:26
  56.5 1.0 event_rows.1
  57.6 2.6 %collective-permute-done.15 = f32[4,32,512]{2,1,0:T(8,128)S(1)} collective-permute-done((f32[4,32,512]{2,1,0:T(8,128)S(1)}, f32[4,32,512]{2,1,0:T(8,128)S(1)}, u32[]{:S(2)}, u32[]{:S(2)}) %collective-permute-start.15) | collective-permute-done | bytes 262176 | tf_op jit(solution)/shard_map/ppermute | solution.py:26
  60.2 1.6 %collective-permute-done.16 = f32[4,32,512]{2,1,0:T(8,128)S(1)} collective-permute-done((f32[4,32,512]{2,1,0:T(8,128)S(1)}, f32[4,32,512]{2,1,0:T(8,128)S(1)}, u32[]{:S(2)}, u32[]{:S(2)}) %collective-permute-start.16) | collective-permute-done | bytes 262176 | tf_op jit(solution)/shard_map/ppermute | solution.py:26
  61.8 0.6 collective-permute-start.19
  62.4 1.8 %collective-permute-start.18 = (f32[2,32,512]{2,1,0:T(8,128)S(1)}, f32[2,32,512]{2,1,0:T(8,128)S(1)}, u32[]{:S(2)}, u32[]{:S(2)}) collective-permute-start(f32[2,32,512]{2,1,0:T(8,128)S(1)} %get-tuple-element.78), channel_id=1, source_target_pairs={{0,2},{1,3},{2,0},{3,1},{4,6},{5,7},{6,4},{7,5},{8,10},{9,11},{10,... | collective-permute-start | bytes 393224 | tf_op jit(solution)/shard_map/ppermute | solution.py:26
  64.2 2.6 %collective-permute-done.19 = f32[2,32,512]{2,1,0:T(8,128)S(1)} collective-permute-done((f32[2,32,512]{2,1,0:T(8,128)S(1)}, f32[2,32,512]{2,1,0:T(8,128)S(1)}, u32[]{:S(2)}, u32[]{:S(2)}) %collective-permute-start.19) | collective-permute-done | bytes 131104 | tf_op jit(solution)/shard_map/ppermute | solution.py:26
  66.9 0.6 collective-permute-done.18
  67.6 3.7 %collective-permute-start.20 = (f32[136,512]{1,0:T(8,128)S(1)}, f32[136,512]{1,0:T(8,128)S(1)}, u32[]{:S(2)}, u32[]{:S(2)}) collective-permute-start(f32[136,512]{1,0:T(8,128)S(1)} %maximum_maximum_fusion), channel_id=1, source_target_pairs={{0,4},{1,5},{2,6},{3,7},{4,0},{5,1},{6,2},{7,3},{8,12},{9,13},{10,... | collective-permute-start | bytes 835592 | tf_op jit(solution)/shard_map/ppermute | solution.py:26
  71.2 0.1 slice_add_fusion
  71.3 0.6 collective-permute-start.21
  71.9 8.5 %collective-permute-done.20 = f32[136,512]{1,0:T(8,128)S(1)} collective-permute-done((f32[136,512]{1,0:T(8,128)S(1)}, f32[136,512]{1,0:T(8,128)S(1)}, u32[]{:S(2)}, u32[]{:S(2)}) %collective-permute-start.20) | collective-permute-done | bytes 278560 | tf_op jit(solution)/shard_map/ppermute | solution.py:26
  80.5 0.6 collective-permute-start.22
  81.1 1.6 %collective-permute-start.24 = (f32[32,512]{1,0:T(8,128)S(1)}, f32[32,512]{1,0:T(8,128)S(1)}, u32[]{:S(2)}, u32[]{:S(2)}) collective-permute-start(f32[32,512]{1,0:T(8,128)S(1)} %pad_maximum_fusion.7), channel_id=1, source_target_pairs={{0,24},{8,16},{16,8},{24,0},{1,25},{9,17},{17,9},{25,1},{2,26},{10... | collective-permute-start | bytes 196616 | tf_op jit(solution)/shard_map/ppermute | solution.py:31
  82.7 2.8 %collective-permute-done.22.refs_1_ = f32[32,512]{1,0:T(8,128)S(1)} collective-permute-done((f32[32,512]{1,0:T(8,128)S(1)}, f32[32,512]{1,0:T(8,128)S(1)}, u32[]{:S(2)}, u32[]{:S(2)}) %collective-permute-start.22) | collective-permute-done | bytes 65568 | tf_op jit(solution)/shard_map/ppermute | solution.py:31
  85.5 0.0 collective-permute-done.24.refs_3_
  85.5 2.0 %spread_rows.1 = (f32[264,128]{1,0:T(8,128)S(1)}, f32[264,128]{1,0:T(8,128)S(1)}, f32[264,128]{1,0:T(8,128)S(1)}, f32[264,128]{1,0:T(8,128)S(1)}) custom-call(s32[4]{0:T(128)S(1)} %copy-done.7, s32[4,512]{1,0:T(4,128)S(1)} %copy-done.6, f32[8,128]{1,0:T(8,128)S(1)} %slice_add_fusion.12.loss, f32[32,512]{1,0:T(8,128)S(1)} %pad_maximum_fusion.4.refs_0_, ...), custom_call_target="tpu_custom_call" | custom-call | flops 268435456 | bytes 2097152 | tf_op jit(solution)/shard_map/spread_rows/pallas_call | solution.py:438
  87.6 1.6 %collective-permute-start.28 = (f32[264,128]{1,0:T(8,128)S(1)}, f32[264,128]{1,0:T(8,128)S(1)}, u32[]{:S(2)}, u32[]{:S(2)}) collective-permute-start(f32[264,128]{1,0:T(8,128)S(1)} %get-tuple-element.69), channel_id=1, source_target_pairs={{0,1},{1,0},{2,3},{3,2},{4,5},{5,4},{6,7},{7,6},{8,9},{9,8},{10,11... | collective-permute-start | bytes 405512 | tf_op jit(solution)/shard_map/ppermute | solution.py:31
  89.2 1.0 collective-permute-start.25
  90.1 3.5 %collective-permute-done.28 = f32[264,128]{1,0:T(8,128)S(1)} collective-permute-done((f32[264,128]{1,0:T(8,128)S(1)}, f32[264,128]{1,0:T(8,128)S(1)}, u32[]{:S(2)}, u32[]{:S(2)}) %collective-permute-start.28) | collective-permute-done | bytes 135200 | tf_op jit(solution)/shard_map/ppermute | solution.py:31
  93.6 1.2 %collective-permute-done.29 = f32[264,128]{1,0:T(8,128)S(1)} collective-permute-done((f32[264,128]{1,0:T(8,128)S(1)}, f32[264,128]{1,0:T(8,128)S(1)}, u32[]{:S(2)}, u32[]{:S(2)}) %collective-permute-start.29) | collective-permute-done | bytes 135200 | tf_op jit(solution)/shard_map/ppermute | solution.py:31
  94.9 0.9 collective-permute-start.30
  95.8 0.8 collective-permute-start.33
  96.6 0.5 collective-permute-start.31
  97.1 4.6 %collective-permute-done.33 = f32[264,128]{1,0:T(8,128)S(1)} collective-permute-done((f32[264,128]{1,0:T(8,128)S(1)}, f32[264,128]{1,0:T(8,128)S(1)}, u32[]{:S(2)}, u32[]{:S(2)}) %collective-permute-start.33) | collective-permute-done | bytes 135200 | tf_op jit(solution)/shard_map/ppermute | solution.py:31
  101.7 1.2 %collective-permute-start.34 = (f32[1,264,128]{2,1,0:T(8,128)S(1)}, f32[1,264,128]{2,1,0:T(8,128)S(1)}, u32[]{:S(2)}, u32[]{:S(2)}) collective-permute-start(f32[1,264,128]{2,1,0:T(8,128)S(1)} %bitcast.41), channel_id=1, source_target_pairs={{0,16},{8,24},{16,0},{24,8},{1,17},{9,25},{17,1},{25,9},{2,18},{10... | collective-permute-start | bytes 405512 | tf_op jit(solution)/shard_map/ppermute | solution.py:26
  102.9 0.4 collective-permute-done.30.refs_5_
  103.3 0.5 collective-permute-start.27
  103.8 2.9 %collective-permute-done.34.refs_9_ = f32[1,264,128]{2,1,0:T(8,128)S(1)} collective-permute-done((f32[1,264,128]{2,1,0:T(8,128)S(1)}, f32[1,264,128]{2,1,0:T(8,128)S(1)}, u32[]{:S(2)}, u32[]{:S(2)}) %collective-permute-start.34) | collective-permute-done | bytes 135200 | tf_op jit(solution)/shard_map/ppermute | solution.py:26
  106.7 1.3 %collective-permute-done.36.refs_11_ = f32[1,264,128]{2,1,0:T(8,128)S(1)} collective-permute-done((f32[1,264,128]{2,1,0:T(8,128)S(1)}, f32[1,264,128]{2,1,0:T(8,128)S(1)}, u32[]{:S(2)}, u32[]{:S(2)}) %collective-permute-start.36) | collective-permute-done | bytes 135200 | tf_op jit(solution)/shard_map/ppermute | solution.py:26
  108.1 2.5 %assemble.1 = (f32[1024,512]{1,0:T(8,128)}, f32[1,1]{1,0:T(1,128)}, f32[1,128,512]{2,1,0:T(8,128)}) custom-call(f32[1,128,512]{2,1,0:T(8,128)S(1)} %get-tuple-element.76.kept, f32[1,128,512]{2,1,0:T(8,128)S(1)} %collective-permute-done.21.got, f32[1,264,128]{2,1,0:T(8,128)S(1)} %bitcast.40, f32[1,264,128]{2,1,0:T(8,128)S(1)} %collective-permute-done.25.refs_1_, ...), custom_call_target="tpu_custom_call" | custom-call | bytes 4194304 | tf_op jit(solution)/shard_map/assemble/pallas_call | solution.py:485
  (67 shorter events, 0.5 us)
Async XLA Ops:
  0.6 8.2 %copy-start.1 = (f32[1,128,512]{2,1,0:T(8,128)S(1)}, f32[1,128,512]{2,1,0:T(8,128)}, u32[]{:S(2)}) copy-start(f32[1,128,512]{2,1,0:T(8,128)} %param.10) | copy-start | bytes 786436
  0.6 10.4 %copy-start.7 = (s32[4]{0:T(128)S(1)}, s32[4]{0:T(128)}, u32[]{:S(2)}) copy-start(s32[4]{0:T(128)} %owner.1) | copy-start | bytes 52
  0.7 15.5 %collective-permute-start.4 = (f32[128,512]{1,0:T(8,128)}, f32[128,512]{1,0:T(8,128)S(1)}, u32[]{:S(2)}, u32[]{:S(2)}) collective-permute-start(f32[128,512]{1,0:T(8,128)} %bitcast.30), channel_id=1, source_target_pairs={{0,16},{8,24},{16,0},{24,8},{1,17},{9,25},{17,1},{25,9},{2,18},{10... | collective-permute-start | bytes 786440 | tf_op jit(solution)/shard_map/ppermute | solution.py:26
  7.3 9.2 %collective-permute-start = (f32[4,32,512]{2,1,0:T(8,128)}, f32[4,32,512]{2,1,0:T(8,128)S(1)}, u32[]{:S(2)}, u32[]{:S(2)}) collective-permute-start(f32[4,32,512]{2,1,0:T(8,128)} %get-tuple-element.40), channel_id=1, source_target_pairs={{0,1},{1,0},{2,3},{3,2},{4,5},{5,4},{6,7},{7,6},{8,9},{9,8},{10,11... | collective-permute-start | bytes 786440 | tf_op jit(solution)/shard_map/ppermute | solution.py:26
  8.8 9.7 %collective-permute-start.5 = (f32[128,512]{1,0:T(8,128)S(1)}, f32[128,512]{1,0:T(8,128)S(1)}, u32[]{:S(2)}, u32[]{:S(2)}) collective-permute-start(f32[128,512]{1,0:T(8,128)S(1)} %bitcast.31), channel_id=1, source_target_pairs={{0,8},{8,0},{16,24},{24,16},{1,9},{9,1},{17,25},{25,17},{2,10},{10... | collective-permute-start | bytes 786440 | tf_op jit(solution)/shard_map/ppermute | solution.py:26
  8.8 8.9 %collective-permute-start.2 = (f32[4,32,512]{2,1,0:T(8,128)}, f32[4,32,512]{2,1,0:T(8,128)S(1)}, u32[]{:S(2)}, u32[]{:S(2)}) collective-permute-start(f32[4,32,512]{2,1,0:T(8,128)} %get-tuple-element.42), channel_id=1, source_target_pairs={{0,2},{1,3},{2,0},{3,1},{4,6},{5,7},{6,4},{7,5},{8,10},{9,11},{10,... | collective-permute-start | bytes 786440 | tf_op jit(solution)/shard_map/ppermute | solution.py:26
  12.3 2.2 %copy-start = (f32[512,2048]{1,0:T(8,128)S(1)}, f32[512,2048]{1,0:T(8,128)}, u32[]{:S(2)}) copy-start(f32[512,2048]{1,0:T(8,128)} %refs_6_.4) | copy-start | bytes 12582916
  14.5 1.9 %copy-start.8 = (f32[4,32,512]{2,1,0:T(8,128)S(1)}, f32[4,32,512]{2,1,0:T(8,128)}, u32[]{:S(2)}) copy-start(f32[4,32,512]{2,1,0:T(8,128)} %get-tuple-element.39) | copy-start | bytes 786436
  14.5 3.3 %copy-start.9 = (f32[4,32,512]{2,1,0:T(8,128)S(1)}, f32[4,32,512]{2,1,0:T(8,128)}, u32[]{:S(2)}) copy-start(f32[4,32,512]{2,1,0:T(8,128)} %get-tuple-element.41) | copy-start | bytes 786436
  14.5 4.1 %copy-start.4 = (s32[1,4]{1,0:T(1,128)S(1)}, s32[1,4]{1,0:T(1,128)}, u32[]{:S(2)}) copy-start(s32[1,4]{1,0:T(1,128)} %lengths.3) | copy-start | bytes 52
  16.2 2.4 %collective-permute-start.6 = (f32[128,512]{1,0:T(8,128)S(1)}, f32[128,512]{1,0:T(8,128)S(1)}, u32[]{:S(2)}, u32[]{:S(2)}) collective-permute-start(f32[128,512]{1,0:T(8,128)S(1)} %collective-permute-done.4.refs_1_), channel_id=1, source_target_pairs={{0,8},{8,0},{16,24},{24,16},{1,9},{9,1},{17,25},{25,17},{2,10},{10... | collective-permute-start | bytes 786440 | tf_op jit(solution)/shard_map/ppermute | solution.py:26
  16.5 5.8 %collective-permute-start.1 = (f32[2,32,512]{2,1,0:T(8,128)S(1)}, f32[2,32,512]{2,1,0:T(8,128)S(1)}, u32[]{:S(2)}, u32[]{:S(2)}) collective-permute-start(f32[2,32,512]{2,1,0:T(8,128)S(1)} %slice_select_fusion.3), channel_id=1, source_target_pairs={{0,2},{1,3},{2,0},{3,1},{4,6},{5,7},{6,4},{7,5},{8,10},{9,11},{10,... | collective-permute-start | bytes 393224 | tf_op jit(solution)/shard_map/ppermute | solution.py:26
  17.8 5.2 %collective-permute-start.3 = (f32[2,32,512]{2,1,0:T(8,128)S(1)}, f32[2,32,512]{2,1,0:T(8,128)S(1)}, u32[]{:S(2)}, u32[]{:S(2)}) collective-permute-start(f32[2,32,512]{2,1,0:T(8,128)S(1)} %slice_select_fusion.2), channel_id=1, source_target_pairs={{0,1},{1,0},{2,3},{3,2},{4,5},{5,4},{6,7},{7,6},{8,9},{9,8},{10,11... | collective-permute-start | bytes 393224 | tf_op jit(solution)/shard_map/ppermute | solution.py:26
  23.1 10.1 %copy-start.2 = (f32[512,512]{1,0:T(8,128)S(1)}, f32[512,512]{1,0:T(8,128)}, u32[]{:S(2)}) copy-start(f32[512,512]{1,0:T(8,128)} %refs_4_.1) | copy-start | bytes 3145732
  23.1 10.1 %copy-start.3 = (f32[512]{0:T(512)S(1)}, f32[512]{0:T(512)}, u32[]{:S(2)}) copy-start(f32[512]{0:T(512)} %param.12) | copy-start | bytes 6148
  23.1 10.1 %copy-start.5 = (s32[1,128]{1,0:T(1,128)S(1)}, s32[1,128]{1,0:T(1,128)}, u32[]{:S(2)}) copy-start(s32[1,128]{1,0:T(1,128)} %refs_6_.5) | copy-start | bytes 1540
  23.1 13.6 %collective-permute-start.10 = (f32[2,2,32,512]{3,2,1,0:T(8,128)S(1)}, f32[2,2,32,512]{3,2,1,0:T(8,128)S(1)}, u32[]{:S(2)}, u32[]{:S(2)}) collective-permute-start(f32[2,2,32,512]{3,2,1,0:T(8,128)S(1)} %pad_maximum_fusion.1), channel_id=1, source_target_pairs={{0,4},{1,5},{2,6},{3,7},{4,0},{5,1},{6,2},{7,3},{8,12},{9,13},{10,... | collective-permute-start | bytes 786440 | tf_op jit(solution)/shard_map/ppermute | solution.py:26
  33.9 7.2 %collective-permute-start.7 = (f32[136,512]{1,0:T(8,128)S(1)}, f32[136,512]{1,0:T(8,128)S(1)}, u32[]{:S(2)}, u32[]{:S(2)}) collective-permute-start(f32[136,512]{1,0:T(8,128)S(1)} %project.1.refs_0_), channel_id=1, source_target_pairs={{0,16},{8,24},{16,0},{24,8},{1,17},{9,25},{17,1},{25,9},{2,18},{10... | collective-permute-start | bytes 835592 | tf_op jit(solution)/shard_map/ppermute | solution.py:26
  36.8 5.0 %collective-permute-start.11 = (f32[2,32,512]{2,1,0:T(8,128)S(1)}, f32[2,32,512]{2,1,0:T(8,128)S(1)}, u32[]{:S(2)}, u32[]{:S(2)}) collective-permute-start(f32[2,32,512]{2,1,0:T(8,128)S(1)} %maximum_select_fusion), channel_id=1, source_target_pairs={{0,2},{1,3},{2,0},{3,1},{4,6},{5,7},{6,4},{7,5},{8,10},{9,11},{10,... | collective-permute-start | bytes 393224 | tf_op jit(solution)/shard_map/ppermute | solution.py:26
  37.6 5.2 %collective-permute-start.13 = (f32[2,32,512]{2,1,0:T(8,128)S(1)}, f32[2,32,512]{2,1,0:T(8,128)S(1)}, u32[]{:S(2)}, u32[]{:S(2)}) collective-permute-start(f32[2,32,512]{2,1,0:T(8,128)S(1)} %maximum_select_fusion.1), channel_id=1, source_target_pairs={{0,1},{1,0},{2,3},{3,2},{4,5},{5,4},{6,7},{7,6},{8,9},{9,8},{10,11... | collective-permute-start | bytes 393224 | tf_op jit(solution)/shard_map/ppermute | solution.py:26
  38.0 6.0 %collective-permute-start.8 = (f32[136,512]{1,0:T(8,128)S(1)}, f32[136,512]{1,0:T(8,128)S(1)}, u32[]{:S(2)}, u32[]{:S(2)}) collective-permute-start(f32[136,512]{1,0:T(8,128)S(1)} %project.1.refs_0_), channel_id=1, source_target_pairs={{0,8},{8,0},{16,24},{24,16},{1,9},{9,1},{17,25},{25,17},{2,10},{10... | collective-permute-start | bytes 835592 | tf_op jit(solution)/shard_map/ppermute | solution.py:26
  41.0 3.0 %collective-permute-start.9 = (f32[136,512]{1,0:T(8,128)S(1)}, f32[136,512]{1,0:T(8,128)S(1)}, u32[]{:S(2)}, u32[]{:S(2)}) collective-permute-start(f32[136,512]{1,0:T(8,128)S(1)} %collective-permute-done.7.refs_1_), channel_id=1, source_target_pairs={{0,8},{8,0},{16,24},{24,16},{1,9},{9,1},{17,25},{25,17},{2,10},{10... | collective-permute-start | bytes 835592 | tf_op jit(solution)/shard_map/ppermute | solution.py:26
  41.9 8.0 %collective-permute-start.12 = (f32[4,32,512]{2,1,0:T(8,128)S(1)}, f32[4,32,512]{2,1,0:T(8,128)S(1)}, u32[]{:S(2)}, u32[]{:S(2)}) collective-permute-start(f32[4,32,512]{2,1,0:T(8,128)S(1)} %pad_maximum_fusion.2), channel_id=1, source_target_pairs={{0,1},{1,0},{2,3},{3,2},{4,5},{5,4},{6,7},{7,6},{8,9},{9,8},{10,11... | collective-permute-start | bytes 786440 | tf_op jit(solution)/shard_map/ppermute | solution.py:26
  42.8 7.3 %collective-permute-start.14 = (f32[4,32,512]{2,1,0:T(8,128)S(1)}, f32[4,32,512]{2,1,0:T(8,128)S(1)}, u32[]{:S(2)}, u32[]{:S(2)}) collective-permute-start(f32[4,32,512]{2,1,0:T(8,128)S(1)} %pad_maximum_fusion.3), channel_id=1, source_target_pairs={{0,2},{1,3},{2,0},{3,1},{4,6},{5,7},{6,4},{7,5},{8,10},{9,11},{10,... | collective-permute-start | bytes 786440 | tf_op jit(solution)/shard_map/ppermute | solution.py:26
  53.3 6.9 %collective-permute-start.15 = (f32[4,32,512]{2,1,0:T(8,128)S(1)}, f32[4,32,512]{2,1,0:T(8,128)S(1)}, u32[]{:S(2)}, u32[]{:S(2)}) collective-permute-start(f32[4,32,512]{2,1,0:T(8,128)S(1)} %get-tuple-element.50), channel_id=1, source_target_pairs={{0,1},{1,0},{2,3},{3,2},{4,5},{5,4},{6,7},{7,6},{8,9},{9,8},{10,11... | collective-permute-start | bytes 786440 | tf_op jit(solution)/shard_map/ppermute | solution.py:26
  55.0 6.8 %collective-permute-start.16 = (f32[4,32,512]{2,1,0:T(8,128)S(1)}, f32[4,32,512]{2,1,0:T(8,128)S(1)}, u32[]{:S(2)}, u32[]{:S(2)}) collective-permute-start(f32[4,32,512]{2,1,0:T(8,128)S(1)} %get-tuple-element.51), channel_id=1, source_target_pairs={{0,2},{1,3},{2,0},{3,1},{4,6},{5,7},{6,4},{7,5},{8,10},{9,11},{10,... | collective-permute-start | bytes 786440 | tf_op jit(solution)/shard_map/ppermute | solution.py:26
  61.8 5.0 %collective-permute-start.19 = (f32[2,32,512]{2,1,0:T(8,128)S(1)}, f32[2,32,512]{2,1,0:T(8,128)S(1)}, u32[]{:S(2)}, u32[]{:S(2)}) collective-permute-start(f32[2,32,512]{2,1,0:T(8,128)S(1)} %get-tuple-element.80), channel_id=1, source_target_pairs={{0,1},{1,0},{2,3},{3,2},{4,5},{5,4},{6,7},{7,6},{8,9},{9,8},{10,11... | collective-permute-start | bytes 393224 | tf_op jit(solution)/shard_map/ppermute | solution.py:26
  62.4 5.0 %collective-permute-start.18 = (f32[2,32,512]{2,1,0:T(8,128)S(1)}, f32[2,32,512]{2,1,0:T(8,128)S(1)}, u32[]{:S(2)}, u32[]{:S(2)}) collective-permute-start(f32[2,32,512]{2,1,0:T(8,128)S(1)} %get-tuple-element.78), channel_id=1, source_target_pairs={{0,2},{1,3},{2,0},{3,1},{4,6},{5,7},{6,4},{7,5},{8,10},{9,11},{10,... | collective-permute-start | bytes 393224 | tf_op jit(solution)/shard_map/ppermute | solution.py:26
  64.2 7.0 %collective-permute-start.17 = (f32[2,128,512]{2,1,0:T(8,128)S(1)}, f32[2,128,512]{2,1,0:T(8,128)S(1)}, u32[]{:S(2)}, u32[]{:S(2)}) collective-permute-start(f32[2,128,512]{2,1,0:T(8,128)S(1)} %get-tuple-element.58), channel_id=1, source_target_pairs={{0,8},{8,0},{16,24},{24,16},{1,9},{9,1},{17,25},{25,17},{2,10},{10... | collective-permute-start | bytes 1572872 | tf_op jit(solution)/shard_map/ppermute | solution.py:26
  67.5 18.0 %copy-start.6 = (s32[4,512]{1,0:T(4,128)S(1)}, s32[4,512]{1,0:T(4,128)}, u32[]{:S(2)}) copy-start(s32[4,512]{1,0:T(4,128)} %ids.1) | copy-start | bytes 24580
  67.6 12.8 %collective-permute-start.20 = (f32[136,512]{1,0:T(8,128)S(1)}, f32[136,512]{1,0:T(8,128)S(1)}, u32[]{:S(2)}, u32[]{:S(2)}) collective-permute-start(f32[136,512]{1,0:T(8,128)S(1)} %maximum_maximum_fusion), channel_id=1, source_target_pairs={{0,4},{1,5},{2,6},{3,7},{4,0},{5,1},{6,2},{7,3},{8,12},{9,13},{10,... | collective-permute-start | bytes 835592 | tf_op jit(solution)/shard_map/ppermute | solution.py:26
  71.3 9.1 %collective-permute-start.21 = (f32[1,128,512]{2,1,0:T(8,128)S(1)}, f32[1,128,512]{2,1,0:T(8,128)S(1)}, u32[]{:S(2)}, u32[]{:S(2)}) collective-permute-start(f32[1,128,512]{2,1,0:T(8,128)S(1)} %get-tuple-element.75), channel_id=1, source_target_pairs={{0,16},{8,24},{16,0},{24,8},{1,17},{9,25},{17,1},{25,9},{2,18},{10... | collective-permute-start | bytes 786440 | tf_op jit(solution)/shard_map/ppermute | solution.py:26
  80.5 5.0 %collective-permute-start.22 = (f32[32,512]{1,0:T(8,128)S(1)}, f32[32,512]{1,0:T(8,128)S(1)}, u32[]{:S(2)}, u32[]{:S(2)}) collective-permute-start(f32[32,512]{1,0:T(8,128)S(1)} %pad_maximum_fusion.5), channel_id=1, source_target_pairs={{0,16},{8,24},{16,0},{24,8},{1,17},{9,25},{17,1},{25,9},{2,18},{10... | collective-permute-start | bytes 196616 | tf_op jit(solution)/shard_map/ppermute | solution.py:31
  81.1 4.4 %collective-permute-start.23 = (f32[32,512]{1,0:T(8,128)S(1)}, f32[32,512]{1,0:T(8,128)S(1)}, u32[]{:S(2)}, u32[]{:S(2)}) collective-permute-start(f32[32,512]{1,0:T(8,128)S(1)} %pad_maximum_fusion.6), channel_id=1, source_target_pairs={{0,8},{8,0},{16,24},{24,16},{1,9},{9,1},{17,25},{25,17},{2,10},{10... | collective-permute-start | bytes 196616 | tf_op jit(solution)/shard_map/ppermute | solution.py:31
  81.1 4.5 %collective-permute-start.24 = (f32[32,512]{1,0:T(8,128)S(1)}, f32[32,512]{1,0:T(8,128)S(1)}, u32[]{:S(2)}, u32[]{:S(2)}) collective-permute-start(f32[32,512]{1,0:T(8,128)S(1)} %pad_maximum_fusion.7), channel_id=1, source_target_pairs={{0,24},{8,16},{16,8},{24,0},{1,25},{9,17},{17,9},{25,1},{2,26},{10... | collective-permute-start | bytes 196616 | tf_op jit(solution)/shard_map/ppermute | solution.py:31
  87.6 6.1 %collective-permute-start.28 = (f32[264,128]{1,0:T(8,128)S(1)}, f32[264,128]{1,0:T(8,128)S(1)}, u32[]{:S(2)}, u32[]{:S(2)}) collective-permute-start(f32[264,128]{1,0:T(8,128)S(1)} %get-tuple-element.69), channel_id=1, source_target_pairs={{0,1},{1,0},{2,3},{3,2},{4,5},{5,4},{6,7},{7,6},{8,9},{9,8},{10,11... | collective-permute-start | bytes 405512 | tf_op jit(solution)/shard_map/ppermute | solution.py:31
  89.2 5.7 %collective-permute-start.29 = (f32[264,128]{1,0:T(8,128)S(1)}, f32[264,128]{1,0:T(8,128)S(1)}, u32[]{:S(2)}, u32[]{:S(2)}) collective-permute-start(f32[264,128]{1,0:T(8,128)S(1)} %get-tuple-element.70), channel_id=1, source_target_pairs={{0,2},{1,3},{2,0},{3,1},{4,6},{5,7},{6,4},{7,5},{8,10},{9,11},{10,... | collective-permute-start | bytes 405512 | tf_op jit(solution)/shard_map/ppermute | solution.py:31
  89.2 6.6 %collective-permute-start.25 = (f32[1,264,128]{2,1,0:T(8,128)S(1)}, f32[1,264,128]{2,1,0:T(8,128)S(1)}, u32[]{:S(2)}, u32[]{:S(2)}) collective-permute-start(f32[1,264,128]{2,1,0:T(8,128)S(1)} %bitcast.38), channel_id=1, source_target_pairs={{0,16},{8,24},{16,0},{24,8},{1,17},{9,25},{17,1},{25,9},{2,18},{10... | collective-permute-start | bytes 405512 | tf_op jit(solution)/shard_map/ppermute | solution.py:26
  94.9 8.4 %collective-permute-start.30 = (f32[2,264,128]{2,1,0:T(8,128)S(1)}, f32[2,264,128]{2,1,0:T(8,128)S(1)}, u32[]{:S(2)}, u32[]{:S(2)}) collective-permute-start(f32[2,264,128]{2,1,0:T(8,128)S(1)} %pad_maximum_fusion.refs_4_), channel_id=1, source_target_pairs={{0,16},{8,24},{16,0},{24,8},{1,17},{9,25},{17,1},{25,9},{2,18},{10... | collective-permute-start | bytes 811016 | tf_op jit(solution)/shard_map/ppermute | solution.py:26
  95.8 5.9 %collective-permute-start.33 = (f32[264,128]{1,0:T(8,128)S(1)}, f32[264,128]{1,0:T(8,128)S(1)}, u32[]{:S(2)}, u32[]{:S(2)}) collective-permute-start(f32[264,128]{1,0:T(8,128)S(1)} %get-tuple-element.71), channel_id=1, source_target_pairs={{0,3},{1,2},{2,1},{3,0},{4,7},{5,6},{6,5},{7,4},{8,11},{9,10},{10,... | collective-permute-start | bytes 405512 | tf_op jit(solution)/shard_map/ppermute | solution.py:31
  96.6 7.3 %collective-permute-start.26 = (f32[1,264,128]{2,1,0:T(8,128)S(1)}, f32[1,264,128]{2,1,0:T(8,128)S(1)}, u32[]{:S(2)}, u32[]{:S(2)}) collective-permute-start(f32[1,264,128]{2,1,0:T(8,128)S(1)} %bitcast.39), channel_id=1, source_target_pairs={{0,8},{8,0},{16,24},{24,16},{1,9},{9,1},{17,25},{25,17},{2,10},{10... | collective-permute-start | bytes 405512 | tf_op jit(solution)/shard_map/ppermute | solution.py:26
  96.6 10.2 %collective-permute-start.31 = (f32[2,264,128]{2,1,0:T(8,128)S(1)}, f32[2,264,128]{2,1,0:T(8,128)S(1)}, u32[]{:S(2)}, u32[]{:S(2)}) collective-permute-start(f32[2,264,128]{2,1,0:T(8,128)S(1)} %pad_maximum_fusion.refs_4_), channel_id=1, source_target_pairs={{0,8},{8,0},{16,24},{24,16},{1,9},{9,1},{17,25},{25,17},{2,10},{10... | collective-permute-start | bytes 811016 | tf_op jit(solution)/shard_map/ppermute | solution.py:26
  101.7 5.0 %collective-permute-start.34 = (f32[1,264,128]{2,1,0:T(8,128)S(1)}, f32[1,264,128]{2,1,0:T(8,128)S(1)}, u32[]{:S(2)}, u32[]{:S(2)}) collective-permute-start(f32[1,264,128]{2,1,0:T(8,128)S(1)} %bitcast.41), channel_id=1, source_target_pairs={{0,16},{8,24},{16,0},{24,8},{1,17},{9,25},{17,1},{25,9},{2,18},{10... | collective-permute-start | bytes 405512 | tf_op jit(solution)/shard_map/ppermute | solution.py:26
  103.3 4.8 %collective-permute-start.32 = (f32[2,264,128]{2,1,0:T(8,128)S(1)}, f32[2,264,128]{2,1,0:T(8,128)S(1)}, u32[]{:S(2)}, u32[]{:S(2)}) collective-permute-start(f32[2,264,128]{2,1,0:T(8,128)S(1)} %collective-permute-done.30.refs_5_), channel_id=1, source_target_pairs={{0,8},{8,0},{16,24},{24,16},{1,9},{9,1},{17,25},{25,17},{2,10},{10... | collective-permute-start | bytes 811016 | tf_op jit(solution)/shard_map/ppermute | solution.py:26
  103.3 3.4 %collective-permute-start.27 = (f32[1,264,128]{2,1,0:T(8,128)S(1)}, f32[1,264,128]{2,1,0:T(8,128)S(1)}, u32[]{:S(2)}, u32[]{:S(2)}) collective-permute-start(f32[1,264,128]{2,1,0:T(8,128)S(1)} %collective-permute-done.25.refs_1_), channel_id=1, source_target_pairs={{0,8},{8,0},{16,24},{24,16},{1,9},{9,1},{17,25},{25,17},{2,10},{10... | collective-permute-start | bytes 405512 | tf_op jit(solution)/shard_map/ppermute | solution.py:26
  103.8 2.9 %collective-permute-start.35 = (f32[1,264,128]{2,1,0:T(8,128)S(1)}, f32[1,264,128]{2,1,0:T(8,128)S(1)}, u32[]{:S(2)}, u32[]{:S(2)}) collective-permute-start(f32[1,264,128]{2,1,0:T(8,128)S(1)} %bitcast.42), channel_id=1, source_target_pairs={{0,8},{8,0},{16,24},{24,16},{1,9},{9,1},{17,25},{25,17},{2,10},{10... | collective-permute-start | bytes 405512 | tf_op jit(solution)/shard_map/ppermute | solution.py:26
  106.7 1.4 %collective-permute-start.36 = (f32[1,264,128]{2,1,0:T(8,128)S(1)}, f32[1,264,128]{2,1,0:T(8,128)S(1)}, u32[]{:S(2)}, u32[]{:S(2)}) collective-permute-start(f32[1,264,128]{2,1,0:T(8,128)S(1)} %collective-permute-done.34.refs_9_), channel_id=1, source_target_pairs={{0,8},{8,0},{16,24},{24,16},{1,9},{9,1},{17,25},{25,17},{2,10},{10... | collective-permute-start | bytes 405512 | tf_op jit(solution)/shard_map/ppermute | solution.py:26

commit v8 on v7

--- a/solution.py
+++ b/solution.py
@@ -410,7 +410,7 @@
             total = total + jnp.where(owners[p] == item ^ r, spread[p], 0.0)
         for c in range(n_rows // LANES):
             out[c * n_dim : (c + 1) * n_dim] = total[:, c * LANES : (c + 1) * LANES]
-        out[n_rows // LANES * n_dim :] = loss[...]
+        out[n_rows // LANES * n_dim :] = loss
 
 
 def owners_of(order, per_panel, owner):
@@ -425,9 +425,13 @@
     spread = []
     for p, r in enumerate(order):
         hot = jnp.where(row == ids[pl.ds(lax.axis_index("seq") ^ r, 1), :], 1.0, 0.0).astype(bf16)
-        both = dot(jnp.concatenate(split(moved[p][...]), axis=0), hot, NT)
+        both = dot(jnp.concatenate(split(moved[p][:n_dim]), axis=0), hot, NT)
         spread.append(both[:n_dim] + both[n_dim:])
-    pieces_kernel(spread, owners_of(order, per_panel, owner), which, loss, outs)
+    total = loss[...]
+    for block in moved:
+        if block.shape[0] > n_dim:
+            total = total + block[n_dim:, :LANES]
+    pieces_kernel(spread, owners_of(order, per_panel, owner), which, total, outs)
 
 
 def spread_rows(order, per_panel, owner, moved, ids, loss, n_item, n_rows):
@@ -446,44 +450,45 @@
     )(owner, ids, loss, *moved)
 
 
-def assemble_kernel(order, members, n_item, n_dim, events, kept, got, *refs):
+def assemble_kernel(order, pair, members, n_item, n_dim, events, kept, got, *refs):
     groups, (out_ref, loss_ref, event_ref, quarter) = refs[:-4], refs[-4:]
     event_ref[...] = kept[...] + got[...]
-    n_seq = len(order)
+    n_rest = len(order)
     me, item = lax.axis_index("seq"), lax.axis_index("item")
     cols = n_item * n_dim
     n_tiles = out_ref.shape[0] // LANES
     block = pl.program_id(0)
 
     def places(k):
-        return [(groups[g], m) for g in range(k, len(groups), n_seq) for m in range(groups[g].shape[0])]
+        return [(groups[g], m) for g in range(k, len(groups), n_rest) for m in range(groups[g].shape[0])]
 
     for c in range(n_tiles):
-        first = (block * n_tiles + c) * 2 * n_dim
         for k, q in enumerate(order):
-            for r, (group, m) in zip(members, places(k)):
-                for chunk in range(2):
-                    place = pl.ds(pl.multiple_of((item ^ r ^ (chunk * n_item // 2)) * n_dim, n_dim), n_dim)
-                    quarter[place] = group[m, pl.ds(pl.multiple_of(first + chunk * n_dim, n_dim), n_dim)]
-            place = pl.ds(pl.multiple_of((me ^ q) * cols, cols), cols)
-            out_ref[c * LANES : (c + 1) * LANES, place] = quarter[...].T
+            for d, across in enumerate(pair):
+                first = ((block * n_tiles + c) * 4 + 2 * d) * n_dim
+                for r, (group, m) in zip(members, places(k)):
+                    for chunk in range(2):
+                        place = pl.ds(pl.multiple_of((item ^ r ^ (chunk * n_item // 2)) * n_dim, n_dim), n_dim)
+                        quarter[2 * k + d, place] = group[m, pl.ds(pl.multiple_of(first + chunk * n_dim, n_dim), n_dim)]
+                place = pl.ds(pl.multiple_of((me ^ q ^ across) * cols, cols), cols)
+                out_ref[c * LANES : (c + 1) * LANES, place] = quarter[2 * k + d].T
 
     @pl.when(block == 0)
     def _():
         total = jnp.zeros((EXTRA, LANES), f32)
-        for k in range(n_seq):
+        for k in range(n_rest):
             for group, m in places(k):
                 total = total + group[m, group.shape[1] - EXTRA :]
         loss_ref[0, 0] = jnp.sum(total) / (EXTRA * LANES * events)
 
 
-def assemble(table, kept, got, order, members, n_item, n_dim, n_rows, events):
-    width = n_item * n_dim * len(order)
-    step = min(n_rows, 256)
+def assemble(table, kept, got, order, pair, members, n_item, n_dim, n_rows, events):
+    width = n_item * n_dim * len(order) * len(pair)
+    step = min(n_rows, 512)
     pieces = sum(table, [])
     rows = pl.BlockSpec((1, kept.shape[1] * step // n_rows, width), lambda j: (0, j, 0))
     return pl.pallas_call(
-        functools.partial(assemble_kernel, order, members, n_item, n_dim, events),
+        functools.partial(assemble_kernel, order, pair, members, n_item, n_dim, events),
         grid=(n_rows // step,),
         in_specs=[rows, rows] + [pl.BlockSpec(memory_space=pltpu.VMEM)] * len(pieces),
         out_specs=[pl.BlockSpec((step, width), lambda j: (j, 0)), pl.BlockSpec(memory_space=pltpu.SMEM), rows],
@@ -492,7 +497,7 @@
             jax.ShapeDtypeStruct((1, 1), f32),
             jax.ShapeDtypeStruct(kept.shape, f32),
         ],
-        scratch_shapes=[pltpu.VMEM((n_item * n_dim, LANES), f32)],
+        scratch_shapes=[pltpu.VMEM((2 * len(order), n_item * n_dim, LANES), f32)],
         compiler_params=params,
         cost_estimate=pl.CostEstimate(flops=0, bytes_accessed=8 * n_rows * width, transcendentals=0),
         name="assemble",
@@ -624,10 +629,17 @@
     total = [kept[0] + other[rows : 2 * rows], sent[0] + other[:rows]]
     loss = loss + other[2 * rows :, :LANES]
     part = n_dim // 2
+    pair = (0, 1 << seq_bits[0])
     moved = []
-    for k, r in enumerate(seq_order):
-        spans = [slice(h * n_seq * part + k * part, h * n_seq * part + (k + 1) * part) for h in range(2)]
-        block = jnp.concatenate([chunk[span] for chunk in total for span in spans], axis=0)
+    for r in seq_order:
+        block = []
+        for d in pair:
+            k = seq_order.index(r ^ d)
+            spans = [slice(h * n_seq * part + k * part, h * n_seq * part + (k + 1) * part) for h in range(2)]
+            block += [chunk[span] for chunk in total for span in spans]
+        if r == pair[1]:
+            block.append(jnp.concatenate([loss] * (n_neg // LANES), axis=1))
+        block = jnp.concatenate(block, axis=0)
         moved.append(send(block, "seq", r) if r else block)
     n_near, top = n_item // 2, 1 << shared[0]
     if aligned:
@@ -636,36 +648,30 @@
         source = s ^ jnp.array(seq_order, i32)
         ids, owner = ids_by_seq[source], panel_owner[source // per_panel]
         hot = (ids[:, :, None] == jnp.arange(n_rows, dtype=i32)).astype(f32)
-        spread = jnp.einsum("pdc,pcr->pdr", jnp.stack(moved), hot, precision=high)
+        loss = loss + moved[seq_order.index(pair[1])][4 * n_dim :, :LANES]
+        moved = jnp.stack([block[: 4 * n_dim] for block in moved])
+        spread = jnp.einsum("pdc,pcr->pdr", moved, hot, precision=high)
         mine = (owner[None, :] == (i ^ jnp.arange(n_near, dtype=i32))[:, None]).astype(f32)
         sent = jnp.sum(mine[:, :, None, None] * spread[None], axis=1)
-        sent = sent.reshape(n_near, 2 * n_dim, -1, LANES).transpose(0, 2, 1, 3).reshape(n_near, -1, LANES)
+        sent = sent.reshape(n_near, 4 * n_dim, -1, LANES).transpose(0, 2, 1, 3).reshape(n_near, -1, LANES)
         sent = [jnp.concatenate([sent[r], loss], axis=0) for r in range(n_near)]
 
-    sent = list(sent)
-    own = sent[0][None]
-    own = [own, swap(own, "seq", seq_bits[0])]
-    sent[3], own[1] = lax.optimization_barrier((sent[3], own[1]))
     taken = [send(sent[r], "item", r) if r else sent[r] for r in range(n_near)]
-    which = [[0], [1, 2], list(range(3, n_near))]
-    table = [own]
-    for members in which[1:]:
-        group = jnp.stack([taken[r] for r in members])
-        table.append([group, swap(group, "seq", seq_bits[0])])
-    members = sum(which, [])
-    for bit in seq_bits[1:]:
-        table = [group + [swap(piece, "seq", bit) for piece in group] for group in table]
+    which = [[0], [1], [2], list(range(3, n_near))]
+    table = [gather_pieces(jnp.stack([taken[r] for r in members]), "seq", seq_bits[1:]) for members in which]
+    members, rest_order = sum(which, []), orders(seq_bits[1:])
     if aligned:
-        table_grad, mean_loss, event_grad = assemble(table, kept_rows, got_rows, seq_order, members, n_item, n_dim, n_rows, group_len * n_item)
+        table_grad, mean_loss, event_grad = assemble(table, kept_rows, got_rows, rest_order, pair, members, n_item, n_dim, n_rows, group_len * n_item)
         mean_loss = mean_loss.reshape(())
     else:
         table = jnp.stack([jnp.concatenate(groups, axis=0) for groups in zip(*table)])
         event_grad = kept_rows + got_rows
         mean_loss = jnp.sum(table[:, :, -1, 0]) / (group_len * n_item)
-        table = table[:, :, :-EXTRA].reshape(n_seq, n_near, -1, 2, n_dim, LANES).transpose(1, 3, 0, 2, 4, 5)
+        table = table[:, :, :-EXTRA].reshape(len(rest_order), n_near, -1, 2, 2, n_dim, LANES).transpose(1, 4, 0, 3, 2, 5, 6)
         table = table.reshape(n_item, n_seq, -1, n_dim, LANES)
         table = true_order(table, [r ^ chunk for r in members for chunk in (0, top)], i).swapaxes(0, 1)
-        table_grad = true_order(table, seq_order, s).transpose(2, 4, 0, 1, 3).reshape(n_rows, width)
+        table = true_order(table, [r ^ d for r in rest_order for d in pair], s)
+        table_grad = table.transpose(2, 4, 0, 1, 3).reshape(n_rows, width)
     return (mean_loss, event_grad, table_grad)
 
 

time: 111 us -> 110 us (level)
  starting transfers between devices: 32.4 us -> 30.5 us
    ppermute x6, waiting for transfers between devices: 12.2 us -> 16.4 us  [send(): return lax.ppermute(block, axis, [(i, i ^ r) for i in range(size)])]
    ppermute x31 -> x26, waiting for transfers between devices: 35.3 us -> 32.1 us  [swap(): return lax.ppermute(block, axis, [(i, i ^ 1 << bit) for i in range(size)])]
    ppermute x31 -> x26, starting transfers between devices: 27.9 us -> 24.8 us  [swap(): return lax.ppermute(block, axis, [(i, i ^ 1 << bit) for i in range(size)])]
    ppermute x6, starting transfers between devices: 4.55 us -> 5.76 us  [send(): return lax.ppermute(block, axis, [(i, i ^ r) for i in range(size)])]
    unnamed x20 -> x32, local copies, waits for them, and re-layouts: 2.23 us -> 2.3 us
  transfers between devices with their start and end apart: 37 -> 32, of which waited for: 21 -> 20; matrix products, arithmetic and copies ran while one was open for 1% -> 1% of each run, Pallas kernels for 16% -> 16%
where the time goes in v8:
time: 110 us; the launch traced here: 109 us
  waiting for transfers between devices  48.5 us (44%)
  starting transfers between devices  30.5 us (28%)
  Pallas kernels  24.6 us (22%)
  local copies, waits for them, and re-layouts  2.91 us (3%)
  between operations  2.35 us (2%)
    ppermute x26, waiting for transfers between devices, swap(): return lax.ppermute(block, axis, [(i, i ^ 1 << bit) for i in range(size)])  32.1 us
    ppermute x26, starting transfers between devices, swap(): return lax.ppermute(block, axis, [(i, i ^ 1 << bit) for i in range(size)])  24.8 us
    ppermute x6, waiting for transfers between devices, send(): return lax.ppermute(block, axis, [(i, i ^ r) for i in range(size)])  16.4 us
    pallas_call x2, Pallas kernels, attend(): pl.pallas_call(functools.partial(attend_kernel, order, n_seq), grid=(coun...  10.1 us
    ppermute x6, starting transfers between devices, send(): return lax.ppermute(block, axis, [(i, i ^ r) for i in range(size)])  5.76 us
    pallas_call x1, Pallas kernels, pick_rows(): pl.pallas_call(functools.partial(pick_kernel, plan), in_specs=[pl.BlockSp...  3.6 us
    pallas_call x1, Pallas kernels, loss_terms(): pl.pallas_call(functools.partial(loss_kernel, plan), in_specs=[vmem] * (2...  3.21 us
    unnamed x32, local copies, waits for them, and re-layouts  2.3 us
  transfers between devices with their start and end apart: 32, of which 20 were waited for; matrix products, arithmetic and copies ran while one was open for 1% of the time, Pallas kernels for 16%

profile of v8, /device:TPU:0, one launch (start us, length us, event | category | flops | bytes accessed | tf_op | source)
XLA Modules:
  0.0 109.4 jit_solution(14619138797810266601)
XLA Ops:
  0.7 3.0 %collective-permute-start.4 = (f32[128,512]{1,0:T(8,128)}, f32[128,512]{1,0:T(8,128)S(1)}, u32[]{:S(2)}, u32[]{:S(2)}) collective-permute-start(f32[128,512]{1,0:T(8,128)} %bitcast.30), channel_id=1, source_target_pairs={{0,16},{8,24},{16,0},{24,8},{1,17},{9,25},{17,1},{25,9},{2,18},{10... | collective-permute-start | bytes 786440 | tf_op jit(solution)/shard_map/ppermute | solution.py:26
  3.7 3.6 %pick_rows.1 = (f32[4,32,512]{2,1,0:T(8,128)}, f32[4,32,512]{2,1,0:T(8,128)}, f32[4,32,512]{2,1,0:T(8,128)}, f32[4,32,512]{2,1,0:T(8,128)}) custom-call(s32[4,512]{1,0:T(4,128)} %ids.1, f32[1024,512]{1,0:T(8,128)} %table_hbm.1), custom_call_target="tpu_custom_call" | custom-call | flops 1073741824 | bytes 2097152 | tf_op jit(solution)/shard_map/pick_rows/pallas_call | solution.py:129
  7.3 1.6 %collective-permute-start = (f32[4,32,512]{2,1,0:T(8,128)}, f32[4,32,512]{2,1,0:T(8,128)S(1)}, u32[]{:S(2)}, u32[]{:S(2)}) collective-permute-start(f32[4,32,512]{2,1,0:T(8,128)} %get-tuple-element.38), channel_id=1, source_target_pairs={{0,1},{1,0},{2,3},{3,2},{4,5},{5,4},{6,7},{7,6},{8,9},{9,8},{10,11... | collective-permute-start | bytes 786440 | tf_op jit(solution)/shard_map/ppermute | solution.py:26
  8.9 1.6 %collective-permute-start.2 = (f32[4,32,512]{2,1,0:T(8,128)}, f32[4,32,512]{2,1,0:T(8,128)S(1)}, u32[]{:S(2)}, u32[]{:S(2)}) collective-permute-start(f32[4,32,512]{2,1,0:T(8,128)} %get-tuple-element.40), channel_id=1, source_target_pairs={{0,2},{1,3},{2,0},{3,1},{4,6},{5,7},{6,4},{7,5},{8,10},{9,11},{10,... | collective-permute-start | bytes 786440 | tf_op jit(solution)/shard_map/ppermute | solution.py:26
  11.1 0.6 dynamic_slice.3
  12.3 0.0 copy-start
  12.4 2.2 %copy-done = f32[512,2048]{1,0:T(8,128)S(1)} copy-done((f32[512,2048]{1,0:T(8,128)S(1)}, f32[512,2048]{1,0:T(8,128)}, u32[]{:S(2)}) %copy-start) | copy-done | bytes 4194328
  14.5 1.6 %prepare.1 = (f32[128,512]{1,0:T(8,128)S(1)}, f32[128,512]{1,0:T(8,128)S(1)}) custom-call(f32[128,512]{1,0:T(8,128)S(1)} %bitcast.32, f32[512,2048]{1,0:T(8,128)S(1)} %copy-done, f32[512,2048]{1,0:T(8,128)S(1)} %copy-done), custom_call_target="tpu_custom_call" | custom-call | flops 402653184 | bytes 2097152 | tf_op jit(solution)/shard_map/prepare/pallas_call | solution.py:155
  16.2 0.3 collective-permute-start.6
  16.5 0.5 collective-permute-start.1
  17.0 0.8 collective-permute-done.2
  17.8 0.8 collective-permute-start.3
  18.6 2.6 %attend.2.refs_0_ = f32[128,128]{1,0:T(8,128)S(1)} custom-call(s32[1,4]{1,0:T(1,128)S(1)} %copy-done.4, f32[128,512]{1,0:T(8,128)S(1)} %bitcast.33, f32[128,512]{1,0:T(8,128)S(1)} %collective-permute-done.4.refs_1_, f32[128,512]{1,0:T(8,128)S(1)} %collective-permute-done.5.refs_2_, f32[128,512]{1,0:T(8,128)S(1)} %collective-permute-done.6.refs_3_, ...), custom_call_target="tpu_custom_call" | custom-call | flops 2000000000 | bytes 2097152 | tf_op jit(solution)/shard_map/attend/pallas_call | solution.py:227
  21.2 1.0 collective-permute-done.1
  22.3 0.7 collective-permute-done.3
  23.0 0.1 fusion
  23.1 0.0 copy-start.2
  23.1 0.0 copy-start.3
  23.1 2.7 %collective-permute-start.10 = (f32[2,2,32,512]{3,2,1,0:T(8,128)S(1)}, f32[2,2,32,512]{3,2,1,0:T(8,128)S(1)}, u32[]{:S(2)}, u32[]{:S(2)}) collective-permute-start(f32[2,2,32,512]{3,2,1,0:T(8,128)S(1)} %pad_maximum_fusion), channel_id=1, source_target_pairs={{0,4},{1,5},{2,6},{3,7},{4,0},{5,1},{6,2},{7,3},{8,12},{9,13},{10,... | collective-permute-start | bytes 786440 | tf_op jit(solution)/shard_map/ppermute | solution.py:26
  25.8 7.4 %attend.3.refs_1_ = f32[128,384]{1,0:T(8,128)S(1)} custom-call(s32[1,4]{1,0:T(1,128)S(1)} %copy-done.4, f32[128,512]{1,0:T(8,128)S(1)} %bitcast.34, f32[128,512]{1,0:T(8,128)S(1)} %collective-permute-done.4.refs_1_, f32[128,512]{1,0:T(8,128)S(1)} %collective-permute-done.5.refs_2_, f32[128,512]{1,0:T(8,128)S(1)} %collective-permute-done.6.refs_3_, ...), custom_call_target="tpu_custom_call" | custom-call | flops 6000000000 | bytes 2097152 | tf_op jit(solution)/shard_map/attend/pallas_call | solution.py:227
  33.3 0.6 project.1.refs_0_
  33.9 0.6 collective-permute-start.7
  34.4 2.3 %collective-permute-done.10 = f32[2,2,32,512]{3,2,1,0:T(8,128)S(1)} collective-permute-done((f32[2,2,32,512]{3,2,1,0:T(8,128)S(1)}, f32[2,2,32,512]{3,2,1,0:T(8,128)S(1)}, u32[]{:S(2)}, u32[]{:S(2)}) %collective-permute-start.10) | collective-permute-done | bytes 262176 | tf_op jit(solution)/shard_map/ppermute | solution.py:26
  36.8 0.7 collective-permute-start.11
  37.6 0.5 collective-permute-start.13
  38.1 3.0 %collective-permute-done.7.refs_1_ = f32[136,512]{1,0:T(8,128)S(1)} collective-permute-done((f32[136,512]{1,0:T(8,128)S(1)}, f32[136,512]{1,0:T(8,128)S(1)}, u32[]{:S(2)}, u32[]{:S(2)}) %collective-permute-start.7) | collective-permute-done | bytes 278560 | tf_op jit(solution)/shard_map/ppermute | solution.py:26
  41.0 0.8 collective-permute-done.11
  41.9 0.5 collective-permute-start.12
  42.4 0.4 collective-permute-done.13
  42.8 1.2 %collective-permute-start.14 = (f32[4,32,512]{2,1,0:T(8,128)S(1)}, f32[4,32,512]{2,1,0:T(8,128)S(1)}, u32[]{:S(2)}, u32[]{:S(2)}) collective-permute-start(f32[4,32,512]{2,1,0:T(8,128)S(1)} %pad_maximum_fusion.2), channel_id=1, source_target_pairs={{0,2},{1,3},{2,0},{3,1},{4,6},{5,7},{6,4},{7,5},{8,10},{9,11},{10,... | collective-permute-start | bytes 786440 | tf_op jit(solution)/shard_map/ppermute | solution.py:26
  44.0 0.3 transpose_outputs.1
  44.4 5.5 %collective-permute-done.12 = f32[4,32,512]{2,1,0:T(8,128)S(1)} collective-permute-done((f32[4,32,512]{2,1,0:T(8,128)S(1)}, f32[4,32,512]{2,1,0:T(8,128)S(1)}, u32[]{:S(2)}, u32[]{:S(2)}) %collective-permute-start.12) | collective-permute-done | bytes 262176 | tf_op jit(solution)/shard_map/ppermute | solution.py:26
  49.9 0.2 collective-permute-done.14
  50.1 3.2 %loss_terms.1 = (f32[4,32,512]{2,1,0:T(8,128)S(1)}, f32[4,32,512]{2,1,0:T(8,128)S(1)}, f32[4,32,512]{2,1,0:T(8,128)S(1)}, f32[4,32,512]{2,1,0:T(8,128)S(1)}, f32...) custom-call(bf16[512,512]{1,0:T(8,128)(2,1)S(1)} %get-tuple-element.44., ...), custom_call_target="tpu_custom_call" | custom-call | flops 1610612736 | bytes 4194304 | tf_op jit(solution)/shard_map/loss_terms/pallas_call | solution.py:366
  53.3 1.7 %collective-permute-start.15 = (f32[4,32,512]{2,1,0:T(8,128)S(1)}, f32[4,32,512]{2,1,0:T(8,128)S(1)}, u32[]{:S(2)}, u32[]{:S(2)}) collective-permute-start(f32[4,32,512]{2,1,0:T(8,128)S(1)} %get-tuple-element.48), channel_id=1, source_target_pairs={{0,1},{1,0},{2,3},{3,2},{4,5},{5,4},{6,7},{7,6},{8,9},{9,8},{10,11... | collective-permute-start | bytes 786440 | tf_op jit(solution)/shard_map/ppermute | solution.py:26
  55.0 1.6 %collective-permute-start.16 = (f32[4,32,512]{2,1,0:T(8,128)S(1)}, f32[4,32,512]{2,1,0:T(8,128)S(1)}, u32[]{:S(2)}, u32[]{:S(2)}) collective-permute-start(f32[4,32,512]{2,1,0:T(8,128)S(1)} %get-tuple-element.49), channel_id=1, source_target_pairs={{0,2},{1,3},{2,0},{3,1},{4,6},{5,7},{6,4},{7,5},{8,10},{9,11},{10,... | collective-permute-start | bytes 786440 | tf_op jit(solution)/shard_map/ppermute | solution.py:26
  56.6 1.0 event_rows.1
  57.6 2.6 %collective-permute-done.15 = f32[4,32,512]{2,1,0:T(8,128)S(1)} collective-permute-done((f32[4,32,512]{2,1,0:T(8,128)S(1)}, f32[4,32,512]{2,1,0:T(8,128)S(1)}, u32[]{:S(2)}, u32[]{:S(2)}) %collective-permute-start.15) | collective-permute-done | bytes 262176 | tf_op jit(solution)/shard_map/ppermute | solution.py:26
  60.2 1.6 %collective-permute-done.16 = f32[4,32,512]{2,1,0:T(8,128)S(1)} collective-permute-done((f32[4,32,512]{2,1,0:T(8,128)S(1)}, f32[4,32,512]{2,1,0:T(8,128)S(1)}, u32[]{:S(2)}, u32[]{:S(2)}) %collective-permute-start.16) | collective-permute-done | bytes 262176 | tf_op jit(solution)/shard_map/ppermute | solution.py:26
  61.8 0.6 collective-permute-start.19
  62.4 1.8 %collective-permute-start.18 = (f32[2,32,512]{2,1,0:T(8,128)S(1)}, f32[2,32,512]{2,1,0:T(8,128)S(1)}, u32[]{:S(2)}, u32[]{:S(2)}) collective-permute-start(f32[2,32,512]{2,1,0:T(8,128)S(1)} %get-tuple-element.74), channel_id=1, source_target_pairs={{0,2},{1,3},{2,0},{3,1},{4,6},{5,7},{6,4},{7,5},{8,10},{9,11},{10,... | collective-permute-start | bytes 393224 | tf_op jit(solution)/shard_map/ppermute | solution.py:26
  64.2 2.6 %collective-permute-done.19 = f32[2,32,512]{2,1,0:T(8,128)S(1)} collective-permute-done((f32[2,32,512]{2,1,0:T(8,128)S(1)}, f32[2,32,512]{2,1,0:T(8,128)S(1)}, u32[]{:S(2)}, u32[]{:S(2)}) %collective-permute-start.19) | collective-permute-done | bytes 131104 | tf_op jit(solution)/shard_map/ppermute | solution.py:26
  66.9 0.6 collective-permute-done.18
  67.5 0.0 copy-start.6
  67.6 3.7 %collective-permute-start.20 = (f32[136,512]{1,0:T(8,128)S(1)}, f32[136,512]{1,0:T(8,128)S(1)}, u32[]{:S(2)}, u32[]{:S(2)}) collective-permute-start(f32[136,512]{1,0:T(8,128)S(1)} %maximum_maximum_fusion), channel_id=1, source_target_pairs={{0,4},{1,5},{2,6},{3,7},{4,0},{5,1},{6,2},{7,3},{8,12},{9,13},{10,... | collective-permute-start | bytes 835592 | tf_op jit(solution)/shard_map/ppermute | solution.py:26
  71.2 0.1 slice_add_fusion
  71.3 0.6 collective-permute-start.21
  71.9 8.5 %collective-permute-done.20 = f32[136,512]{1,0:T(8,128)S(1)} collective-permute-done((f32[136,512]{1,0:T(8,128)S(1)}, f32[136,512]{1,0:T(8,128)S(1)}, u32[]{:S(2)}, u32[]{:S(2)}) %collective-permute-start.20) | collective-permute-done | bytes 278560 | tf_op jit(solution)/shard_map/ppermute | solution.py:26
  80.6 0.6 collective-permute-start.22
  81.2 1.6 %collective-permute-start.23 = (f32[64,512]{1,0:T(8,128)S(1)}, f32[64,512]{1,0:T(8,128)S(1)}, u32[]{:S(2)}, u32[]{:S(2)}) collective-permute-start(f32[64,512]{1,0:T(8,128)S(1)} %get-tuple-element.89), channel_id=1, source_target_pairs={{0,8},{8,0},{16,24},{24,16},{1,9},{9,1},{17,25},{25,17},{2,10},{10... | collective-permute-start | bytes 393224 | tf_op jit(solution)/shard_map/ppermute | solution.py:31
  82.8 4.1 %collective-permute-done.24.refs_3_ = f32[64,512]{1,0:T(8,128)S(1)} collective-permute-done((f32[64,512]{1,0:T(8,128)S(1)}, f32[64,512]{1,0:T(8,128)S(1)}, u32[]{:S(2)}, u32[]{:S(2)}) %collective-permute-start.24) | collective-permute-done | bytes 131104 | tf_op jit(solution)/shard_map/ppermute | solution.py:31
  86.9 0.2 collective-permute-done.22.refs_1_
  87.2 2.2 %spread_rows.1 = (f32[520,128]{1,0:T(8,128)S(1)}, f32[520,128]{1,0:T(8,128)S(1)}, f32[520,128]{1,0:T(8,128)S(1)}, f32[520,128]{1,0:T(8,128)S(1)}) custom-call(s32[4]{0:T(128)S(1)} %copy-done.7, s32[4,512]{1,0:T(4,128)S(1)} %copy-done.6, f32[8,128]{1,0:T(8,128)S(1)} %slice_add_fusion.12.loss, f32[64,512]{1,0:T(8,128)S(1)} %get-tuple-element.90.refs_0_, ...), custom_call_target="tpu_custom_call" | custom-call | flops 536870912 | bytes 2097152 | tf_op jit(solution)/shard_map/spread_rows/pallas_call | solution.py:442
  89.4 1.6 %collective-permute-start.26 = (f32[520,128]{1,0:T(8,128)S(1)}, f32[520,128]{1,0:T(8,128)S(1)}, u32[]{:S(2)}, u32[]{:S(2)}) collective-permute-start(f32[520,128]{1,0:T(8,128)S(1)} %get-tuple-element.65), channel_id=1, source_target_pairs={{0,1},{1,0},{2,3},{3,2},{4,5},{5,4},{6,7},{7,6},{8,9},{9,8},{10,11... | collective-permute-start | bytes 798728 | tf_op jit(solution)/shard_map/ppermute | solution.py:31
  91.1 1.9 %collective-permute-start.30 = (f32[520,128]{1,0:T(8,128)S(1)}, f32[520,128]{1,0:T(8,128)S(1)}, u32[]{:S(2)}, u32[]{:S(2)}) collective-permute-start(f32[520,128]{1,0:T(8,128)S(1)} %get-tuple-element.67), channel_id=1, source_target_pairs={{0,3},{1,2},{2,1},{3,0},{4,7},{5,6},{6,5},{7,4},{8,11},{9,10},{10,... | collective-permute-start | bytes 798728 | tf_op jit(solution)/shard_map/ppermute | solution.py:31
  93.0 0.4 collective-permute-start.25
  93.4 5.1 %collective-permute-done.26 = f32[520,128]{1,0:T(8,128)S(1)} collective-permute-done((f32[520,128]{1,0:T(8,128)S(1)}, f32[520,128]{1,0:T(8,128)S(1)}, u32[]{:S(2)}, u32[]{:S(2)}) %collective-permute-start.26) | collective-permute-done | bytes 266272 | tf_op jit(solution)/shard_map/ppermute | solution.py:31
  98.5 0.4 collective-permute-start.27
  98.9 1.5 %collective-permute-done.28 = f32[520,128]{1,0:T(8,128)S(1)} collective-permute-done((f32[520,128]{1,0:T(8,128)S(1)}, f32[520,128]{1,0:T(8,128)S(1)}, u32[]{:S(2)}, u32[]{:S(2)}) %collective-permute-start.28) | collective-permute-done | bytes 266272 | tf_op jit(solution)/shard_map/ppermute | solution.py:31
  100.3 0.1 collective-permute-start.29
  100.4 5.5 %collective-permute-done.30 = f32[520,128]{1,0:T(8,128)S(1)} collective-permute-done((f32[520,128]{1,0:T(8,128)S(1)}, f32[520,128]{1,0:T(8,128)S(1)}, u32[]{:S(2)}, u32[]{:S(2)}) %collective-permute-start.30) | collective-permute-done | bytes 266272 | tf_op jit(solution)/shard_map/ppermute | solution.py:31
  105.9 0.1 collective-permute-start.31
  106.0 1.4 %collective-permute-done.31.refs_7_ = f32[1,520,128]{2,1,0:T(8,128)S(1)} collective-permute-done((f32[1,520,128]{2,1,0:T(8,128)S(1)}, f32[1,520,128]{2,1,0:T(8,128)S(1)}, u32[]{:S(2)}, u32[]{:S(2)}) %collective-permute-start.31) | collective-permute-done | bytes 266272 | tf_op jit(solution)/shard_map/ppermute | solution.py:26
  107.5 1.9 %assemble.1 = (f32[1024,512]{1,0:T(8,128)}, f32[1,1]{1,0:T(1,128)}, f32[1,128,512]{2,1,0:T(8,128)}) custom-call(f32[1,128,512]{2,1,0:T(8,128)S(1)} %get-tuple-element.72.kept, f32[1,128,512]{2,1,0:T(8,128)S(1)} %collective-permute-done.21.got, f32[1,520,128]{2,1,0:T(8,128)S(1)} %bitcast.37, f32[1,520,128]{2,1,0:T(8,128)S(1)} %collective-permute-done.25.refs_1_, ...), custom_call_target="tpu_custom_call" | custom-call | bytes 4194304 | tf_op jit(solution)/shard_map/assemble/pallas_call | solution.py:490
  (64 shorter events, 0.5 us)
Async XLA Ops:
  0.6 8.2 %copy-start.1 = (f32[1,128,512]{2,1,0:T(8,128)S(1)}, f32[1,128,512]{2,1,0:T(8,128)}, u32[]{:S(2)}) copy-start(f32[1,128,512]{2,1,0:T(8,128)} %param.10) | copy-start | bytes 786436
  0.6 10.4 %copy-start.7 = (s32[4]{0:T(128)S(1)}, s32[4]{0:T(128)}, u32[]{:S(2)}) copy-start(s32[4]{0:T(128)} %owner.1) | copy-start | bytes 52
  0.7 15.5 %collective-permute-start.4 = (f32[128,512]{1,0:T(8,128)}, f32[128,512]{1,0:T(8,128)S(1)}, u32[]{:S(2)}, u32[]{:S(2)}) collective-permute-start(f32[128,512]{1,0:T(8,128)} %bitcast.30), channel_id=1, source_target_pairs={{0,16},{8,24},{16,0},{24,8},{1,17},{9,25},{17,1},{25,9},{2,18},{10... | collective-permute-start | bytes 786440 | tf_op jit(solution)/shard_map/ppermute | solution.py:26
  7.3 9.2 %collective-permute-start = (f32[4,32,512]{2,1,0:T(8,128)}, f32[4,32,512]{2,1,0:T(8,128)S(1)}, u32[]{:S(2)}, u32[]{:S(2)}) collective-permute-start(f32[4,32,512]{2,1,0:T(8,128)} %get-tuple-element.38), channel_id=1, source_target_pairs={{0,1},{1,0},{2,3},{3,2},{4,5},{5,4},{6,7},{7,6},{8,9},{9,8},{10,11... | collective-permute-start | bytes 786440 | tf_op jit(solution)/shard_map/ppermute | solution.py:26
  8.9 9.7 %collective-permute-start.5 = (f32[128,512]{1,0:T(8,128)S(1)}, f32[128,512]{1,0:T(8,128)S(1)}, u32[]{:S(2)}, u32[]{:S(2)}) collective-permute-start(f32[128,512]{1,0:T(8,128)S(1)} %bitcast.31), channel_id=1, source_target_pairs={{0,8},{8,0},{16,24},{24,16},{1,9},{9,1},{17,25},{25,17},{2,10},{10... | collective-permute-start | bytes 786440 | tf_op jit(solution)/shard_map/ppermute | solution.py:26
  8.9 8.9 %collective-permute-start.2 = (f32[4,32,512]{2,1,0:T(8,128)}, f32[4,32,512]{2,1,0:T(8,128)S(1)}, u32[]{:S(2)}, u32[]{:S(2)}) collective-permute-start(f32[4,32,512]{2,1,0:T(8,128)} %get-tuple-element.40), channel_id=1, source_target_pairs={{0,2},{1,3},{2,0},{3,1},{4,6},{5,7},{6,4},{7,5},{8,10},{9,11},{10,... | collective-permute-start | bytes 786440 | tf_op jit(solution)/shard_map/ppermute | solution.py:26
  12.3 2.2 %copy-start = (f32[512,2048]{1,0:T(8,128)S(1)}, f32[512,2048]{1,0:T(8,128)}, u32[]{:S(2)}) copy-start(f32[512,2048]{1,0:T(8,128)} %refs_6_.4) | copy-start | bytes 12582916
  14.5 1.9 %copy-start.8 = (f32[4,32,512]{2,1,0:T(8,128)S(1)}, f32[4,32,512]{2,1,0:T(8,128)}, u32[]{:S(2)}) copy-start(f32[4,32,512]{2,1,0:T(8,128)} %get-tuple-element.37) | copy-start | bytes 786436
  14.5 3.3 %copy-start.9 = (f32[4,32,512]{2,1,0:T(8,128)S(1)}, f32[4,32,512]{2,1,0:T(8,128)}, u32[]{:S(2)}) copy-start(f32[4,32,512]{2,1,0:T(8,128)} %get-tuple-element.39) | copy-start | bytes 786436
  14.5 4.1 %copy-start.4 = (s32[1,4]{1,0:T(1,128)S(1)}, s32[1,4]{1,0:T(1,128)}, u32[]{:S(2)}) copy-start(s32[1,4]{1,0:T(1,128)} %lengths.3) | copy-start | bytes 52
  16.2 2.4 %collective-permute-start.6 = (f32[128,512]{1,0:T(8,128)S(1)}, f32[128,512]{1,0:T(8,128)S(1)}, u32[]{:S(2)}, u32[]{:S(2)}) collective-permute-start(f32[128,512]{1,0:T(8,128)S(1)} %collective-permute-done.4.refs_1_), channel_id=1, source_target_pairs={{0,8},{8,0},{16,24},{24,16},{1,9},{9,1},{17,25},{25,17},{2,10},{10... | collective-permute-start | bytes 786440 | tf_op jit(solution)/shard_map/ppermute | solution.py:26
  16.5 5.8 %collective-permute-start.1 = (f32[2,32,512]{2,1,0:T(8,128)S(1)}, f32[2,32,512]{2,1,0:T(8,128)S(1)}, u32[]{:S(2)}, u32[]{:S(2)}) collective-permute-start(f32[2,32,512]{2,1,0:T(8,128)S(1)} %slice_select_fusion.3), channel_id=1, source_target_pairs={{0,2},{1,3},{2,0},{3,1},{4,6},{5,7},{6,4},{7,5},{8,10},{9,11},{10,... | collective-permute-start | bytes 393224 | tf_op jit(solution)/shard_map/ppermute | solution.py:26
  17.8 5.2 %collective-permute-start.3 = (f32[2,32,512]{2,1,0:T(8,128)S(1)}, f32[2,32,512]{2,1,0:T(8,128)S(1)}, u32[]{:S(2)}, u32[]{:S(2)}) collective-permute-start(f32[2,32,512]{2,1,0:T(8,128)S(1)} %slice_select_fusion.2), channel_id=1, source_target_pairs={{0,1},{1,0},{2,3},{3,2},{4,5},{5,4},{6,7},{7,6},{8,9},{9,8},{10,11... | collective-permute-start | bytes 393224 | tf_op jit(solution)/shard_map/ppermute | solution.py:26
  23.1 10.1 %copy-start.2 = (f32[512,512]{1,0:T(8,128)S(1)}, f32[512,512]{1,0:T(8,128)}, u32[]{:S(2)}) copy-start(f32[512,512]{1,0:T(8,128)} %refs_4_.1) | copy-start | bytes 3145732
  23.1 10.1 %copy-start.3 = (f32[512]{0:T(512)S(1)}, f32[512]{0:T(512)}, u32[]{:S(2)}) copy-start(f32[512]{0:T(512)} %param.12) | copy-start | bytes 6148
  23.1 10.1 %copy-start.5 = (s32[1,128]{1,0:T(1,128)S(1)}, s32[1,128]{1,0:T(1,128)}, u32[]{:S(2)}) copy-start(s32[1,128]{1,0:T(1,128)} %refs_6_.5) | copy-start | bytes 1540
  23.1 13.6 %collective-permute-start.10 = (f32[2,2,32,512]{3,2,1,0:T(8,128)S(1)}, f32[2,2,32,512]{3,2,1,0:T(8,128)S(1)}, u32[]{:S(2)}, u32[]{:S(2)}) collective-permute-start(f32[2,2,32,512]{3,2,1,0:T(8,128)S(1)} %pad_maximum_fusion), channel_id=1, source_target_pairs={{0,4},{1,5},{2,6},{3,7},{4,0},{5,1},{6,2},{7,3},{8,12},{9,13},{10,... | collective-permute-start | bytes 786440 | tf_op jit(solution)/shard_map/ppermute | solution.py:26
  33.9 7.2 %collective-permute-start.7 = (f32[136,512]{1,0:T(8,128)S(1)}, f32[136,512]{1,0:T(8,128)S(1)}, u32[]{:S(2)}, u32[]{:S(2)}) collective-permute-start(f32[136,512]{1,0:T(8,128)S(1)} %project.1.refs_0_), channel_id=1, source_target_pairs={{0,16},{8,24},{16,0},{24,8},{1,17},{9,25},{17,1},{25,9},{2,18},{10... | collective-permute-start | bytes 835592 | tf_op jit(solution)/shard_map/ppermute | solution.py:26
  36.8 5.0 %collective-permute-start.11 = (f32[2,32,512]{2,1,0:T(8,128)S(1)}, f32[2,32,512]{2,1,0:T(8,128)S(1)}, u32[]{:S(2)}, u32[]{:S(2)}) collective-permute-start(f32[2,32,512]{2,1,0:T(8,128)S(1)} %maximum_select_fusion), channel_id=1, source_target_pairs={{0,2},{1,3},{2,0},{3,1},{4,6},{5,7},{6,4},{7,5},{8,10},{9,11},{10,... | collective-permute-start | bytes 393224 | tf_op jit(solution)/shard_map/ppermute | solution.py:26
  37.6 5.2 %collective-permute-start.13 = (f32[2,32,512]{2,1,0:T(8,128)S(1)}, f32[2,32,512]{2,1,0:T(8,128)S(1)}, u32[]{:S(2)}, u32[]{:S(2)}) collective-permute-start(f32[2,32,512]{2,1,0:T(8,128)S(1)} %maximum_select_fusion.1), channel_id=1, source_target_pairs={{0,1},{1,0},{2,3},{3,2},{4,5},{5,4},{6,7},{7,6},{8,9},{9,8},{10,11... | collective-permute-start | bytes 393224 | tf_op jit(solution)/shard_map/ppermute | solution.py:26
  38.1 6.0 %collective-permute-start.8 = (f32[136,512]{1,0:T(8,128)S(1)}, f32[136,512]{1,0:T(8,128)S(1)}, u32[]{:S(2)}, u32[]{:S(2)}) collective-permute-start(f32[136,512]{1,0:T(8,128)S(1)} %project.1.refs_0_), channel_id=1, source_target_pairs={{0,8},{8,0},{16,24},{24,16},{1,9},{9,1},{17,25},{25,17},{2,10},{10... | collective-permute-start | bytes 835592 | tf_op jit(solution)/shard_map/ppermute | solution.py:26
  41.0 3.0 %collective-permute-start.9 = (f32[136,512]{1,0:T(8,128)S(1)}, f32[136,512]{1,0:T(8,128)S(1)}, u32[]{:S(2)}, u32[]{:S(2)}) collective-permute-start(f32[136,512]{1,0:T(8,128)S(1)} %collective-permute-done.7.refs_1_), channel_id=1, source_target_pairs={{0,8},{8,0},{16,24},{24,16},{1,9},{9,1},{17,25},{25,17},{2,10},{10... | collective-permute-start | bytes 835592 | tf_op jit(solution)/shard_map/ppermute | solution.py:26
  41.9 8.0 %collective-permute-start.12 = (f32[4,32,512]{2,1,0:T(8,128)S(1)}, f32[4,32,512]{2,1,0:T(8,128)S(1)}, u32[]{:S(2)}, u32[]{:S(2)}) collective-permute-start(f32[4,32,512]{2,1,0:T(8,128)S(1)} %pad_maximum_fusion.1), channel_id=1, source_target_pairs={{0,1},{1,0},{2,3},{3,2},{4,5},{5,4},{6,7},{7,6},{8,9},{9,8},{10,11... | collective-permute-start | bytes 786440 | tf_op jit(solution)/shard_map/ppermute | solution.py:26
  42.8 7.3 %collective-permute-start.14 = (f32[4,32,512]{2,1,0:T(8,128)S(1)}, f32[4,32,512]{2,1,0:T(8,128)S(1)}, u32[]{:S(2)}, u32[]{:S(2)}) collective-permute-start(f32[4,32,512]{2,1,0:T(8,128)S(1)} %pad_maximum_fusion.2), channel_id=1, source_target_pairs={{0,2},{1,3},{2,0},{3,1},{4,6},{5,7},{6,4},{7,5},{8,10},{9,11},{10,... | collective-permute-start | bytes 786440 | tf_op jit(solution)/shard_map/ppermute | solution.py:26
  53.3 6.9 %collective-permute-start.15 = (f32[4,32,512]{2,1,0:T(8,128)S(1)}, f32[4,32,512]{2,1,0:T(8,128)S(1)}, u32[]{:S(2)}, u32[]{:S(2)}) collective-permute-start(f32[4,32,512]{2,1,0:T(8,128)S(1)} %get-tuple-element.48), channel_id=1, source_target_pairs={{0,1},{1,0},{2,3},{3,2},{4,5},{5,4},{6,7},{7,6},{8,9},{9,8},{10,11... | collective-permute-start | bytes 786440 | tf_op jit(solution)/shard_map/ppermute | solution.py:26
  55.0 6.8 %collective-permute-start.16 = (f32[4,32,512]{2,1,0:T(8,128)S(1)}, f32[4,32,512]{2,1,0:T(8,128)S(1)}, u32[]{:S(2)}, u32[]{:S(2)}) collective-permute-start(f32[4,32,512]{2,1,0:T(8,128)S(1)} %get-tuple-element.49), channel_id=1, source_target_pairs={{0,2},{1,3},{2,0},{3,1},{4,6},{5,7},{6,4},{7,5},{8,10},{9,11},{10,... | collective-permute-start | bytes 786440 | tf_op jit(solution)/shard_map/ppermute | solution.py:26
  61.8 5.0 %collective-permute-start.19 = (f32[2,32,512]{2,1,0:T(8,128)S(1)}, f32[2,32,512]{2,1,0:T(8,128)S(1)}, u32[]{:S(2)}, u32[]{:S(2)}) collective-permute-start(f32[2,32,512]{2,1,0:T(8,128)S(1)} %get-tuple-element.76), channel_id=1, source_target_pairs={{0,1},{1,0},{2,3},{3,2},{4,5},{5,4},{6,7},{7,6},{8,9},{9,8},{10,11... | collective-permute-start | bytes 393224 | tf_op jit(solution)/shard_map/ppermute | solution.py:26
  62.4 5.0 %collective-permute-start.18 = (f32[2,32,512]{2,1,0:T(8,128)S(1)}, f32[2,32,512]{2,1,0:T(8,128)S(1)}, u32[]{:S(2)}, u32[]{:S(2)}) collective-permute-start(f32[2,32,512]{2,1,0:T(8,128)S(1)} %get-tuple-element.74), channel_id=1, source_target_pairs={{0,2},{1,3},{2,0},{3,1},{4,6},{5,7},{6,4},{7,5},{8,10},{9,11},{10,... | collective-permute-start | bytes 393224 | tf_op jit(solution)/shard_map/ppermute | solution.py:26
  64.2 7.0 %collective-permute-start.17 = (f32[2,128,512]{2,1,0:T(8,128)S(1)}, f32[2,128,512]{2,1,0:T(8,128)S(1)}, u32[]{:S(2)}, u32[]{:S(2)}) collective-permute-start(f32[2,128,512]{2,1,0:T(8,128)S(1)} %get-tuple-element.56), channel_id=1, source_target_pairs={{0,8},{8,0},{16,24},{24,16},{1,9},{9,1},{17,25},{25,17},{2,10},{10... | collective-permute-start | bytes 1572872 | tf_op jit(solution)/shard_map/ppermute | solution.py:26
  67.5 19.7 %copy-start.6 = (s32[4,512]{1,0:T(4,128)S(1)}, s32[4,512]{1,0:T(4,128)}, u32[]{:S(2)}) copy-start(s32[4,512]{1,0:T(4,128)} %ids.1) | copy-start | bytes 24580
  67.6 12.8 %collective-permute-start.20 = (f32[136,512]{1,0:T(8,128)S(1)}, f32[136,512]{1,0:T(8,128)S(1)}, u32[]{:S(2)}, u32[]{:S(2)}) collective-permute-start(f32[136,512]{1,0:T(8,128)S(1)} %maximum_maximum_fusion), channel_id=1, source_target_pairs={{0,4},{1,5},{2,6},{3,7},{4,0},{5,1},{6,2},{7,3},{8,12},{9,13},{10,... | collective-permute-start | bytes 835592 | tf_op jit(solution)/shard_map/ppermute | solution.py:26
  71.3 9.1 %collective-permute-start.21 = (f32[1,128,512]{2,1,0:T(8,128)S(1)}, f32[1,128,512]{2,1,0:T(8,128)S(1)}, u32[]{:S(2)}, u32[]{:S(2)}) collective-permute-start(f32[1,128,512]{2,1,0:T(8,128)S(1)} %get-tuple-element.71), channel_id=1, source_target_pairs={{0,16},{8,24},{16,0},{24,8},{1,17},{9,25},{17,1},{25,9},{2,18},{10... | collective-permute-start | bytes 786440 | tf_op jit(solution)/shard_map/ppermute | solution.py:26
  80.6 6.5 %collective-permute-start.22 = (f32[72,512]{1,0:T(8,128)S(1)}, f32[72,512]{1,0:T(8,128)S(1)}, u32[]{:S(2)}, u32[]{:S(2)}) collective-permute-start(f32[72,512]{1,0:T(8,128)S(1)} %constant_dynamic-update-slice_fusion.8), channel_id=1, source_target_pairs={{0,16},{8,24},{16,0},{24,8},{1,17},{9,25},{17,1},{25,9},{2,18},{10... | collective-permute-start | bytes 442376 | tf_op jit(solution)/shard_map/ppermute | solution.py:31
  81.2 5.7 %collective-permute-start.24 = (f32[64,512]{1,0:T(8,128)S(1)}, f32[64,512]{1,0:T(8,128)S(1)}, u32[]{:S(2)}, u32[]{:S(2)}) collective-permute-start(f32[64,512]{1,0:T(8,128)S(1)} %get-tuple-element.87), channel_id=1, source_target_pairs={{0,24},{8,16},{16,8},{24,0},{1,25},{9,17},{17,9},{25,1},{2,26},{10... | collective-permute-start | bytes 393224 | tf_op jit(solution)/shard_map/ppermute | solution.py:31
  81.2 5.7 %collective-permute-start.23 = (f32[64,512]{1,0:T(8,128)S(1)}, f32[64,512]{1,0:T(8,128)S(1)}, u32[]{:S(2)}, u32[]{:S(2)}) collective-permute-start(f32[64,512]{1,0:T(8,128)S(1)} %get-tuple-element.89), channel_id=1, source_target_pairs={{0,8},{8,0},{16,24},{24,16},{1,9},{9,1},{17,25},{25,17},{2,10},{10... | collective-permute-start | bytes 393224 | tf_op jit(solution)/shard_map/ppermute | solution.py:31
  89.4 9.1 %collective-permute-start.26 = (f32[520,128]{1,0:T(8,128)S(1)}, f32[520,128]{1,0:T(8,128)S(1)}, u32[]{:S(2)}, u32[]{:S(2)}) collective-permute-start(f32[520,128]{1,0:T(8,128)S(1)} %get-tuple-element.65), channel_id=1, source_target_pairs={{0,1},{1,0},{2,3},{3,2},{4,5},{5,4},{6,7},{7,6},{8,9},{9,8},{10,11... | collective-permute-start | bytes 798728 | tf_op jit(solution)/shard_map/ppermute | solution.py:31
  91.1 9.3 %collective-permute-start.28 = (f32[520,128]{1,0:T(8,128)S(1)}, f32[520,128]{1,0:T(8,128)S(1)}, u32[]{:S(2)}, u32[]{:S(2)}) collective-permute-start(f32[520,128]{1,0:T(8,128)S(1)} %get-tuple-element.66), channel_id=1, source_target_pairs={{0,2},{1,3},{2,0},{3,1},{4,6},{5,7},{6,4},{7,5},{8,10},{9,11},{10,... | collective-permute-start | bytes 798728 | tf_op jit(solution)/shard_map/ppermute | solution.py:31
  91.1 14.8 %collective-permute-start.30 = (f32[520,128]{1,0:T(8,128)S(1)}, f32[520,128]{1,0:T(8,128)S(1)}, u32[]{:S(2)}, u32[]{:S(2)}) collective-permute-start(f32[520,128]{1,0:T(8,128)S(1)} %get-tuple-element.67), channel_id=1, source_target_pairs={{0,3},{1,2},{2,1},{3,0},{4,7},{5,6},{6,5},{7,4},{8,11},{9,10},{10,... | collective-permute-start | bytes 798728 | tf_op jit(solution)/shard_map/ppermute | solution.py:31
  93.0 13.0 %collective-permute-start.25 = (f32[1,520,128]{2,1,0:T(8,128)S(1)}, f32[1,520,128]{2,1,0:T(8,128)S(1)}, u32[]{:S(2)}, u32[]{:S(2)}) collective-permute-start(f32[1,520,128]{2,1,0:T(8,128)S(1)} %bitcast.36), channel_id=1, source_target_pairs={{0,8},{8,0},{16,24},{24,16},{1,9},{9,1},{17,25},{25,17},{2,10},{10... | collective-permute-start | bytes 798728 | tf_op jit(solution)/shard_map/ppermute | solution.py:26
  98.5 7.5 %collective-permute-start.27 = (f32[1,520,128]{2,1,0:T(8,128)S(1)}, f32[1,520,128]{2,1,0:T(8,128)S(1)}, u32[]{:S(2)}, u32[]{:S(2)}) collective-permute-start(f32[1,520,128]{2,1,0:T(8,128)S(1)} %bitcast.38), channel_id=1, source_target_pairs={{0,8},{8,0},{16,24},{24,16},{1,9},{9,1},{17,25},{25,17},{2,10},{10... | collective-permute-start | bytes 798728 | tf_op jit(solution)/shard_map/ppermute | solution.py:26
  100.3 5.7 %collective-permute-start.29 = (f32[1,520,128]{2,1,0:T(8,128)S(1)}, f32[1,520,128]{2,1,0:T(8,128)S(1)}, u32[]{:S(2)}, u32[]{:S(2)}) collective-permute-start(f32[1,520,128]{2,1,0:T(8,128)S(1)} %bitcast.40), channel_id=1, source_target_pairs={{0,8},{8,0},{16,24},{24,16},{1,9},{9,1},{17,25},{25,17},{2,10},{10... | collective-permute-start | bytes 798728 | tf_op jit(solution)/shard_map/ppermute | solution.py:26
  105.9 1.5 %collective-permute-start.31 = (f32[1,520,128]{2,1,0:T(8,128)S(1)}, f32[1,520,128]{2,1,0:T(8,128)S(1)}, u32[]{:S(2)}, u32[]{:S(2)}) collective-permute-start(f32[1,520,128]{2,1,0:T(8,128)S(1)} %bitcast.42), channel_id=1, source_target_pairs={{0,8},{8,0},{16,24},{24,16},{1,9},{9,1},{17,25},{25,17},{2,10},{10... | collective-permute-start | bytes 798728 | tf_op jit(solution)/shard_map/ppermute | solution.py:26

commit v9 on v8

--- a/solution.py
+++ b/solution.py
@@ -417,15 +417,32 @@
     return [owner[(lax.axis_index("seq") ^ r) // per_panel] for r in order]
 
 
-def spread_kernel(order, per_panel, which, owner, ids, loss, *refs):
+def hot_kernel(order, ids, out_ref):
+    _, n_rows, n_neg = out_ref.shape
+    row = lax.broadcasted_iota(i32, (n_rows, n_neg), 0)
+    for p, r in enumerate(order):
+        out_ref[p] = jnp.where(row == ids[pl.ds(lax.axis_index("seq") ^ r, 1), :], 1.0, 0.0).astype(bf16)
+
+
+def hot_rows(order, ids, n_rows):
+    vmem = pl.BlockSpec(memory_space=pltpu.VMEM)
+    return pl.pallas_call(
+        functools.partial(hot_kernel, order),
+        in_specs=[vmem],
+        out_specs=vmem,
+        out_shape=jax.ShapeDtypeStruct((len(order), n_rows, ids.shape[1]), bf16),
+        compiler_params=params,
+        cost_estimate=pl.CostEstimate(flops=0, bytes_accessed=2**22, transcendentals=0),
+        name="hot_rows",
+    )(ids)
+
+
+def spread_kernel(order, per_panel, which, owner, hot, loss, *refs):
     moved, outs = refs[: len(order)], refs[len(order) :]
-    n_dim, n_neg = moved[0].shape
-    n_rows = (outs[0].shape[0] - EXTRA) // n_dim * LANES
-    row = lax.broadcasted_iota(i32, (n_rows, n_neg), 0)
+    n_dim = moved[0].shape[0]
     spread = []
-    for p, r in enumerate(order):
-        hot = jnp.where(row == ids[pl.ds(lax.axis_index("seq") ^ r, 1), :], 1.0, 0.0).astype(bf16)
-        both = dot(jnp.concatenate(split(moved[p][:n_dim]), axis=0), hot, NT)
+    for p in range(len(order)):
+        both = dot(jnp.concatenate(split(moved[p][:n_dim]), axis=0), hot[p], NT)
         spread.append(both[:n_dim] + both[n_dim:])
     total = loss[...]
     for block in moved:
@@ -434,7 +451,7 @@
     pieces_kernel(spread, owners_of(order, per_panel, owner), which, total, outs)
 
 
-def spread_rows(order, per_panel, owner, moved, ids, loss, n_item, n_rows):
+def spread_rows(order, per_panel, owner, moved, hot, loss, n_item, n_rows):
     vmem = pl.BlockSpec(memory_space=pltpu.VMEM)
     smem = pl.BlockSpec(memory_space=pltpu.SMEM)
     n_dim = moved[0].shape[0]
@@ -447,7 +464,7 @@
         compiler_params=params,
         cost_estimate=pl.CostEstimate(flops=4 * len(moved) * moved[0].size * n_rows, bytes_accessed=2**21, transcendentals=0),
         name="spread_rows",
-    )(owner, ids, loss, *moved)
+    )(owner, hot, loss, *moved)
 
 
 def assemble_kernel(order, pair, members, n_item, n_dim, events, kept, got, *refs):
@@ -624,7 +641,8 @@
             half = kept_rows.shape[0] // 2
             sent_rows = kept_rows[half:] + got_rows[half:]
             kept_rows = kept_rows[:half] + got_rows[:half]
-    other, got_rows = lax.optimization_barrier((other, got_rows))
+    hot = hot_rows(tuple(seq_order), ids_by_seq, n_rows) if aligned else ids_by_seq
+    other, got_rows, hot = lax.optimization_barrier((other, got_rows, hot))
     rows = kept.shape[1]
     total = [kept[0] + other[rows : 2 * rows], sent[0] + other[:rows]]
     loss = loss + other[2 * rows :, :LANES]
@@ -643,7 +661,7 @@
         moved.append(send(block, "seq", r) if r else block)
     n_near, top = n_item // 2, 1 << shared[0]
     if aligned:
-        sent = spread_rows(seq_order, per_panel, panel_owner, moved, ids_by_seq, loss, n_near, n_rows)
+        sent = spread_rows(seq_order, per_panel, panel_owner, moved, hot, loss, n_near, n_rows)
     else:
         source = s ^ jnp.array(seq_order, i32)
         ids, owner = ids_by_seq[source], panel_owner[source // per_panel]

time: 110 us -> 110 us (level)
  waiting for transfers between devices: 48.5 us -> 47 us
    ppermute x26, waiting for transfers between devices: 32.1 us -> 30.6 us  [swap(): return lax.ppermute(block, axis, [(i, i ^ 1 << bit) for i in range(size)])]
  transfers between devices with their start and end apart: 32 -> 32, of which waited for: 20 -> 20; matrix products, arithmetic and copies ran while one was open for 1% -> 1% of each run, Pallas kernels for 16% -> 17%
where the time goes in v9:
time: 110 us
  waiting for transfers between devices  47 us (43%)
  starting transfers between devices  30.8 us (28%)
  Pallas kernels  25.3 us (23%)
  local copies, waits for them, and re-layouts  3.57 us (3%)
  between operations  2.35 us (2%)
    ppermute x26, waiting for transfers between devices, swap(): return lax.ppermute(block, axis, [(i, i ^ 1 << bit) for i in range(size)])  30.6 us
    ppermute x26, starting transfers between devices, swap(): return lax.ppermute(block, axis, [(i, i ^ 1 << bit) for i in range(size)])  25 us
    ppermute x6, waiting for transfers between devices, send(): return lax.ppermute(block, axis, [(i, i ^ r) for i in range(size)])  16.4 us
    pallas_call x2, Pallas kernels, attend(): pl.pallas_call(functools.partial(attend_kernel, order, n_seq), grid=(coun...  10.1 us
    ppermute x6, starting transfers between devices, send(): return lax.ppermute(block, axis, [(i, i ^ r) for i in range(size)])  5.76 us
    pallas_call x1, Pallas kernels, pick_rows(): pl.pallas_call(functools.partial(pick_kernel, plan), in_specs=[pl.BlockSp...  3.6 us
    pallas_call x1, Pallas kernels, loss_terms(): pl.pallas_call(functools.partial(loss_kernel, plan), in_specs=[vmem] * (2...  3.22 us
    unnamed x32, local copies, waits for them, and re-layouts  2.3 us
  transfers between devices with their start and end apart: 32, of which 20 were waited for; matrix products, arithmetic and copies ran while one was open for 1% of the time, Pallas kernels for 17%

profile of v9, /device:TPU:0, one launch (start us, length us, event | category | flops | bytes accessed | tf_op | source)
XLA Modules:
  0.0 109.6 jit_solution(3595237343271962139)
XLA Ops:
  0.6 0.0 copy-start.1
  0.6 3.0 %collective-permute-start.4 = (f32[128,512]{1,0:T(8,128)}, f32[128,512]{1,0:T(8,128)S(1)}, u32[]{:S(2)}, u32[]{:S(2)}) collective-permute-start(f32[128,512]{1,0:T(8,128)} %bitcast.30), channel_id=1, source_target_pairs={{0,16},{8,24},{16,0},{24,8},{1,17},{9,25},{17,1},{25,9},{2,18},{10... | collective-permute-start | bytes 786440 | tf_op jit(solution)/shard_map/ppermute | solution.py:26
  3.7 3.6 %pick_rows.1 = (f32[4,32,512]{2,1,0:T(8,128)}, f32[4,32,512]{2,1,0:T(8,128)}, f32[4,32,512]{2,1,0:T(8,128)}, f32[4,32,512]{2,1,0:T(8,128)}) custom-call(s32[4,512]{1,0:T(4,128)} %ids.1, f32[1024,512]{1,0:T(8,128)} %table_hbm.1), custom_call_target="tpu_custom_call" | custom-call | flops 1073741824 | bytes 2097152 | tf_op jit(solution)/shard_map/pick_rows/pallas_call | solution.py:129
  7.3 1.6 %collective-permute-start = (f32[4,32,512]{2,1,0:T(8,128)}, f32[4,32,512]{2,1,0:T(8,128)S(1)}, u32[]{:S(2)}, u32[]{:S(2)}) collective-permute-start(f32[4,32,512]{2,1,0:T(8,128)} %get-tuple-element.39), channel_id=1, source_target_pairs={{0,1},{1,0},{2,3},{3,2},{4,5},{5,4},{6,7},{7,6},{8,9},{9,8},{10,11... | collective-permute-start | bytes 786440 | tf_op jit(solution)/shard_map/ppermute | solution.py:26
  8.8 1.6 %collective-permute-start.2 = (f32[4,32,512]{2,1,0:T(8,128)}, f32[4,32,512]{2,1,0:T(8,128)S(1)}, u32[]{:S(2)}, u32[]{:S(2)}) collective-permute-start(f32[4,32,512]{2,1,0:T(8,128)} %get-tuple-element.41), channel_id=1, source_target_pairs={{0,2},{1,3},{2,0},{3,1},{4,6},{5,7},{6,4},{7,5},{8,10},{9,11},{10,... | collective-permute-start | bytes 786440 | tf_op jit(solution)/shard_map/ppermute | solution.py:26
  11.1 1.2 %dynamic_slice.3 = s32[1]{0:T(128)} dynamic-slice(s32[4]{0:T(128)} %owner.1, s32[]{:T(128)S(6)} %select_n.46), dynamic_slice_sizes={1} | dynamic-slice | bytes 12 | tf_op jit(solution)/shard_map/dynamic_slice | solution.py:557
  13.0 2.2 %copy-done = f32[512,2048]{1,0:T(8,128)S(1)} copy-done((f32[512,2048]{1,0:T(8,128)S(1)}, f32[512,2048]{1,0:T(8,128)}, u32[]{:S(2)}) %copy-start) | copy-done | bytes 4194328
  15.2 1.6 %prepare.1 = (f32[128,512]{1,0:T(8,128)S(1)}, f32[128,512]{1,0:T(8,128)S(1)}) custom-call(f32[128,512]{1,0:T(8,128)S(1)} %bitcast.32, f32[512,2048]{1,0:T(8,128)S(1)} %copy-done, f32[512,2048]{1,0:T(8,128)S(1)} %copy-done), custom_call_target="tpu_custom_call" | custom-call | flops 402653184 | bytes 2097152 | tf_op jit(solution)/shard_map/prepare/pallas_call | solution.py:155
  16.8 0.3 collective-permute-start.6
  17.2 0.5 collective-permute-start.1
  17.7 0.1 collective-permute-done.2
  17.8 0.8 collective-permute-start.3
  18.6 2.6 %attend.2.refs_0_ = f32[128,128]{1,0:T(8,128)S(1)} custom-call(s32[1,4]{1,0:T(1,128)S(1)} %copy-done.5, f32[128,512]{1,0:T(8,128)S(1)} %bitcast.33, f32[128,512]{1,0:T(8,128)S(1)} %collective-permute-done.4.refs_1_, f32[128,512]{1,0:T(8,128)S(1)} %collective-permute-done.5.refs_2_, f32[128,512]{1,0:T(8,128)S(1)} %collective-permute-done.6.refs_3_, ...), custom_call_target="tpu_custom_call" | custom-call | flops 2000000000 | bytes 2097152 | tf_op jit(solution)/shard_map/attend/pallas_call | solution.py:227
  21.2 1.7 %collective-permute-done.1 = f32[2,32,512]{2,1,0:T(8,128)S(1)} collective-permute-done((f32[2,32,512]{2,1,0:T(8,128)S(1)}, f32[2,32,512]{2,1,0:T(8,128)S(1)}, u32[]{:S(2)}, u32[]{:S(2)}) %collective-permute-start.1) | collective-permute-done | bytes 131104 | tf_op jit(solution)/shard_map/ppermute | solution.py:26
  22.9 0.3 collective-permute-done.3
  23.2 0.1 fusion
  23.3 0.0 copy-start.4
  23.3 0.0 copy-start.6
  23.3 2.7 %collective-permute-start.10 = (f32[2,2,32,512]{3,2,1,0:T(8,128)S(1)}, f32[2,2,32,512]{3,2,1,0:T(8,128)S(1)}, u32[]{:S(2)}, u32[]{:S(2)}) collective-permute-start(f32[2,2,32,512]{3,2,1,0:T(8,128)S(1)} %pad_maximum_fusion), channel_id=1, source_target_pairs={{0,4},{1,5},{2,6},{3,7},{4,0},{5,1},{6,2},{7,3},{8,12},{9,13},{10,... | collective-permute-start | bytes 786440 | tf_op jit(solution)/shard_map/ppermute | solution.py:26
  25.9 7.4 %attend.3.refs_1_ = f32[128,384]{1,0:T(8,128)S(1)} custom-call(s32[1,4]{1,0:T(1,128)S(1)} %copy-done.5, f32[128,512]{1,0:T(8,128)S(1)} %bitcast.34, f32[128,512]{1,0:T(8,128)S(1)} %collective-permute-done.4.refs_1_, f32[128,512]{1,0:T(8,128)S(1)} %collective-permute-done.5.refs_2_, f32[128,512]{1,0:T(8,128)S(1)} %collective-permute-done.6.refs_3_, ...), custom_call_target="tpu_custom_call" | custom-call | flops 6000000000 | bytes 2097152 | tf_op jit(solution)/shard_map/attend/pallas_call | solution.py:227
  33.4 0.6 project.1.refs_0_
  34.0 0.6 collective-permute-start.7
  34.6 2.7 %collective-permute-done.10 = f32[2,2,32,512]{3,2,1,0:T(8,128)S(1)} collective-permute-done((f32[2,2,32,512]{3,2,1,0:T(8,128)S(1)}, f32[2,2,32,512]{3,2,1,0:T(8,128)S(1)}, u32[]{:S(2)}, u32[]{:S(2)}) %collective-permute-start.10) | collective-permute-done | bytes 262176 | tf_op jit(solution)/shard_map/ppermute | solution.py:26
  37.3 0.7 collective-permute-start.11
  38.0 0.6 collective-permute-start.13
  38.7 2.9 %collective-permute-done.7.refs_1_ = f32[136,512]{1,0:T(8,128)S(1)} collective-permute-done((f32[136,512]{1,0:T(8,128)S(1)}, f32[136,512]{1,0:T(8,128)S(1)}, u32[]{:S(2)}, u32[]{:S(2)}) %collective-permute-start.7) | collective-permute-done | bytes 278560 | tf_op jit(solution)/shard_map/ppermute | solution.py:26
  41.6 0.8 collective-permute-done.11
  42.4 0.6 collective-permute-start.12
  43.0 0.2 collective-permute-done.13
  43.2 1.4 %collective-permute-start.14 = (f32[4,32,512]{2,1,0:T(8,128)S(1)}, f32[4,32,512]{2,1,0:T(8,128)S(1)}, u32[]{:S(2)}, u32[]{:S(2)}) collective-permute-start(f32[4,32,512]{2,1,0:T(8,128)S(1)} %pad_maximum_fusion.2), channel_id=1, source_target_pairs={{0,2},{1,3},{2,0},{3,1},{4,6},{5,7},{6,4},{7,5},{8,10},{9,11},{10,... | collective-permute-start | bytes 786440 | tf_op jit(solution)/shard_map/ppermute | solution.py:26
  44.6 0.3 transpose_outputs.1
  44.9 5.5 %collective-permute-done.12 = f32[4,32,512]{2,1,0:T(8,128)S(1)} collective-permute-done((f32[4,32,512]{2,1,0:T(8,128)S(1)}, f32[4,32,512]{2,1,0:T(8,128)S(1)}, u32[]{:S(2)}, u32[]{:S(2)}) %collective-permute-start.12) | collective-permute-done | bytes 262176 | tf_op jit(solution)/shard_map/ppermute | solution.py:26
  50.4 0.3 collective-permute-done.14
  50.7 3.2 %loss_terms.1 = (f32[4,32,512]{2,1,0:T(8,128)S(1)}, f32[4,32,512]{2,1,0:T(8,128)S(1)}, f32[4,32,512]{2,1,0:T(8,128)S(1)}, f32[4,32,512]{2,1,0:T(8,128)S(1)}, f32...) custom-call(bf16[512,512]{1,0:T(8,128)(2,1)S(1)} %get-tuple-element.45., ...), custom_call_target="tpu_custom_call" | custom-call | flops 1610612736 | bytes 4194304 | tf_op jit(solution)/shard_map/loss_terms/pallas_call | solution.py:366
  54.0 1.5 %collective-permute-start.15 = (f32[4,32,512]{2,1,0:T(8,128)S(1)}, f32[4,32,512]{2,1,0:T(8,128)S(1)}, u32[]{:S(2)}, u32[]{:S(2)}) collective-permute-start(f32[4,32,512]{2,1,0:T(8,128)S(1)} %get-tuple-element.49), channel_id=1, source_target_pairs={{0,1},{1,0},{2,3},{3,2},{4,5},{5,4},{6,7},{7,6},{8,9},{9,8},{10,11... | collective-permute-start | bytes 786440 | tf_op jit(solution)/shard_map/ppermute | solution.py:26
  55.5 1.4 %collective-permute-start.16 = (f32[4,32,512]{2,1,0:T(8,128)S(1)}, f32[4,32,512]{2,1,0:T(8,128)S(1)}, u32[]{:S(2)}, u32[]{:S(2)}) collective-permute-start(f32[4,32,512]{2,1,0:T(8,128)S(1)} %get-tuple-element.50), channel_id=1, source_target_pairs={{0,2},{1,3},{2,0},{3,1},{4,6},{5,7},{6,4},{7,5},{8,10},{9,11},{10,... | collective-permute-start | bytes 786440 | tf_op jit(solution)/shard_map/ppermute | solution.py:26
  56.9 1.0 event_rows.1
  58.0 2.8 %collective-permute-done.15 = f32[4,32,512]{2,1,0:T(8,128)S(1)} collective-permute-done((f32[4,32,512]{2,1,0:T(8,128)S(1)}, f32[4,32,512]{2,1,0:T(8,128)S(1)}, u32[]{:S(2)}, u32[]{:S(2)}) %collective-permute-start.15) | collective-permute-done | bytes 262176 | tf_op jit(solution)/shard_map/ppermute | solution.py:26
  60.8 1.3 %collective-permute-done.16 = f32[4,32,512]{2,1,0:T(8,128)S(1)} collective-permute-done((f32[4,32,512]{2,1,0:T(8,128)S(1)}, f32[4,32,512]{2,1,0:T(8,128)S(1)}, u32[]{:S(2)}, u32[]{:S(2)}) %collective-permute-start.16) | collective-permute-done | bytes 262176 | tf_op jit(solution)/shard_map/ppermute | solution.py:26
  62.1 0.6 collective-permute-start.19
  62.7 1.8 %collective-permute-start.18 = (f32[2,32,512]{2,1,0:T(8,128)S(1)}, f32[2,32,512]{2,1,0:T(8,128)S(1)}, u32[]{:S(2)}, u32[]{:S(2)}) collective-permute-start(f32[2,32,512]{2,1,0:T(8,128)S(1)} %get-tuple-element.76), channel_id=1, source_target_pairs={{0,2},{1,3},{2,0},{3,1},{4,6},{5,7},{6,4},{7,5},{8,10},{9,11},{10,... | collective-permute-start | bytes 393224 | tf_op jit(solution)/shard_map/ppermute | solution.py:26
  64.6 2.6 %collective-permute-done.19 = f32[2,32,512]{2,1,0:T(8,128)S(1)} collective-permute-done((f32[2,32,512]{2,1,0:T(8,128)S(1)}, f32[2,32,512]{2,1,0:T(8,128)S(1)}, u32[]{:S(2)}, u32[]{:S(2)}) %collective-permute-start.19) | collective-permute-done | bytes 131104 | tf_op jit(solution)/shard_map/ppermute | solution.py:26
  67.2 0.6 collective-permute-done.18
  67.9 3.9 %collective-permute-start.20 = (f32[136,512]{1,0:T(8,128)S(1)}, f32[136,512]{1,0:T(8,128)S(1)}, u32[]{:S(2)}, u32[]{:S(2)}) collective-permute-start(f32[136,512]{1,0:T(8,128)S(1)} %maximum_maximum_fusion), channel_id=1, source_target_pairs={{0,4},{1,5},{2,6},{3,7},{4,0},{5,1},{6,2},{7,3},{8,12},{9,13},{10,... | collective-permute-start | bytes 835592 | tf_op jit(solution)/shard_map/ppermute | solution.py:26
  71.8 0.1 slice_add_fusion
  71.8 0.6 collective-permute-start.21
  72.4 0.9 hot_rows.1.hot
  73.3 7.4 %collective-permute-done.20 = f32[136,512]{1,0:T(8,128)S(1)} collective-permute-done((f32[136,512]{1,0:T(8,128)S(1)}, f32[136,512]{1,0:T(8,128)S(1)}, u32[]{:S(2)}, u32[]{:S(2)}) %collective-permute-start.20) | collective-permute-done | bytes 278560 | tf_op jit(solution)/shard_map/ppermute | solution.py:26
  80.9 0.6 collective-permute-start.22
  81.5 1.6 %collective-permute-start.23 = (f32[64,512]{1,0:T(8,128)S(1)}, f32[64,512]{1,0:T(8,128)S(1)}, u32[]{:S(2)}, u32[]{:S(2)}) collective-permute-start(f32[64,512]{1,0:T(8,128)S(1)} %get-tuple-element.91), channel_id=1, source_target_pairs={{0,8},{8,0},{16,24},{24,16},{1,9},{9,1},{17,25},{25,17},{2,10},{10... | collective-permute-start | bytes 393224 | tf_op jit(solution)/shard_map/ppermute | solution.py:31
  83.2 4.1 %collective-permute-done.24.refs_3_ = f32[64,512]{1,0:T(8,128)S(1)} collective-permute-done((f32[64,512]{1,0:T(8,128)S(1)}, f32[64,512]{1,0:T(8,128)S(1)}, u32[]{:S(2)}, u32[]{:S(2)}) %collective-permute-start.24) | collective-permute-done | bytes 131104 | tf_op jit(solution)/shard_map/ppermute | solution.py:31
  87.3 0.2 collective-permute-done.22.refs_1_
  87.5 2.1 %spread_rows.1 = (f32[520,128]{1,0:T(8,128)S(1)}, f32[520,128]{1,0:T(8,128)S(1)}, f32[520,128]{1,0:T(8,128)S(1)}, f32[520,128]{1,0:T(8,128)S(1)}) custom-call(s32[4]{0:T(128)S(1)} %copy-done.7, bf16[4,1024,512]{2,1,0:T(8,128)(2,1)S(1)} %hot_rows.1.hot, f32[8,128]{1,0:T(8,128)S(1)} %slice_add_fusion.12.loss, f32[64,512]{1,0:T(8,128)S(1)} %get-tuple-element.92.refs_0_, ...), custom_call_target="tpu_custom_call" | custom-call | flops 536870912 | bytes 2097152 | tf_op jit(solution)/shard_map/spread_rows/pallas_call | solution.py:459
  89.6 1.6 %collective-permute-start.26 = (f32[520,128]{1,0:T(8,128)S(1)}, f32[520,128]{1,0:T(8,128)S(1)}, u32[]{:S(2)}, u32[]{:S(2)}) collective-permute-start(f32[520,128]{1,0:T(8,128)S(1)} %get-tuple-element.67), channel_id=1, source_target_pairs={{0,1},{1,0},{2,3},{3,2},{4,5},{5,4},{6,7},{7,6},{8,9},{9,8},{10,11... | collective-permute-start | bytes 798728 | tf_op jit(solution)/shard_map/ppermute | solution.py:31
  91.2 1.9 %collective-permute-start.30 = (f32[520,128]{1,0:T(8,128)S(1)}, f32[520,128]{1,0:T(8,128)S(1)}, u32[]{:S(2)}, u32[]{:S(2)}) collective-permute-start(f32[520,128]{1,0:T(8,128)S(1)} %get-tuple-element.69), channel_id=1, source_target_pairs={{0,3},{1,2},{2,1},{3,0},{4,7},{5,6},{6,5},{7,4},{8,11},{9,10},{10,... | collective-permute-start | bytes 798728 | tf_op jit(solution)/shard_map/ppermute | solution.py:31
  93.1 0.4 collective-permute-start.25
  93.5 5.1 %collective-permute-done.26 = f32[520,128]{1,0:T(8,128)S(1)} collective-permute-done((f32[520,128]{1,0:T(8,128)S(1)}, f32[520,128]{1,0:T(8,128)S(1)}, u32[]{:S(2)}, u32[]{:S(2)}) %collective-permute-start.26) | collective-permute-done | bytes 266272 | tf_op jit(solution)/shard_map/ppermute | solution.py:31
  98.6 0.4 collective-permute-start.27
  99.0 1.5 %collective-permute-done.28 = f32[520,128]{1,0:T(8,128)S(1)} collective-permute-done((f32[520,128]{1,0:T(8,128)S(1)}, f32[520,128]{1,0:T(8,128)S(1)}, u32[]{:S(2)}, u32[]{:S(2)}) %collective-permute-start.28) | collective-permute-done | bytes 266272 | tf_op jit(solution)/shard_map/ppermute | solution.py:31
  100.5 0.1 collective-permute-start.29
  100.6 5.5 %collective-permute-done.30 = f32[520,128]{1,0:T(8,128)S(1)} collective-permute-done((f32[520,128]{1,0:T(8,128)S(1)}, f32[520,128]{1,0:T(8,128)S(1)}, u32[]{:S(2)}, u32[]{:S(2)}) %collective-permute-start.30) | collective-permute-done | bytes 266272 | tf_op jit(solution)/shard_map/ppermute | solution.py:31
  106.1 0.1 collective-permute-start.31
  106.2 1.4 %collective-permute-done.31.refs_7_ = f32[1,520,128]{2,1,0:T(8,128)S(1)} collective-permute-done((f32[1,520,128]{2,1,0:T(8,128)S(1)}, f32[1,520,128]{2,1,0:T(8,128)S(1)}, u32[]{:S(2)}, u32[]{:S(2)}) %collective-permute-start.31) | collective-permute-done | bytes 266272 | tf_op jit(solution)/shard_map/ppermute | solution.py:26
  107.6 1.9 %assemble.1 = (f32[1024,512]{1,0:T(8,128)}, f32[1,1]{1,0:T(1,128)}, f32[1,128,512]{2,1,0:T(8,128)}) custom-call(f32[1,128,512]{2,1,0:T(8,128)S(1)} %get-tuple-element.74.kept, f32[1,128,512]{2,1,0:T(8,128)S(1)} %collective-permute-done.21.got, f32[1,520,128]{2,1,0:T(8,128)S(1)} %bitcast.37, f32[1,520,128]{2,1,0:T(8,128)S(1)} %collective-permute-done.25.refs_1_, ...), custom_call_target="tpu_custom_call" | custom-call | bytes 4194304 | tf_op jit(solution)/shard_map/assemble/pallas_call | solution.py:507
  (65 shorter events, 0.5 us)
Async XLA Ops:
  0.6 12.3 %copy-start.1 = (f32[1,128,512]{2,1,0:T(8,128)S(1)}, f32[1,128,512]{2,1,0:T(8,128)}, u32[]{:S(2)}) copy-start(f32[1,128,512]{2,1,0:T(8,128)} %param.10) | copy-start | bytes 786436
  0.6 16.2 %collective-permute-start.4 = (f32[128,512]{1,0:T(8,128)}, f32[128,512]{1,0:T(8,128)S(1)}, u32[]{:S(2)}, u32[]{:S(2)}) collective-permute-start(f32[128,512]{1,0:T(8,128)} %bitcast.30), channel_id=1, source_target_pairs={{0,16},{8,24},{16,0},{24,8},{1,17},{9,25},{17,1},{25,9},{2,18},{10... | collective-permute-start | bytes 786440 | tf_op jit(solution)/shard_map/ppermute | solution.py:26
  7.3 9.8 %collective-permute-start = (f32[4,32,512]{2,1,0:T(8,128)}, f32[4,32,512]{2,1,0:T(8,128)S(1)}, u32[]{:S(2)}, u32[]{:S(2)}) collective-permute-start(f32[4,32,512]{2,1,0:T(8,128)} %get-tuple-element.39), channel_id=1, source_target_pairs={{0,1},{1,0},{2,3},{3,2},{4,5},{5,4},{6,7},{7,6},{8,9},{9,8},{10,11... | collective-permute-start | bytes 786440 | tf_op jit(solution)/shard_map/ppermute | solution.py:26
  8.8 9.7 %collective-permute-start.5 = (f32[128,512]{1,0:T(8,128)}, f32[128,512]{1,0:T(8,128)S(1)}, u32[]{:S(2)}, u32[]{:S(2)}) collective-permute-start(f32[128,512]{1,0:T(8,128)} %bitcast.31), channel_id=1, source_target_pairs={{0,8},{8,0},{16,24},{24,16},{1,9},{9,1},{17,25},{25,17},{2,10},{10... | collective-permute-start | bytes 786440 | tf_op jit(solution)/shard_map/ppermute | solution.py:26
  8.8 8.9 %collective-permute-start.2 = (f32[4,32,512]{2,1,0:T(8,128)}, f32[4,32,512]{2,1,0:T(8,128)S(1)}, u32[]{:S(2)}, u32[]{:S(2)}) collective-permute-start(f32[4,32,512]{2,1,0:T(8,128)} %get-tuple-element.41), channel_id=1, source_target_pairs={{0,2},{1,3},{2,0},{3,1},{4,6},{5,7},{6,4},{7,5},{8,10},{9,11},{10,... | collective-permute-start | bytes 786440 | tf_op jit(solution)/shard_map/ppermute | solution.py:26
  13.0 2.2 %copy-start = (f32[512,2048]{1,0:T(8,128)S(1)}, f32[512,2048]{1,0:T(8,128)}, u32[]{:S(2)}) copy-start(f32[512,2048]{1,0:T(8,128)} %refs_6_.4) | copy-start | bytes 12582916
  15.2 2.0 %copy-start.8 = (f32[4,32,512]{2,1,0:T(8,128)S(1)}, f32[4,32,512]{2,1,0:T(8,128)}, u32[]{:S(2)}) copy-start(f32[4,32,512]{2,1,0:T(8,128)} %get-tuple-element.38) | copy-start | bytes 786436
  15.2 2.6 %copy-start.9 = (f32[4,32,512]{2,1,0:T(8,128)S(1)}, f32[4,32,512]{2,1,0:T(8,128)}, u32[]{:S(2)}) copy-start(f32[4,32,512]{2,1,0:T(8,128)} %get-tuple-element.40) | copy-start | bytes 786436
  15.2 3.4 %copy-start.5 = (s32[1,4]{1,0:T(1,128)S(1)}, s32[1,4]{1,0:T(1,128)}, u32[]{:S(2)}) copy-start(s32[1,4]{1,0:T(1,128)} %lengths.3) | copy-start | bytes 52
  16.8 1.8 %collective-permute-start.6 = (f32[128,512]{1,0:T(8,128)S(1)}, f32[128,512]{1,0:T(8,128)S(1)}, u32[]{:S(2)}, u32[]{:S(2)}) collective-permute-start(f32[128,512]{1,0:T(8,128)S(1)} %collective-permute-done.4.refs_1_), channel_id=1, source_target_pairs={{0,8},{8,0},{16,24},{24,16},{1,9},{9,1},{17,25},{25,17},{2,10},{10... | collective-permute-start | bytes 786440 | tf_op jit(solution)/shard_map/ppermute | solution.py:26
  17.2 5.7 %collective-permute-start.1 = (f32[2,32,512]{2,1,0:T(8,128)S(1)}, f32[2,32,512]{2,1,0:T(8,128)S(1)}, u32[]{:S(2)}, u32[]{:S(2)}) collective-permute-start(f32[2,32,512]{2,1,0:T(8,128)S(1)} %slice_select_fusion.3), channel_id=1, source_target_pairs={{0,2},{1,3},{2,0},{3,1},{4,6},{5,7},{6,4},{7,5},{8,10},{9,11},{10,... | collective-permute-start | bytes 393224 | tf_op jit(solution)/shard_map/ppermute | solution.py:26
  17.8 5.4 %collective-permute-start.3 = (f32[2,32,512]{2,1,0:T(8,128)S(1)}, f32[2,32,512]{2,1,0:T(8,128)S(1)}, u32[]{:S(2)}, u32[]{:S(2)}) collective-permute-start(f32[2,32,512]{2,1,0:T(8,128)S(1)} %slice_select_fusion.2), channel_id=1, source_target_pairs={{0,1},{1,0},{2,3},{3,2},{4,5},{5,4},{6,7},{7,6},{8,9},{9,8},{10,11... | collective-permute-start | bytes 393224 | tf_op jit(solution)/shard_map/ppermute | solution.py:26
  23.3 10.1 %copy-start.2 = (f32[512,512]{1,0:T(8,128)S(1)}, f32[512,512]{1,0:T(8,128)}, u32[]{:S(2)}) copy-start(f32[512,512]{1,0:T(8,128)} %refs_4_.1) | copy-start | bytes 3145732
  23.3 10.1 %copy-start.4 = (f32[512]{0:T(512)S(1)}, f32[512]{0:T(512)}, u32[]{:S(2)}) copy-start(f32[512]{0:T(512)} %param.12) | copy-start | bytes 6148
  23.3 10.1 %copy-start.6 = (s32[1,128]{1,0:T(1,128)S(1)}, s32[1,128]{1,0:T(1,128)}, u32[]{:S(2)}) copy-start(s32[1,128]{1,0:T(1,128)} %refs_6_.5) | copy-start | bytes 1540
  23.3 14.0 %collective-permute-start.10 = (f32[2,2,32,512]{3,2,1,0:T(8,128)S(1)}, f32[2,2,32,512]{3,2,1,0:T(8,128)S(1)}, u32[]{:S(2)}, u32[]{:S(2)}) collective-permute-start(f32[2,2,32,512]{3,2,1,0:T(8,128)S(1)} %pad_maximum_fusion), channel_id=1, source_target_pairs={{0,4},{1,5},{2,6},{3,7},{4,0},{5,1},{6,2},{7,3},{8,12},{9,13},{10,... | collective-permute-start | bytes 786440 | tf_op jit(solution)/shard_map/ppermute | solution.py:26
  34.0 7.6 %collective-permute-start.7 = (f32[136,512]{1,0:T(8,128)S(1)}, f32[136,512]{1,0:T(8,128)S(1)}, u32[]{:S(2)}, u32[]{:S(2)}) collective-permute-start(f32[136,512]{1,0:T(8,128)S(1)} %project.1.refs_0_), channel_id=1, source_target_pairs={{0,16},{8,24},{16,0},{24,8},{1,17},{9,25},{17,1},{25,9},{2,18},{10... | collective-permute-start | bytes 835592 | tf_op jit(solution)/shard_map/ppermute | solution.py:26
  37.3 5.0 %collective-permute-start.11 = (f32[2,32,512]{2,1,0:T(8,128)S(1)}, f32[2,32,512]{2,1,0:T(8,128)S(1)}, u32[]{:S(2)}, u32[]{:S(2)}) collective-permute-start(f32[2,32,512]{2,1,0:T(8,128)S(1)} %maximum_select_fusion), channel_id=1, source_target_pairs={{0,2},{1,3},{2,0},{3,1},{4,6},{5,7},{6,4},{7,5},{8,10},{9,11},{10,... | collective-permute-start | bytes 393224 | tf_op jit(solution)/shard_map/ppermute | solution.py:26
  38.0 5.1 %collective-permute-start.13 = (f32[2,32,512]{2,1,0:T(8,128)S(1)}, f32[2,32,512]{2,1,0:T(8,128)S(1)}, u32[]{:S(2)}, u32[]{:S(2)}) collective-permute-start(f32[2,32,512]{2,1,0:T(8,128)S(1)} %maximum_select_fusion.1), channel_id=1, source_target_pairs={{0,1},{1,0},{2,3},{3,2},{4,5},{5,4},{6,7},{7,6},{8,9},{9,8},{10,11... | collective-permute-start | bytes 393224 | tf_op jit(solution)/shard_map/ppermute | solution.py:26
  38.6 5.9 %collective-permute-start.8 = (f32[136,512]{1,0:T(8,128)S(1)}, f32[136,512]{1,0:T(8,128)S(1)}, u32[]{:S(2)}, u32[]{:S(2)}) collective-permute-start(f32[136,512]{1,0:T(8,128)S(1)} %project.1.refs_0_), channel_id=1, source_target_pairs={{0,8},{8,0},{16,24},{24,16},{1,9},{9,1},{17,25},{25,17},{2,10},{10... | collective-permute-start | bytes 835592 | tf_op jit(solution)/shard_map/ppermute | solution.py:26
  41.6 3.0 %collective-permute-start.9 = (f32[136,512]{1,0:T(8,128)S(1)}, f32[136,512]{1,0:T(8,128)S(1)}, u32[]{:S(2)}, u32[]{:S(2)}) collective-permute-start(f32[136,512]{1,0:T(8,128)S(1)} %collective-permute-done.7.refs_1_), channel_id=1, source_target_pairs={{0,8},{8,0},{16,24},{24,16},{1,9},{9,1},{17,25},{25,17},{2,10},{10... | collective-permute-start | bytes 835592 | tf_op jit(solution)/shard_map/ppermute | solution.py:26
  42.4 8.0 %collective-permute-start.12 = (f32[4,32,512]{2,1,0:T(8,128)S(1)}, f32[4,32,512]{2,1,0:T(8,128)S(1)}, u32[]{:S(2)}, u32[]{:S(2)}) collective-permute-start(f32[4,32,512]{2,1,0:T(8,128)S(1)} %pad_maximum_fusion.1), channel_id=1, source_target_pairs={{0,1},{1,0},{2,3},{3,2},{4,5},{5,4},{6,7},{7,6},{8,9},{9,8},{10,11... | collective-permute-start | bytes 786440 | tf_op jit(solution)/shard_map/ppermute | solution.py:26
  43.2 7.5 %collective-permute-start.14 = (f32[4,32,512]{2,1,0:T(8,128)S(1)}, f32[4,32,512]{2,1,0:T(8,128)S(1)}, u32[]{:S(2)}, u32[]{:S(2)}) collective-permute-start(f32[4,32,512]{2,1,0:T(8,128)S(1)} %pad_maximum_fusion.2), channel_id=1, source_target_pairs={{0,2},{1,3},{2,0},{3,1},{4,6},{5,7},{6,4},{7,5},{8,10},{9,11},{10,... | collective-permute-start | bytes 786440 | tf_op jit(solution)/shard_map/ppermute | solution.py:26
  54.0 18.4 %copy-start.3 = (s32[4,512]{1,0:T(4,128)S(1)}, s32[4,512]{1,0:T(4,128)}, u32[]{:S(2)}) copy-start(s32[4,512]{1,0:T(4,128)} %ids.1) | copy-start | bytes 24580
  54.0 6.8 %collective-permute-start.15 = (f32[4,32,512]{2,1,0:T(8,128)S(1)}, f32[4,32,512]{2,1,0:T(8,128)S(1)}, u32[]{:S(2)}, u32[]{:S(2)}) collective-permute-start(f32[4,32,512]{2,1,0:T(8,128)S(1)} %get-tuple-element.49), channel_id=1, source_target_pairs={{0,1},{1,0},{2,3},{3,2},{4,5},{5,4},{6,7},{7,6},{8,9},{9,8},{10,11... | collective-permute-start | bytes 786440 | tf_op jit(solution)/shard_map/ppermute | solution.py:26
  55.5 6.6 %collective-permute-start.16 = (f32[4,32,512]{2,1,0:T(8,128)S(1)}, f32[4,32,512]{2,1,0:T(8,128)S(1)}, u32[]{:S(2)}, u32[]{:S(2)}) collective-permute-start(f32[4,32,512]{2,1,0:T(8,128)S(1)} %get-tuple-element.50), channel_id=1, source_target_pairs={{0,2},{1,3},{2,0},{3,1},{4,6},{5,7},{6,4},{7,5},{8,10},{9,11},{10,... | collective-permute-start | bytes 786440 | tf_op jit(solution)/shard_map/ppermute | solution.py:26
  62.1 5.0 %collective-permute-start.19 = (f32[2,32,512]{2,1,0:T(8,128)S(1)}, f32[2,32,512]{2,1,0:T(8,128)S(1)}, u32[]{:S(2)}, u32[]{:S(2)}) collective-permute-start(f32[2,32,512]{2,1,0:T(8,128)S(1)} %get-tuple-element.78), channel_id=1, source_target_pairs={{0,1},{1,0},{2,3},{3,2},{4,5},{5,4},{6,7},{7,6},{8,9},{9,8},{10,11... | collective-permute-start | bytes 393224 | tf_op jit(solution)/shard_map/ppermute | solution.py:26
  62.7 5.0 %collective-permute-start.18 = (f32[2,32,512]{2,1,0:T(8,128)S(1)}, f32[2,32,512]{2,1,0:T(8,128)S(1)}, u32[]{:S(2)}, u32[]{:S(2)}) collective-permute-start(f32[2,32,512]{2,1,0:T(8,128)S(1)} %get-tuple-element.76), channel_id=1, source_target_pairs={{0,2},{1,3},{2,0},{3,1},{4,6},{5,7},{6,4},{7,5},{8,10},{9,11},{10,... | collective-permute-start | bytes 393224 | tf_op jit(solution)/shard_map/ppermute | solution.py:26
  64.6 7.2 %collective-permute-start.17 = (f32[2,128,512]{2,1,0:T(8,128)S(1)}, f32[2,128,512]{2,1,0:T(8,128)S(1)}, u32[]{:S(2)}, u32[]{:S(2)}) collective-permute-start(f32[2,128,512]{2,1,0:T(8,128)S(1)} %get-tuple-element.57), channel_id=1, source_target_pairs={{0,8},{8,0},{16,24},{24,16},{1,9},{9,1},{17,25},{25,17},{2,10},{10... | collective-permute-start | bytes 1572872 | tf_op jit(solution)/shard_map/ppermute | solution.py:26
  67.8 19.7 %copy-start.7 = (s32[4]{0:T(128)S(1)}, s32[4]{0:T(128)}, u32[]{:S(2)}) copy-start(s32[4]{0:T(128)} %owner.1) | copy-start | bytes 52
  67.9 12.8 %collective-permute-start.20 = (f32[136,512]{1,0:T(8,128)S(1)}, f32[136,512]{1,0:T(8,128)S(1)}, u32[]{:S(2)}, u32[]{:S(2)}) collective-permute-start(f32[136,512]{1,0:T(8,128)S(1)} %maximum_maximum_fusion), channel_id=1, source_target_pairs={{0,4},{1,5},{2,6},{3,7},{4,0},{5,1},{6,2},{7,3},{8,12},{9,13},{10,... | collective-permute-start | bytes 835592 | tf_op jit(solution)/shard_map/ppermute | solution.py:26
  71.8 8.9 %collective-permute-start.21 = (f32[1,128,512]{2,1,0:T(8,128)S(1)}, f32[1,128,512]{2,1,0:T(8,128)S(1)}, u32[]{:S(2)}, u32[]{:S(2)}) collective-permute-start(f32[1,128,512]{2,1,0:T(8,128)S(1)} %get-tuple-element.73), channel_id=1, source_target_pairs={{0,16},{8,24},{16,0},{24,8},{1,17},{9,25},{17,1},{25,9},{2,18},{10... | collective-permute-start | bytes 786440 | tf_op jit(solution)/shard_map/ppermute | solution.py:26
  80.9 6.5 %collective-permute-start.22 = (f32[72,512]{1,0:T(8,128)S(1)}, f32[72,512]{1,0:T(8,128)S(1)}, u32[]{:S(2)}, u32[]{:S(2)}) collective-permute-start(f32[72,512]{1,0:T(8,128)S(1)} %constant_dynamic-update-slice_fusion.8), channel_id=1, source_target_pairs={{0,16},{8,24},{16,0},{24,8},{1,17},{9,25},{17,1},{25,9},{2,18},{10... | collective-permute-start | bytes 442376 | tf_op jit(solution)/shard_map/ppermute | solution.py:31
  81.5 5.7 %collective-permute-start.24 = (f32[64,512]{1,0:T(8,128)S(1)}, f32[64,512]{1,0:T(8,128)S(1)}, u32[]{:S(2)}, u32[]{:S(2)}) collective-permute-start(f32[64,512]{1,0:T(8,128)S(1)} %get-tuple-element.89), channel_id=1, source_target_pairs={{0,24},{8,16},{16,8},{24,0},{1,25},{9,17},{17,9},{25,1},{2,26},{10... | collective-permute-start | bytes 393224 | tf_op jit(solution)/shard_map/ppermute | solution.py:31
  81.5 5.7 %collective-permute-start.23 = (f32[64,512]{1,0:T(8,128)S(1)}, f32[64,512]{1,0:T(8,128)S(1)}, u32[]{:S(2)}, u32[]{:S(2)}) collective-permute-start(f32[64,512]{1,0:T(8,128)S(1)} %get-tuple-element.91), channel_id=1, source_target_pairs={{0,8},{8,0},{16,24},{24,16},{1,9},{9,1},{17,25},{25,17},{2,10},{10... | collective-permute-start | bytes 393224 | tf_op jit(solution)/shard_map/ppermute | solution.py:31
  89.6 9.1 %collective-permute-start.26 = (f32[520,128]{1,0:T(8,128)S(1)}, f32[520,128]{1,0:T(8,128)S(1)}, u32[]{:S(2)}, u32[]{:S(2)}) collective-permute-start(f32[520,128]{1,0:T(8,128)S(1)} %get-tuple-element.67), channel_id=1, source_target_pairs={{0,1},{1,0},{2,3},{3,2},{4,5},{5,4},{6,7},{7,6},{8,9},{9,8},{10,11... | collective-permute-start | bytes 798728 | tf_op jit(solution)/shard_map/ppermute | solution.py:31
  91.2 9.3 %collective-permute-start.28 = (f32[520,128]{1,0:T(8,128)S(1)}, f32[520,128]{1,0:T(8,128)S(1)}, u32[]{:S(2)}, u32[]{:S(2)}) collective-permute-start(f32[520,128]{1,0:T(8,128)S(1)} %get-tuple-element.68), channel_id=1, source_target_pairs={{0,2},{1,3},{2,0},{3,1},{4,6},{5,7},{6,4},{7,5},{8,10},{9,11},{10,... | collective-permute-start | bytes 798728 | tf_op jit(solution)/shard_map/ppermute | solution.py:31
  91.2 14.8 %collective-permute-start.30 = (f32[520,128]{1,0:T(8,128)S(1)}, f32[520,128]{1,0:T(8,128)S(1)}, u32[]{:S(2)}, u32[]{:S(2)}) collective-permute-start(f32[520,128]{1,0:T(8,128)S(1)} %get-tuple-element.69), channel_id=1, source_target_pairs={{0,3},{1,2},{2,1},{3,0},{4,7},{5,6},{6,5},{7,4},{8,11},{9,10},{10,... | collective-permute-start | bytes 798728 | tf_op jit(solution)/shard_map/ppermute | solution.py:31
  93.1 13.0 %collective-permute-start.25 = (f32[1,520,128]{2,1,0:T(8,128)S(1)}, f32[1,520,128]{2,1,0:T(8,128)S(1)}, u32[]{:S(2)}, u32[]{:S(2)}) collective-permute-start(f32[1,520,128]{2,1,0:T(8,128)S(1)} %bitcast.36), channel_id=1, source_target_pairs={{0,8},{8,0},{16,24},{24,16},{1,9},{9,1},{17,25},{25,17},{2,10},{10... | collective-permute-start | bytes 798728 | tf_op jit(solution)/shard_map/ppermute | solution.py:26
  98.6 7.5 %collective-permute-start.27 = (f32[1,520,128]{2,1,0:T(8,128)S(1)}, f32[1,520,128]{2,1,0:T(8,128)S(1)}, u32[]{:S(2)}, u32[]{:S(2)}) collective-permute-start(f32[1,520,128]{2,1,0:T(8,128)S(1)} %bitcast.38), channel_id=1, source_target_pairs={{0,8},{8,0},{16,24},{24,16},{1,9},{9,1},{17,25},{25,17},{2,10},{10... | collective-permute-start | bytes 798728 | tf_op jit(solution)/shard_map/ppermute | solution.py:26
  100.5 5.7 %collective-permute-start.29 = (f32[1,520,128]{2,1,0:T(8,128)S(1)}, f32[1,520,128]{2,1,0:T(8,128)S(1)}, u32[]{:S(2)}, u32[]{:S(2)}) collective-permute-start(f32[1,520,128]{2,1,0:T(8,128)S(1)} %bitcast.40), channel_id=1, source_target_pairs={{0,8},{8,0},{16,24},{24,16},{1,9},{9,1},{17,25},{25,17},{2,10},{10... | collective-permute-start | bytes 798728 | tf_op jit(solution)/shard_map/ppermute | solution.py:26
  106.1 1.5 %collective-permute-start.31 = (f32[1,520,128]{2,1,0:T(8,128)S(1)}, f32[1,520,128]{2,1,0:T(8,128)S(1)}, u32[]{:S(2)}, u32[]{:S(2)}) collective-permute-start(f32[1,520,128]{2,1,0:T(8,128)S(1)} %bitcast.42), channel_id=1, source_target_pairs={{0,8},{8,0},{16,24},{24,16},{1,9},{9,1},{17,25},{25,17},{2,10},{10... | collective-permute-start | bytes 798728 | tf_op jit(solution)/shard_map/ppermute | solution.py:26

commit v10 on v8

--- a/solution.py
+++ b/solution.py
@@ -124,7 +124,7 @@
 def pick_rows(plan, ids, table):
     n_rows, width = table.shape
     n_item, n_neg = plan[1], ids.shape[1]
-    step = 256
+    step = 512
     out = (n_item // 2, n_neg // (2 * n_item), width)
     return pl.pallas_call(
         functools.partial(pick_kernel, plan),

time: 110 us -> 110 us (level)
  no operation moved by 1% of the time
where the time goes in v10:
time: 110 us; the launch traced here: 109 us
  waiting for transfers between devices  48.4 us (44%)
  starting transfers between devices  30.6 us (28%)
  Pallas kernels  24.6 us (22%)
  local copies, waits for them, and re-layouts  2.91 us (3%)
  between operations  2.35 us (2%)
    ppermute x26, waiting for transfers between devices, swap(): return lax.ppermute(block, axis, [(i, i ^ 1 << bit) for i in range(size)])  32 us
    ppermute x26, starting transfers between devices, swap(): return lax.ppermute(block, axis, [(i, i ^ 1 << bit) for i in range(size)])  24.9 us
    ppermute x6, waiting for transfers between devices, send(): return lax.ppermute(block, axis, [(i, i ^ r) for i in range(size)])  16.4 us
    pallas_call x2, Pallas kernels, attend(): pl.pallas_call(functools.partial(attend_kernel, order, n_seq), grid=(coun...  10.1 us
    ppermute x6, starting transfers between devices, send(): return lax.ppermute(block, axis, [(i, i ^ r) for i in range(size)])  5.76 us
    pallas_call x1, Pallas kernels, pick_rows(): pl.pallas_call(functools.partial(pick_kernel, plan), in_specs=[pl.BlockSp...  3.63 us
    pallas_call x1, Pallas kernels, loss_terms(): pl.pallas_call(functools.partial(loss_kernel, plan), in_specs=[vmem] * (2...  3.21 us
    unnamed x32, local copies, waits for them, and re-layouts  2.3 us
  transfers between devices with their start and end apart: 32, of which 20 were waited for; matrix products, arithmetic and copies ran while one was open for 1% of the time, Pallas kernels for 16%

profile of v10, /device:TPU:0, one launch (start us, length us, event | category | flops | bytes accessed | tf_op | source)
XLA Modules:
  0.0 109.4 jit_solution(17715876871903530250)
XLA Ops:
  0.7 3.0 %collective-permute-start.4 = (f32[128,512]{1,0:T(8,128)}, f32[128,512]{1,0:T(8,128)S(1)}, u32[]{:S(2)}, u32[]{:S(2)}) collective-permute-start(f32[128,512]{1,0:T(8,128)} %bitcast.30), channel_id=1, source_target_pairs={{0,16},{8,24},{16,0},{24,8},{1,17},{9,25},{17,1},{25,9},{2,18},{10... | collective-permute-start | bytes 786440 | tf_op jit(solution)/shard_map/ppermute | solution.py:26
  3.7 3.6 %pick_rows.1 = (f32[4,32,512]{2,1,0:T(8,128)}, f32[4,32,512]{2,1,0:T(8,128)}, f32[4,32,512]{2,1,0:T(8,128)}, f32[4,32,512]{2,1,0:T(8,128)}) custom-call(s32[4,512]{1,0:T(4,128)} %ids.1, f32[1024,512]{1,0:T(8,128)} %table_hbm.1), custom_call_target="tpu_custom_call" | custom-call | flops 1073741824 | bytes 2097152 | tf_op jit(solution)/shard_map/pick_rows/pallas_call | solution.py:129
  7.3 1.6 %collective-permute-start = (f32[4,32,512]{2,1,0:T(8,128)}, f32[4,32,512]{2,1,0:T(8,128)S(1)}, u32[]{:S(2)}, u32[]{:S(2)}) collective-permute-start(f32[4,32,512]{2,1,0:T(8,128)} %get-tuple-element.38), channel_id=1, source_target_pairs={{0,1},{1,0},{2,3},{3,2},{4,5},{5,4},{6,7},{7,6},{8,9},{9,8},{10,11... | collective-permute-start | bytes 786440 | tf_op jit(solution)/shard_map/ppermute | solution.py:26
  8.9 1.6 %collective-permute-start.2 = (f32[4,32,512]{2,1,0:T(8,128)}, f32[4,32,512]{2,1,0:T(8,128)S(1)}, u32[]{:S(2)}, u32[]{:S(2)}) collective-permute-start(f32[4,32,512]{2,1,0:T(8,128)} %get-tuple-element.40), channel_id=1, source_target_pairs={{0,2},{1,3},{2,0},{3,1},{4,6},{5,7},{6,4},{7,5},{8,10},{9,11},{10,... | collective-permute-start | bytes 786440 | tf_op jit(solution)/shard_map/ppermute | solution.py:26
  11.1 0.6 dynamic_slice.3
  12.4 0.0 copy-start
  12.4 2.2 %copy-done = f32[512,2048]{1,0:T(8,128)S(1)} copy-done((f32[512,2048]{1,0:T(8,128)S(1)}, f32[512,2048]{1,0:T(8,128)}, u32[]{:S(2)}) %copy-start) | copy-done | bytes 4194328
  14.6 1.6 %prepare.1 = (f32[128,512]{1,0:T(8,128)S(1)}, f32[128,512]{1,0:T(8,128)S(1)}) custom-call(f32[128,512]{1,0:T(8,128)S(1)} %bitcast.32, f32[512,2048]{1,0:T(8,128)S(1)} %copy-done, f32[512,2048]{1,0:T(8,128)S(1)} %copy-done), custom_call_target="tpu_custom_call" | custom-call | flops 402653184 | bytes 2097152 | tf_op jit(solution)/shard_map/prepare/pallas_call | solution.py:155
  16.2 0.3 collective-permute-start.6
  16.5 0.5 collective-permute-start.1
  17.0 0.8 collective-permute-done.2
  17.8 0.8 collective-permute-start.3
  18.6 2.6 %attend.2.refs_0_ = f32[128,128]{1,0:T(8,128)S(1)} custom-call(s32[1,4]{1,0:T(1,128)S(1)} %copy-done.4, f32[128,512]{1,0:T(8,128)S(1)} %bitcast.33, f32[128,512]{1,0:T(8,128)S(1)} %collective-permute-done.4.refs_1_, f32[128,512]{1,0:T(8,128)S(1)} %collective-permute-done.5.refs_2_, f32[128,512]{1,0:T(8,128)S(1)} %collective-permute-done.6.refs_3_, ...), custom_call_target="tpu_custom_call" | custom-call | flops 2000000000 | bytes 2097152 | tf_op jit(solution)/shard_map/attend/pallas_call | solution.py:227
  21.3 1.0 collective-permute-done.1
  22.3 0.7 collective-permute-done.3
  23.0 0.1 fusion
  23.1 0.0 copy-start.2
  23.1 0.0 copy-start.3
  23.2 2.7 %collective-permute-start.10 = (f32[2,2,32,512]{3,2,1,0:T(8,128)S(1)}, f32[2,2,32,512]{3,2,1,0:T(8,128)S(1)}, u32[]{:S(2)}, u32[]{:S(2)}) collective-permute-start(f32[2,2,32,512]{3,2,1,0:T(8,128)S(1)} %pad_maximum_fusion), channel_id=1, source_target_pairs={{0,4},{1,5},{2,6},{3,7},{4,0},{5,1},{6,2},{7,3},{8,12},{9,13},{10,... | collective-permute-start | bytes 786440 | tf_op jit(solution)/shard_map/ppermute | solution.py:26
  25.8 7.4 %attend.3.refs_1_ = f32[128,384]{1,0:T(8,128)S(1)} custom-call(s32[1,4]{1,0:T(1,128)S(1)} %copy-done.4, f32[128,512]{1,0:T(8,128)S(1)} %bitcast.34, f32[128,512]{1,0:T(8,128)S(1)} %collective-permute-done.4.refs_1_, f32[128,512]{1,0:T(8,128)S(1)} %collective-permute-done.5.refs_2_, f32[128,512]{1,0:T(8,128)S(1)} %collective-permute-done.6.refs_3_, ...), custom_call_target="tpu_custom_call" | custom-call | flops 6000000000 | bytes 2097152 | tf_op jit(solution)/shard_map/attend/pallas_call | solution.py:227
  33.3 0.6 project.1.refs_0_
  33.9 0.6 collective-permute-start.7
  34.5 2.3 %collective-permute-done.10 = f32[2,2,32,512]{3,2,1,0:T(8,128)S(1)} collective-permute-done((f32[2,2,32,512]{3,2,1,0:T(8,128)S(1)}, f32[2,2,32,512]{3,2,1,0:T(8,128)S(1)}, u32[]{:S(2)}, u32[]{:S(2)}) %collective-permute-start.10) | collective-permute-done | bytes 262176 | tf_op jit(solution)/shard_map/ppermute | solution.py:26
  36.8 0.7 collective-permute-start.11
  37.6 0.5 collective-permute-start.13
  38.1 3.0 %collective-permute-done.7.refs_1_ = f32[136,512]{1,0:T(8,128)S(1)} collective-permute-done((f32[136,512]{1,0:T(8,128)S(1)}, f32[136,512]{1,0:T(8,128)S(1)}, u32[]{:S(2)}, u32[]{:S(2)}) %collective-permute-start.7) | collective-permute-done | bytes 278560 | tf_op jit(solution)/shard_map/ppermute | solution.py:26
  41.1 0.8 collective-permute-done.11
  41.9 0.5 collective-permute-start.12
  42.4 0.4 collective-permute-done.13
  42.8 1.2 %collective-permute-start.14 = (f32[4,32,512]{2,1,0:T(8,128)S(1)}, f32[4,32,512]{2,1,0:T(8,128)S(1)}, u32[]{:S(2)}, u32[]{:S(2)}) collective-permute-start(f32[4,32,512]{2,1,0:T(8,128)S(1)} %pad_maximum_fusion.2), channel_id=1, source_target_pairs={{0,2},{1,3},{2,0},{3,1},{4,6},{5,7},{6,4},{7,5},{8,10},{9,11},{10,... | collective-permute-start | bytes 786440 | tf_op jit(solution)/shard_map/ppermute | solution.py:26
  44.1 0.3 transpose_outputs.1
  44.4 5.5 %collective-permute-done.12 = f32[4,32,512]{2,1,0:T(8,128)S(1)} collective-permute-done((f32[4,32,512]{2,1,0:T(8,128)S(1)}, f32[4,32,512]{2,1,0:T(8,128)S(1)}, u32[]{:S(2)}, u32[]{:S(2)}) %collective-permute-start.12) | collective-permute-done | bytes 262176 | tf_op jit(solution)/shard_map/ppermute | solution.py:26
  49.9 0.2 collective-permute-done.14
  50.1 3.2 %loss_terms.1 = (f32[4,32,512]{2,1,0:T(8,128)S(1)}, f32[4,32,512]{2,1,0:T(8,128)S(1)}, f32[4,32,512]{2,1,0:T(8,128)S(1)}, f32[4,32,512]{2,1,0:T(8,128)S(1)}, f32...) custom-call(bf16[512,512]{1,0:T(8,128)(2,1)S(1)} %get-tuple-element.44., ...), custom_call_target="tpu_custom_call" | custom-call | flops 1610612736 | bytes 4194304 | tf_op jit(solution)/shard_map/loss_terms/pallas_call | solution.py:366
  53.3 1.7 %collective-permute-start.15 = (f32[4,32,512]{2,1,0:T(8,128)S(1)}, f32[4,32,512]{2,1,0:T(8,128)S(1)}, u32[]{:S(2)}, u32[]{:S(2)}) collective-permute-start(f32[4,32,512]{2,1,0:T(8,128)S(1)} %get-tuple-element.48), channel_id=1, source_target_pairs={{0,1},{1,0},{2,3},{3,2},{4,5},{5,4},{6,7},{7,6},{8,9},{9,8},{10,11... | collective-permute-start | bytes 786440 | tf_op jit(solution)/shard_map/ppermute | solution.py:26
  55.0 1.6 %collective-permute-start.16 = (f32[4,32,512]{2,1,0:T(8,128)S(1)}, f32[4,32,512]{2,1,0:T(8,128)S(1)}, u32[]{:S(2)}, u32[]{:S(2)}) collective-permute-start(f32[4,32,512]{2,1,0:T(8,128)S(1)} %get-tuple-element.49), channel_id=1, source_target_pairs={{0,2},{1,3},{2,0},{3,1},{4,6},{5,7},{6,4},{7,5},{8,10},{9,11},{10,... | collective-permute-start | bytes 786440 | tf_op jit(solution)/shard_map/ppermute | solution.py:26
  56.6 1.0 event_rows.1
  57.6 2.6 %collective-permute-done.15 = f32[4,32,512]{2,1,0:T(8,128)S(1)} collective-permute-done((f32[4,32,512]{2,1,0:T(8,128)S(1)}, f32[4,32,512]{2,1,0:T(8,128)S(1)}, u32[]{:S(2)}, u32[]{:S(2)}) %collective-permute-start.15) | collective-permute-done | bytes 262176 | tf_op jit(solution)/shard_map/ppermute | solution.py:26
  60.2 1.6 %collective-permute-done.16 = f32[4,32,512]{2,1,0:T(8,128)S(1)} collective-permute-done((f32[4,32,512]{2,1,0:T(8,128)S(1)}, f32[4,32,512]{2,1,0:T(8,128)S(1)}, u32[]{:S(2)}, u32[]{:S(2)}) %collective-permute-start.16) | collective-permute-done | bytes 262176 | tf_op jit(solution)/shard_map/ppermute | solution.py:26
  61.8 0.6 collective-permute-start.19
  62.5 1.8 %collective-permute-start.18 = (f32[2,32,512]{2,1,0:T(8,128)S(1)}, f32[2,32,512]{2,1,0:T(8,128)S(1)}, u32[]{:S(2)}, u32[]{:S(2)}) collective-permute-start(f32[2,32,512]{2,1,0:T(8,128)S(1)} %get-tuple-element.74), channel_id=1, source_target_pairs={{0,2},{1,3},{2,0},{3,1},{4,6},{5,7},{6,4},{7,5},{8,10},{9,11},{10,... | collective-permute-start | bytes 393224 | tf_op jit(solution)/shard_map/ppermute | solution.py:26
  64.3 2.6 %collective-permute-done.19 = f32[2,32,512]{2,1,0:T(8,128)S(1)} collective-permute-done((f32[2,32,512]{2,1,0:T(8,128)S(1)}, f32[2,32,512]{2,1,0:T(8,128)S(1)}, u32[]{:S(2)}, u32[]{:S(2)}) %collective-permute-start.19) | collective-permute-done | bytes 131104 | tf_op jit(solution)/shard_map/ppermute | solution.py:26
  66.9 0.6 collective-permute-done.18
  67.5 0.0 copy-start.6
  67.6 3.7 %collective-permute-start.20 = (f32[136,512]{1,0:T(8,128)S(1)}, f32[136,512]{1,0:T(8,128)S(1)}, u32[]{:S(2)}, u32[]{:S(2)}) collective-permute-start(f32[136,512]{1,0:T(8,128)S(1)} %maximum_maximum_fusion), channel_id=1, source_target_pairs={{0,4},{1,5},{2,6},{3,7},{4,0},{5,1},{6,2},{7,3},{8,12},{9,13},{10,... | collective-permute-start | bytes 835592 | tf_op jit(solution)/shard_map/ppermute | solution.py:26
  71.3 0.1 slice_add_fusion
  71.4 0.6 collective-permute-start.21
  71.9 8.5 %collective-permute-done.20 = f32[136,512]{1,0:T(8,128)S(1)} collective-permute-done((f32[136,512]{1,0:T(8,128)S(1)}, f32[136,512]{1,0:T(8,128)S(1)}, u32[]{:S(2)}, u32[]{:S(2)}) %collective-permute-start.20) | collective-permute-done | bytes 278560 | tf_op jit(solution)/shard_map/ppermute | solution.py:26
  80.7 0.6 collective-permute-start.22
  81.2 1.6 %collective-permute-start.23 = (f32[64,512]{1,0:T(8,128)S(1)}, f32[64,512]{1,0:T(8,128)S(1)}, u32[]{:S(2)}, u32[]{:S(2)}) collective-permute-start(f32[64,512]{1,0:T(8,128)S(1)} %get-tuple-element.89), channel_id=1, source_target_pairs={{0,8},{8,0},{16,24},{24,16},{1,9},{9,1},{17,25},{25,17},{2,10},{10... | collective-permute-start | bytes 393224 | tf_op jit(solution)/shard_map/ppermute | solution.py:31
  82.9 4.1 %collective-permute-done.24.refs_3_ = f32[64,512]{1,0:T(8,128)S(1)} collective-permute-done((f32[64,512]{1,0:T(8,128)S(1)}, f32[64,512]{1,0:T(8,128)S(1)}, u32[]{:S(2)}, u32[]{:S(2)}) %collective-permute-start.24) | collective-permute-done | bytes 131104 | tf_op jit(solution)/shard_map/ppermute | solution.py:31
  87.0 0.2 collective-permute-done.22.refs_1_
  87.2 2.2 %spread_rows.1 = (f32[520,128]{1,0:T(8,128)S(1)}, f32[520,128]{1,0:T(8,128)S(1)}, f32[520,128]{1,0:T(8,128)S(1)}, f32[520,128]{1,0:T(8,128)S(1)}) custom-call(s32[4]{0:T(128)S(1)} %copy-done.7, s32[4,512]{1,0:T(4,128)S(1)} %copy-done.6, f32[8,128]{1,0:T(8,128)S(1)} %slice_add_fusion.12.loss, f32[64,512]{1,0:T(8,128)S(1)} %get-tuple-element.90.refs_0_, ...), custom_call_target="tpu_custom_call" | custom-call | flops 536870912 | bytes 2097152 | tf_op jit(solution)/shard_map/spread_rows/pallas_call | solution.py:442
  89.4 1.6 %collective-permute-start.26 = (f32[520,128]{1,0:T(8,128)S(1)}, f32[520,128]{1,0:T(8,128)S(1)}, u32[]{:S(2)}, u32[]{:S(2)}) collective-permute-start(f32[520,128]{1,0:T(8,128)S(1)} %get-tuple-element.65), channel_id=1, source_target_pairs={{0,1},{1,0},{2,3},{3,2},{4,5},{5,4},{6,7},{7,6},{8,9},{9,8},{10,11... | collective-permute-start | bytes 798728 | tf_op jit(solution)/shard_map/ppermute | solution.py:31
  91.1 1.9 %collective-permute-start.30 = (f32[520,128]{1,0:T(8,128)S(1)}, f32[520,128]{1,0:T(8,128)S(1)}, u32[]{:S(2)}, u32[]{:S(2)}) collective-permute-start(f32[520,128]{1,0:T(8,128)S(1)} %get-tuple-element.67), channel_id=1, source_target_pairs={{0,3},{1,2},{2,1},{3,0},{4,7},{5,6},{6,5},{7,4},{8,11},{9,10},{10,... | collective-permute-start | bytes 798728 | tf_op jit(solution)/shard_map/ppermute | solution.py:31
  93.0 0.4 collective-permute-start.25
  93.4 5.1 %collective-permute-done.26 = f32[520,128]{1,0:T(8,128)S(1)} collective-permute-done((f32[520,128]{1,0:T(8,128)S(1)}, f32[520,128]{1,0:T(8,128)S(1)}, u32[]{:S(2)}, u32[]{:S(2)}) %collective-permute-start.26) | collective-permute-done | bytes 266272 | tf_op jit(solution)/shard_map/ppermute | solution.py:31
  98.5 0.4 collective-permute-start.27
  98.9 1.4 %collective-permute-done.28 = f32[520,128]{1,0:T(8,128)S(1)} collective-permute-done((f32[520,128]{1,0:T(8,128)S(1)}, f32[520,128]{1,0:T(8,128)S(1)}, u32[]{:S(2)}, u32[]{:S(2)}) %collective-permute-start.28) | collective-permute-done | bytes 266272 | tf_op jit(solution)/shard_map/ppermute | solution.py:31
  100.3 0.1 collective-permute-start.29
  100.4 5.5 %collective-permute-done.30 = f32[520,128]{1,0:T(8,128)S(1)} collective-permute-done((f32[520,128]{1,0:T(8,128)S(1)}, f32[520,128]{1,0:T(8,128)S(1)}, u32[]{:S(2)}, u32[]{:S(2)}) %collective-permute-start.30) | collective-permute-done | bytes 266272 | tf_op jit(solution)/shard_map/ppermute | solution.py:31
  105.9 0.1 collective-permute-start.31
  106.0 1.4 %collective-permute-done.31.refs_7_ = f32[1,520,128]{2,1,0:T(8,128)S(1)} collective-permute-done((f32[1,520,128]{2,1,0:T(8,128)S(1)}, f32[1,520,128]{2,1,0:T(8,128)S(1)}, u32[]{:S(2)}, u32[]{:S(2)}) %collective-permute-start.31) | collective-permute-done | bytes 266272 | tf_op jit(solution)/shard_map/ppermute | solution.py:26
  107.5 1.9 %assemble.1 = (f32[1024,512]{1,0:T(8,128)}, f32[1,1]{1,0:T(1,128)}, f32[1,128,512]{2,1,0:T(8,128)}) custom-call(f32[1,128,512]{2,1,0:T(8,128)S(1)} %get-tuple-element.72.kept, f32[1,128,512]{2,1,0:T(8,128)S(1)} %collective-permute-done.21.got, f32[1,520,128]{2,1,0:T(8,128)S(1)} %bitcast.37, f32[1,520,128]{2,1,0:T(8,128)S(1)} %collective-permute-done.25.refs_1_, ...), custom_call_target="tpu_custom_call" | custom-call | bytes 4194304 | tf_op jit(solution)/shard_map/assemble/pallas_call | solution.py:490
  (64 shorter events, 0.5 us)
Async XLA Ops:
  0.6 8.2 %copy-start.1 = (f32[1,128,512]{2,1,0:T(8,128)S(1)}, f32[1,128,512]{2,1,0:T(8,128)}, u32[]{:S(2)}) copy-start(f32[1,128,512]{2,1,0:T(8,128)} %param.10) | copy-start | bytes 786436
  0.6 10.5 %copy-start.7 = (s32[4]{0:T(128)S(1)}, s32[4]{0:T(128)}, u32[]{:S(2)}) copy-start(s32[4]{0:T(128)} %owner.1) | copy-start | bytes 52
  0.7 15.6 %collective-permute-start.4 = (f32[128,512]{1,0:T(8,128)}, f32[128,512]{1,0:T(8,128)S(1)}, u32[]{:S(2)}, u32[]{:S(2)}) collective-permute-start(f32[128,512]{1,0:T(8,128)} %bitcast.30), channel_id=1, source_target_pairs={{0,16},{8,24},{16,0},{24,8},{1,17},{9,25},{17,1},{25,9},{2,18},{10... | collective-permute-start | bytes 786440 | tf_op jit(solution)/shard_map/ppermute | solution.py:26
  7.3 9.2 %collective-permute-start = (f32[4,32,512]{2,1,0:T(8,128)}, f32[4,32,512]{2,1,0:T(8,128)S(1)}, u32[]{:S(2)}, u32[]{:S(2)}) collective-permute-start(f32[4,32,512]{2,1,0:T(8,128)} %get-tuple-element.38), channel_id=1, source_target_pairs={{0,1},{1,0},{2,3},{3,2},{4,5},{5,4},{6,7},{7,6},{8,9},{9,8},{10,11... | collective-permute-start | bytes 786440 | tf_op jit(solution)/shard_map/ppermute | solution.py:26
  8.9 9.7 %collective-permute-start.5 = (f32[128,512]{1,0:T(8,128)S(1)}, f32[128,512]{1,0:T(8,128)S(1)}, u32[]{:S(2)}, u32[]{:S(2)}) collective-permute-start(f32[128,512]{1,0:T(8,128)S(1)} %bitcast.31), channel_id=1, source_target_pairs={{0,8},{8,0},{16,24},{24,16},{1,9},{9,1},{17,25},{25,17},{2,10},{10... | collective-permute-start | bytes 786440 | tf_op jit(solution)/shard_map/ppermute | solution.py:26
  8.9 8.9 %collective-permute-start.2 = (f32[4,32,512]{2,1,0:T(8,128)}, f32[4,32,512]{2,1,0:T(8,128)S(1)}, u32[]{:S(2)}, u32[]{:S(2)}) collective-permute-start(f32[4,32,512]{2,1,0:T(8,128)} %get-tuple-element.40), channel_id=1, source_target_pairs={{0,2},{1,3},{2,0},{3,1},{4,6},{5,7},{6,4},{7,5},{8,10},{9,11},{10,... | collective-permute-start | bytes 786440 | tf_op jit(solution)/shard_map/ppermute | solution.py:26
  12.4 2.2 %copy-start = (f32[512,2048]{1,0:T(8,128)S(1)}, f32[512,2048]{1,0:T(8,128)}, u32[]{:S(2)}) copy-start(f32[512,2048]{1,0:T(8,128)} %refs_6_.4) | copy-start | bytes 12582916
  14.6 1.9 %copy-start.8 = (f32[4,32,512]{2,1,0:T(8,128)S(1)}, f32[4,32,512]{2,1,0:T(8,128)}, u32[]{:S(2)}) copy-start(f32[4,32,512]{2,1,0:T(8,128)} %get-tuple-element.37) | copy-start | bytes 786436
  14.6 3.3 %copy-start.9 = (f32[4,32,512]{2,1,0:T(8,128)S(1)}, f32[4,32,512]{2,1,0:T(8,128)}, u32[]{:S(2)}) copy-start(f32[4,32,512]{2,1,0:T(8,128)} %get-tuple-element.39) | copy-start | bytes 786436
  14.6 4.1 %copy-start.4 = (s32[1,4]{1,0:T(1,128)S(1)}, s32[1,4]{1,0:T(1,128)}, u32[]{:S(2)}) copy-start(s32[1,4]{1,0:T(1,128)} %lengths.3) | copy-start | bytes 52
  16.2 2.4 %collective-permute-start.6 = (f32[128,512]{1,0:T(8,128)S(1)}, f32[128,512]{1,0:T(8,128)S(1)}, u32[]{:S(2)}, u32[]{:S(2)}) collective-permute-start(f32[128,512]{1,0:T(8,128)S(1)} %collective-permute-done.4.refs_1_), channel_id=1, source_target_pairs={{0,8},{8,0},{16,24},{24,16},{1,9},{9,1},{17,25},{25,17},{2,10},{10... | collective-permute-start | bytes 786440 | tf_op jit(solution)/shard_map/ppermute | solution.py:26
  16.5 5.8 %collective-permute-start.1 = (f32[2,32,512]{2,1,0:T(8,128)S(1)}, f32[2,32,512]{2,1,0:T(8,128)S(1)}, u32[]{:S(2)}, u32[]{:S(2)}) collective-permute-start(f32[2,32,512]{2,1,0:T(8,128)S(1)} %slice_select_fusion.3), channel_id=1, source_target_pairs={{0,2},{1,3},{2,0},{3,1},{4,6},{5,7},{6,4},{7,5},{8,10},{9,11},{10,... | collective-permute-start | bytes 393224 | tf_op jit(solution)/shard_map/ppermute | solution.py:26
  17.8 5.2 %collective-permute-start.3 = (f32[2,32,512]{2,1,0:T(8,128)S(1)}, f32[2,32,512]{2,1,0:T(8,128)S(1)}, u32[]{:S(2)}, u32[]{:S(2)}) collective-permute-start(f32[2,32,512]{2,1,0:T(8,128)S(1)} %slice_select_fusion.2), channel_id=1, source_target_pairs={{0,1},{1,0},{2,3},{3,2},{4,5},{5,4},{6,7},{7,6},{8,9},{9,8},{10,11... | collective-permute-start | bytes 393224 | tf_op jit(solution)/shard_map/ppermute | solution.py:26
  23.1 10.1 %copy-start.2 = (f32[512,512]{1,0:T(8,128)S(1)}, f32[512,512]{1,0:T(8,128)}, u32[]{:S(2)}) copy-start(f32[512,512]{1,0:T(8,128)} %refs_4_.1) | copy-start | bytes 3145732
  23.1 10.1 %copy-start.3 = (f32[512]{0:T(512)S(1)}, f32[512]{0:T(512)}, u32[]{:S(2)}) copy-start(f32[512]{0:T(512)} %param.12) | copy-start | bytes 6148
  23.1 10.1 %copy-start.5 = (s32[1,128]{1,0:T(1,128)S(1)}, s32[1,128]{1,0:T(1,128)}, u32[]{:S(2)}) copy-start(s32[1,128]{1,0:T(1,128)} %refs_6_.5) | copy-start | bytes 1540
  23.2 13.6 %collective-permute-start.10 = (f32[2,2,32,512]{3,2,1,0:T(8,128)S(1)}, f32[2,2,32,512]{3,2,1,0:T(8,128)S(1)}, u32[]{:S(2)}, u32[]{:S(2)}) collective-permute-start(f32[2,2,32,512]{3,2,1,0:T(8,128)S(1)} %pad_maximum_fusion), channel_id=1, source_target_pairs={{0,4},{1,5},{2,6},{3,7},{4,0},{5,1},{6,2},{7,3},{8,12},{9,13},{10,... | collective-permute-start | bytes 786440 | tf_op jit(solution)/shard_map/ppermute | solution.py:26
  33.9 7.2 %collective-permute-start.7 = (f32[136,512]{1,0:T(8,128)S(1)}, f32[136,512]{1,0:T(8,128)S(1)}, u32[]{:S(2)}, u32[]{:S(2)}) collective-permute-start(f32[136,512]{1,0:T(8,128)S(1)} %project.1.refs_0_), channel_id=1, source_target_pairs={{0,16},{8,24},{16,0},{24,8},{1,17},{9,25},{17,1},{25,9},{2,18},{10... | collective-permute-start | bytes 835592 | tf_op jit(solution)/shard_map/ppermute | solution.py:26
  36.8 5.0 %collective-permute-start.11 = (f32[2,32,512]{2,1,0:T(8,128)S(1)}, f32[2,32,512]{2,1,0:T(8,128)S(1)}, u32[]{:S(2)}, u32[]{:S(2)}) collective-permute-start(f32[2,32,512]{2,1,0:T(8,128)S(1)} %maximum_select_fusion), channel_id=1, source_target_pairs={{0,2},{1,3},{2,0},{3,1},{4,6},{5,7},{6,4},{7,5},{8,10},{9,11},{10,... | collective-permute-start | bytes 393224 | tf_op jit(solution)/shard_map/ppermute | solution.py:26
  37.6 5.2 %collective-permute-start.13 = (f32[2,32,512]{2,1,0:T(8,128)S(1)}, f32[2,32,512]{2,1,0:T(8,128)S(1)}, u32[]{:S(2)}, u32[]{:S(2)}) collective-permute-start(f32[2,32,512]{2,1,0:T(8,128)S(1)} %maximum_select_fusion.1), channel_id=1, source_target_pairs={{0,1},{1,0},{2,3},{3,2},{4,5},{5,4},{6,7},{7,6},{8,9},{9,8},{10,11... | collective-permute-start | bytes 393224 | tf_op jit(solution)/shard_map/ppermute | solution.py:26
  38.1 6.0 %collective-permute-start.8 = (f32[136,512]{1,0:T(8,128)S(1)}, f32[136,512]{1,0:T(8,128)S(1)}, u32[]{:S(2)}, u32[]{:S(2)}) collective-permute-start(f32[136,512]{1,0:T(8,128)S(1)} %project.1.refs_0_), channel_id=1, source_target_pairs={{0,8},{8,0},{16,24},{24,16},{1,9},{9,1},{17,25},{25,17},{2,10},{10... | collective-permute-start | bytes 835592 | tf_op jit(solution)/shard_map/ppermute | solution.py:26
  41.1 3.0 %collective-permute-start.9 = (f32[136,512]{1,0:T(8,128)S(1)}, f32[136,512]{1,0:T(8,128)S(1)}, u32[]{:S(2)}, u32[]{:S(2)}) collective-permute-start(f32[136,512]{1,0:T(8,128)S(1)} %collective-permute-done.7.refs_1_), channel_id=1, source_target_pairs={{0,8},{8,0},{16,24},{24,16},{1,9},{9,1},{17,25},{25,17},{2,10},{10... | collective-permute-start | bytes 835592 | tf_op jit(solution)/shard_map/ppermute | solution.py:26
  41.9 8.0 %collective-permute-start.12 = (f32[4,32,512]{2,1,0:T(8,128)S(1)}, f32[4,32,512]{2,1,0:T(8,128)S(1)}, u32[]{:S(2)}, u32[]{:S(2)}) collective-permute-start(f32[4,32,512]{2,1,0:T(8,128)S(1)} %pad_maximum_fusion.1), channel_id=1, source_target_pairs={{0,1},{1,0},{2,3},{3,2},{4,5},{5,4},{6,7},{7,6},{8,9},{9,8},{10,11... | collective-permute-start | bytes 786440 | tf_op jit(solution)/shard_map/ppermute | solution.py:26
  42.8 7.3 %collective-permute-start.14 = (f32[4,32,512]{2,1,0:T(8,128)S(1)}, f32[4,32,512]{2,1,0:T(8,128)S(1)}, u32[]{:S(2)}, u32[]{:S(2)}) collective-permute-start(f32[4,32,512]{2,1,0:T(8,128)S(1)} %pad_maximum_fusion.2), channel_id=1, source_target_pairs={{0,2},{1,3},{2,0},{3,1},{4,6},{5,7},{6,4},{7,5},{8,10},{9,11},{10,... | collective-permute-start | bytes 786440 | tf_op jit(solution)/shard_map/ppermute | solution.py:26
  53.3 6.9 %collective-permute-start.15 = (f32[4,32,512]{2,1,0:T(8,128)S(1)}, f32[4,32,512]{2,1,0:T(8,128)S(1)}, u32[]{:S(2)}, u32[]{:S(2)}) collective-permute-start(f32[4,32,512]{2,1,0:T(8,128)S(1)} %get-tuple-element.48), channel_id=1, source_target_pairs={{0,1},{1,0},{2,3},{3,2},{4,5},{5,4},{6,7},{7,6},{8,9},{9,8},{10,11... | collective-permute-start | bytes 786440 | tf_op jit(solution)/shard_map/ppermute | solution.py:26
  55.0 6.8 %collective-permute-start.16 = (f32[4,32,512]{2,1,0:T(8,128)S(1)}, f32[4,32,512]{2,1,0:T(8,128)S(1)}, u32[]{:S(2)}, u32[]{:S(2)}) collective-permute-start(f32[4,32,512]{2,1,0:T(8,128)S(1)} %get-tuple-element.49), channel_id=1, source_target_pairs={{0,2},{1,3},{2,0},{3,1},{4,6},{5,7},{6,4},{7,5},{8,10},{9,11},{10,... | collective-permute-start | bytes 786440 | tf_op jit(solution)/shard_map/ppermute | solution.py:26
  61.8 5.0 %collective-permute-start.19 = (f32[2,32,512]{2,1,0:T(8,128)S(1)}, f32[2,32,512]{2,1,0:T(8,128)S(1)}, u32[]{:S(2)}, u32[]{:S(2)}) collective-permute-start(f32[2,32,512]{2,1,0:T(8,128)S(1)} %get-tuple-element.76), channel_id=1, source_target_pairs={{0,1},{1,0},{2,3},{3,2},{4,5},{5,4},{6,7},{7,6},{8,9},{9,8},{10,11... | collective-permute-start | bytes 393224 | tf_op jit(solution)/shard_map/ppermute | solution.py:26
  62.5 5.0 %collective-permute-start.18 = (f32[2,32,512]{2,1,0:T(8,128)S(1)}, f32[2,32,512]{2,1,0:T(8,128)S(1)}, u32[]{:S(2)}, u32[]{:S(2)}) collective-permute-start(f32[2,32,512]{2,1,0:T(8,128)S(1)} %get-tuple-element.74), channel_id=1, source_target_pairs={{0,2},{1,3},{2,0},{3,1},{4,6},{5,7},{6,4},{7,5},{8,10},{9,11},{10,... | collective-permute-start | bytes 393224 | tf_op jit(solution)/shard_map/ppermute | solution.py:26
  64.3 7.0 %collective-permute-start.17 = (f32[2,128,512]{2,1,0:T(8,128)S(1)}, f32[2,128,512]{2,1,0:T(8,128)S(1)}, u32[]{:S(2)}, u32[]{:S(2)}) collective-permute-start(f32[2,128,512]{2,1,0:T(8,128)S(1)} %get-tuple-element.56), channel_id=1, source_target_pairs={{0,8},{8,0},{16,24},{24,16},{1,9},{9,1},{17,25},{25,17},{2,10},{10... | collective-permute-start | bytes 1572872 | tf_op jit(solution)/shard_map/ppermute | solution.py:26
  67.5 19.7 %copy-start.6 = (s32[4,512]{1,0:T(4,128)S(1)}, s32[4,512]{1,0:T(4,128)}, u32[]{:S(2)}) copy-start(s32[4,512]{1,0:T(4,128)} %ids.1) | copy-start | bytes 24580
  67.6 12.8 %collective-permute-start.20 = (f32[136,512]{1,0:T(8,128)S(1)}, f32[136,512]{1,0:T(8,128)S(1)}, u32[]{:S(2)}, u32[]{:S(2)}) collective-permute-start(f32[136,512]{1,0:T(8,128)S(1)} %maximum_maximum_fusion), channel_id=1, source_target_pairs={{0,4},{1,5},{2,6},{3,7},{4,0},{5,1},{6,2},{7,3},{8,12},{9,13},{10,... | collective-permute-start | bytes 835592 | tf_op jit(solution)/shard_map/ppermute | solution.py:26
  71.4 9.1 %collective-permute-start.21 = (f32[1,128,512]{2,1,0:T(8,128)S(1)}, f32[1,128,512]{2,1,0:T(8,128)S(1)}, u32[]{:S(2)}, u32[]{:S(2)}) collective-permute-start(f32[1,128,512]{2,1,0:T(8,128)S(1)} %get-tuple-element.71), channel_id=1, source_target_pairs={{0,16},{8,24},{16,0},{24,8},{1,17},{9,25},{17,1},{25,9},{2,18},{10... | collective-permute-start | bytes 786440 | tf_op jit(solution)/shard_map/ppermute | solution.py:26
  80.7 6.5 %collective-permute-start.22 = (f32[72,512]{1,0:T(8,128)S(1)}, f32[72,512]{1,0:T(8,128)S(1)}, u32[]{:S(2)}, u32[]{:S(2)}) collective-permute-start(f32[72,512]{1,0:T(8,128)S(1)} %constant_dynamic-update-slice_fusion.8), channel_id=1, source_target_pairs={{0,16},{8,24},{16,0},{24,8},{1,17},{9,25},{17,1},{25,9},{2,18},{10... | collective-permute-start | bytes 442376 | tf_op jit(solution)/shard_map/ppermute | solution.py:31
  81.2 5.7 %collective-permute-start.24 = (f32[64,512]{1,0:T(8,128)S(1)}, f32[64,512]{1,0:T(8,128)S(1)}, u32[]{:S(2)}, u32[]{:S(2)}) collective-permute-start(f32[64,512]{1,0:T(8,128)S(1)} %get-tuple-element.87), channel_id=1, source_target_pairs={{0,24},{8,16},{16,8},{24,0},{1,25},{9,17},{17,9},{25,1},{2,26},{10... | collective-permute-start | bytes 393224 | tf_op jit(solution)/shard_map/ppermute | solution.py:31
  81.2 5.7 %collective-permute-start.23 = (f32[64,512]{1,0:T(8,128)S(1)}, f32[64,512]{1,0:T(8,128)S(1)}, u32[]{:S(2)}, u32[]{:S(2)}) collective-permute-start(f32[64,512]{1,0:T(8,128)S(1)} %get-tuple-element.89), channel_id=1, source_target_pairs={{0,8},{8,0},{16,24},{24,16},{1,9},{9,1},{17,25},{25,17},{2,10},{10... | collective-permute-start | bytes 393224 | tf_op jit(solution)/shard_map/ppermute | solution.py:31
  89.4 9.1 %collective-permute-start.26 = (f32[520,128]{1,0:T(8,128)S(1)}, f32[520,128]{1,0:T(8,128)S(1)}, u32[]{:S(2)}, u32[]{:S(2)}) collective-permute-start(f32[520,128]{1,0:T(8,128)S(1)} %get-tuple-element.65), channel_id=1, source_target_pairs={{0,1},{1,0},{2,3},{3,2},{4,5},{5,4},{6,7},{7,6},{8,9},{9,8},{10,11... | collective-permute-start | bytes 798728 | tf_op jit(solution)/shard_map/ppermute | solution.py:31
  91.1 9.3 %collective-permute-start.28 = (f32[520,128]{1,0:T(8,128)S(1)}, f32[520,128]{1,0:T(8,128)S(1)}, u32[]{:S(2)}, u32[]{:S(2)}) collective-permute-start(f32[520,128]{1,0:T(8,128)S(1)} %get-tuple-element.66), channel_id=1, source_target_pairs={{0,2},{1,3},{2,0},{3,1},{4,6},{5,7},{6,4},{7,5},{8,10},{9,11},{10,... | collective-permute-start | bytes 798728 | tf_op jit(solution)/shard_map/ppermute | solution.py:31
  91.1 14.9 %collective-permute-start.30 = (f32[520,128]{1,0:T(8,128)S(1)}, f32[520,128]{1,0:T(8,128)S(1)}, u32[]{:S(2)}, u32[]{:S(2)}) collective-permute-start(f32[520,128]{1,0:T(8,128)S(1)} %get-tuple-element.67), channel_id=1, source_target_pairs={{0,3},{1,2},{2,1},{3,0},{4,7},{5,6},{6,5},{7,4},{8,11},{9,10},{10,... | collective-permute-start | bytes 798728 | tf_op jit(solution)/shard_map/ppermute | solution.py:31
  93.0 13.0 %collective-permute-start.25 = (f32[1,520,128]{2,1,0:T(8,128)S(1)}, f32[1,520,128]{2,1,0:T(8,128)S(1)}, u32[]{:S(2)}, u32[]{:S(2)}) collective-permute-start(f32[1,520,128]{2,1,0:T(8,128)S(1)} %bitcast.36), channel_id=1, source_target_pairs={{0,8},{8,0},{16,24},{24,16},{1,9},{9,1},{17,25},{25,17},{2,10},{10... | collective-permute-start | bytes 798728 | tf_op jit(solution)/shard_map/ppermute | solution.py:26
  98.5 7.5 %collective-permute-start.27 = (f32[1,520,128]{2,1,0:T(8,128)S(1)}, f32[1,520,128]{2,1,0:T(8,128)S(1)}, u32[]{:S(2)}, u32[]{:S(2)}) collective-permute-start(f32[1,520,128]{2,1,0:T(8,128)S(1)} %bitcast.38), channel_id=1, source_target_pairs={{0,8},{8,0},{16,24},{24,16},{1,9},{9,1},{17,25},{25,17},{2,10},{10... | collective-permute-start | bytes 798728 | tf_op jit(solution)/shard_map/ppermute | solution.py:26
  100.3 5.7 %collective-permute-start.29 = (f32[1,520,128]{2,1,0:T(8,128)S(1)}, f32[1,520,128]{2,1,0:T(8,128)S(1)}, u32[]{:S(2)}, u32[]{:S(2)}) collective-permute-start(f32[1,520,128]{2,1,0:T(8,128)S(1)} %bitcast.40), channel_id=1, source_target_pairs={{0,8},{8,0},{16,24},{24,16},{1,9},{9,1},{17,25},{25,17},{2,10},{10... | collective-permute-start | bytes 798728 | tf_op jit(solution)/shard_map/ppermute | solution.py:26
  105.9 1.5 %collective-permute-start.31 = (f32[1,520,128]{2,1,0:T(8,128)S(1)}, f32[1,520,128]{2,1,0:T(8,128)S(1)}, u32[]{:S(2)}, u32[]{:S(2)}) collective-permute-start(f32[1,520,128]{2,1,0:T(8,128)S(1)} %bitcast.42), channel_id=1, source_target_pairs={{0,8},{8,0},{16,24},{24,16},{1,9},{9,1},{17,25},{25,17},{2,10},{10... | collective-permute-start | bytes 798728 | tf_op jit(solution)/shard_map/ppermute | solution.py:26
